TPU v7x, 32 devices: a whole 2x2x4 slice. The times are simulated.
32 devices in a mesh: head: 4 (over x, core), blk: 8 (over z, y).
Axes of the slice: x: 2, y: 2, z: 4, core: 2. Of those that a mesh axis runs over, the one named last changes fastest.
Arguments:
- queries: bfloat16 [1, 2816, 640], P(None, ('blk', 'head')), may hold values from -6 to 6
- keys: bfloat16 [1, 2816, 640], P(None, ('blk', 'head')), may hold values from -6 to 6
- values: bfloat16 [1, 2816, 640], P(None, ('blk', 'head')), may hold values from -6 to 6
- outputs: bfloat16 [1, 2816, 640], P(None, ('blk', 'head')), may hold values from -6 to 6
- grad_out: bfloat16 [1, 2816, 640], P(None, ('blk', 'head')), may hold values from -384 to 384
- lse: float32 [1, 8, 2816], P(None, 'head', 'blk'), may hold values from 8.5 to 10
Outputs:
- grad_queries: bfloat16 [1, 2816, 640], P(None, ('blk', 'head'))
- grad_keys: bfloat16 [1, 2816, 640], P(None, ('blk', 'head'))
- grad_values: bfloat16 [1, 2816, 640], P(None, ('blk', 'head'))
All inputs are finite; a program needn't handle non-finite values.
Results may differ from a plain program's by a relative error of at most 0.0085.
Values may be sent and summed in bfloat16 or wider, within the bound.
No kernel may reach another device: no remote copies, remote signals or barrier semaphores. Data moves between devices by JAX's collectives and lax.ppermute only.
A program may use at most 64 MiB of HBM per device.

v0:
```python
import jax
import jax.numpy as jnp
from jax import lax
from jax.sharding import PartitionSpec as P

HDIM = 80


def shifted(block, axis, distance):
    devices = range(lax.axis_size(axis))
    route = [((i - distance) % len(devices), i) for i in devices]
    return lax.ppermute(block, axis, route)


def tile_terms(query_h, cotan_h, lse_rows, delta_rows, key_h, value_h):
    scaling = HDIM ** (-0.5)
    query_rows = query_h.shape[0]
    key_rows = key_h.shape[0]
    groups = query_h.shape[1]
    scores = (
        jnp.einsum("qhd,khd->hqk", query_h, key_h, preferred_element_type=jnp.float32) * scaling
    )
    probs = jnp.exp(scores - lse_rows[:, :, None])
    probs16 = probs.astype(jnp.bfloat16)
    value_part = jnp.einsum("hqk,qhd->khd", probs16, cotan_h, preferred_element_type=jnp.float32)
    dprobs = jnp.einsum("qhd,khd->hqk", cotan_h, value_h, preferred_element_type=jnp.float32)
    dscores = (probs * (dprobs - delta_rows[:, :, None])).astype(jnp.bfloat16)
    query_part = jnp.einsum("hqk,khd->qhd", dscores, key_h, preferred_element_type=jnp.float32)
    key_part = jnp.einsum("hqk,qhd->khd", dscores, query_h, preferred_element_type=jnp.float32)
    return (
        query_part.reshape(query_rows, groups * HDIM),
        key_part.reshape(key_rows, groups * HDIM),
        value_part.reshape(key_rows, groups * HDIM),
    )


def crop_terms(query_h, cotan_h, lse_rows, delta_rows, key_h, value_h):
    return lax.map(
        lambda pieces: tile_terms(*pieces), (query_h, cotan_h, lse_rows, delta_rows, key_h, value_h)
    )


def body(queries, keys, values, outputs, grad_out, lse):
    scaling = HDIM ** (-0.5)
    crops = queries.shape[0]
    groups = lse.shape[1]
    rows = lse.shape[2]
    sent = (queries, keys, values, grad_out, outputs)
    moved = (
        lax.all_to_all(sent[0], "head", split_axis=2, concat_axis=1, tiled=True),
        lax.all_to_all(sent[1], "head", split_axis=2, concat_axis=1, tiled=True),
        lax.all_to_all(sent[2], "head", split_axis=2, concat_axis=1, tiled=True),
        lax.all_to_all(sent[3], "head", split_axis=2, concat_axis=1, tiled=True),
        lax.all_to_all(sent[4], "head", split_axis=2, concat_axis=1, tiled=True),
    )
    query_own, key_own, value_own, cotan_own = (moved[0], moved[1], moved[2], moved[3])
    output_own = moved[4]
    products = cotan_own.astype(jnp.float32) * output_own.astype(jnp.float32)
    delta_rows = jnp.transpose(
        jnp.sum(products.reshape(crops, rows, groups, HDIM), axis=-1), (0, 2, 1)
    )
    query_h = query_own.reshape(crops, rows, groups, HDIM)
    cotan_h = cotan_own.reshape(crops, rows, groups, HDIM)
    key_h = key_own.reshape(crops, rows, groups, HDIM)
    value_h = value_own.reshape(crops, rows, groups, HDIM)
    width = groups * HDIM
    nblocks = lax.axis_size("blk")
    zeros_acc = jnp.zeros((crops, rows, width), jnp.float32)
    start = (query_h, cotan_h, lse, delta_rows, zeros_acc, zeros_acc, zeros_acc)

    def cycle_step(index, carry):
        query_cur, cotan_cur, lse_cur, delta_cur, query_acc, key_acc, value_acc = carry
        query_part, key_part, value_part = crop_terms(
            query_cur, cotan_cur, lse_cur, delta_cur, key_h, value_h
        )
        query_acc, lse_cur, delta_cur = shifted(
            (query_acc + query_part, lse_cur, delta_cur), "blk", 1
        )
        query_cur, cotan_cur = shifted((query_cur, cotan_cur), "blk", 1)
        return (
            query_cur,
            cotan_cur,
            lse_cur,
            delta_cur,
            query_acc,
            key_acc + key_part,
            value_acc + value_part,
        )

    query_cur, cotan_cur, lse_cur, delta_cur, query_acc, key_acc, value_acc = lax.fori_loop(
        0, nblocks - 1, cycle_step, start
    )
    query_part, key_part, value_part = crop_terms(
        query_cur, cotan_cur, lse_cur, delta_cur, key_h, value_h
    )
    query_total = shifted((query_acc + query_part).astype(jnp.bfloat16), "blk", 1).astype(
        jnp.float32
    )
    key_total = key_acc + key_part
    value_total = value_acc + value_part
    grad_q16 = (query_total * scaling).astype(jnp.bfloat16)
    grad_k16 = (key_total * scaling).astype(jnp.bfloat16)
    grad_v16 = value_total.astype(jnp.bfloat16)
    grad_queries, grad_keys, grad_values = (
        lax.all_to_all(grad_q16, "head", split_axis=1, concat_axis=2, tiled=True),
        lax.all_to_all(grad_k16, "head", split_axis=1, concat_axis=2, tiled=True),
        lax.all_to_all(grad_v16, "head", split_axis=1, concat_axis=2, tiled=True),
    )
    return (grad_queries, grad_keys, grad_values)


def solution(mesh):
    placed = (
        P(None, ("blk", "head"), None),
        P(None, ("blk", "head"), None),
        P(None, ("blk", "head"), None),
        P(None, ("blk", "head"), None),
        P(None, ("blk", "head"), None),
        P(None, "head", "blk"),
    )
    return jax.shard_map(
        body,
        mesh=mesh,
        in_specs=placed,
        out_specs=(
            P(None, ("blk", "head"), None),
            P(None, ("blk", "head"), None),
            P(None, ("blk", "head"), None),
        ),
        check_vma=False,
    )
```

profile of v0, /device:TPU:0, one launch (start us, length us, event | category | flops | bytes accessed | tf_op | source)
XLA Modules:
  0.0 187.3 jit_solution(13242001888745762578)
XLA Ops:
  2.3 1.7 reduce.1
  4.9 4.2 %all-to-all-start = ((bf16[4,2,7040]{2,1,0:T(2,128)(2,1)}), bf16[4,2,7040]{2,1,0:T(2,128)(2,1)S(1)}, u32[]{:S(2)}, u32[]{:S(2)}) async-start(bf16[4,2,7040]{2,1,0:T(2,128)(2,1)} %reshape.92), calls=%async_computation | async-start | bytes 225280 | tf_op jit(solution)/shard_map/all_to_all | solution.py:50
  9.3 1.7 reduce.4
  11.9 1.6 all-to-all-done
  13.5 3.3 %all-to-all-start.3 = ((bf16[4,2,7040]{2,1,0:T(2,128)(2,1)}), bf16[4,2,7040]{2,1,0:T(2,128)(2,1)S(1)}, u32[]{:S(2)}, u32[]{:S(2)}) async-start(bf16[4,2,7040]{2,1,0:T(2,128)(2,1)} %reshape.98), calls=%async_computation.3 | async-start | bytes 225280 | tf_op jit(solution)/shard_map/all_to_all | solution.py:51
  17.1 1.7 reduce.5
  21.3 3.3 %all-to-all-start.4 = ((bf16[4,2,7040]{2,1,0:T(2,128)(2,1)}), bf16[4,2,7040]{2,1,0:T(2,128)(2,1)S(1)}, u32[]{:S(2)}, u32[]{:S(2)}) async-start(bf16[4,2,7040]{2,1,0:T(2,128)(2,1)} %reshape.100), calls=%async_computation.4 | async-start | bytes 225280 | tf_op jit(solution)/shard_map/all_to_all | solution.py:52
  24.8 1.7 reduce.3
  27.4 1.6 all-to-all-done.4
  29.0 3.3 %all-to-all-start.2 = ((bf16[4,2,7040]{2,1,0:T(2,128)(2,1)}), bf16[4,2,7040]{2,1,0:T(2,128)(2,1)S(1)}, u32[]{:S(2)}, u32[]{:S(2)}) async-start(bf16[4,2,7040]{2,1,0:T(2,128)(2,1)} %reshape.96), calls=%async_computation.2 | async-start | bytes 225280 | tf_op jit(solution)/shard_map/all_to_all | solution.py:54
  32.5 1.7 reduce.2
  35.1 1.6 all-to-all-done.2
  36.7 3.5 %all-to-all-start.1 = ((bf16[4,2,7040]{2,1,0:T(2,128)(2,1)}), bf16[4,2,7040]{2,1,0:T(2,128)(2,1)S(1)}, u32[]{:S(2)}, u32[]{:S(2)}) async-start(bf16[4,2,7040]{2,1,0:T(2,128)(2,1)} %reshape.94), calls=%async_computation.1 | async-start | bytes 225280 | tf_op jit(solution)/shard_map/all_to_all | solution.py:53
  47.4 110.4 %while.5 = (s32[]{:T(128)}, bf16[1,352,2,80]{1,3,2,0:T(8,128)(2,1)S(1)}, bf16[1,352,2,80]{1,3,2,0:T(8,128)(2,1)S(1)}, f32[1,2,352]{2,1,0:T(2,128)S(1)}, f32[1,2,...) while((s32[]{:T(128)}, ...), condition=%wide.region_2.3_spmd.clone, body=%wide.region_1.2_spmd.clone.sunk | while | flops 200014848 | bytes 10244935 | solution.py:90
  47.4 2.1 %collective-permute-start.2 = (f32[1,2,352]{2,1,0:T(2,128)S(1)}, f32[1,2,352]{2,1,0:T(2,128)S(1)}, u32[]{:S(2)}, u32[]{:S(2)}) collective-permute-start(f32[1,2,352]{2,1,0:T(2,128)S(1)} %copy.124), channel_id=1, source_target_pairs={{7,0},{0,1},{1,2},{2,3},{3,4},{4,5},{5,6},{6,7},{15,8},{8,9},{9,10... | collective-permute-start | bytes 8456 | tf_op jit(solution)/shard_map/while/body/eval_jaxpr/ppermute | solution.py:12
  51.0 1.6 collective-permute-start
  57.5 2.5 %collective-permute-done = bf16[1,352,2,80]{1,3,2,0:T(8,128)(2,1)S(1)} collective-permute-done((bf16[1,352,2,80]{1,3,2,0:T(8,128)(2,1)S(1)}, bf16[1,352,2,80]{1,3,2,0:T(8,128)(2,1)S(1)}, u32[]{:S(2)}, u32[]{:S(2)}) %collective-permute-start) | collective-permute-done | bytes 112672 | tf_op jit(solution)/shard_map/while/body/eval_jaxpr/ppermute | solution.py:12
  60.0 2.6 %collective-permute-done.1 = bf16[1,352,2,80]{1,3,2,0:T(8,128)(2,1)S(1)} collective-permute-done((bf16[1,352,2,80]{1,3,2,0:T(8,128)(2,1)S(1)}, bf16[1,352,2,80]{1,3,2,0:T(8,128)(2,1)S(1)}, u32[]{:S(2)}, u32[]{:S(2)}) %collective-permute-start.1) | collective-permute-done | bytes 112672 | tf_op jit(solution)/shard_map/while/body/eval_jaxpr/ppermute | solution.py:12
  62.7 4.0 %collective-permute-done.4 = f32[1,352,160]{1,2,0:T(8,128)S(1)} collective-permute-done((f32[1,352,160]{1,2,0:T(8,128)S(1)}, f32[1,352,160]{1,2,0:T(8,128)S(1)}, u32[]{:S(2)}, u32[]{:S(2)}) %collective-permute-start.4) | collective-permute-done | bytes 225312 | tf_op jit(solution)/shard_map/while/body/eval_jaxpr/ppermute | solution.py:12
  68.6 2.5 %collective-permute-start.1 = (bf16[1,352,2,80]{1,3,2,0:T(8,128)(2,1)S(1)}, bf16[1,352,2,80]{1,3,2,0:T(8,128)(2,1)S(1)}, u32[]{:S(2)}, u32[]{:S(2)}) collective-permute-start(bf16[1,352,2,80]{1,3,2,0:T(8,128)(2,1)S(1)} %copy.123), channel_id=1, source_target_pairs={{7,0},{0,1},{1,2},{2,3},{3,4},{4,5},{5,6},{6,7},{15,8},{8,9},{9,10... | collective-permute-start | bytes 337928 | tf_op jit(solution)/shard_map/while/body/eval_jaxpr/ppermute | solution.py:12
  73.4 2.4 %collective-permute-done = bf16[1,352,2,80]{1,3,2,0:T(8,128)(2,1)S(1)} collective-permute-done((bf16[1,352,2,80]{1,3,2,0:T(8,128)(2,1)S(1)}, bf16[1,352,2,80]{1,3,2,0:T(8,128)(2,1)S(1)}, u32[]{:S(2)}, u32[]{:S(2)}) %collective-permute-start) | collective-permute-done | bytes 112672 | tf_op jit(solution)/shard_map/while/body/eval_jaxpr/ppermute | solution.py:12
  75.9 2.6 %collective-permute-done.1 = bf16[1,352,2,80]{1,3,2,0:T(8,128)(2,1)S(1)} collective-permute-done((bf16[1,352,2,80]{1,3,2,0:T(8,128)(2,1)S(1)}, bf16[1,352,2,80]{1,3,2,0:T(8,128)(2,1)S(1)}, u32[]{:S(2)}, u32[]{:S(2)}) %collective-permute-start.1) | collective-permute-done | bytes 112672 | tf_op jit(solution)/shard_map/while/body/eval_jaxpr/ppermute | solution.py:12
  78.5 3.6 %collective-permute-done.4 = f32[1,352,160]{1,2,0:T(8,128)S(1)} collective-permute-done((f32[1,352,160]{1,2,0:T(8,128)S(1)}, f32[1,352,160]{1,2,0:T(8,128)S(1)}, u32[]{:S(2)}, u32[]{:S(2)}) %collective-permute-start.4) | collective-permute-done | bytes 225312 | tf_op jit(solution)/shard_map/while/body/eval_jaxpr/ppermute | solution.py:12
  83.5 2.4 %collective-permute-start.1 = (bf16[1,352,2,80]{1,3,2,0:T(8,128)(2,1)S(1)}, bf16[1,352,2,80]{1,3,2,0:T(8,128)(2,1)S(1)}, u32[]{:S(2)}, u32[]{:S(2)}) collective-permute-start(bf16[1,352,2,80]{1,3,2,0:T(8,128)(2,1)S(1)} %copy.123), channel_id=1, source_target_pairs={{7,0},{0,1},{1,2},{2,3},{3,4},{4,5},{5,6},{6,7},{15,8},{8,9},{9,10... | collective-permute-start | bytes 337928 | tf_op jit(solution)/shard_map/while/body/eval_jaxpr/ppermute | solution.py:12
  88.6 3.8 %collective-permute-done = bf16[1,352,2,80]{1,3,2,0:T(8,128)(2,1)S(1)} collective-permute-done((bf16[1,352,2,80]{1,3,2,0:T(8,128)(2,1)S(1)}, bf16[1,352,2,80]{1,3,2,0:T(8,128)(2,1)S(1)}, u32[]{:S(2)}, u32[]{:S(2)}) %collective-permute-start) | collective-permute-done | bytes 112672 | tf_op jit(solution)/shard_map/while/body/eval_jaxpr/ppermute | solution.py:12
  93.9 2.6 %collective-permute-done.4 = f32[1,352,160]{1,2,0:T(8,128)S(1)} collective-permute-done((f32[1,352,160]{1,2,0:T(8,128)S(1)}, f32[1,352,160]{1,2,0:T(8,128)S(1)}, u32[]{:S(2)}, u32[]{:S(2)}) %collective-permute-start.4) | collective-permute-done | bytes 225312 | tf_op jit(solution)/shard_map/while/body/eval_jaxpr/ppermute | solution.py:12
  96.6 1.7 collective-permute-start.3
  98.9 3.4 %collective-permute-start.1 = (bf16[1,352,2,80]{1,3,2,0:T(8,128)(2,1)S(1)}, bf16[1,352,2,80]{1,3,2,0:T(8,128)(2,1)S(1)}, u32[]{:S(2)}, u32[]{:S(2)}) collective-permute-start(bf16[1,352,2,80]{1,3,2,0:T(8,128)(2,1)S(1)} %copy.123), channel_id=1, source_target_pairs={{7,0},{0,1},{1,2},{2,3},{3,4},{4,5},{5,6},{6,7},{15,8},{8,9},{9,10... | collective-permute-start | bytes 337928 | tf_op jit(solution)/shard_map/while/body/eval_jaxpr/ppermute | solution.py:12
  104.4 1.6 collective-permute-done
  106.0 2.6 %collective-permute-done.1 = bf16[1,352,2,80]{1,3,2,0:T(8,128)(2,1)S(1)} collective-permute-done((bf16[1,352,2,80]{1,3,2,0:T(8,128)(2,1)S(1)}, bf16[1,352,2,80]{1,3,2,0:T(8,128)(2,1)S(1)}, u32[]{:S(2)}, u32[]{:S(2)}) %collective-permute-start.1) | collective-permute-done | bytes 112672 | tf_op jit(solution)/shard_map/while/body/eval_jaxpr/ppermute | solution.py:12
  108.6 3.8 %collective-permute-done.4 = f32[1,352,160]{1,2,0:T(8,128)S(1)} collective-permute-done((f32[1,352,160]{1,2,0:T(8,128)S(1)}, f32[1,352,160]{1,2,0:T(8,128)S(1)}, u32[]{:S(2)}, u32[]{:S(2)}) %collective-permute-start.4) | collective-permute-done | bytes 225312 | tf_op jit(solution)/shard_map/while/body/eval_jaxpr/ppermute | solution.py:12
  114.0 1.9 %collective-permute-start.1 = (bf16[1,352,2,80]{1,3,2,0:T(8,128)(2,1)S(1)}, bf16[1,352,2,80]{1,3,2,0:T(8,128)(2,1)S(1)}, u32[]{:S(2)}, u32[]{:S(2)}) collective-permute-start(bf16[1,352,2,80]{1,3,2,0:T(8,128)(2,1)S(1)} %copy.123), channel_id=1, source_target_pairs={{7,0},{0,1},{1,2},{2,3},{3,4},{4,5},{5,6},{6,7},{15,8},{8,9},{9,10... | collective-permute-start | bytes 337928 | tf_op jit(solution)/shard_map/while/body/eval_jaxpr/ppermute | solution.py:12
  118.9 3.1 %collective-permute-done = bf16[1,352,2,80]{1,3,2,0:T(8,128)(2,1)S(1)} collective-permute-done((bf16[1,352,2,80]{1,3,2,0:T(8,128)(2,1)S(1)}, bf16[1,352,2,80]{1,3,2,0:T(8,128)(2,1)S(1)}, u32[]{:S(2)}, u32[]{:S(2)}) %collective-permute-start) | collective-permute-done | bytes 112672 | tf_op jit(solution)/shard_map/while/body/eval_jaxpr/ppermute | solution.py:12
  123.3 2.6 %collective-permute-done.4 = f32[1,352,160]{1,2,0:T(8,128)S(1)} collective-permute-done((f32[1,352,160]{1,2,0:T(8,128)S(1)}, f32[1,352,160]{1,2,0:T(8,128)S(1)}, u32[]{:S(2)}, u32[]{:S(2)}) %collective-permute-start.4) | collective-permute-done | bytes 225312 | tf_op jit(solution)/shard_map/while/body/eval_jaxpr/ppermute | solution.py:12
  126.4 1.9 %collective-permute-start = (bf16[1,352,2,80]{1,3,2,0:T(8,128)(2,1)S(1)}, bf16[1,352,2,80]{1,3,2,0:T(8,128)(2,1)S(1)}, u32[]{:S(2)}, u32[]{:S(2)}) collective-permute-start(bf16[1,352,2,80]{1,3,2,0:T(8,128)(2,1)S(1)} %copy.122), channel_id=1, source_target_pairs={{7,0},{0,1},{1,2},{2,3},{3,4},{4,5},{5,6},{6,7},{15,8},{8,9},{9,10... | collective-permute-start | bytes 337928 | tf_op jit(solution)/shard_map/while/body/eval_jaxpr/ppermute | solution.py:12
  128.4 3.4 %collective-permute-start.1 = (bf16[1,352,2,80]{1,3,2,0:T(8,128)(2,1)S(1)}, bf16[1,352,2,80]{1,3,2,0:T(8,128)(2,1)S(1)}, u32[]{:S(2)}, u32[]{:S(2)}) collective-permute-start(bf16[1,352,2,80]{1,3,2,0:T(8,128)(2,1)S(1)} %copy.123), channel_id=1, source_target_pairs={{7,0},{0,1},{1,2},{2,3},{3,4},{4,5},{5,6},{6,7},{15,8},{8,9},{9,10... | collective-permute-start | bytes 337928 | tf_op jit(solution)/shard_map/while/body/eval_jaxpr/ppermute | solution.py:12
  135.1 2.6 %collective-permute-done.1 = bf16[1,352,2,80]{1,3,2,0:T(8,128)(2,1)S(1)} collective-permute-done((bf16[1,352,2,80]{1,3,2,0:T(8,128)(2,1)S(1)}, bf16[1,352,2,80]{1,3,2,0:T(8,128)(2,1)S(1)}, u32[]{:S(2)}, u32[]{:S(2)}) %collective-permute-start.1) | collective-permute-done | bytes 112672 | tf_op jit(solution)/shard_map/while/body/eval_jaxpr/ppermute | solution.py:12
  137.8 4.1 %collective-permute-done.4 = f32[1,352,160]{1,2,0:T(8,128)S(1)} collective-permute-done((f32[1,352,160]{1,2,0:T(8,128)S(1)}, f32[1,352,160]{1,2,0:T(8,128)S(1)}, u32[]{:S(2)}, u32[]{:S(2)}) %collective-permute-start.4) | collective-permute-done | bytes 225312 | tf_op jit(solution)/shard_map/while/body/eval_jaxpr/ppermute | solution.py:12
  141.8 2.2 %collective-permute-start.3 = (f32[1,2,352]{2,1,0:T(2,128)S(1)}, f32[1,2,352]{2,1,0:T(2,128)S(1)}, u32[]{:S(2)}, u32[]{:S(2)}) collective-permute-start(f32[1,2,352]{2,1,0:T(2,128)S(1)} %copy.125), channel_id=1, source_target_pairs={{7,0},{0,1},{1,2},{2,3},{3,4},{4,5},{5,6},{6,7},{15,8},{8,9},{9,10... | collective-permute-start | bytes 8456 | tf_op jit(solution)/shard_map/while/body/eval_jaxpr/ppermute | solution.py:12
  144.2 2.4 %collective-permute-start.1 = (bf16[1,352,2,80]{1,3,2,0:T(8,128)(2,1)S(1)}, bf16[1,352,2,80]{1,3,2,0:T(8,128)(2,1)S(1)}, u32[]{:S(2)}, u32[]{:S(2)}) collective-permute-start(bf16[1,352,2,80]{1,3,2,0:T(8,128)(2,1)S(1)} %copy.123), channel_id=1, source_target_pairs={{7,0},{0,1},{1,2},{2,3},{3,4},{4,5},{5,6},{6,7},{15,8},{8,9},{9,10... | collective-permute-start | bytes 337928 | tf_op jit(solution)/shard_map/while/body/eval_jaxpr/ppermute | solution.py:12
  148.4 3.2 %collective-permute-done = bf16[1,352,2,80]{1,3,2,0:T(8,128)(2,1)S(1)} collective-permute-done((bf16[1,352,2,80]{1,3,2,0:T(8,128)(2,1)S(1)}, bf16[1,352,2,80]{1,3,2,0:T(8,128)(2,1)S(1)}, u32[]{:S(2)}, u32[]{:S(2)}) %collective-permute-start) | collective-permute-done | bytes 112672 | tf_op jit(solution)/shard_map/while/body/eval_jaxpr/ppermute | solution.py:12
  153.0 4.8 %collective-permute-done.4 = f32[1,352,160]{1,2,0:T(8,128)S(1)} collective-permute-done((f32[1,352,160]{1,2,0:T(8,128)S(1)}, f32[1,352,160]{1,2,0:T(8,128)S(1)}, u32[]{:S(2)}, u32[]{:S(2)}) %collective-permute-start.4) | collective-permute-done | bytes 225312 | tf_op jit(solution)/shard_map/while/body/eval_jaxpr/ppermute | solution.py:12
  159.7 1.8 reduce.8
  162.5 3.3 %all-to-all-start.7 = ((bf16[4,2,7040]{2,1,0:T(2,128)(2,1)}), bf16[4,2,7040]{2,1,0:T(2,128)(2,1)S(1)}, u32[]{:S(2)}, u32[]{:S(2)}) async-start(bf16[4,2,7040]{2,1,0:T(2,128)(2,1)} %reshape.106), calls=%async_computation.7 | async-start | bytes 225280 | tf_op jit(solution)/shard_map/all_to_all | solution.py:107
  166.0 1.8 reduce.7
  170.2 3.5 %all-to-all-start.6 = ((bf16[4,2,7040]{2,1,0:T(2,128)(2,1)}), bf16[4,2,7040]{2,1,0:T(2,128)(2,1)S(1)}, u32[]{:S(2)}, u32[]{:S(2)}) async-start(bf16[4,2,7040]{2,1,0:T(2,128)(2,1)} %reshape.104), calls=%async_computation.6 | async-start | bytes 225280 | tf_op jit(solution)/shard_map/all_to_all | solution.py:106
  174.0 1.8 reduce.6
  177.9 3.3 %all-to-all-start.5 = ((bf16[4,2,7040]{2,1,0:T(2,128)(2,1)}), bf16[4,2,7040]{2,1,0:T(2,128)(2,1)S(1)}, u32[]{:S(2)}, u32[]{:S(2)}) async-start(bf16[4,2,7040]{2,1,0:T(2,128)(2,1)} %reshape.102), calls=%async_computation.5 | async-start | bytes 225280 | tf_op jit(solution)/shard_map/all_to_all | solution.py:105
  (207 shorter events, 60.9 us)
Async XLA Ops:
  0.6 8.5 %copy-start.1 = (bf16[1,88,640]{2,1,0:T(8,128)(2,1)S(1)}, bf16[1,88,640]{2,1,0:T(8,128)(2,1)}, u32[]{:S(2)}) copy-start(bf16[1,88,640]{2,1,0:T(8,128)(2,1)} %param.9) | copy-start | bytes 337924
  4.0 12.9 %copy-start.2 = (bf16[1,88,640]{2,1,0:T(8,128)(2,1)S(1)}, bf16[1,88,640]{2,1,0:T(8,128)(2,1)}, u32[]{:S(2)}) copy-start(bf16[1,88,640]{2,1,0:T(8,128)(2,1)} %param.10) | copy-start | bytes 337924
  4.9 8.6 %all-to-all-start = ((bf16[4,2,7040]{2,1,0:T(2,128)(2,1)}), bf16[4,2,7040]{2,1,0:T(2,128)(2,1)S(1)}, u32[]{:S(2)}, u32[]{:S(2)}) async-start(bf16[4,2,7040]{2,1,0:T(2,128)(2,1)} %reshape.92), calls=%async_computation | async-start | bytes 225280 | tf_op jit(solution)/shard_map/all_to_all | solution.py:50
  11.0 13.6 %copy-start.3 = (bf16[1,88,640]{2,1,0:T(8,128)(2,1)S(1)}, bf16[1,88,640]{2,1,0:T(8,128)(2,1)}, u32[]{:S(2)}) copy-start(bf16[1,88,640]{2,1,0:T(8,128)(2,1)} %param.11) | copy-start | bytes 337924
  13.5 7.7 %all-to-all-start.3 = ((bf16[4,2,7040]{2,1,0:T(2,128)(2,1)}), bf16[4,2,7040]{2,1,0:T(2,128)(2,1)S(1)}, u32[]{:S(2)}, u32[]{:S(2)}) async-start(bf16[4,2,7040]{2,1,0:T(2,128)(2,1)} %reshape.98), calls=%async_computation.3 | async-start | bytes 225280 | tf_op jit(solution)/shard_map/all_to_all | solution.py:51
  18.8 13.6 %copy-start.4 = (bf16[1,88,640]{2,1,0:T(8,128)(2,1)S(1)}, bf16[1,88,640]{2,1,0:T(8,128)(2,1)}, u32[]{:S(2)}) copy-start(bf16[1,88,640]{2,1,0:T(8,128)(2,1)} %param.12) | copy-start | bytes 337924
  21.3 7.7 %all-to-all-start.4 = ((bf16[4,2,7040]{2,1,0:T(2,128)(2,1)}), bf16[4,2,7040]{2,1,0:T(2,128)(2,1)S(1)}, u32[]{:S(2)}, u32[]{:S(2)}) async-start(bf16[4,2,7040]{2,1,0:T(2,128)(2,1)} %reshape.100), calls=%async_computation.4 | async-start | bytes 225280 | tf_op jit(solution)/shard_map/all_to_all | solution.py:52
  29.0 7.7 %all-to-all-start.2 = ((bf16[4,2,7040]{2,1,0:T(2,128)(2,1)}), bf16[4,2,7040]{2,1,0:T(2,128)(2,1)S(1)}, u32[]{:S(2)}, u32[]{:S(2)}) async-start(bf16[4,2,7040]{2,1,0:T(2,128)(2,1)} %reshape.96), calls=%async_computation.2 | async-start | bytes 225280 | tf_op jit(solution)/shard_map/all_to_all | solution.py:54
  36.7 9.3 %all-to-all-start.1 = ((bf16[4,2,7040]{2,1,0:T(2,128)(2,1)}), bf16[4,2,7040]{2,1,0:T(2,128)(2,1)S(1)}, u32[]{:S(2)}, u32[]{:S(2)}) async-start(bf16[4,2,7040]{2,1,0:T(2,128)(2,1)} %reshape.94), calls=%async_computation.1 | async-start | bytes 225280 | tf_op jit(solution)/shard_map/all_to_all | solution.py:53
  47.4 10.1 %collective-permute-start.2 = (f32[1,2,352]{2,1,0:T(2,128)S(1)}, f32[1,2,352]{2,1,0:T(2,128)S(1)}, u32[]{:S(2)}, u32[]{:S(2)}) collective-permute-start(f32[1,2,352]{2,1,0:T(2,128)S(1)} %copy.124), channel_id=1, source_target_pairs={{7,0},{0,1},{1,2},{2,3},{3,4},{4,5},{5,6},{6,7},{15,8},{8,9},{9,10... | collective-permute-start | bytes 8456 | tf_op jit(solution)/shard_map/while/body/eval_jaxpr/ppermute | solution.py:12
  49.5 8.0 %collective-permute-start.3 = (f32[1,2,352]{2,1,0:T(2,128)S(1)}, f32[1,2,352]{2,1,0:T(2,128)S(1)}, u32[]{:S(2)}, u32[]{:S(2)}) collective-permute-start(f32[1,2,352]{2,1,0:T(2,128)S(1)} %copy.125), channel_id=1, source_target_pairs={{7,0},{0,1},{1,2},{2,3},{3,4},{4,5},{5,6},{6,7},{15,8},{8,9},{9,10... | collective-permute-start | bytes 8456 | tf_op jit(solution)/shard_map/while/body/eval_jaxpr/ppermute | solution.py:12
  51.0 9.0 %collective-permute-start = (bf16[1,352,2,80]{1,3,2,0:T(8,128)(2,1)S(1)}, bf16[1,352,2,80]{1,3,2,0:T(8,128)(2,1)S(1)}, u32[]{:S(2)}, u32[]{:S(2)}) collective-permute-start(bf16[1,352,2,80]{1,3,2,0:T(8,128)(2,1)S(1)} %copy.122), channel_id=1, source_target_pairs={{7,0},{0,1},{1,2},{2,3},{3,4},{4,5},{5,6},{6,7},{15,8},{8,9},{9,10... | collective-permute-start | bytes 337928 | tf_op jit(solution)/shard_map/while/body/eval_jaxpr/ppermute | solution.py:12
  52.6 10.0 %collective-permute-start.1 = (bf16[1,352,2,80]{1,3,2,0:T(8,128)(2,1)S(1)}, bf16[1,352,2,80]{1,3,2,0:T(8,128)(2,1)S(1)}, u32[]{:S(2)}, u32[]{:S(2)}) collective-permute-start(bf16[1,352,2,80]{1,3,2,0:T(8,128)(2,1)S(1)} %copy.123), channel_id=1, source_target_pairs={{7,0},{0,1},{1,2},{2,3},{3,4},{4,5},{5,6},{6,7},{15,8},{8,9},{9,10... | collective-permute-start | bytes 337928 | tf_op jit(solution)/shard_map/while/body/eval_jaxpr/ppermute | solution.py:12
  55.3 11.4 %collective-permute-start.4 = (f32[1,352,160]{1,2,0:T(8,128)S(1)}, f32[1,352,160]{1,2,0:T(8,128)S(1)}, u32[]{:S(2)}, u32[]{:S(2)}) collective-permute-start(f32[1,352,160]{1,2,0:T(8,128)S(1)} %bitcast_add_fusion.8), channel_id=1, source_target_pairs={{7,0},{0,1},{1,2},{2,3},{3,4},{4,5},{5,6},{6,7},{15,8},{8,9},{9,10... | collective-permute-start | bytes 675848 | tf_op jit(solution)/shard_map/while/body/eval_jaxpr/ppermute | solution.py:12
  66.6 6.8 %collective-permute-start.2 = (f32[1,2,352]{2,1,0:T(2,128)S(1)}, f32[1,2,352]{2,1,0:T(2,128)S(1)}, u32[]{:S(2)}, u32[]{:S(2)}) collective-permute-start(f32[1,2,352]{2,1,0:T(2,128)S(1)} %copy.124), channel_id=1, source_target_pairs={{7,0},{0,1},{1,2},{2,3},{3,4},{4,5},{5,6},{6,7},{15,8},{8,9},{9,10... | collective-permute-start | bytes 8456 | tf_op jit(solution)/shard_map/while/body/eval_jaxpr/ppermute | solution.py:12
  66.6 6.8 %collective-permute-start.3 = (f32[1,2,352]{2,1,0:T(2,128)S(1)}, f32[1,2,352]{2,1,0:T(2,128)S(1)}, u32[]{:S(2)}, u32[]{:S(2)}) collective-permute-start(f32[1,2,352]{2,1,0:T(2,128)S(1)} %copy.125), channel_id=1, source_target_pairs={{7,0},{0,1},{1,2},{2,3},{3,4},{4,5},{5,6},{6,7},{15,8},{8,9},{9,10... | collective-permute-start | bytes 8456 | tf_op jit(solution)/shard_map/while/body/eval_jaxpr/ppermute | solution.py:12
  67.9 8.0 %collective-permute-start = (bf16[1,352,2,80]{1,3,2,0:T(8,128)(2,1)S(1)}, bf16[1,352,2,80]{1,3,2,0:T(8,128)(2,1)S(1)}, u32[]{:S(2)}, u32[]{:S(2)}) collective-permute-start(bf16[1,352,2,80]{1,3,2,0:T(8,128)(2,1)S(1)} %copy.122), channel_id=1, source_target_pairs={{7,0},{0,1},{1,2},{2,3},{3,4},{4,5},{5,6},{6,7},{15,8},{8,9},{9,10... | collective-permute-start | bytes 337928 | tf_op jit(solution)/shard_map/while/body/eval_jaxpr/ppermute | solution.py:12
  68.6 9.9 %collective-permute-start.1 = (bf16[1,352,2,80]{1,3,2,0:T(8,128)(2,1)S(1)}, bf16[1,352,2,80]{1,3,2,0:T(8,128)(2,1)S(1)}, u32[]{:S(2)}, u32[]{:S(2)}) collective-permute-start(bf16[1,352,2,80]{1,3,2,0:T(8,128)(2,1)S(1)} %copy.123), channel_id=1, source_target_pairs={{7,0},{0,1},{1,2},{2,3},{3,4},{4,5},{5,6},{6,7},{15,8},{8,9},{9,10... | collective-permute-start | bytes 337928 | tf_op jit(solution)/shard_map/while/body/eval_jaxpr/ppermute | solution.py:12
  72.1 10.0 %collective-permute-start.4 = (f32[1,352,160]{1,2,0:T(8,128)S(1)}, f32[1,352,160]{1,2,0:T(8,128)S(1)}, u32[]{:S(2)}, u32[]{:S(2)}) collective-permute-start(f32[1,352,160]{1,2,0:T(8,128)S(1)} %bitcast_add_fusion.8), channel_id=1, source_target_pairs={{7,0},{0,1},{1,2},{2,3},{3,4},{4,5},{5,6},{6,7},{15,8},{8,9},{9,10... | collective-permute-start | bytes 675848 | tf_op jit(solution)/shard_map/while/body/eval_jaxpr/ppermute | solution.py:12
  82.1 6.4 %collective-permute-start.2 = (f32[1,2,352]{2,1,0:T(2,128)S(1)}, f32[1,2,352]{2,1,0:T(2,128)S(1)}, u32[]{:S(2)}, u32[]{:S(2)}) collective-permute-start(f32[1,2,352]{2,1,0:T(2,128)S(1)} %copy.124), channel_id=1, source_target_pairs={{7,0},{0,1},{1,2},{2,3},{3,4},{4,5},{5,6},{6,7},{15,8},{8,9},{9,10... | collective-permute-start | bytes 8456 | tf_op jit(solution)/shard_map/while/body/eval_jaxpr/ppermute | solution.py:12
  82.1 6.5 %collective-permute-start.3 = (f32[1,2,352]{2,1,0:T(2,128)S(1)}, f32[1,2,352]{2,1,0:T(2,128)S(1)}, u32[]{:S(2)}, u32[]{:S(2)}) collective-permute-start(f32[1,2,352]{2,1,0:T(2,128)S(1)} %copy.125), channel_id=1, source_target_pairs={{7,0},{0,1},{1,2},{2,3},{3,4},{4,5},{5,6},{6,7},{15,8},{8,9},{9,10... | collective-permute-start | bytes 8456 | tf_op jit(solution)/shard_map/while/body/eval_jaxpr/ppermute | solution.py:12
  83.4 9.0 %collective-permute-start = (bf16[1,352,2,80]{1,3,2,0:T(8,128)(2,1)S(1)}, bf16[1,352,2,80]{1,3,2,0:T(8,128)(2,1)S(1)}, u32[]{:S(2)}, u32[]{:S(2)}) collective-permute-start(bf16[1,352,2,80]{1,3,2,0:T(8,128)(2,1)S(1)} %copy.122), channel_id=1, source_target_pairs={{7,0},{0,1},{1,2},{2,3},{3,4},{4,5},{5,6},{6,7},{15,8},{8,9},{9,10... | collective-permute-start | bytes 337928 | tf_op jit(solution)/shard_map/while/body/eval_jaxpr/ppermute | solution.py:12
  83.5 10.4 %collective-permute-start.1 = (bf16[1,352,2,80]{1,3,2,0:T(8,128)(2,1)S(1)}, bf16[1,352,2,80]{1,3,2,0:T(8,128)(2,1)S(1)}, u32[]{:S(2)}, u32[]{:S(2)}) collective-permute-start(bf16[1,352,2,80]{1,3,2,0:T(8,128)(2,1)S(1)} %copy.123), channel_id=1, source_target_pairs={{7,0},{0,1},{1,2},{2,3},{3,4},{4,5},{5,6},{6,7},{15,8},{8,9},{9,10... | collective-permute-start | bytes 337928 | tf_op jit(solution)/shard_map/while/body/eval_jaxpr/ppermute | solution.py:12
  87.0 9.6 %collective-permute-start.4 = (f32[1,352,160]{1,2,0:T(8,128)S(1)}, f32[1,352,160]{1,2,0:T(8,128)S(1)}, u32[]{:S(2)}, u32[]{:S(2)}) collective-permute-start(f32[1,352,160]{1,2,0:T(8,128)S(1)} %bitcast_add_fusion.8), channel_id=1, source_target_pairs={{7,0},{0,1},{1,2},{2,3},{3,4},{4,5},{5,6},{6,7},{15,8},{8,9},{9,10... | collective-permute-start | bytes 675848 | tf_op jit(solution)/shard_map/while/body/eval_jaxpr/ppermute | solution.py:12
  96.6 7.8 %collective-permute-start.2 = (f32[1,2,352]{2,1,0:T(2,128)S(1)}, f32[1,2,352]{2,1,0:T(2,128)S(1)}, u32[]{:S(2)}, u32[]{:S(2)}) collective-permute-start(f32[1,2,352]{2,1,0:T(2,128)S(1)} %copy.124), channel_id=1, source_target_pairs={{7,0},{0,1},{1,2},{2,3},{3,4},{4,5},{5,6},{6,7},{15,8},{8,9},{9,10... | collective-permute-start | bytes 8456 | tf_op jit(solution)/shard_map/while/body/eval_jaxpr/ppermute | solution.py:12
  96.6 7.8 %collective-permute-start.3 = (f32[1,2,352]{2,1,0:T(2,128)S(1)}, f32[1,2,352]{2,1,0:T(2,128)S(1)}, u32[]{:S(2)}, u32[]{:S(2)}) collective-permute-start(f32[1,2,352]{2,1,0:T(2,128)S(1)} %copy.125), channel_id=1, source_target_pairs={{7,0},{0,1},{1,2},{2,3},{3,4},{4,5},{5,6},{6,7},{15,8},{8,9},{9,10... | collective-permute-start | bytes 8456 | tf_op jit(solution)/shard_map/while/body/eval_jaxpr/ppermute | solution.py:12
  98.2 7.8 %collective-permute-start = (bf16[1,352,2,80]{1,3,2,0:T(8,128)(2,1)S(1)}, bf16[1,352,2,80]{1,3,2,0:T(8,128)(2,1)S(1)}, u32[]{:S(2)}, u32[]{:S(2)}) collective-permute-start(bf16[1,352,2,80]{1,3,2,0:T(8,128)(2,1)S(1)} %copy.122), channel_id=1, source_target_pairs={{7,0},{0,1},{1,2},{2,3},{3,4},{4,5},{5,6},{6,7},{15,8},{8,9},{9,10... | collective-permute-start | bytes 337928 | tf_op jit(solution)/shard_map/while/body/eval_jaxpr/ppermute | solution.py:12
  98.9 9.7 %collective-permute-start.1 = (bf16[1,352,2,80]{1,3,2,0:T(8,128)(2,1)S(1)}, bf16[1,352,2,80]{1,3,2,0:T(8,128)(2,1)S(1)}, u32[]{:S(2)}, u32[]{:S(2)}) collective-permute-start(bf16[1,352,2,80]{1,3,2,0:T(8,128)(2,1)S(1)} %copy.123), channel_id=1, source_target_pairs={{7,0},{0,1},{1,2},{2,3},{3,4},{4,5},{5,6},{6,7},{15,8},{8,9},{9,10... | collective-permute-start | bytes 337928 | tf_op jit(solution)/shard_map/while/body/eval_jaxpr/ppermute | solution.py:12
  103.4 9.0 %collective-permute-start.4 = (f32[1,352,160]{1,2,0:T(8,128)S(1)}, f32[1,352,160]{1,2,0:T(8,128)S(1)}, u32[]{:S(2)}, u32[]{:S(2)}) collective-permute-start(f32[1,352,160]{1,2,0:T(8,128)S(1)} %bitcast_add_fusion.8), channel_id=1, source_target_pairs={{7,0},{0,1},{1,2},{2,3},{3,4},{4,5},{5,6},{6,7},{15,8},{8,9},{9,10... | collective-permute-start | bytes 675848 | tf_op jit(solution)/shard_map/while/body/eval_jaxpr/ppermute | solution.py:12
  112.5 6.4 %collective-permute-start.2 = (f32[1,2,352]{2,1,0:T(2,128)S(1)}, f32[1,2,352]{2,1,0:T(2,128)S(1)}, u32[]{:S(2)}, u32[]{:S(2)}) collective-permute-start(f32[1,2,352]{2,1,0:T(2,128)S(1)} %copy.124), channel_id=1, source_target_pairs={{7,0},{0,1},{1,2},{2,3},{3,4},{4,5},{5,6},{6,7},{15,8},{8,9},{9,10... | collective-permute-start | bytes 8456 | tf_op jit(solution)/shard_map/while/body/eval_jaxpr/ppermute | solution.py:12
  112.5 6.5 %collective-permute-start.3 = (f32[1,2,352]{2,1,0:T(2,128)S(1)}, f32[1,2,352]{2,1,0:T(2,128)S(1)}, u32[]{:S(2)}, u32[]{:S(2)}) collective-permute-start(f32[1,2,352]{2,1,0:T(2,128)S(1)} %copy.125), channel_id=1, source_target_pairs={{7,0},{0,1},{1,2},{2,3},{3,4},{4,5},{5,6},{6,7},{15,8},{8,9},{9,10... | collective-permute-start | bytes 8456 | tf_op jit(solution)/shard_map/while/body/eval_jaxpr/ppermute | solution.py:12
  113.9 8.2 %collective-permute-start = (bf16[1,352,2,80]{1,3,2,0:T(8,128)(2,1)S(1)}, bf16[1,352,2,80]{1,3,2,0:T(8,128)(2,1)S(1)}, u32[]{:S(2)}, u32[]{:S(2)}) collective-permute-start(bf16[1,352,2,80]{1,3,2,0:T(8,128)(2,1)S(1)} %copy.122), channel_id=1, source_target_pairs={{7,0},{0,1},{1,2},{2,3},{3,4},{4,5},{5,6},{6,7},{15,8},{8,9},{9,10... | collective-permute-start | bytes 337928 | tf_op jit(solution)/shard_map/while/body/eval_jaxpr/ppermute | solution.py:12
  114.0 9.3 %collective-permute-start.1 = (bf16[1,352,2,80]{1,3,2,0:T(8,128)(2,1)S(1)}, bf16[1,352,2,80]{1,3,2,0:T(8,128)(2,1)S(1)}, u32[]{:S(2)}, u32[]{:S(2)}) collective-permute-start(bf16[1,352,2,80]{1,3,2,0:T(8,128)(2,1)S(1)} %copy.123), channel_id=1, source_target_pairs={{7,0},{0,1},{1,2},{2,3},{3,4},{4,5},{5,6},{6,7},{15,8},{8,9},{9,10... | collective-permute-start | bytes 337928 | tf_op jit(solution)/shard_map/while/body/eval_jaxpr/ppermute | solution.py:12
  117.0 9.0 %collective-permute-start.4 = (f32[1,352,160]{1,2,0:T(8,128)S(1)}, f32[1,352,160]{1,2,0:T(8,128)S(1)}, u32[]{:S(2)}, u32[]{:S(2)}) collective-permute-start(f32[1,352,160]{1,2,0:T(8,128)S(1)} %bitcast_add_fusion.8), channel_id=1, source_target_pairs={{7,0},{0,1},{1,2},{2,3},{3,4},{4,5},{5,6},{6,7},{15,8},{8,9},{9,10... | collective-permute-start | bytes 675848 | tf_op jit(solution)/shard_map/while/body/eval_jaxpr/ppermute | solution.py:12
  126.0 7.6 %collective-permute-start.2 = (f32[1,2,352]{2,1,0:T(2,128)S(1)}, f32[1,2,352]{2,1,0:T(2,128)S(1)}, u32[]{:S(2)}, u32[]{:S(2)}) collective-permute-start(f32[1,2,352]{2,1,0:T(2,128)S(1)} %copy.124), channel_id=1, source_target_pairs={{7,0},{0,1},{1,2},{2,3},{3,4},{4,5},{5,6},{6,7},{15,8},{8,9},{9,10... | collective-permute-start | bytes 8456 | tf_op jit(solution)/shard_map/while/body/eval_jaxpr/ppermute | solution.py:12
  126.0 7.7 %collective-permute-start.3 = (f32[1,2,352]{2,1,0:T(2,128)S(1)}, f32[1,2,352]{2,1,0:T(2,128)S(1)}, u32[]{:S(2)}, u32[]{:S(2)}) collective-permute-start(f32[1,2,352]{2,1,0:T(2,128)S(1)} %copy.125), channel_id=1, source_target_pairs={{7,0},{0,1},{1,2},{2,3},{3,4},{4,5},{5,6},{6,7},{15,8},{8,9},{9,10... | collective-permute-start | bytes 8456 | tf_op jit(solution)/shard_map/while/body/eval_jaxpr/ppermute | solution.py:12
  126.4 8.7 %collective-permute-start = (bf16[1,352,2,80]{1,3,2,0:T(8,128)(2,1)S(1)}, bf16[1,352,2,80]{1,3,2,0:T(8,128)(2,1)S(1)}, u32[]{:S(2)}, u32[]{:S(2)}) collective-permute-start(bf16[1,352,2,80]{1,3,2,0:T(8,128)(2,1)S(1)} %copy.122), channel_id=1, source_target_pairs={{7,0},{0,1},{1,2},{2,3},{3,4},{4,5},{5,6},{6,7},{15,8},{8,9},{9,10... | collective-permute-start | bytes 337928 | tf_op jit(solution)/shard_map/while/body/eval_jaxpr/ppermute | solution.py:12
  128.4 9.4 %collective-permute-start.1 = (bf16[1,352,2,80]{1,3,2,0:T(8,128)(2,1)S(1)}, bf16[1,352,2,80]{1,3,2,0:T(8,128)(2,1)S(1)}, u32[]{:S(2)}, u32[]{:S(2)}) collective-permute-start(bf16[1,352,2,80]{1,3,2,0:T(8,128)(2,1)S(1)} %copy.123), channel_id=1, source_target_pairs={{7,0},{0,1},{1,2},{2,3},{3,4},{4,5},{5,6},{6,7},{15,8},{8,9},{9,10... | collective-permute-start | bytes 337928 | tf_op jit(solution)/shard_map/while/body/eval_jaxpr/ppermute | solution.py:12
  132.9 8.9 %collective-permute-start.4 = (f32[1,352,160]{1,2,0:T(8,128)S(1)}, f32[1,352,160]{1,2,0:T(8,128)S(1)}, u32[]{:S(2)}, u32[]{:S(2)}) collective-permute-start(f32[1,352,160]{1,2,0:T(8,128)S(1)} %bitcast_add_fusion.8), channel_id=1, source_target_pairs={{7,0},{0,1},{1,2},{2,3},{3,4},{4,5},{5,6},{6,7},{15,8},{8,9},{9,10... | collective-permute-start | bytes 675848 | tf_op jit(solution)/shard_map/while/body/eval_jaxpr/ppermute | solution.py:12
  141.8 6.6 %collective-permute-start.2 = (f32[1,2,352]{2,1,0:T(2,128)S(1)}, f32[1,2,352]{2,1,0:T(2,128)S(1)}, u32[]{:S(2)}, u32[]{:S(2)}) collective-permute-start(f32[1,2,352]{2,1,0:T(2,128)S(1)} %copy.124), channel_id=1, source_target_pairs={{7,0},{0,1},{1,2},{2,3},{3,4},{4,5},{5,6},{6,7},{15,8},{8,9},{9,10... | collective-permute-start | bytes 8456 | tf_op jit(solution)/shard_map/while/body/eval_jaxpr/ppermute | solution.py:12
  141.8 6.6 %collective-permute-start.3 = (f32[1,2,352]{2,1,0:T(2,128)S(1)}, f32[1,2,352]{2,1,0:T(2,128)S(1)}, u32[]{:S(2)}, u32[]{:S(2)}) collective-permute-start(f32[1,2,352]{2,1,0:T(2,128)S(1)} %copy.125), channel_id=1, source_target_pairs={{7,0},{0,1},{1,2},{2,3},{3,4},{4,5},{5,6},{6,7},{15,8},{8,9},{9,10... | collective-permute-start | bytes 8456 | tf_op jit(solution)/shard_map/while/body/eval_jaxpr/ppermute | solution.py:12
  144.0 7.6 %collective-permute-start = (bf16[1,352,2,80]{1,3,2,0:T(8,128)(2,1)S(1)}, bf16[1,352,2,80]{1,3,2,0:T(8,128)(2,1)S(1)}, u32[]{:S(2)}, u32[]{:S(2)}) collective-permute-start(bf16[1,352,2,80]{1,3,2,0:T(8,128)(2,1)S(1)} %copy.122), channel_id=1, source_target_pairs={{7,0},{0,1},{1,2},{2,3},{3,4},{4,5},{5,6},{6,7},{15,8},{8,9},{9,10... | collective-permute-start | bytes 337928 | tf_op jit(solution)/shard_map/while/body/eval_jaxpr/ppermute | solution.py:12
  144.2 8.8 %collective-permute-start.1 = (bf16[1,352,2,80]{1,3,2,0:T(8,128)(2,1)S(1)}, bf16[1,352,2,80]{1,3,2,0:T(8,128)(2,1)S(1)}, u32[]{:S(2)}, u32[]{:S(2)}) collective-permute-start(bf16[1,352,2,80]{1,3,2,0:T(8,128)(2,1)S(1)} %copy.123), channel_id=1, source_target_pairs={{7,0},{0,1},{1,2},{2,3},{3,4},{4,5},{5,6},{6,7},{15,8},{8,9},{9,10... | collective-permute-start | bytes 337928 | tf_op jit(solution)/shard_map/while/body/eval_jaxpr/ppermute | solution.py:12
  147.7 10.1 %collective-permute-start.4 = (f32[1,352,160]{1,2,0:T(8,128)S(1)}, f32[1,352,160]{1,2,0:T(8,128)S(1)}, u32[]{:S(2)}, u32[]{:S(2)}) collective-permute-start(f32[1,352,160]{1,2,0:T(8,128)S(1)} %bitcast_add_fusion.8), channel_id=1, source_target_pairs={{7,0},{0,1},{1,2},{2,3},{3,4},{4,5},{5,6},{6,7},{15,8},{8,9},{9,10... | collective-permute-start | bytes 675848 | tf_op jit(solution)/shard_map/while/body/eval_jaxpr/ppermute | solution.py:12
  159.3 14.4 %collective-permute-start.5 = (bf16[1,352,160]{1,2,0:T(8,128)(2,1)S(1)}, bf16[1,352,160]{1,2,0:T(8,128)(2,1)S(1)}, u32[]{:S(2)}, u32[]{:S(2)}) collective-permute-start(bf16[1,352,160]{1,2,0:T(8,128)(2,1)S(1)} %fusion.24), channel_id=1, source_target_pairs={{7,0},{0,1},{1,2},{2,3},{3,4},{4,5},{5,6},{6,7},{15,8},{8,9},{9,10... | collective-permute-start | bytes 337928 | tf_op jit(solution)/shard_map/ppermute | solution.py:12
  162.5 7.7 %all-to-all-start.7 = ((bf16[4,2,7040]{2,1,0:T(2,128)(2,1)}), bf16[4,2,7040]{2,1,0:T(2,128)(2,1)S(1)}, u32[]{:S(2)}, u32[]{:S(2)}) async-start(bf16[4,2,7040]{2,1,0:T(2,128)(2,1)} %reshape.106), calls=%async_computation.7 | async-start | bytes 225280 | tf_op jit(solution)/shard_map/all_to_all | solution.py:107
  170.2 7.7 %all-to-all-start.6 = ((bf16[4,2,7040]{2,1,0:T(2,128)(2,1)}), bf16[4,2,7040]{2,1,0:T(2,128)(2,1)S(1)}, u32[]{:S(2)}, u32[]{:S(2)}) async-start(bf16[4,2,7040]{2,1,0:T(2,128)(2,1)} %reshape.104), calls=%async_computation.6 | async-start | bytes 225280 | tf_op jit(solution)/shard_map/all_to_all | solution.py:106
  177.9 7.7 %all-to-all-start.5 = ((bf16[4,2,7040]{2,1,0:T(2,128)(2,1)}), bf16[4,2,7040]{2,1,0:T(2,128)(2,1)S(1)}, u32[]{:S(2)}, u32[]{:S(2)}) async-start(bf16[4,2,7040]{2,1,0:T(2,128)(2,1)} %reshape.102), calls=%async_computation.5 | async-start | bytes 225280 | tf_op jit(solution)/shard_map/all_to_all | solution.py:105
  (1 other events, 0.8 us)
where the time goes:
time: 188 us; the launch traced here: 187 us
  waiting for transfers between devices  70 us (37%)
  starting transfers between devices  66.1 us (35%)
  local copies, waits for them, and re-layouts  22.6 us (12%)
  other arithmetic  14.9 us (8%)
  matrix products  11.8 us (6%)
    ppermute x36, waiting for transfers between devices, shifted(): return lax.ppermute(block, axis, route)  59.9 us
    ppermute x36, starting transfers between devices, shifted(): return lax.ppermute(block, axis, route)  38.3 us
    unnamed x32, local copies, waits for them, and re-layouts  13.8 us
    unnamed x10, other arithmetic  13.6 us
    all_to_all x1, starting transfers between devices, body(): lax.all_to_all(sent[0], 'head', split_axis=2, concat_axis=1, tiled=True)  4.21 us
  transfers between devices with their start and end apart: 44, of which 32 were waited for; matrix products, arithmetic and copies ran while one was open for 20% of the time, Pallas kernels for 0%

commit v1 on v0

v1 whole, which is shorter than its diff:
```python
import functools
import math

import jax
import jax.numpy as jnp
from jax import lax
from jax.experimental import pallas as pl
from jax.experimental.pallas import tpu as pltpu
from jax.sharding import PartitionSpec as P

HDIM = 80
SCALING = HDIM ** (-0.5)
LOG2E = math.log2(math.e)
PADDED = 96
VMEM_LIMIT = 24 * 1024 * 1024
F32 = jnp.float32
BF16 = jnp.bfloat16


def shifted(block, axis, distance):
    devices = range(lax.axis_size(axis))
    route = [((i - distance) % len(devices), i) for i in devices]
    return lax.ppermute(block, axis, route)


def tile_terms(query_h, cotan_h, lse_rows, delta_rows, key_h, value_h):
    query_rows = query_h.shape[0]
    key_rows = key_h.shape[0]
    groups = query_h.shape[1]
    scores = (
        jnp.einsum("qhd,khd->hqk", query_h, key_h, preferred_element_type=jnp.float32) * SCALING
    )
    probs = jnp.exp(scores - lse_rows[:, :, None])
    probs16 = probs.astype(jnp.bfloat16)
    value_part = jnp.einsum("hqk,qhd->khd", probs16, cotan_h, preferred_element_type=jnp.float32)
    dprobs = jnp.einsum("qhd,khd->hqk", cotan_h, value_h, preferred_element_type=jnp.float32)
    dscores = (probs * (dprobs - delta_rows[:, :, None])).astype(jnp.bfloat16)
    query_part = jnp.einsum("hqk,khd->qhd", dscores, key_h, preferred_element_type=jnp.float32)
    key_part = jnp.einsum("hqk,qhd->khd", dscores, query_h, preferred_element_type=jnp.float32)
    return (
        query_part.reshape(query_rows, groups * HDIM),
        key_part.reshape(key_rows, groups * HDIM),
        value_part.reshape(key_rows, groups * HDIM),
    )


def crop_terms(query_h, cotan_h, lse_rows, delta_rows, key_h, value_h):
    return lax.map(
        lambda pieces: tile_terms(*pieces), (query_h, cotan_h, lse_rows, delta_rows, key_h, value_h)
    )


def ring_body(queries, keys, values, outputs, grad_out, lse):
    crops = queries.shape[0]
    groups = lse.shape[1]
    rows = lse.shape[2]
    query_own, key_own, value_own, cotan_own, output_own = (
        lax.all_to_all(sent, "head", split_axis=2, concat_axis=1, tiled=True)
        for sent in (queries, keys, values, grad_out, outputs)
    )
    products = cotan_own.astype(jnp.float32) * output_own.astype(jnp.float32)
    delta_rows = jnp.transpose(
        jnp.sum(products.reshape(crops, rows, groups, HDIM), axis=-1), (0, 2, 1)
    )
    query_h = query_own.reshape(crops, rows, groups, HDIM)
    cotan_h = cotan_own.reshape(crops, rows, groups, HDIM)
    key_h = key_own.reshape(crops, rows, groups, HDIM)
    value_h = value_own.reshape(crops, rows, groups, HDIM)
    width = groups * HDIM
    nblocks = lax.axis_size("blk")
    zeros_acc = jnp.zeros((crops, rows, width), jnp.float32)
    start = (query_h, cotan_h, lse, delta_rows, zeros_acc, zeros_acc, zeros_acc)

    def cycle_step(index, carry):
        query_cur, cotan_cur, lse_cur, delta_cur, query_acc, key_acc, value_acc = carry
        query_part, key_part, value_part = crop_terms(
            query_cur, cotan_cur, lse_cur, delta_cur, key_h, value_h
        )
        query_acc, lse_cur, delta_cur = shifted(
            (query_acc + query_part, lse_cur, delta_cur), "blk", 1
        )
        query_cur, cotan_cur = shifted((query_cur, cotan_cur), "blk", 1)
        return (
            query_cur,
            cotan_cur,
            lse_cur,
            delta_cur,
            query_acc,
            key_acc + key_part,
            value_acc + value_part,
        )

    query_cur, cotan_cur, lse_cur, delta_cur, query_acc, key_acc, value_acc = lax.fori_loop(
        0, nblocks - 1, cycle_step, start
    )
    query_part, key_part, value_part = crop_terms(
        query_cur, cotan_cur, lse_cur, delta_cur, key_h, value_h
    )
    query_total = shifted((query_acc + query_part).astype(jnp.bfloat16), "blk", 1).astype(
        jnp.float32
    )
    grad_q16 = (query_total * SCALING).astype(jnp.bfloat16)
    grad_k16 = ((key_acc + key_part) * SCALING).astype(jnp.bfloat16)
    grad_v16 = (value_acc + value_part).astype(jnp.bfloat16)
    return tuple(
        lax.all_to_all(grad, "head", split_axis=1, concat_axis=2, tiled=True)
        for grad in (grad_q16, grad_k16, grad_v16)
    )


def call(kernel, out_shape, *operands, scratch=()):
    specs = [
        pl.BlockSpec(memory_space=pltpu.SMEM if a.dtype == jnp.int32 else pltpu.VMEM)
        for a in operands
    ]
    return pl.pallas_call(
        kernel,
        out_shape=out_shape,
        in_specs=specs,
        out_specs=jax.tree.map(lambda _: pl.BlockSpec(memory_space=pltpu.VMEM), out_shape),
        scratch_shapes=list(scratch),
        compiler_params=pltpu.CompilerParams(vmem_limit_bytes=VMEM_LIMIT),
    )(*operands)


def shape(*dims, dtype=BF16):
    return jax.ShapeDtypeStruct(dims, dtype)


def head_of(array, head):
    return array[:, HDIM * head : HDIM * (head + 1)]


def pieces_of(column):
    high = column.astype(BF16)
    rest = column - high.astype(F32)
    middle = rest.astype(BF16)
    low = (rest - middle.astype(F32)).astype(BF16)
    return [high.astype(F32), middle.astype(F32), low.astype(F32)]


def pack_queries_kernel(place, q_ref, do_ref, o_ref, out_ref):
    x, w, c = place[0], place[1], place[2]
    rows = q_ref.shape[0]
    q = q_ref[...].astype(F32)
    do = do_ref[...].astype(F32)
    products = do * o_ref[...].astype(F32)
    zeros = jnp.zeros((rows, 58), F32)
    for xs in range(2):
        for ws in range(2):
            sides, deltas = [], []
            for cs in range(2):
                head = 4 * xs + 2 * cs + ws
                sides.append(jnp.concatenate([head_of(q, head), head_of(do, head)], axis=1))
                delta = jnp.sum(head_of(products, head), axis=1, keepdims=True)
                deltas.append(jnp.concatenate(pieces_of(delta), axis=1))
            kept = jnp.where(c == 0, sides[0], sides[1])
            given = jnp.where(c == 0, sides[1], sides[0])
            kept_delta = jnp.where(c == 0, deltas[0], deltas[1])
            given_delta = jnp.where(c == 0, deltas[1], deltas[0])
            row = jnp.concatenate([kept, given, kept_delta, given_delta, zeros], axis=1)
            out_ref[2 * (x ^ xs) + (w ^ ws)] = row.astype(BF16)


def pack_keys_kernel(place, k_ref, v_ref, out_ref):
    x, w, c = place[0], place[1], place[2]
    rows = k_ref.shape[0]
    k = k_ref[...].astype(F32)
    v = v_ref[...].astype(F32)
    zeros = jnp.zeros((rows, 64), F32)
    for xs in range(2):
        for ws in range(2):
            sides = []
            for cs in range(2):
                head = 4 * xs + 2 * cs + ws
                sides.append(jnp.concatenate([head_of(k, head), head_of(v, head)], axis=1))
            kept = jnp.where(c == 0, sides[0], sides[1])
            given = jnp.where(c == 0, sides[1], sides[0])
            row = jnp.concatenate([kept, given, zeros], axis=1)
            out_ref[2 * (x ^ xs) + (w ^ ws)] = row.astype(BF16)


def lined_up(own, near, other):
    blocks = []
    for j in range(4):
        held = own if j == 0 else near[j - 1][...]
        blocks.append(held[:, :160].astype(F32))
        blocks.append(other[j][:, 32:192].astype(F32))
    return jnp.concatenate(blocks, axis=1).astype(BF16)


def gather_queries_kernel(place, own, near1, near2, near3, other, lse_own, lse_near, wide, aux, tall):
    rows = wide.shape[0]
    near = (near1, near2, near3)
    wide[...] = lined_up(own[0], near, other)
    pad = jnp.zeros((PADDED - rows, 128), BF16)
    for j in range(4):
        held = own[0] if j == 0 else near[j - 1][...]
        tall[2 * j, 0:rows] = held[:, 256:384]
        tall[2 * j + 1, 0:rows] = other[j][:, 128:256]
        tall[2 * j, rows:PADDED] = pad
        tall[2 * j + 1, rows:PADDED] = pad
    spots = tall[...].reshape(8 * PADDED, 128)
    row = lax.broadcasted_iota(jnp.int32, (8, 128), 0)
    lane = lax.broadcasted_iota(jnp.int32, (8, 128), 1)
    first = 64 + 3 * row
    chosen = jnp.where((row < 2) & (lane >= first) & (lane < first + 3), 1.0, 0.0).astype(BF16)
    sums = lax.dot_general(
        chosen, spots, (((1,), (1,)), ((), ())), preferred_element_type=F32
    )
    at = lax.broadcasted_iota(jnp.int32, (1, 8 * PADDED), 1)
    odd = lax.rem(lax.div(at, PADDED), 2)
    delta = jnp.where(odd == 0, sums[0:1], sums[1:2])
    h = place[3]
    parts = []
    for i in range(8):
        source = lse_near if (i // 2) % 2 else lse_own
        part = source[pl.ds(h ^ (2 * (i // 4) + i % 2), 1), :]
        parts += [part, jnp.zeros((1, PADDED - rows), F32)]
    lse = jnp.concatenate(parts, axis=1) * LOG2E
    aux[...] = jnp.concatenate([lse, delta], axis=0)


def gather_keys_kernel(own, near1, near2, near3, other, wide):
    wide[...] = lined_up(own[0], (near1, near2, near3), other)


def spread(wide_ref, left, right):
    rows = wide_ref.shape[0]
    wide = wide_ref[...].astype(F32)
    pad = jnp.zeros((PADDED - rows, HDIM), F32)
    for i in range(8):
        at = 2 * HDIM * i
        spot = pl.ds(PADDED * i, PADDED)
        left[spot, :] = jnp.concatenate([wide[:, at : at + HDIM], pad], axis=0).astype(BF16)
        right[spot, :] = jnp.concatenate(
            [wide[:, at + HDIM : at + 2 * HDIM], pad], axis=0
        ).astype(BF16)


def tile_step(q_wide, aux, k_wide, scratch, chunk):
    q_s, do_s, k_s, v_s = scratch
    spread(q_wide, q_s, do_s)
    spread(k_wide, k_s, v_s)
    q, do = q_s[...], do_s[...]
    q_t, do_t = q.T, do.T
    k_t = k_s[...].T
    lse, delta = aux[0:1, :], aux[1:2, :]
    total = q.shape[0]
    dq_t = None
    parts = []
    for start in range(0, total, chunk):
        spot = slice(start, start + chunk)
        k, v = k_s[spot, :], v_s[spot, :]
        scores = jnp.dot(k, q_t, preferred_element_type=F32)
        probs = jnp.exp2(scores * (SCALING * LOG2E) - lse)
        dv = jnp.dot(probs.astype(BF16), do, preferred_element_type=F32)
        dprobs = jnp.dot(v, do_t, preferred_element_type=F32)
        dscores = (probs * (dprobs - delta)).astype(BF16)
        dk = jnp.dot(dscores, q, preferred_element_type=F32)
        more = jnp.dot(k_t[:, spot], dscores, preferred_element_type=F32)
        dq_t = more if dq_t is None else dq_t + more
        parts.append((spot, dk, dv))
    return dq_t, parts


CHUNK = 256


def own_own_kernel(q_wide, aux, k_wide, dq_t, dk, dv, *scratch):
    dq_t[...], parts = tile_step(q_wide, aux, k_wide, scratch, CHUNK)
    for spot, dk_part, dv_part in parts:
        dk[spot, :] = dk_part
        dv[spot, :] = dv_part


def own_far_kernel(q_wide, aux, k_wide, dq_before, dq_t, dk, dv, *scratch):
    more, parts = tile_step(q_wide, aux, k_wide, scratch, CHUNK)
    dq_t[...] = dq_before[...] + more
    for spot, dk_part, dv_part in parts:
        dk[spot, :] = dk_part
        dv[spot, :] = dv_part


def far_far_kernel(q_wide, aux, k_wide, dk_before, dv_before, dq_t, wire, dk, dv, *scratch):
    dq_t[...], parts = tile_step(q_wide, aux, k_wide, scratch, CHUNK)
    for spot, dk_part, dv_part in parts:
        dk[spot, :] = (dk_before[spot, :] + dk_part) * SCALING
        dv[spot, :] = dv_before[spot, :] + dv_part
    rows = wire.shape[0]
    blocks = []
    for i in range(8):
        spot = slice(PADDED * i, PADDED * i + rows)
        blocks += [dk[spot, :], dv[spot, :]]
    wire[...] = jnp.concatenate(blocks, axis=1).astype(BF16)


def far_own_kernel(q_wide, aux, k_wide, dq_before, dk_before, dv_before, wire, dk, dv, *scratch):
    more, parts = tile_step(q_wide, aux, k_wide, scratch, CHUNK)
    dq = ((dq_before[...] + more) * SCALING).T
    rows = wire.shape[0]
    wire[...] = jnp.concatenate(
        [dq[PADDED * i : PADDED * i + rows] for i in range(8)], axis=1
    ).astype(BF16)
    for spot, dk_part, dv_part in parts:
        dk[spot, :] = dk_before[spot, :] + dk_part
        dv[spot, :] = dv_before[spot, :] + dv_part


def pack_grads_kernel(dq_t, dk, dv, dq_wire, dkv_wire, out):
    rows = dq_wire.shape[0]
    dq = dq_t[...].T
    dq_far = dq_wire[...].astype(F32)
    dkv_far = dkv_wire[...].astype(F32)
    zeros = jnp.zeros((rows, 16), F32)
    for i in range(8):
        spot = slice(PADDED * i, PADDED * i + rows)
        at = 2 * HDIM * i
        block = jnp.concatenate(
            [
                dq[spot] * SCALING + dq_far[:, HDIM * i : HDIM * (i + 1)],
                dk[spot, :] * SCALING + dkv_far[:, at : at + HDIM],
                dv[spot, :] + dkv_far[:, at + HDIM : at + 2 * HDIM],
                zeros,
            ],
            axis=1,
        )
        out[i // 2, :, 256 * (i % 2) : 256 * (i % 2) + 256] = block.astype(BF16)


def unpack_grads_kernel(place, held, other, dq, dk, dv):
    x, w, c = place[0], place[1], place[2]
    blocks = []
    for head in range(8):
        xs, cs, ws = head // 4, (head // 2) % 2, head % 2
        j = 2 * (x ^ xs) + (w ^ ws)
        blocks.append(
            jnp.where(c == cs, held[j][:, :256].astype(F32), other[j].astype(F32))
        )
    for k, out in enumerate((dq, dk, dv)):
        out[...] = jnp.concatenate(
            [block[:, HDIM * k : HDIM * (k + 1)] for block in blocks], axis=1
        ).astype(BF16)


def flipped(array, head_bits, blk_bits):
    heads, blks = lax.axis_size("head"), lax.axis_size("blk")
    if not blk_bits:
        return lax.ppermute(array, "head", [(i, i ^ head_bits) for i in range(heads)])
    if not head_bits:
        return lax.ppermute(array, "blk", [(i, i ^ blk_bits) for i in range(blks)])
    bits = head_bits * blks + blk_bits
    return lax.ppermute(array, ("head", "blk"), [(i, i ^ bits) for i in range(heads * blks)])


def to_chips(packed):
    return [flipped(packed[1], 0, 2), flipped(packed[2], 2, 0), flipped(packed[3], 2, 2)]


def grid_body(queries, keys, values, outputs, grad_out, lse):
    rows = queries.shape[1]
    h, b = lax.axis_index("head"), lax.axis_index("blk")
    x, c, w = h // 2, h % 2, (b // 2) % 2
    place = jnp.stack([x, w, c, h]).astype(jnp.int32)
    padded = 8 * PADDED
    tile_scratch = [pltpu.VMEM((padded, HDIM), BF16)] * 4

    packed_q = call(
        pack_queries_kernel, shape(4, rows, 384), place, queries[0], grad_out[0], outputs[0]
    )
    near_q = to_chips(packed_q)
    packed_k = call(pack_keys_kernel, shape(4, rows, 384), place, keys[0], values[0])
    near_k = to_chips(packed_k)
    lse_rows = lse[0].reshape(2, 4, rows)
    lse_own = lax.dynamic_index_in_dim(lse_rows, w, 0, keepdims=False)
    lse_near = flipped(lax.dynamic_index_in_dim(lse_rows, 1 - w, 0, keepdims=False), 0, 2)

    other_q = flipped(jnp.stack([a[:, 128:] for a in [packed_q[0]] + near_q]), 1, 0)
    q_own, aux_own = call(
        gather_queries_kernel,
        (shape(rows, 1280), shape(2, padded, dtype=F32)),
        place,
        packed_q,
        *near_q,
        other_q,
        lse_own,
        lse_near,
        scratch=[pltpu.VMEM((8, PADDED, 128), BF16)],
    )
    q_far = flipped(q_own, 0, 4)
    aux_far = flipped(aux_own, 0, 4)
    other_k = flipped(jnp.stack([a[:, 128:] for a in [packed_k[0]] + near_k]), 1, 0)
    k_own = call(gather_keys_kernel, shape(rows, 1280), packed_k, *near_k, other_k)
    k_far = flipped(k_own, 0, 1)

    grad_shape = shape(padded, HDIM, dtype=F32)
    dq_shape = shape(HDIM, padded, dtype=F32)
    dq_own, dk_own, dv_own = call(
        own_own_kernel, (dq_shape, grad_shape, grad_shape), q_own, aux_own, k_own,
        scratch=tile_scratch,
    )
    dq_own, dk_far, dv_far = call(
        own_far_kernel, (dq_shape, grad_shape, grad_shape), q_own, aux_own, k_far, dq_own,
        scratch=tile_scratch,
    )
    sums = [pltpu.VMEM((padded, HDIM), F32)] * 2
    dq_far, dkv_wire = call(
        far_far_kernel, (dq_shape, shape(rows, 1280)), q_far, aux_far, k_far, dk_far, dv_far,
        scratch=sums + tile_scratch,
    )
    dkv_back = flipped(dkv_wire, 0, 1)
    dq_wire, dk_own, dv_own = call(
        far_own_kernel, (shape(rows, 640), grad_shape, grad_shape),
        q_far, aux_far, k_own, dq_far, dk_own, dv_own,
        scratch=tile_scratch,
    )
    dq_back = flipped(dq_wire, 0, 4)

    packed_g = call(
        pack_grads_kernel, shape(4, rows, 512), dq_own, dk_own, dv_own, dq_back, dkv_back
    )
    held = jnp.stack([packed_g[0]] + to_chips(packed_g))
    other = flipped(held[:, :, 256:], 1, 0)
    out = shape(rows, queries.shape[2])
    grads = call(unpack_grads_kernel, (out, out, out), place, held, other)
    return tuple(grad[None] for grad in grads)


def solution(mesh):
    placed = P(None, ("blk", "head"), None)
    on_grid = mesh.shape["head"] == 4 and mesh.shape["blk"] == 8
    return jax.shard_map(
        grid_body if on_grid else ring_body,
        mesh=mesh,
        in_specs=(placed,) * 5 + (P(None, "head", "blk"),),
        out_specs=(placed,) * 3,
        check_vma=False,
    )
```

time: 188 us -> 64.3 us (0.34)
  starting transfers between devices: 66.1 us -> 20.7 us
  waiting for transfers between devices: 70 us -> 25.2 us
  local copies, waits for them, and re-layouts: 22.6 us -> 2.94 us
  other arithmetic: 14.9 us -> 0.18 us
  Pallas kernels: 0 us -> 14.1 us
  matrix products: 11.8 us -> 0 us
    ppermute x36 -> x18, waiting for transfers between devices: 59.9 us -> 25.2 us  [the longest x9 14.6 us: flipped(): return lax.ppermute(array, 'blk', [(i, i ^ blk_bits) for i in range(blks)])]
    all_to_all x8 -> x0, starting transfers between devices: 27.8 us -> none  [the longest x1 4.21 us: body(): lax.all_to_all(sent[0], 'head', split_axis=2, concat_axis=1, tiled=True)]
    ppermute x36 -> x18, starting transfers between devices: 38.3 us -> 20.7 us  [the longest x9 14.6 us: flipped(): return lax.ppermute(array, 'blk', [(i, i ^ blk_bits) for i in range(blks)])]
    pallas_call x0 -> x10, Pallas kernels: none -> 14.1 us  [call(): pl.pallas_call(kernel, out_shape=out_shape, in_specs=specs, out_specs=jax...]
    unnamed x10 -> x0, other arithmetic: 13.6 us -> none
    dot_general x40 -> x0, matrix products: 11.8 us -> none  [the longest x8 2.9 us: tile_terms(): jnp.einsum('qhd,khd->hqk', query_h, key_h, preferred_element_type=jnp.flo...]
    unnamed x32 -> x12, local copies, waits for them, and re-layouts: 13.8 us -> 2.71 us
    all_to_all x8 -> x0, waiting for transfers between devices: 10.1 us -> none  [the longest x1 1.61 us: body(): lax.all_to_all(sent[0], 'head', split_axis=2, concat_axis=1, tiled=True)]
  transfers between devices with their start and end apart: 44 -> 18, of which waited for: 32 -> 9; matrix products, arithmetic and copies ran while one was open for 20% -> 0% of each run, Pallas kernels for 0% -> 12%
where the time goes in v1:
time: 64.3 us; the launch traced here: 64.1 us
  waiting for transfers between devices  25.2 us (39%)
  starting transfers between devices  20.7 us (32%)
  Pallas kernels  14.1 us (22%)
  local copies, waits for them, and re-layouts  2.94 us (5%)
  between operations  0.92 us (1%)
    ppermute x9, waiting for transfers between devices, flipped(): return lax.ppermute(array, 'blk', [(i, i ^ blk_bits) for i in range(blks)])  14.6 us
    ppermute x9, starting transfers between devices, flipped(): return lax.ppermute(array, 'blk', [(i, i ^ blk_bits) for i in range(blks)])  14.6 us
    pallas_call x10, Pallas kernels, call(): pl.pallas_call(kernel, out_shape=out_shape, in_specs=specs, out_specs=jax...  14.1 us
    ppermute x3, waiting for transfers between devices, flipped(): lax.ppermute(array, ('head', 'blk'), [(i, i ^ bits) for i in range(heads...  6.28 us
    ppermute x6, starting transfers between devices, flipped(): lax.ppermute(array, 'head', [(i, i ^ head_bits) for i in range(heads)])  4.62 us
    ppermute x6, waiting for transfers between devices, flipped(): lax.ppermute(array, 'head', [(i, i ^ head_bits) for i in range(heads)])  4.29 us
    unnamed x12, local copies, waits for them, and re-layouts  2.71 us
    ppermute x3, starting transfers between devices, flipped(): lax.ppermute(array, ('head', 'blk'), [(i, i ^ bits) for i in range(heads...  1.5 us
  transfers between devices with their start and end apart: 18, of which 9 were waited for; matrix products, arithmetic and copies ran while one was open for 0% of the time, Pallas kernels for 12%

profile of v1, /device:TPU:0, one launch (start us, length us, event | category | flops | bytes accessed | tf_op | source)
XLA Modules:
  0.0 64.1 jit_solution(1542110923202787353)
XLA Ops:
  0.7 0.1 pad_add_fusion.place
  0.8 0.8 %copy-done.2 = bf16[1,88,640]{2,1,0:T(8,128)(2,1)S(1)} copy-done((bf16[1,88,640]{2,1,0:T(8,128)(2,1)S(1)}, bf16[1,88,640]{2,1,0:T(8,128)(2,1)}, u32[]{:S(2)}) %copy-start.2) | copy-done | bytes 112664
  1.5 0.9 %copy-done.3 = bf16[1,88,640]{2,1,0:T(8,128)(2,1)S(1)} copy-done((bf16[1,88,640]{2,1,0:T(8,128)(2,1)S(1)}, bf16[1,88,640]{2,1,0:T(8,128)(2,1)}, u32[]{:S(2)}) %copy-start.3) | copy-done | bytes 112664
  2.4 0.9 %copy-done.4 = bf16[1,88,640]{2,1,0:T(8,128)(2,1)S(1)} copy-done((bf16[1,88,640]{2,1,0:T(8,128)(2,1)S(1)}, bf16[1,88,640]{2,1,0:T(8,128)(2,1)}, u32[]{:S(2)}) %copy-start.4) | copy-done | bytes 112664
  3.3 1.8 %shard_map.85.own = bf16[4,88,384]{2,1,0:T(8,128)(2,1)S(1)} custom-call(s32[4]{0:T(128)S(1)} %pad_add_fusion.place, bf16[88,640]{1,0:T(8,128)(2,1)S(1)} %bitcast.59, bf16[88,640]{1,0:T(8,128)(2,1)S(1)} %bitcast.60, bf16[88,640]{1,0:T(8,128)(2,1)S(1)} %bitcast.61), custom_call_target="tpu_custom_call" | custom-call | tf_op jit(solution)/shard_map/pallas_call | solution.py:116
  5.1 0.0 copy-start
  5.2 0.0 copy-start.1
  5.2 3.1 %collective-permute-start = (bf16[88,384]{1,0:T(8,128)(2,1)S(1)}, bf16[88,384]{1,0:T(8,128)(2,1)S(1)}, u32[]{:S(2)}, u32[]{:S(2)}) collective-permute-start(bf16[88,384]{1,0:T(8,128)(2,1)S(1)} %get-tuple-element.46), channel_id=1, source_target_pairs={{0,2},{1,3},{2,0},{3,1},{4,6},{5,7},{6,4},{7,5},{8,10},{9,11},{10,... | collective-permute-start | bytes 202760 | tf_op jit(solution)/shard_map/ppermute | solution.py:351
  8.3 1.5 %collective-permute-start.1 = (bf16[88,384]{1,0:T(8,128)(2,1)S(1)}, bf16[88,384]{1,0:T(8,128)(2,1)S(1)}, u32[]{:S(2)}, u32[]{:S(2)}) collective-permute-start(bf16[88,384]{1,0:T(8,128)(2,1)S(1)} %get-tuple-element.45), channel_id=1, source_target_pairs={{0,16},{8,24},{16,0},{24,8},{1,17},{9,25},{17,1},{25,9},{2,18},{10... | collective-permute-start | bytes 202760 | tf_op jit(solution)/shard_map/ppermute | solution.py:349
  9.8 0.0 collective-permute-start.2
  9.8 1.0 %shard_map.87.own = bf16[4,88,384]{2,1,0:T(8,128)(2,1)S(1)} custom-call(s32[4]{0:T(128)S(1)} %pad_add_fusion.place, bf16[88,640]{1,0:T(8,128)(2,1)S(1)} %bitcast.57, bf16[88,640]{1,0:T(8,128)(2,1)S(1)} %bitcast.58), custom_call_target="tpu_custom_call" | custom-call | tf_op jit(solution)/shard_map/pallas_call | solution.py:116
  10.8 2.0 %collective-permute-start.5 = (bf16[88,384]{1,0:T(8,128)(2,1)S(1)}, bf16[88,384]{1,0:T(8,128)(2,1)S(1)}, u32[]{:S(2)}, u32[]{:S(2)}) collective-permute-start(bf16[88,384]{1,0:T(8,128)(2,1)S(1)} %get-tuple-element.42), channel_id=1, source_target_pairs={{0,2},{1,3},{2,0},{3,1},{4,6},{5,7},{6,4},{7,5},{8,10},{9,11},{10,... | collective-permute-start | bytes 202760 | tf_op jit(solution)/shard_map/ppermute | solution.py:351
  12.9 1.4 %collective-permute-start.7 = (bf16[88,384]{1,0:T(8,128)(2,1)S(1)}, bf16[88,384]{1,0:T(8,128)(2,1)S(1)}, u32[]{:S(2)}, u32[]{:S(2)}) collective-permute-start(bf16[88,384]{1,0:T(8,128)(2,1)S(1)} %get-tuple-element.40), channel_id=1, source_target_pairs={{0,18},{1,19},{2,16},{3,17},{4,22},{5,23},{6,20},{7,21},{8,26},{9,... | collective-permute-start | bytes 202760 | tf_op jit(solution)/shard_map/ppermute | solution.py:353
  14.2 3.8 %collective-permute-done.7.near3 = bf16[88,384]{1,0:T(8,128)(2,1)S(1)} collective-permute-done((bf16[88,384]{1,0:T(8,128)(2,1)S(1)}, bf16[88,384]{1,0:T(8,128)(2,1)S(1)}, u32[]{:S(2)}, u32[]{:S(2)}) %collective-permute-start.7) | collective-permute-done | bytes 67616 | tf_op jit(solution)/shard_map/ppermute | solution.py:353
  18.0 1.5 %collective-permute-start.6 = (bf16[88,384]{1,0:T(8,128)(2,1)S(1)}, bf16[88,384]{1,0:T(8,128)(2,1)S(1)}, u32[]{:S(2)}, u32[]{:S(2)}) collective-permute-start(bf16[88,384]{1,0:T(8,128)(2,1)S(1)} %get-tuple-element.41), channel_id=1, source_target_pairs={{0,16},{8,24},{16,0},{24,8},{1,17},{9,25},{17,1},{25,9},{2,18},{10... | collective-permute-start | bytes 202760 | tf_op jit(solution)/shard_map/ppermute | solution.py:349
  19.5 2.8 %collective-permute-done.6.near2 = bf16[88,384]{1,0:T(8,128)(2,1)S(1)} collective-permute-done((bf16[88,384]{1,0:T(8,128)(2,1)S(1)}, bf16[88,384]{1,0:T(8,128)(2,1)S(1)}, u32[]{:S(2)}, u32[]{:S(2)}) %collective-permute-start.6) | collective-permute-done | bytes 67616 | tf_op jit(solution)/shard_map/ppermute | solution.py:349
  22.4 0.1 collective-permute-start.8
  22.5 0.0 collective-permute-done.2.near3
  22.6 0.0 copy-start.5
  22.6 0.5 collective-permute-start.3
  23.1 0.1 copy-done.5
  23.3 0.1 reshape_squeeze.3
  23.3 0.8 %collective-permute-start.4 = (f32[4,88]{1,0:T(4,128)S(1)}, f32[4,88]{1,0:T(4,128)S(1)}, u32[]{:S(2)}, u32[]{:S(2)}) collective-permute-start(f32[4,88]{1,0:T(4,128)S(1)} %get-tuple-element.47), channel_id=1, source_target_pairs={{0,2},{1,3},{2,0},{3,1},{4,6},{5,7},{6,4},{7,5},{8,10},{9,11},{10,... | collective-permute-start | bytes 4232 | tf_op jit(solution)/shard_map/ppermute | solution.py:351
  24.1 0.0 collective-permute-done.8.other
  24.1 0.1 shard_map.88.k_wide
  24.2 1.6 %collective-permute-start.9 = (bf16[88,1280]{1,0:T(8,128)(2,1)S(1)}, bf16[88,1280]{1,0:T(8,128)(2,1)S(1)}, u32[]{:S(2)}, u32[]{:S(2)}) collective-permute-start(bf16[88,1280]{1,0:T(8,128)(2,1)S(1)} %shard_map.88.k_wide), channel_id=1, source_target_pairs={{0,1},{1,0},{2,3},{3,2},{4,5},{5,4},{6,7},{7,6},{8,9},{9,8},{10,11... | collective-permute-start | bytes 675848 | tf_op jit(solution)/shard_map/ppermute | solution.py:351
  25.8 1.1 %collective-permute-done.4.lse_near = f32[4,88]{1,0:T(4,128)S(1)} collective-permute-done((f32[4,88]{1,0:T(4,128)S(1)}, f32[4,88]{1,0:T(4,128)S(1)}, u32[]{:S(2)}, u32[]{:S(2)}) %collective-permute-start.4) | collective-permute-done | bytes 1440 | tf_op jit(solution)/shard_map/ppermute | solution.py:351
  27.0 0.7 %shard_map.86 = (bf16[88,1280]{1,0:T(8,128)(2,1)S(1)}, f32[2,768]{1,0:T(2,128)S(1)}) custom-call(s32[4]{0:T(128)S(1)} %pad_add_fusion.place, bf16[4,88,384]{2,1,0:T(8,128)(2,1)S(1)} %shard_map.85.own, bf16[88,384]{1,0:T(8,128)(2,1)S(1)} %collective-permute-done.near1, bf16[88,384]{1,0:T(8,128)(2,1)S(1)} %collective-permute-done.1.near2, ...), custom_call_target="tpu_custom_call" | custom-call | tf_op jit(solution)/shard_map/pallas_call | solution.py:116
  27.7 2.6 %collective-permute-start.10 = (bf16[88,1280]{1,0:T(8,128)(2,1)S(1)}, bf16[88,1280]{1,0:T(8,128)(2,1)S(1)}, u32[]{:S(2)}, u32[]{:S(2)}) collective-permute-start(bf16[88,1280]{1,0:T(8,128)(2,1)S(1)} %get-tuple-element.19.q_wide), channel_id=1, source_target_pairs={{0,4},{1,5},{2,6},{3,7},{4,0},{5,1},{6,2},{7,3},{8,12},{9,13},{10,... | collective-permute-start | bytes 675848 | tf_op jit(solution)/shard_map/ppermute | solution.py:351
  30.3 0.3 collective-permute-start.11
  30.7 1.9 %shard_map.89 = (f32[80,768]{1,0:T(8,128)S(1)}, f32[768,80]{1,0:T(8,128)S(1)}, f32[768,80]{1,0:T(8,128)S(1)}) custom-call(bf16[88,1280]{1,0:T(8,128)(2,1)S(1)} %get-tuple-element.19.q_wide, f32[2,768]{1,0:T(2,128)S(1)} %get-tuple-element.20.aux, bf16[88,1280]{1,0:T(8,128)(2,1)S(1)} %shard_map.88.k_wide), custom_call_target="tpu_custom_call" | custom-call | tf_op jit(solution)/shard_map/pallas_call | solution.py:116
  32.6 1.9 %shard_map.90 = (f32[80,768]{1,0:T(8,128)S(1)}, f32[768,80]{1,0:T(8,128)S(1)}, f32[768,80]{1,0:T(8,128)S(1)}) custom-call(bf16[88,1280]{1,0:T(8,128)(2,1)S(1)} %get-tuple-element.19.q_wide, f32[2,768]{1,0:T(2,128)S(1)} %get-tuple-element.20.aux, bf16[88,1280]{1,0:T(8,128)(2,1)S(1)} %collective-permute-done.9.k_wide, f32[80,768]{1,0:T(8,128)S(1)} %get-tuple-element.21.dq_before), custom_call_target="tpu_custom_call" | custom-call | tf_op jit(solution)/shard_map/pallas_call | solution.py:116
  34.6 5.9 %collective-permute-done.11.aux = f32[2,768]{1,0:T(2,128)S(1)} collective-permute-done((f32[2,768]{1,0:T(2,128)S(1)}, f32[2,768]{1,0:T(2,128)S(1)}, u32[]{:S(2)}, u32[]{:S(2)}) %collective-permute-start.11) | collective-permute-done | bytes 6176 | tf_op jit(solution)/shard_map/ppermute | solution.py:351
  40.5 2.1 %shard_map.91 = (f32[80,768]{1,0:T(8,128)S(1)}, bf16[88,1280]{1,0:T(8,128)(2,1)S(1)}) custom-call(bf16[88,1280]{1,0:T(8,128)(2,1)S(1)} %collective-permute-done.10.q_wide, f32[2,768]{1,0:T(2,128)S(1)} %collective-permute-done.11.aux, bf16[88,1280]{1,0:T(8,128)(2,1)S(1)} %collective-permute-done.9.k_wide, f32[768,80]{1,0:T(8,128)S(1)} %get-tuple-element.23.dk_before, ...), custom_call_target="tpu_custom_call" | custom-call | tf_op jit(solution)/shard_map/pallas_call | solution.py:116
  42.5 1.6 %collective-permute-start.13 = (bf16[88,1280]{1,0:T(8,128)(2,1)S(1)}, bf16[88,1280]{1,0:T(8,128)(2,1)S(1)}, u32[]{:S(2)}, u32[]{:S(2)}) collective-permute-start(bf16[88,1280]{1,0:T(8,128)(2,1)S(1)} %get-tuple-element.31), channel_id=1, source_target_pairs={{0,1},{1,0},{2,3},{3,2},{4,5},{5,4},{6,7},{7,6},{8,9},{9,8},{10,11... | collective-permute-start | bytes 675848 | tf_op jit(solution)/shard_map/ppermute | solution.py:351
  44.1 2.1 %shard_map.92 = (bf16[88,640]{1,0:T(8,128)(2,1)S(1)}, f32[768,80]{1,0:T(8,128)S(1)}, f32[768,80]{1,0:T(8,128)S(1)}) custom-call(bf16[88,1280]{1,0:T(8,128)(2,1)S(1)} %collective-permute-done.10.q_wide, f32[2,768]{1,0:T(2,128)S(1)} %collective-permute-done.11.aux, bf16[88,1280]{1,0:T(8,128)(2,1)S(1)} %shard_map.88.k_wide, ...), custom_call_target="tpu_custom_call" | custom-call | tf_op jit(solution)/shard_map/pallas_call | solution.py:116
  46.3 0.1 collective-permute-start.12
  46.4 7.4 %collective-permute-done.12.dq_wire = bf16[88,640]{1,0:T(8,128)(2,1)S(1)} collective-permute-done((bf16[88,640]{1,0:T(8,128)(2,1)S(1)}, bf16[88,640]{1,0:T(8,128)(2,1)S(1)}, u32[]{:S(2)}, u32[]{:S(2)}) %collective-permute-start.12) | collective-permute-done | bytes 112672 | tf_op jit(solution)/shard_map/ppermute | solution.py:351
  53.8 1.0 %shard_map.93 = bf16[4,88,512]{2,1,0:T(8,128)(2,1)S(1)} custom-call(f32[80,768]{1,0:T(8,128)S(1)} %get-tuple-element.22.dq_t, f32[768,80]{1,0:T(8,128)S(1)} %get-tuple-element.28.dk, f32[768,80]{1,0:T(8,128)S(1)} %get-tuple-element.29.dv, bf16[88,640]{1,0:T(8,128)(2,1)S(1)} %collective-permute-done.12.dq_wire, ...), custom_call_target="tpu_custom_call" | custom-call | tf_op jit(solution)/shard_map/pallas_call | solution.py:116
  54.8 0.1 collective-permute-start.16
  54.9 1.0 %collective-permute-start.15 = (bf16[88,512]{1,0:T(8,128)(2,1)S(1)}, bf16[88,512]{1,0:T(8,128)(2,1)S(1)}, u32[]{:S(2)}, u32[]{:S(2)}) collective-permute-start(bf16[88,512]{1,0:T(8,128)(2,1)S(1)} %get-tuple-element.37), channel_id=1, source_target_pairs={{0,16},{8,24},{16,0},{24,8},{1,17},{9,25},{17,1},{25,9},{2,18},{10... | collective-permute-start | bytes 270344 | tf_op jit(solution)/shard_map/ppermute | solution.py:349
  55.8 2.5 %collective-permute-start.14 = (bf16[88,512]{1,0:T(8,128)(2,1)S(1)}, bf16[88,512]{1,0:T(8,128)(2,1)S(1)}, u32[]{:S(2)}, u32[]{:S(2)}) collective-permute-start(bf16[88,512]{1,0:T(8,128)(2,1)S(1)} %get-tuple-element.38), channel_id=1, source_target_pairs={{0,2},{1,3},{2,0},{3,1},{4,6},{5,7},{6,4},{7,5},{8,10},{9,11},{10,... | collective-permute-start | bytes 270344 | tf_op jit(solution)/shard_map/ppermute | solution.py:351
  58.3 2.5 %collective-permute-done.16 = bf16[88,512]{1,0:T(8,128)(2,1)S(1)} collective-permute-done((bf16[88,512]{1,0:T(8,128)(2,1)S(1)}, bf16[88,512]{1,0:T(8,128)(2,1)S(1)}, u32[]{:S(2)}, u32[]{:S(2)}) %collective-permute-start.16) | collective-permute-done | bytes 90144 | tf_op jit(solution)/shard_map/ppermute | solution.py:353
  60.8 0.1 collective-permute-done.15
  60.9 0.1 collective-permute-done.14
  61.1 0.1 collective-permute-start.17
  61.2 1.4 %collective-permute-done.17.other = bf16[4,88,256]{2,1,0:T(8,128)(2,1)S(1)} collective-permute-done((bf16[4,88,256]{2,1,0:T(8,128)(2,1)S(1)}, bf16[4,88,256]{2,1,0:T(8,128)(2,1)S(1)}, u32[]{:S(2)}, u32[]{:S(2)}) %collective-permute-start.17) | collective-permute-done | bytes 180256 | tf_op jit(solution)/shard_map/ppermute | solution.py:349
  62.6 1.5 %shard_map.94 = (bf16[88,640]{1,0:T(8,128)(2,1)}, bf16[88,640]{1,0:T(8,128)(2,1)}, bf16[88,640]{1,0:T(8,128)(2,1)}) custom-call(s32[4]{0:T(128)S(1)} %pad_add_fusion.place, bf16[4,88,512]{2,1,0:T(8,128)(2,1)S(1)} %pad_maximum_fusion.held, bf16[4,88,256]{2,1,0:T(8,128)(2,1)S(1)} %collective-permute-done.17.other), custom_call_target="tpu_custom_call" | custom-call | tf_op jit(solution)/shard_map/pallas_call | solution.py:116
  (28 shorter events, 0.3 us)
Async XLA Ops:
  0.6 0.9 %copy-start.2 = (bf16[1,88,640]{2,1,0:T(8,128)(2,1)S(1)}, bf16[1,88,640]{2,1,0:T(8,128)(2,1)}, u32[]{:S(2)}) copy-start(bf16[1,88,640]{2,1,0:T(8,128)(2,1)} %param.6) | copy-start | bytes 337924
  1.5 0.9 %copy-start.3 = (bf16[1,88,640]{2,1,0:T(8,128)(2,1)S(1)}, bf16[1,88,640]{2,1,0:T(8,128)(2,1)}, u32[]{:S(2)}) copy-start(bf16[1,88,640]{2,1,0:T(8,128)(2,1)} %param.10) | copy-start | bytes 337924
  2.4 0.9 %copy-start.4 = (bf16[1,88,640]{2,1,0:T(8,128)(2,1)S(1)}, bf16[1,88,640]{2,1,0:T(8,128)(2,1)}, u32[]{:S(2)}) copy-start(bf16[1,88,640]{2,1,0:T(8,128)(2,1)} %param.9) | copy-start | bytes 337924
  5.1 4.7 %copy-start = (bf16[1,88,640]{2,1,0:T(8,128)(2,1)S(1)}, bf16[1,88,640]{2,1,0:T(8,128)(2,1)}, u32[]{:S(2)}) copy-start(bf16[1,88,640]{2,1,0:T(8,128)(2,1)} %param.7) | copy-start | bytes 337924
  5.2 4.7 %copy-start.1 = (bf16[1,88,640]{2,1,0:T(8,128)(2,1)S(1)}, bf16[1,88,640]{2,1,0:T(8,128)(2,1)}, u32[]{:S(2)}) copy-start(bf16[1,88,640]{2,1,0:T(8,128)(2,1)} %param.8) | copy-start | bytes 337924
  5.2 17.3 %collective-permute-start = (bf16[88,384]{1,0:T(8,128)(2,1)S(1)}, bf16[88,384]{1,0:T(8,128)(2,1)S(1)}, u32[]{:S(2)}, u32[]{:S(2)}) collective-permute-start(bf16[88,384]{1,0:T(8,128)(2,1)S(1)} %get-tuple-element.46), channel_id=1, source_target_pairs={{0,2},{1,3},{2,0},{3,1},{4,6},{5,7},{6,4},{7,5},{8,10},{9,11},{10,... | collective-permute-start | bytes 202760 | tf_op jit(solution)/shard_map/ppermute | solution.py:351
  8.3 14.2 %collective-permute-start.1 = (bf16[88,384]{1,0:T(8,128)(2,1)S(1)}, bf16[88,384]{1,0:T(8,128)(2,1)S(1)}, u32[]{:S(2)}, u32[]{:S(2)}) collective-permute-start(bf16[88,384]{1,0:T(8,128)(2,1)S(1)} %get-tuple-element.45), channel_id=1, source_target_pairs={{0,16},{8,24},{16,0},{24,8},{1,17},{9,25},{17,1},{25,9},{2,18},{10... | collective-permute-start | bytes 202760 | tf_op jit(solution)/shard_map/ppermute | solution.py:349
  9.8 12.7 %collective-permute-start.2 = (bf16[88,384]{1,0:T(8,128)(2,1)S(1)}, bf16[88,384]{1,0:T(8,128)(2,1)S(1)}, u32[]{:S(2)}, u32[]{:S(2)}) collective-permute-start(bf16[88,384]{1,0:T(8,128)(2,1)S(1)} %get-tuple-element.44), channel_id=1, source_target_pairs={{0,18},{1,19},{2,16},{3,17},{4,22},{5,23},{6,20},{7,21},{8,26},{9,... | collective-permute-start | bytes 202760 | tf_op jit(solution)/shard_map/ppermute | solution.py:353
  10.8 11.5 %collective-permute-start.5 = (bf16[88,384]{1,0:T(8,128)(2,1)S(1)}, bf16[88,384]{1,0:T(8,128)(2,1)S(1)}, u32[]{:S(2)}, u32[]{:S(2)}) collective-permute-start(bf16[88,384]{1,0:T(8,128)(2,1)S(1)} %get-tuple-element.42), channel_id=1, source_target_pairs={{0,2},{1,3},{2,0},{3,1},{4,6},{5,7},{6,4},{7,5},{8,10},{9,11},{10,... | collective-permute-start | bytes 202760 | tf_op jit(solution)/shard_map/ppermute | solution.py:351
  12.9 5.2 %collective-permute-start.7 = (bf16[88,384]{1,0:T(8,128)(2,1)S(1)}, bf16[88,384]{1,0:T(8,128)(2,1)S(1)}, u32[]{:S(2)}, u32[]{:S(2)}) collective-permute-start(bf16[88,384]{1,0:T(8,128)(2,1)S(1)} %get-tuple-element.40), channel_id=1, source_target_pairs={{0,18},{1,19},{2,16},{3,17},{4,22},{5,23},{6,20},{7,21},{8,26},{9,... | collective-permute-start | bytes 202760 | tf_op jit(solution)/shard_map/ppermute | solution.py:353
  18.0 4.3 %collective-permute-start.6 = (bf16[88,384]{1,0:T(8,128)(2,1)S(1)}, bf16[88,384]{1,0:T(8,128)(2,1)S(1)}, u32[]{:S(2)}, u32[]{:S(2)}) collective-permute-start(bf16[88,384]{1,0:T(8,128)(2,1)S(1)} %get-tuple-element.41), channel_id=1, source_target_pairs={{0,16},{8,24},{16,0},{24,8},{1,17},{9,25},{17,1},{25,9},{2,18},{10... | collective-permute-start | bytes 202760 | tf_op jit(solution)/shard_map/ppermute | solution.py:349
  22.4 1.7 %collective-permute-start.8 = (bf16[4,88,256]{2,1,0:T(8,128)(2,1)S(1)}, bf16[4,88,256]{2,1,0:T(8,128)(2,1)S(1)}, u32[]{:S(2)}, u32[]{:S(2)}) collective-permute-start(bf16[4,88,256]{2,1,0:T(8,128)(2,1)S(1)} %pad_maximum_fusion.2), channel_id=1, source_target_pairs={{0,8},{8,0},{16,24},{24,16},{1,9},{9,1},{17,25},{25,17},{2,10},{10... | collective-permute-start | bytes 540680 | tf_op jit(solution)/shard_map/ppermute | solution.py:349
  22.6 0.7 %copy-start.5 = (f32[1,2,352]{2,1,0:T(2,128)S(1)}, f32[1,2,352]{2,1,0:T(2,128)}, u32[]{:S(2)}) copy-start(f32[1,2,352]{2,1,0:T(2,128)} %param.11) | copy-start | bytes 8452
  22.6 4.4 %collective-permute-start.3 = (bf16[4,88,256]{2,1,0:T(8,128)(2,1)S(1)}, bf16[4,88,256]{2,1,0:T(8,128)(2,1)S(1)}, u32[]{:S(2)}, u32[]{:S(2)}) collective-permute-start(bf16[4,88,256]{2,1,0:T(8,128)(2,1)S(1)} %pad_maximum_fusion.1), channel_id=1, source_target_pairs={{0,8},{8,0},{16,24},{24,16},{1,9},{9,1},{17,25},{25,17},{2,10},{10... | collective-permute-start | bytes 540680 | tf_op jit(solution)/shard_map/ppermute | solution.py:349
  23.3 3.6 %collective-permute-start.4 = (f32[4,88]{1,0:T(4,128)S(1)}, f32[4,88]{1,0:T(4,128)S(1)}, u32[]{:S(2)}, u32[]{:S(2)}) collective-permute-start(f32[4,88]{1,0:T(4,128)S(1)} %get-tuple-element.47), channel_id=1, source_target_pairs={{0,2},{1,3},{2,0},{3,1},{4,6},{5,7},{6,4},{7,5},{8,10},{9,11},{10,... | collective-permute-start | bytes 4232 | tf_op jit(solution)/shard_map/ppermute | solution.py:351
  24.2 8.4 %collective-permute-start.9 = (bf16[88,1280]{1,0:T(8,128)(2,1)S(1)}, bf16[88,1280]{1,0:T(8,128)(2,1)S(1)}, u32[]{:S(2)}, u32[]{:S(2)}) collective-permute-start(bf16[88,1280]{1,0:T(8,128)(2,1)S(1)} %shard_map.88.k_wide), channel_id=1, source_target_pairs={{0,1},{1,0},{2,3},{3,2},{4,5},{5,4},{6,7},{7,6},{8,9},{9,8},{10,11... | collective-permute-start | bytes 675848 | tf_op jit(solution)/shard_map/ppermute | solution.py:351
  27.7 12.8 %collective-permute-start.10 = (bf16[88,1280]{1,0:T(8,128)(2,1)S(1)}, bf16[88,1280]{1,0:T(8,128)(2,1)S(1)}, u32[]{:S(2)}, u32[]{:S(2)}) collective-permute-start(bf16[88,1280]{1,0:T(8,128)(2,1)S(1)} %get-tuple-element.19.q_wide), channel_id=1, source_target_pairs={{0,4},{1,5},{2,6},{3,7},{4,0},{5,1},{6,2},{7,3},{8,12},{9,13},{10,... | collective-permute-start | bytes 675848 | tf_op jit(solution)/shard_map/ppermute | solution.py:351
  30.3 10.1 %collective-permute-start.11 = (f32[2,768]{1,0:T(2,128)S(1)}, f32[2,768]{1,0:T(2,128)S(1)}, u32[]{:S(2)}, u32[]{:S(2)}) collective-permute-start(f32[2,768]{1,0:T(2,128)S(1)} %get-tuple-element.20.aux), channel_id=1, source_target_pairs={{0,4},{1,5},{2,6},{3,7},{4,0},{5,1},{6,2},{7,3},{8,12},{9,13},{10,... | collective-permute-start | bytes 18440 | tf_op jit(solution)/shard_map/ppermute | solution.py:351
  42.5 11.2 %collective-permute-start.13 = (bf16[88,1280]{1,0:T(8,128)(2,1)S(1)}, bf16[88,1280]{1,0:T(8,128)(2,1)S(1)}, u32[]{:S(2)}, u32[]{:S(2)}) collective-permute-start(bf16[88,1280]{1,0:T(8,128)(2,1)S(1)} %get-tuple-element.31), channel_id=1, source_target_pairs={{0,1},{1,0},{2,3},{3,2},{4,5},{5,4},{6,7},{7,6},{8,9},{9,8},{10,11... | collective-permute-start | bytes 675848 | tf_op jit(solution)/shard_map/ppermute | solution.py:351
  46.3 7.5 %collective-permute-start.12 = (bf16[88,640]{1,0:T(8,128)(2,1)S(1)}, bf16[88,640]{1,0:T(8,128)(2,1)S(1)}, u32[]{:S(2)}, u32[]{:S(2)}) collective-permute-start(bf16[88,640]{1,0:T(8,128)(2,1)S(1)} %get-tuple-element.30), channel_id=1, source_target_pairs={{0,4},{1,5},{2,6},{3,7},{4,0},{5,1},{6,2},{7,3},{8,12},{9,13},{10,... | collective-permute-start | bytes 337928 | tf_op jit(solution)/shard_map/ppermute | solution.py:351
  54.8 6.0 %collective-permute-start.16 = (bf16[88,512]{1,0:T(8,128)(2,1)S(1)}, bf16[88,512]{1,0:T(8,128)(2,1)S(1)}, u32[]{:S(2)}, u32[]{:S(2)}) collective-permute-start(bf16[88,512]{1,0:T(8,128)(2,1)S(1)} %get-tuple-element.36), channel_id=1, source_target_pairs={{0,18},{1,19},{2,16},{3,17},{4,22},{5,23},{6,20},{7,21},{8,26},{9,... | collective-permute-start | bytes 270344 | tf_op jit(solution)/shard_map/ppermute | solution.py:353
  54.9 6.0 %collective-permute-start.15 = (bf16[88,512]{1,0:T(8,128)(2,1)S(1)}, bf16[88,512]{1,0:T(8,128)(2,1)S(1)}, u32[]{:S(2)}, u32[]{:S(2)}) collective-permute-start(bf16[88,512]{1,0:T(8,128)(2,1)S(1)} %get-tuple-element.37), channel_id=1, source_target_pairs={{0,16},{8,24},{16,0},{24,8},{1,17},{9,25},{17,1},{25,9},{2,18},{10... | collective-permute-start | bytes 270344 | tf_op jit(solution)/shard_map/ppermute | solution.py:349
  55.8 5.2 %collective-permute-start.14 = (bf16[88,512]{1,0:T(8,128)(2,1)S(1)}, bf16[88,512]{1,0:T(8,128)(2,1)S(1)}, u32[]{:S(2)}, u32[]{:S(2)}) collective-permute-start(bf16[88,512]{1,0:T(8,128)(2,1)S(1)} %get-tuple-element.38), channel_id=1, source_target_pairs={{0,2},{1,3},{2,0},{3,1},{4,6},{5,7},{6,4},{7,5},{8,10},{9,11},{10,... | collective-permute-start | bytes 270344 | tf_op jit(solution)/shard_map/ppermute | solution.py:351
  61.1 1.5 %collective-permute-start.17 = (bf16[4,88,256]{2,1,0:T(8,128)(2,1)S(1)}, bf16[4,88,256]{2,1,0:T(8,128)(2,1)S(1)}, u32[]{:S(2)}, u32[]{:S(2)}) collective-permute-start(bf16[4,88,256]{2,1,0:T(8,128)(2,1)S(1)} %slice.104), channel_id=1, source_target_pairs={{0,8},{8,0},{16,24},{24,16},{1,9},{9,1},{17,25},{25,17},{2,10},{10... | collective-permute-start | bytes 540680 | tf_op jit(solution)/shard_map/ppermute | solution.py:349

commit v2 on v0

v2 whole, which is shorter than its diff:
```python
import functools
import math

import jax
import jax.numpy as jnp
from jax import lax
from jax.experimental import pallas as pl
from jax.experimental.pallas import tpu as pltpu
from jax.sharding import PartitionSpec as P

HDIM = 80
SCALING = HDIM ** (-0.5)
LOG2E = math.log2(math.e)
PADDED = 96
VMEM_LIMIT = 24 * 1024 * 1024
F32 = jnp.float32
BF16 = jnp.bfloat16


def shifted(block, axis, distance):
    devices = range(lax.axis_size(axis))
    route = [((i - distance) % len(devices), i) for i in devices]
    return lax.ppermute(block, axis, route)


def tile_terms(query_h, cotan_h, lse_rows, delta_rows, key_h, value_h):
    query_rows = query_h.shape[0]
    key_rows = key_h.shape[0]
    groups = query_h.shape[1]
    scores = (
        jnp.einsum("qhd,khd->hqk", query_h, key_h, preferred_element_type=jnp.float32) * SCALING
    )
    probs = jnp.exp(scores - lse_rows[:, :, None])
    probs16 = probs.astype(jnp.bfloat16)
    value_part = jnp.einsum("hqk,qhd->khd", probs16, cotan_h, preferred_element_type=jnp.float32)
    dprobs = jnp.einsum("qhd,khd->hqk", cotan_h, value_h, preferred_element_type=jnp.float32)
    dscores = (probs * (dprobs - delta_rows[:, :, None])).astype(jnp.bfloat16)
    query_part = jnp.einsum("hqk,khd->qhd", dscores, key_h, preferred_element_type=jnp.float32)
    key_part = jnp.einsum("hqk,qhd->khd", dscores, query_h, preferred_element_type=jnp.float32)
    return (
        query_part.reshape(query_rows, groups * HDIM),
        key_part.reshape(key_rows, groups * HDIM),
        value_part.reshape(key_rows, groups * HDIM),
    )


def crop_terms(query_h, cotan_h, lse_rows, delta_rows, key_h, value_h):
    return lax.map(
        lambda pieces: tile_terms(*pieces), (query_h, cotan_h, lse_rows, delta_rows, key_h, value_h)
    )


def ring_body(queries, keys, values, outputs, grad_out, lse):
    crops = queries.shape[0]
    groups = lse.shape[1]
    rows = lse.shape[2]
    query_own, key_own, value_own, cotan_own, output_own = (
        lax.all_to_all(sent, "head", split_axis=2, concat_axis=1, tiled=True)
        for sent in (queries, keys, values, grad_out, outputs)
    )
    products = cotan_own.astype(jnp.float32) * output_own.astype(jnp.float32)
    delta_rows = jnp.transpose(
        jnp.sum(products.reshape(crops, rows, groups, HDIM), axis=-1), (0, 2, 1)
    )
    query_h = query_own.reshape(crops, rows, groups, HDIM)
    cotan_h = cotan_own.reshape(crops, rows, groups, HDIM)
    key_h = key_own.reshape(crops, rows, groups, HDIM)
    value_h = value_own.reshape(crops, rows, groups, HDIM)
    width = groups * HDIM
    nblocks = lax.axis_size("blk")
    zeros_acc = jnp.zeros((crops, rows, width), jnp.float32)
    start = (query_h, cotan_h, lse, delta_rows, zeros_acc, zeros_acc, zeros_acc)

    def cycle_step(index, carry):
        query_cur, cotan_cur, lse_cur, delta_cur, query_acc, key_acc, value_acc = carry
        query_part, key_part, value_part = crop_terms(
            query_cur, cotan_cur, lse_cur, delta_cur, key_h, value_h
        )
        query_acc, lse_cur, delta_cur = shifted(
            (query_acc + query_part, lse_cur, delta_cur), "blk", 1
        )
        query_cur, cotan_cur = shifted((query_cur, cotan_cur), "blk", 1)
        return (
            query_cur,
            cotan_cur,
            lse_cur,
            delta_cur,
            query_acc,
            key_acc + key_part,
            value_acc + value_part,
        )

    query_cur, cotan_cur, lse_cur, delta_cur, query_acc, key_acc, value_acc = lax.fori_loop(
        0, nblocks - 1, cycle_step, start
    )
    query_part, key_part, value_part = crop_terms(
        query_cur, cotan_cur, lse_cur, delta_cur, key_h, value_h
    )
    query_total = shifted((query_acc + query_part).astype(jnp.bfloat16), "blk", 1).astype(
        jnp.float32
    )
    grad_q16 = (query_total * SCALING).astype(jnp.bfloat16)
    grad_k16 = ((key_acc + key_part) * SCALING).astype(jnp.bfloat16)
    grad_v16 = (value_acc + value_part).astype(jnp.bfloat16)
    return tuple(
        lax.all_to_all(grad, "head", split_axis=1, concat_axis=2, tiled=True)
        for grad in (grad_q16, grad_k16, grad_v16)
    )


def call(kernel, out_shape, *operands, scratch=(), remote=0, out_space=pltpu.VMEM, limit=VMEM_LIMIT):
    specs = [
        pl.BlockSpec(memory_space=pltpu.HBM if i < remote else pltpu.VMEM)
        for i in range(len(operands))
    ]
    return pl.pallas_call(
        kernel,
        out_shape=out_shape,
        in_specs=specs,
        out_specs=jax.tree.map(lambda _: pl.BlockSpec(memory_space=out_space), out_shape),
        scratch_shapes=list(scratch),
        compiler_params=pltpu.CompilerParams(vmem_limit_bytes=limit),
    )(*operands)


def place():
    h, b = lax.axis_index("head"), lax.axis_index("blk")
    return lax.div(h, 2), lax.rem(lax.div(b, 2), 2), lax.rem(h, 2), h


def shape(*dims, dtype=BF16):
    return jax.ShapeDtypeStruct(dims, dtype)


def head_of(array, head):
    return array[:, HDIM * head : HDIM * (head + 1)]


def pieces_of(row):
    high = row.astype(BF16)
    rest = row - high.astype(F32)
    middle = rest.astype(BF16)
    low = (rest - middle.astype(F32)).astype(BF16)
    return jnp.concatenate([high.astype(F32), middle.astype(F32), low.astype(F32)], axis=0)


def pack_inputs_kernel(
    q_in, k_in, v_in, o_in, do_in, lse_in, out0, out1, out2, out3,
    q_s, k_s, v_s, o_s, do_s, lse_s, out_ref, done, sent,
):
    x, w, c, _ = place()
    copies = [
        pltpu.make_async_copy(source, target, done.at[i])
        for i, (source, target) in enumerate(
            ((do_in, do_s), (o_in, o_s), (lse_in, lse_s), (q_in, q_s), (k_in, k_s), (v_in, v_s))
        )
    ]
    for copy in copies:
        copy.start()
    rows = q_s.shape[0]
    for copy in copies[:3]:
        copy.wait()
    products = do_s[...].astype(F32) * o_s[...].astype(F32)
    deltas = jnp.concatenate(
        [jnp.sum(head_of(products, head), axis=1, keepdims=True) for head in range(8)], axis=1
    ).T
    lse = lse_s[pl.ds(1 - w, 1), :] * LOG2E
    lse = jnp.concatenate([lse[:, rows * i : rows * (i + 1)] for i in range(4)], axis=0)
    lse = pieces_of(lse)
    for copy in copies[3:]:
        copy.wait()
    q, k, v, do = q_s[...], k_s[...], v_s[...], do_s[...]
    blank = jnp.zeros((3, 128 - rows), F32)
    gap = jnp.zeros((5, 128), F32)
    edge = jnp.zeros((8, 128 - rows), F32)
    side_lse = [
        jnp.concatenate([lse[0:8], edge], axis=1),
        jnp.concatenate([jnp.concatenate([lse[8:12], lse[8:12]], axis=0), edge], axis=1),
    ]
    for side in range(2):

        @pl.when(c == side)
        def _():
            for xs in range(2):
                for ws in range(2):
                    near, deep, spots = [], [], []
                    for i, cs in enumerate((side, 1 - side)):
                        head = 4 * xs + 2 * cs + ws
                        value = head_of(v, head)
                        near += [head_of(q, head), head_of(do, head), head_of(k, head), value[:, :16]]
                        deep.append(value[:, 16:])
                        delta = jnp.concatenate([pieces_of(deltas[head : head + 1, :]), blank], axis=1)
                        spots += [jnp.concatenate([delta, gap], axis=0), side_lse[i]]
                    j = 2 * (x ^ xs) + (w ^ ws)
                    out_ref[j, 0:rows] = jnp.concatenate(near + deep, axis=1)
                    below = jnp.concatenate(spots + [jnp.zeros((8, 128), F32)], axis=1)
                    out_ref[j, rows:PADDED] = below.astype(BF16)

    copies = [
        pltpu.make_async_copy(out_ref.at[j], out, sent.at[j])
        for j, out in enumerate((out0, out1, out2, out3))
    ]
    for copy in copies:
        copy.start()
    for copy in copies:
        copy.wait()


def parts_of(own, near, other, j, r):
    if r:
        return other[j], 320
    return (own if j == 0 else near[j - 1])[...], 512


def gather_queries_kernel(own, near1, near2, near3, other, lse_in, low, high, lse_s):
    rows = PADDED - 8
    near = (near1, near2, near3)
    _, w, _, h = place()
    lse_own = lse_in[pl.ds(w, 1), :] * LOG2E
    below = near1[rows:PADDED, :].astype(F32)
    lse_near = below[0:4, 128 : 128 + rows] + below[4:8, 128 : 128 + rows]
    lse_near = lse_near + below[0:4, 384 : 384 + rows]
    lse_s[...] = jnp.concatenate(
        [lse_own[:, rows * i : rows * (i + 1)] for i in range(4)] + [lse_near], axis=0
    )
    blocks, spots = [], []
    gap = jnp.zeros((6, PADDED - rows), F32)
    for j in range(4):
        for r in range(2):
            held, _ = parts_of(own, near, other, j, r)
            blocks.append(held[0:rows, 0:160])
            delta = held[rows:PADDED, 0:128].astype(F32)[0:3, 0:rows]
            lse = lse_s[pl.ds(4 * (j % 2) + (h ^ (2 * (j // 2) + r)), 1), :]
            spots += [jnp.concatenate([delta, pieces_of(lse)], axis=0), gap]
    for at, wire in ((0, low), (4, high)):
        wire[0:rows] = jnp.concatenate(blocks[at : at + 4], axis=1)
        below = jnp.concatenate(spots[2 * at : 2 * at + 8] + [jnp.zeros((6, 256), F32)], axis=1)
        below = jnp.concatenate([below, jnp.zeros((2, 640), F32)], axis=0)
        wire[rows:PADDED] = below.astype(BF16)


def gather_keys_kernel(own, near1, near2, near3, other, wide):
    rows = wide.shape[0]
    blocks = []
    for j in range(4):
        for r in range(2):
            held, deep = parts_of(own, (near1, near2, near3), other, j, r)
            blocks += [held[0:rows, 160:256], held[0:rows, deep : deep + 64]]
    wide[...] = jnp.concatenate(blocks, axis=1)


def rows_of(wires):
    rows = PADDED - 8
    below = jnp.concatenate(
        [wire[rows:PADDED, 0 : 4 * PADDED].astype(F32) for wire in wires], axis=1
    )
    return below[3:4] + below[4:5] + below[5:6], below[0:1] + below[1:2] + below[2:3]


def spread(wide, left, right, first=0):
    rows = PADDED - 8
    blank = jnp.zeros((16, HDIM), BF16)
    for i in range(wide.shape[1] // (2 * HDIM)):
        at, lane = PADDED * (first + i), 2 * HDIM * i
        for target, start in ((left, lane), (right, lane + HDIM)):
            target[pl.ds(at + PADDED - 16, 16), :] = blank
            target[pl.ds(at, rows), :] = wide[0:rows, start : start + HDIM]


def tile_step(q, do, k_s, v_s, lse, delta, chunk=384):
    q_t, do_t = q.T, do.T
    k_t = k_s[...].T
    dq_t = None
    parts = []
    for start in range(0, k_s.shape[0], chunk):
        spot = slice(start, start + chunk)
        k, v = k_s[spot, :], v_s[spot, :]
        scores = jnp.dot(k, q_t, preferred_element_type=F32)
        probs = jnp.exp2(scores * (SCALING * LOG2E) - lse)
        dv = jnp.dot(probs.astype(BF16), do, preferred_element_type=F32)
        dprobs = jnp.dot(v, do_t, preferred_element_type=F32)
        dscores = (probs * (dprobs - delta)).astype(BF16)
        dk = jnp.dot(dscores, q, preferred_element_type=F32)
        more = jnp.dot(k_t[:, spot], dscores, preferred_element_type=F32)
        dq_t = more if dq_t is None else dq_t + more
        parts.append((spot, dk, dv))
    return dq_t, parts


def to_wire(arrays, rows):
    count = arrays[0].shape[0] // PADDED
    return jnp.concatenate(
        [a[PADDED * i : PADDED * i + rows].astype(BF16) for i in range(count) for a in arrays],
        axis=1,
    )


def own_own_kernel(low, high, keys, dq_t, dk, dv, q_s, do_s, k_s, v_s):
    spread(low, q_s, do_s)
    spread(high, q_s, do_s, 4)
    spread(keys, k_s, v_s)
    dq_t[...], parts = tile_step(q_s[...], do_s[...], k_s, v_s, *rows_of([low, high]))
    for spot, dk_part, dv_part in parts:
        dk[spot, :] = dk_part
        dv[spot, :] = dv_part


def own_far_kernel(low, high, q_s, do_s, keys, dq_before, dq_t, dk, dv, k_s, v_s):
    spread(keys, k_s, v_s)
    more, parts = tile_step(q_s[...], do_s[...], k_s, v_s, *rows_of([low, high]))
    dq_t[...] = dq_before[...] + more
    for spot, dk_part, dv_part in parts:
        dk[spot, :] = dk_part
        dv[spot, :] = dv_part


def low_kernel(
    low, k_far, v_far, k_own, v_own, dk_far_in, dv_far_in, dk_own_in, dv_own_in,
    dq_t, dk_far, dv_far, dk_own, dv_own, q_s, do_s,
):
    spread(low, q_s, do_s)
    q, do = q_s[...], do_s[...]
    lse, delta = rows_of([low])
    total = None
    for k_s, v_s, dk_in, dv_in, dk, dv in (
        (k_far, v_far, dk_far_in, dv_far_in, dk_far, dv_far),
        (k_own, v_own, dk_own_in, dv_own_in, dk_own, dv_own),
    ):
        more, parts = tile_step(q, do, k_s, v_s, lse, delta)
        total = more if total is None else total + more
        for spot, dk_part, dv_part in parts:
            dk[spot, :] = dk_in[spot, :] + dk_part
            dv[spot, :] = dv_in[spot, :] + dv_part
    dq_t[...] = total


def high_far_kernel(high, k_far, v_far, dk_in, dv_in, dq_t, wire, q_s, do_s, dk, dv):
    spread(high, q_s, do_s)
    dq_t[...], parts = tile_step(q_s[...], do_s[...], k_far, v_far, *rows_of([high]))
    for spot, dk_part, dv_part in parts:
        dk[spot, :] = (dk_in[spot, :] + dk_part) * SCALING
        dv[spot, :] = dv_in[spot, :] + dv_part
    wire[...] = to_wire([dk[...], dv[...]], wire.shape[0])


def high_own_kernel(
    high, q_s, do_s, k_own, v_own, dq_low, dq_high, dk_in, dv_in, wire, dk, dv
):
    more, parts = tile_step(q_s[...], do_s[...], k_own, v_own, *rows_of([high]))
    dq = jnp.concatenate([dq_low[...], dq_high[...] + more], axis=1) * SCALING
    wire[...] = to_wire([dq.T], wire.shape[0])
    for spot, dk_part, dv_part in parts:
        dk[spot, :] = dk_in[spot, :] + dk_part
        dv[spot, :] = dv_in[spot, :] + dv_part


def own_grads_kernel(dq_t, dk, dv, out):
    rows = out.shape[1]
    dq = dq_t[...].T * SCALING
    zeros = jnp.zeros((rows, 16), F32)
    for i in range(8):
        spot = slice(PADDED * i, PADDED * i + rows)
        block = jnp.concatenate([dq[spot], dk[spot, :] * SCALING, dv[spot, :], zeros], axis=1)
        out[i // 2, :, 256 * (i % 2) : 256 * (i % 2) + 256] = block


def pack_grads_kernel(own, dkv_wire, dq_wire, out):
    rows = dkv_wire.shape[0]
    dq = dq_wire[...]
    dkv = dkv_wire[...]
    zeros = jnp.zeros((rows, 16), BF16)
    for i in range(8):
        block = jnp.concatenate(
            [
                dq[:, HDIM * i : HDIM * (i + 1)],
                dkv[:, 2 * HDIM * i : 2 * HDIM * (i + 1)],
                zeros,
            ],
            axis=1,
        )
        lanes = slice(256 * (i % 2), 256 * (i % 2) + 256)
        out[i // 2, :, lanes] = (own[i // 2, :, lanes] + block.astype(F32)).astype(BF16)


def unpack_grads_kernel(held, other, dq, dk, dv):
    x, w, c, _ = place()
    blocks = []
    for head in range(8):
        xs, cs, ws = head // 4, (head // 2) % 2, head % 2
        j = 2 * (x ^ xs) + (w ^ ws)
        blocks.append(
            jnp.where(c == cs, held[j][:, :256].astype(F32), other[j].astype(F32))
        )
    for k, out in enumerate((dq, dk, dv)):
        out[...] = jnp.concatenate(
            [block[:, HDIM * k : HDIM * (k + 1)] for block in blocks], axis=1
        ).astype(BF16)


def flipped(array, head_bits, blk_bits):
    heads, blks = lax.axis_size("head"), lax.axis_size("blk")
    if not blk_bits:
        return lax.ppermute(array, "head", [(i, i ^ head_bits) for i in range(heads)])
    if not head_bits:
        return lax.ppermute(array, "blk", [(i, i ^ blk_bits) for i in range(blks)])
    bits = head_bits * blks + blk_bits
    return lax.ppermute(array, ("head", "blk"), [(i, i ^ bits) for i in range(heads * blks)])


def to_chips(packed):
    return [flipped(packed[1], 0, 2), flipped(packed[2], 2, 0), flipped(packed[3], 2, 2)]


def grid_body(queries, keys, values, outputs, grad_out, lse):
    rows = queries.shape[1]
    padded = 8 * PADDED
    half = padded // 2

    packed = call(
        pack_inputs_kernel,
        (shape(PADDED, 640),) * 4,
        queries[0], keys[0], values[0], outputs[0], grad_out[0], lse[0],
        remote=6,
        out_space=pltpu.HBM,
        limit=57 * 1024 * 1024,
        scratch=[pltpu.VMEM(queries.shape[1:], BF16)] * 5
        + [pltpu.VMEM(lse.shape[1:], F32), pltpu.VMEM((4, PADDED, 640), BF16)]
        + [pltpu.SemaphoreType.DMA((6,)), pltpu.SemaphoreType.DMA((4,))],
    )
    own = packed[0]
    near = to_chips(packed)
    other = flipped(jnp.stack([a[:, 256:] for a in [own] + near]), 1, 0)
    low, high = call(
        gather_queries_kernel,
        (shape(PADDED, 640), shape(PADDED, 640)),
        own, *near, other, lse[0],
        scratch=[pltpu.VMEM((8, rows), F32)],
    )
    low_far = flipped(low, 0, 4)
    other, low = lax.optimization_barrier((other, low))
    k_wide = call(gather_keys_kernel, shape(rows, 1280), own, *near, other)
    k_wide_far = flipped(k_wide, 0, 1)

    grad = shape(padded, HDIM, dtype=F32)
    side = shape(padded, HDIM)
    dq_shape = shape(HDIM, padded, dtype=F32)
    dq_own, dk_own, dv_own, q_s, do_s, k_own, v_own = call(
        own_own_kernel, (dq_shape, grad, grad, side, side, side, side), low, high, k_wide
    )
    high, dq_own = lax.optimization_barrier((high, dq_own))
    high_far = flipped(high, 0, 4)
    dq_own, dk_far, dv_far, k_far, v_far = call(
        own_far_kernel, (dq_shape, grad, grad, side, side), low, high, q_s, do_s, k_wide_far, dq_own
    )
    dq_low, dk_far, dv_far, dk_own, dv_own = call(
        low_kernel, (shape(HDIM, half, dtype=F32), grad, grad, grad, grad),
        low_far, k_far, v_far, k_own, v_own, dk_far, dv_far, dk_own, dv_own,
        scratch=[pltpu.VMEM((half, HDIM), BF16)] * 2,
    )
    few = shape(half, HDIM)
    dq_high, dkv_wire, q_s, do_s = call(
        high_far_kernel,
        (shape(HDIM, half, dtype=F32), shape(rows, 1280), few, few),
        high_far, k_far, v_far, dk_far, dv_far,
        scratch=[pltpu.VMEM((padded, HDIM), F32)] * 2,
    )
    dkv_back = flipped(dkv_wire, 0, 1)
    dq_wire, dk_own, dv_own = call(
        high_own_kernel, (shape(rows, 640), grad, grad),
        high_far, q_s, do_s, k_own, v_own, dq_low, dq_high, dk_own, dv_own,
    )
    dq_back = flipped(dq_wire, 0, 4)
    own_g = call(own_grads_kernel, shape(4, rows, 512, dtype=F32), dq_own, dk_own, dv_own)
    packed_g = call(pack_grads_kernel, shape(4, rows, 512), own_g, dkv_back, dq_back)
    held = jnp.stack([packed_g[0]] + to_chips(packed_g))
    other = flipped(held[:, :, 256:], 1, 0)
    out = shape(rows, queries.shape[2])
    grads = call(unpack_grads_kernel, (out, out, out), held, other)
    return tuple(grad[None] for grad in grads)


def solution(mesh):
    placed = P(None, ("blk", "head"), None)
    on_grid = mesh.shape["head"] == 4 and mesh.shape["blk"] == 8
    return jax.shard_map(
        grid_body if on_grid else ring_body,
        mesh=mesh,
        in_specs=(placed,) * 5 + (P(None, "head", "blk"),),
        out_specs=(placed,) * 3,
        check_vma=False,
    )
```

time: 188 us -> 51.9 us (0.28)
  starting transfers between devices: 66.1 us -> 13.5 us
  waiting for transfers between devices: 70 us -> 23.3 us
  local copies, waits for them, and re-layouts: 22.6 us -> 0.97 us
  other arithmetic: 14.9 us -> 0.1 us
  Pallas kernels: 0 us -> 12.9 us
  matrix products: 11.8 us -> 0 us
    ppermute x36 -> x13, waiting for transfers between devices: 59.9 us -> 23.3 us  [the longest x7 14.3 us: flipped(): return lax.ppermute(array, 'blk', [(i, i ^ blk_bits) for i in range(blks)])]
    all_to_all x8 -> x0, starting transfers between devices: 27.8 us -> none  [the longest x1 4.21 us: body(): lax.all_to_all(sent[0], 'head', split_axis=2, concat_axis=1, tiled=True)]
    ppermute x36 -> x13, starting transfers between devices: 38.3 us -> 13.5 us  [the longest x7 10.9 us: flipped(): return lax.ppermute(array, 'blk', [(i, i ^ blk_bits) for i in range(blks)])]
    unnamed x32 -> x4, local copies, waits for them, and re-layouts: 13.8 us -> 0.01 us
    unnamed x10 -> x0, other arithmetic: 13.6 us -> none
    pallas_call x0 -> x11, Pallas kernels: none -> 12.9 us  [call(): pl.pallas_call(kernel, out_shape=out_shape, in_specs=specs, out_specs=jax...]
    dot_general x40 -> x0, matrix products: 11.8 us -> none  [the longest x8 2.9 us: tile_terms(): jnp.einsum('qhd,khd->hqk', query_h, key_h, preferred_element_type=jnp.flo...]
    all_to_all x8 -> x0, waiting for transfers between devices: 10.1 us -> none  [the longest x1 1.61 us: body(): lax.all_to_all(sent[0], 'head', split_axis=2, concat_axis=1, tiled=True)]
  transfers between devices with their start and end apart: 44 -> 13, of which waited for: 32 -> 9; matrix products, arithmetic and copies ran while one was open for 20% -> 2% of each run, Pallas kernels for 0% -> 14%
where the time goes in v2:
time: 51.9 us; the launch traced here: 51.7 us
  waiting for transfers between devices  23.3 us (45%)
  starting transfers between devices  13.5 us (26%)
  Pallas kernels  12.9 us (25%)
  local copies, waits for them, and re-layouts  0.97 us (2%)
  between operations  0.82 us (2%)
    ppermute x7, waiting for transfers between devices, flipped(): return lax.ppermute(array, 'blk', [(i, i ^ blk_bits) for i in range(blks)])  14.3 us
    pallas_call x11, Pallas kernels, call(): pl.pallas_call(kernel, out_shape=out_shape, in_specs=specs, out_specs=jax...  12.9 us
    ppermute x7, starting transfers between devices, flipped(): return lax.ppermute(array, 'blk', [(i, i ^ blk_bits) for i in range(blks)])  10.9 us
    ppermute x4, waiting for transfers between devices, flipped(): lax.ppermute(array, 'head', [(i, i ^ head_bits) for i in range(heads)])  6.68 us
    ppermute x4, starting transfers between devices, flipped(): lax.ppermute(array, 'head', [(i, i ^ head_bits) for i in range(heads)])  2.51 us
    ppermute x2, waiting for transfers between devices, flipped(): lax.ppermute(array, ('head', 'blk'), [(i, i ^ bits) for i in range(heads...  2.34 us
  transfers between devices with their start and end apart: 13, of which 9 were waited for; matrix products, arithmetic and copies ran while one was open for 2% of the time, Pallas kernels for 14%

profile of v2, /device:TPU:0, one launch (start us, length us, event | category | flops | bytes accessed | tf_op | source)
XLA Modules:
  0.0 51.7 jit_solution(10132220478473265056)
XLA Ops:
  0.6 2.9 %shard_map.85 = (bf16[96,640]{1,0:T(8,128)(2,1)}, bf16[96,640]{1,0:T(8,128)(2,1)}, bf16[96,640]{1,0:T(8,128)(2,1)}, bf16[96,640]{1,0:T(8,128)(2,1)}) custom-call(bf16[88,640]{1,0:T(8,128)(2,1)} %bitcast.28, bf16[88,640]{1,0:T(8,128)(2,1)} %bitcast.29, bf16[88,640]{1,0:T(8,128)(2,1)} %bitcast.30, bf16[88,640]{1,0:T(8,128)(2,1)} %bitcast.31, ...), custom_call_target="tpu_custom_call" | custom-call | tf_op jit(solution)/shard_map/pallas_call | solution.py:116
  3.6 3.1 %collective-permute-start = (bf16[96,640]{1,0:T(8,128)(2,1)}, bf16[96,640]{1,0:T(8,128)(2,1)S(1)}, u32[]{:S(2)}, u32[]{:S(2)}) collective-permute-start(bf16[96,640]{1,0:T(8,128)(2,1)} %get-tuple-element.41), channel_id=1, source_target_pairs={{0,2},{1,3},{2,0},{3,1},{4,6},{5,7},{6,4},{7,5},{8,10},{9,11},{10,... | collective-permute-start | bytes 368648 | tf_op jit(solution)/shard_map/ppermute | solution.py:405
  6.7 1.5 %collective-permute-start.1 = (bf16[96,640]{1,0:T(8,128)(2,1)}, bf16[96,640]{1,0:T(8,128)(2,1)S(1)}, u32[]{:S(2)}, u32[]{:S(2)}) collective-permute-start(bf16[96,640]{1,0:T(8,128)(2,1)} %get-tuple-element.42), channel_id=1, source_target_pairs={{0,16},{8,24},{16,0},{24,8},{1,17},{9,25},{17,1},{25,9},{2,18},{10... | collective-permute-start | bytes 368648 | tf_op jit(solution)/shard_map/ppermute | solution.py:403
  8.1 0.0 collective-permute-start.2
  8.2 0.9 %slice_bitcast_fusion.6 = bf16[1,96,384]{2,1,0:T(8,128)(2,1)S(1)} fusion(bf16[96,640]{1,0:T(8,128)(2,1)} %get-tuple-element.40.own), kind=kLoop, calls=%fused_computation.8 | loop fusion | bytes 147456 | tf_op jit(solution)/shard_map/stack | solution.py:432
  9.1 1.6 %collective-permute-done.near1 = bf16[96,640]{1,0:T(8,128)(2,1)S(1)} collective-permute-done((bf16[96,640]{1,0:T(8,128)(2,1)}, bf16[96,640]{1,0:T(8,128)(2,1)S(1)}, u32[]{:S(2)}, u32[]{:S(2)}) %collective-permute-start) | collective-permute-done | bytes 122912 | tf_op jit(solution)/shard_map/ppermute | solution.py:405
  10.7 3.7 %collective-permute-done.1.near2 = bf16[96,640]{1,0:T(8,128)(2,1)S(1)} collective-permute-done((bf16[96,640]{1,0:T(8,128)(2,1)}, bf16[96,640]{1,0:T(8,128)(2,1)S(1)}, u32[]{:S(2)}, u32[]{:S(2)}) %collective-permute-start.1) | collective-permute-done | bytes 122912 | tf_op jit(solution)/shard_map/ppermute | solution.py:403
  14.4 0.0 collective-permute-done.2.near3
  14.4 0.0 copy-start
  14.4 0.0 copy-start.1
  14.4 0.1 pad_maximum_fusion.1
  14.5 0.1 collective-permute-start.3
  14.6 1.6 %collective-permute-done.3.other = bf16[4,96,384]{2,1,0:T(8,128)(2,1)S(1)} collective-permute-done((bf16[4,96,384]{2,1,0:T(8,128)(2,1)S(1)}, bf16[4,96,384]{2,1,0:T(8,128)(2,1)S(1)}, u32[]{:S(2)}, u32[]{:S(2)}) %collective-permute-start.3) | collective-permute-done | bytes 294944 | tf_op jit(solution)/shard_map/ppermute | solution.py:403
  16.1 0.0 copy-done
  16.1 0.0 copy-done.1
  16.1 0.2 shard_map.86
  16.3 0.1 shard_map.87.keys
  16.5 1.6 %collective-permute-start.4 = (bf16[88,1280]{1,0:T(8,128)(2,1)S(1)}, bf16[88,1280]{1,0:T(8,128)(2,1)S(1)}, u32[]{:S(2)}, u32[]{:S(2)}) collective-permute-start(bf16[88,1280]{1,0:T(8,128)(2,1)S(1)} %shard_map.87.keys), channel_id=1, source_target_pairs={{0,1},{1,0},{2,3},{3,2},{4,5},{5,4},{6,7},{7,6},{8,9},{9,8},{10,11... | collective-permute-start | bytes 675848 | tf_op jit(solution)/shard_map/ppermute | solution.py:405
  18.1 2.6 %collective-permute-start.6 = (bf16[96,640]{1,0:T(8,128)(2,1)S(1)}, bf16[96,640]{1,0:T(8,128)(2,1)S(1)}, u32[]{:S(2)}, u32[]{:S(2)}) collective-permute-start(bf16[96,640]{1,0:T(8,128)(2,1)S(1)} %get-tuple-element.45.low), channel_id=1, source_target_pairs={{0,4},{1,5},{2,6},{3,7},{4,0},{5,1},{6,2},{7,3},{8,12},{9,13},{10,... | collective-permute-start | bytes 368648 | tf_op jit(solution)/shard_map/ppermute | solution.py:405
  20.7 1.7 %shard_map.88 = (f32[80,768]{1,0:T(8,128)S(1)}, f32[768,80]{1,0:T(8,128)S(1)}, f32[768,80]{1,0:T(8,128)S(1)}, bf16[768,80]{1,0:T(8,128)(2,1)S(1)}, bf16[768,80]{...) custom-call(bf16[96,640]{1,0:T(8,128)(2,1)S(1)} %get-tuple-element.45.low, ...), custom_call_target="tpu_custom_call" | custom-call | tf_op jit(solution)/shard_map/pallas_call | solution.py:116
  22.4 0.4 collective-permute-start.5
  22.8 1.3 %collective-permute-done.4.keys = bf16[88,1280]{1,0:T(8,128)(2,1)S(1)} collective-permute-done((bf16[88,1280]{1,0:T(8,128)(2,1)S(1)}, bf16[88,1280]{1,0:T(8,128)(2,1)S(1)}, u32[]{:S(2)}, u32[]{:S(2)}) %collective-permute-start.4) | collective-permute-done | bytes 225312 | tf_op jit(solution)/shard_map/ppermute | solution.py:405
  24.1 1.6 %shard_map.89 = (f32[80,768]{1,0:T(8,128)S(1)}, f32[768,80]{1,0:T(8,128)S(1)}, f32[768,80]{1,0:T(8,128)S(1)}, bf16[768,80]{1,0:T(8,128)(2,1)S(1)}, bf16[768,80]{1,0:T(8,128)(2,1)S(1)}) custom-call(bf16[96,640]{1,0:T(8,128)(2,1)S(1)} %get-tuple-element.45.low, bf16[96,640]{1,0:T(8,128)(2,1)S(1)} %get-tuple-element.49.high, ...), custom_call_target="tpu_custom_call" | custom-call | tf_op jit(solution)/shard_map/pallas_call | solution.py:116
  25.7 4.2 %collective-permute-done.6.low = bf16[96,640]{1,0:T(8,128)(2,1)S(1)} collective-permute-done((bf16[96,640]{1,0:T(8,128)(2,1)S(1)}, bf16[96,640]{1,0:T(8,128)(2,1)S(1)}, u32[]{:S(2)}, u32[]{:S(2)}) %collective-permute-start.6) | collective-permute-done | bytes 122912 | tf_op jit(solution)/shard_map/ppermute | solution.py:405
  30.0 2.1 %shard_map.90 = (f32[80,384]{1,0:T(8,128)S(1)}, f32[768,80]{1,0:T(8,128)S(1)}, f32[768,80]{1,0:T(8,128)S(1)}, f32[768,80]{1,0:T(8,128)S(1)}, f32[768,80]{1,0:T(8,128)S(1)}) custom-call(bf16[96,640]{1,0:T(8,128)(2,1)S(1)} %collective-permute-done.6.low, bf16[768,80]{1,0:T(8,128)(2,1)S(1)} %get-tuple-element.54.k_far, ...), custom_call_target="tpu_custom_call" | custom-call | tf_op jit(solution)/shard_map/pallas_call | solution.py:116
  32.1 0.0 collective-permute-done.5.high
  32.1 1.3 %shard_map.91 = (f32[80,384]{1,0:T(8,128)S(1)}, bf16[88,1280]{1,0:T(8,128)(2,1)S(1)}, bf16[384,80]{1,0:T(8,128)(2,1)S(1)}, bf16[384,80]{1,0:T(8,128)(2,1)S(1)}) custom-call(bf16[96,640]{1,0:T(8,128)(2,1)S(1)} %collective-permute-done.5.high, bf16[768,80]{1,0:T(8,128)(2,1)S(1)} %get-tuple-element.54.k_far, bf16[768,80]{1,0:T(8,128)(2,1)S(1)} %get-tuple-element.55.v_far, ...), custom_call_target="tpu_custom_call" | custom-call | tf_op jit(solution)/shard_map/pallas_call | solution.py:116
  33.4 0.6 %collective-permute-start.7 = (bf16[88,1280]{1,0:T(8,128)(2,1)S(1)}, bf16[88,1280]{1,0:T(8,128)(2,1)S(1)}, u32[]{:S(2)}, u32[]{:S(2)}) collective-permute-start(bf16[88,1280]{1,0:T(8,128)(2,1)S(1)} %get-tuple-element.72), channel_id=1, source_target_pairs={{0,1},{1,0},{2,3},{3,2},{4,5},{5,4},{6,7},{7,6},{8,9},{9,8},{10,11... | collective-permute-start | bytes 675848 | tf_op jit(solution)/shard_map/ppermute | solution.py:405
  34.0 1.4 %shard_map.92 = (bf16[88,640]{1,0:T(8,128)(2,1)S(1)}, f32[768,80]{1,0:T(8,128)S(1)}, f32[768,80]{1,0:T(8,128)S(1)}) custom-call(bf16[96,640]{1,0:T(8,128)(2,1)S(1)} %collective-permute-done.5.high, bf16[384,80]{1,0:T(8,128)(2,1)S(1)} %get-tuple-element.64.q_s, bf16[384,80]{1,0:T(8,128)(2,1)S(1)} %get-tuple-element.65.do_s, ...), custom_call_target="tpu_custom_call" | custom-call | tf_op jit(solution)/shard_map/pallas_call | solution.py:116
  35.4 0.1 collective-permute-start.8
  35.5 0.4 shard_map.93.own
  35.9 7.0 %collective-permute-done.8.dq_wire = bf16[88,640]{1,0:T(8,128)(2,1)S(1)} collective-permute-done((bf16[88,640]{1,0:T(8,128)(2,1)S(1)}, bf16[88,640]{1,0:T(8,128)(2,1)S(1)}, u32[]{:S(2)}, u32[]{:S(2)}) %collective-permute-start.8) | collective-permute-done | bytes 112672 | tf_op jit(solution)/shard_map/ppermute | solution.py:405
  42.8 0.0 collective-permute-done.7.dkv_wire
  42.8 0.2 shard_map.94
  43.1 0.1 collective-permute-start.11
  43.2 0.9 %collective-permute-start.10 = (bf16[88,512]{1,0:T(8,128)(2,1)S(1)}, bf16[88,512]{1,0:T(8,128)(2,1)S(1)}, u32[]{:S(2)}, u32[]{:S(2)}) collective-permute-start(bf16[88,512]{1,0:T(8,128)(2,1)S(1)} %get-tuple-element.79), channel_id=1, source_target_pairs={{0,16},{8,24},{16,0},{24,8},{1,17},{9,25},{17,1},{25,9},{2,18},{10... | collective-permute-start | bytes 270344 | tf_op jit(solution)/shard_map/ppermute | solution.py:403
  44.1 2.6 %collective-permute-start.9 = (bf16[88,512]{1,0:T(8,128)(2,1)S(1)}, bf16[88,512]{1,0:T(8,128)(2,1)S(1)}, u32[]{:S(2)}, u32[]{:S(2)}) collective-permute-start(bf16[88,512]{1,0:T(8,128)(2,1)S(1)} %get-tuple-element.80), channel_id=1, source_target_pairs={{0,2},{1,3},{2,0},{3,1},{4,6},{5,7},{6,4},{7,5},{8,10},{9,11},{10,... | collective-permute-start | bytes 270344 | tf_op jit(solution)/shard_map/ppermute | solution.py:405
  46.7 2.3 %collective-permute-done.11 = bf16[88,512]{1,0:T(8,128)(2,1)S(1)} collective-permute-done((bf16[88,512]{1,0:T(8,128)(2,1)S(1)}, bf16[88,512]{1,0:T(8,128)(2,1)S(1)}, u32[]{:S(2)}, u32[]{:S(2)}) %collective-permute-start.11) | collective-permute-done | bytes 90144 | tf_op jit(solution)/shard_map/ppermute | solution.py:407
  49.0 0.0 collective-permute-done.10
  49.1 0.1 collective-permute-done.9
  49.3 0.1 collective-permute-start.12
  49.4 1.4 %collective-permute-done.12.other = bf16[4,88,256]{2,1,0:T(8,128)(2,1)S(1)} collective-permute-done((bf16[4,88,256]{2,1,0:T(8,128)(2,1)S(1)}, bf16[4,88,256]{2,1,0:T(8,128)(2,1)S(1)}, u32[]{:S(2)}, u32[]{:S(2)}) %collective-permute-start.12) | collective-permute-done | bytes 180256 | tf_op jit(solution)/shard_map/ppermute | solution.py:403
  50.8 0.9 %shard_map.95 = (bf16[88,640]{1,0:T(8,128)(2,1)}, bf16[88,640]{1,0:T(8,128)(2,1)}, bf16[88,640]{1,0:T(8,128)(2,1)}) custom-call(bf16[4,88,512]{2,1,0:T(8,128)(2,1)S(1)} %pad_maximum_fusion.held, bf16[4,88,256]{2,1,0:T(8,128)(2,1)S(1)} %collective-permute-done.12.other), custom_call_target="tpu_custom_call" | custom-call | tf_op jit(solution)/shard_map/pallas_call | solution.py:116
  (6 shorter events, 0.1 us)
Async XLA Ops:
  3.6 7.1 %collective-permute-start = (bf16[96,640]{1,0:T(8,128)(2,1)}, bf16[96,640]{1,0:T(8,128)(2,1)S(1)}, u32[]{:S(2)}, u32[]{:S(2)}) collective-permute-start(bf16[96,640]{1,0:T(8,128)(2,1)} %get-tuple-element.41), channel_id=1, source_target_pairs={{0,2},{1,3},{2,0},{3,1},{4,6},{5,7},{6,4},{7,5},{8,10},{9,11},{10,... | collective-permute-start | bytes 368648 | tf_op jit(solution)/shard_map/ppermute | solution.py:405
  6.7 7.7 %collective-permute-start.1 = (bf16[96,640]{1,0:T(8,128)(2,1)}, bf16[96,640]{1,0:T(8,128)(2,1)S(1)}, u32[]{:S(2)}, u32[]{:S(2)}) collective-permute-start(bf16[96,640]{1,0:T(8,128)(2,1)} %get-tuple-element.42), channel_id=1, source_target_pairs={{0,16},{8,24},{16,0},{24,8},{1,17},{9,25},{17,1},{25,9},{2,18},{10... | collective-permute-start | bytes 368648 | tf_op jit(solution)/shard_map/ppermute | solution.py:403
  8.1 6.2 %collective-permute-start.2 = (bf16[96,640]{1,0:T(8,128)(2,1)}, bf16[96,640]{1,0:T(8,128)(2,1)S(1)}, u32[]{:S(2)}, u32[]{:S(2)}) collective-permute-start(bf16[96,640]{1,0:T(8,128)(2,1)} %get-tuple-element.43), channel_id=1, source_target_pairs={{0,18},{1,19},{2,16},{3,17},{4,22},{5,23},{6,20},{7,21},{8,26},{9,... | collective-permute-start | bytes 368648 | tf_op jit(solution)/shard_map/ppermute | solution.py:407
  14.4 1.7 %copy-start = (bf16[96,640]{1,0:T(8,128)(2,1)S(1)}, bf16[96,640]{1,0:T(8,128)(2,1)}, u32[]{:S(2)}) copy-start(bf16[96,640]{1,0:T(8,128)(2,1)} %get-tuple-element.40.own) | copy-start | bytes 368644
  14.4 1.7 %copy-start.1 = (f32[1,2,352]{2,1,0:T(2,128)S(1)}, f32[1,2,352]{2,1,0:T(2,128)}, u32[]{:S(2)}) copy-start(f32[1,2,352]{2,1,0:T(2,128)} %param.11) | copy-start | bytes 8452
  14.5 1.6 %collective-permute-start.3 = (bf16[4,96,384]{2,1,0:T(8,128)(2,1)S(1)}, bf16[4,96,384]{2,1,0:T(8,128)(2,1)S(1)}, u32[]{:S(2)}, u32[]{:S(2)}) collective-permute-start(bf16[4,96,384]{2,1,0:T(8,128)(2,1)S(1)} %pad_maximum_fusion.1), channel_id=1, source_target_pairs={{0,8},{8,0},{16,24},{24,16},{1,9},{9,1},{17,25},{25,17},{2,10},{10... | collective-permute-start | bytes 884744 | tf_op jit(solution)/shard_map/ppermute | solution.py:403
  16.5 7.6 %collective-permute-start.4 = (bf16[88,1280]{1,0:T(8,128)(2,1)S(1)}, bf16[88,1280]{1,0:T(8,128)(2,1)S(1)}, u32[]{:S(2)}, u32[]{:S(2)}) collective-permute-start(bf16[88,1280]{1,0:T(8,128)(2,1)S(1)} %shard_map.87.keys), channel_id=1, source_target_pairs={{0,1},{1,0},{2,3},{3,2},{4,5},{5,4},{6,7},{7,6},{8,9},{9,8},{10,11... | collective-permute-start | bytes 675848 | tf_op jit(solution)/shard_map/ppermute | solution.py:405
  18.1 11.9 %collective-permute-start.6 = (bf16[96,640]{1,0:T(8,128)(2,1)S(1)}, bf16[96,640]{1,0:T(8,128)(2,1)S(1)}, u32[]{:S(2)}, u32[]{:S(2)}) collective-permute-start(bf16[96,640]{1,0:T(8,128)(2,1)S(1)} %get-tuple-element.45.low), channel_id=1, source_target_pairs={{0,4},{1,5},{2,6},{3,7},{4,0},{5,1},{6,2},{7,3},{8,12},{9,13},{10,... | collective-permute-start | bytes 368648 | tf_op jit(solution)/shard_map/ppermute | solution.py:405
  22.4 9.7 %collective-permute-start.5 = (bf16[96,640]{1,0:T(8,128)(2,1)S(1)}, bf16[96,640]{1,0:T(8,128)(2,1)S(1)}, u32[]{:S(2)}, u32[]{:S(2)}) collective-permute-start(bf16[96,640]{1,0:T(8,128)(2,1)S(1)} %get-tuple-element.49.high), channel_id=1, source_target_pairs={{0,4},{1,5},{2,6},{3,7},{4,0},{5,1},{6,2},{7,3},{8,12},{9,13},{10,... | collective-permute-start | bytes 368648 | tf_op jit(solution)/shard_map/ppermute | solution.py:405
  33.4 9.4 %collective-permute-start.7 = (bf16[88,1280]{1,0:T(8,128)(2,1)S(1)}, bf16[88,1280]{1,0:T(8,128)(2,1)S(1)}, u32[]{:S(2)}, u32[]{:S(2)}) collective-permute-start(bf16[88,1280]{1,0:T(8,128)(2,1)S(1)} %get-tuple-element.72), channel_id=1, source_target_pairs={{0,1},{1,0},{2,3},{3,2},{4,5},{5,4},{6,7},{7,6},{8,9},{9,8},{10,11... | collective-permute-start | bytes 675848 | tf_op jit(solution)/shard_map/ppermute | solution.py:405
  35.4 7.4 %collective-permute-start.8 = (bf16[88,640]{1,0:T(8,128)(2,1)S(1)}, bf16[88,640]{1,0:T(8,128)(2,1)S(1)}, u32[]{:S(2)}, u32[]{:S(2)}) collective-permute-start(bf16[88,640]{1,0:T(8,128)(2,1)S(1)} %get-tuple-element.73), channel_id=1, source_target_pairs={{0,4},{1,5},{2,6},{3,7},{4,0},{5,1},{6,2},{7,3},{8,12},{9,13},{10,... | collective-permute-start | bytes 337928 | tf_op jit(solution)/shard_map/ppermute | solution.py:405
  43.1 5.9 %collective-permute-start.11 = (bf16[88,512]{1,0:T(8,128)(2,1)S(1)}, bf16[88,512]{1,0:T(8,128)(2,1)S(1)}, u32[]{:S(2)}, u32[]{:S(2)}) collective-permute-start(bf16[88,512]{1,0:T(8,128)(2,1)S(1)} %get-tuple-element.78), channel_id=1, source_target_pairs={{0,18},{1,19},{2,16},{3,17},{4,22},{5,23},{6,20},{7,21},{8,26},{9,... | collective-permute-start | bytes 270344 | tf_op jit(solution)/shard_map/ppermute | solution.py:407
  43.2 5.9 %collective-permute-start.10 = (bf16[88,512]{1,0:T(8,128)(2,1)S(1)}, bf16[88,512]{1,0:T(8,128)(2,1)S(1)}, u32[]{:S(2)}, u32[]{:S(2)}) collective-permute-start(bf16[88,512]{1,0:T(8,128)(2,1)S(1)} %get-tuple-element.79), channel_id=1, source_target_pairs={{0,16},{8,24},{16,0},{24,8},{1,17},{9,25},{17,1},{25,9},{2,18},{10... | collective-permute-start | bytes 270344 | tf_op jit(solution)/shard_map/ppermute | solution.py:403
  44.1 5.1 %collective-permute-start.9 = (bf16[88,512]{1,0:T(8,128)(2,1)S(1)}, bf16[88,512]{1,0:T(8,128)(2,1)S(1)}, u32[]{:S(2)}, u32[]{:S(2)}) collective-permute-start(bf16[88,512]{1,0:T(8,128)(2,1)S(1)} %get-tuple-element.80), channel_id=1, source_target_pairs={{0,2},{1,3},{2,0},{3,1},{4,6},{5,7},{6,4},{7,5},{8,10},{9,11},{10,... | collective-permute-start | bytes 270344 | tf_op jit(solution)/shard_map/ppermute | solution.py:405
  49.3 1.5 %collective-permute-start.12 = (bf16[4,88,256]{2,1,0:T(8,128)(2,1)S(1)}, bf16[4,88,256]{2,1,0:T(8,128)(2,1)S(1)}, u32[]{:S(2)}, u32[]{:S(2)}) collective-permute-start(bf16[4,88,256]{2,1,0:T(8,128)(2,1)S(1)} %slice.43), channel_id=1, source_target_pairs={{0,8},{8,0},{16,24},{24,16},{1,9},{9,1},{17,25},{25,17},{2,10},{10... | collective-permute-start | bytes 540680 | tf_op jit(solution)/shard_map/ppermute | solution.py:403

commit v3 on v2

--- a/solution.py
+++ b/solution.py
@@ -108,7 +108,7 @@
     )
 
 
-def call(kernel, out_shape, *operands, scratch=(), remote=0, out_space=pltpu.VMEM, limit=VMEM_LIMIT):
+def call(kernel, out_shape, *operands, scratch=(), remote=0, flops=0, out_space=pltpu.VMEM, limit=VMEM_LIMIT):
     specs = [
         pl.BlockSpec(memory_space=pltpu.HBM if i < remote else pltpu.VMEM)
         for i in range(len(operands))
@@ -119,6 +119,7 @@
         in_specs=specs,
         out_specs=jax.tree.map(lambda _: pl.BlockSpec(memory_space=out_space), out_shape),
         scratch_shapes=list(scratch),
+        cost_estimate=pl.CostEstimate(flops=flops, bytes_accessed=0, transcendentals=0) if flops else None,
         compiler_params=pltpu.CompilerParams(vmem_limit_bytes=limit),
     )(*operands)
 
@@ -152,58 +153,80 @@
     copies = [
         pltpu.make_async_copy(source, target, done.at[i])
         for i, (source, target) in enumerate(
-            ((do_in, do_s), (o_in, o_s), (lse_in, lse_s), (q_in, q_s), (k_in, k_s), (v_in, v_s))
+            ((q_in, q_s), (k_in, k_s), (v_in, v_s), (do_in, do_s), (o_in, o_s), (lse_in, lse_s))
         )
-    ]
-    for copy in copies:
-        copy.start()
-    rows = q_s.shape[0]
-    for copy in copies[:3]:
-        copy.wait()
-    products = do_s[...].astype(F32) * o_s[...].astype(F32)
-    deltas = jnp.concatenate(
-        [jnp.sum(head_of(products, head), axis=1, keepdims=True) for head in range(8)], axis=1
-    ).T
-    lse = lse_s[pl.ds(1 - w, 1), :] * LOG2E
-    lse = jnp.concatenate([lse[:, rows * i : rows * (i + 1)] for i in range(4)], axis=0)
-    lse = pieces_of(lse)
-    for copy in copies[3:]:
-        copy.wait()
-    q, k, v, do = q_s[...], k_s[...], v_s[...], do_s[...]
-    blank = jnp.zeros((3, 128 - rows), F32)
-    gap = jnp.zeros((5, 128), F32)
-    edge = jnp.zeros((8, 128 - rows), F32)
-    side_lse = [
-        jnp.concatenate([lse[0:8], edge], axis=1),
-        jnp.concatenate([jnp.concatenate([lse[8:12], lse[8:12]], axis=0), edge], axis=1),
-    ]
-    for side in range(2):
-
-        @pl.when(c == side)
-        def _():
-            for xs in range(2):
-                for ws in range(2):
-                    near, deep, spots = [], [], []
-                    for i, cs in enumerate((side, 1 - side)):
-                        head = 4 * xs + 2 * cs + ws
-                        value = head_of(v, head)
-                        near += [head_of(q, head), head_of(do, head), head_of(k, head), value[:, :16]]
-                        deep.append(value[:, 16:])
-                        delta = jnp.concatenate([pieces_of(deltas[head : head + 1, :]), blank], axis=1)
-                        spots += [jnp.concatenate([delta, gap], axis=0), side_lse[i]]
-                    j = 2 * (x ^ xs) + (w ^ ws)
-                    out_ref[j, 0:rows] = jnp.concatenate(near + deep, axis=1)
-                    below = jnp.concatenate(spots + [jnp.zeros((8, 128), F32)], axis=1)
-                    out_ref[j, rows:PADDED] = below.astype(BF16)
-
-    copies = [
-        pltpu.make_async_copy(out_ref.at[j], out, sent.at[j])
-        for j, out in enumerate((out0, out1, out2, out3))
     ]
     for copy in copies:
         copy.start()
     for copy in copies:
         copy.wait()
+    rows = q_s.shape[0]
+    q, k, v, do = q_s[...], k_s[...], v_s[...], do_s[...]
+    outs = (out0, out1, out2, out3)
+
+    def leave(part, spot):
+        return [
+            pltpu.make_async_copy(out_ref.at[j, spot], out.at[spot], sent.at[4 * part + j])
+            for j, out in enumerate(outs)
+        ]
+
+    for side in range(2):
+
+        @pl.when(c == side)
+        def _():
+            for xs in range(2):
+                for ws in range(2):
+                    near, deep = [], []
+                    for cs in (side, 1 - side):
+                        head = 4 * xs + 2 * cs + ws
+                        value = head_of(v, head)
+                        near += [head_of(q, head), head_of(do, head), head_of(k, head), value[:, :16]]
+                        deep.append(value[:, 16:])
+                    j = 2 * (x ^ xs) + (w ^ ws)
+                    out_ref[j, 0:rows] = jnp.concatenate(near + deep, axis=1)
+
+    most = leave(0, pl.ds(0, PADDED - 16))
+    for copy in most:
+        copy.start()
+    products = do.astype(F32) * o_s[...].astype(F32)
+    high = products.astype(BF16)
+    rest = products - high.astype(F32)
+    middle = rest.astype(BF16)
+    low = (rest - middle.astype(F32)).astype(BF16)
+    row = lax.broadcasted_iota(jnp.int32, (8, 640), 0)
+    lane = lax.broadcasted_iota(jnp.int32, (8, 640), 1)
+    mine = jnp.where((lane >= HDIM * row) & (lane < HDIM * (row + 1)), 1.0, 0.0).astype(BF16)
+    deltas = sum(
+        lax.dot_general(mine, part, (((1,), (1,)), ((), ())), preferred_element_type=F32)
+        for part in (low, middle, high)
+    )
+    lse = lse_s[pl.ds(1 - w, 1), :] * LOG2E
+    lse = jnp.concatenate([lse[:, rows * i : rows * (i + 1)] for i in range(4)], axis=0)
+    lse = pieces_of(lse)
+    blank = jnp.zeros((3, 128 - rows), F32)
+    gap = jnp.zeros((5, 128), F32)
+    edge = jnp.zeros((8, 128 - rows), F32)
+    sides = [
+        jnp.concatenate([lse[0:8], edge], axis=1),
+        jnp.concatenate([jnp.concatenate([lse[8:12], lse[8:12]], axis=0), edge], axis=1),
+    ]
+    for xs in range(2):
+        for ws in range(2):
+            j = 2 * (x ^ xs) + (w ^ ws)
+            pair = []
+            for cs in range(2):
+                head = 4 * xs + 2 * cs + ws
+                delta = jnp.concatenate([pieces_of(deltas[head : head + 1, :]), blank], axis=1)
+                pair.append(jnp.concatenate([delta, gap], axis=0))
+            kept = jnp.where(c == 0, pair[0], pair[1])
+            given = jnp.where(c == 0, pair[1], pair[0])
+            spots = [kept, sides[0], given, sides[1], jnp.zeros((8, 128), F32)]
+            out_ref[j, rows:PADDED] = jnp.concatenate(spots, axis=1).astype(BF16)
+    last = leave(1, pl.ds(PADDED - 16, 16))
+    for copy in last:
+        copy.start()
+    for copy in most + last:
+        copy.wait()
 
 
 def parts_of(own, near, other, j, r):
@@ -212,7 +235,8 @@
     return (own if j == 0 else near[j - 1])[...], 512
 
 
-def gather_queries_kernel(own, near1, near2, near3, other, lse_in, low, high, lse_s):
+def gather_queries_kernel(own, near1, near2, near3, other0, other1, other2, other3, lse_in, low, high, lse_s):
+    other = (other0, other1, other2, other3)
     rows = PADDED - 8
     near = (near1, near2, near3)
     _, w, _, h = place()
@@ -239,14 +263,16 @@
         wire[rows:PADDED] = below.astype(BF16)
 
 
-def gather_keys_kernel(own, near1, near2, near3, other, wide):
-    rows = wide.shape[0]
+def gather_keys_kernel(own, near1, near2, near3, other0, other1, other2, other3, low, high):
+    other = (other0, other1, other2, other3)
+    rows = low.shape[0]
     blocks = []
     for j in range(4):
         for r in range(2):
             held, deep = parts_of(own, (near1, near2, near3), other, j, r)
             blocks += [held[0:rows, 160:256], held[0:rows, deep : deep + 64]]
-    wide[...] = jnp.concatenate(blocks, axis=1)
+    low[...] = jnp.concatenate(blocks[:8], axis=1)
+    high[...] = jnp.concatenate(blocks[8:], axis=1)
 
 
 def rows_of(wires):
@@ -295,18 +321,20 @@
     )
 
 
-def own_own_kernel(low, high, keys, dq_t, dk, dv, q_s, do_s, k_s, v_s):
+def own_own_kernel(low, high, k_low, k_high, dq_t, dk, dv, q_s, do_s, k_s, v_s):
     spread(low, q_s, do_s)
     spread(high, q_s, do_s, 4)
-    spread(keys, k_s, v_s)
+    spread(k_low, k_s, v_s)
+    spread(k_high, k_s, v_s, 4)
     dq_t[...], parts = tile_step(q_s[...], do_s[...], k_s, v_s, *rows_of([low, high]))
     for spot, dk_part, dv_part in parts:
         dk[spot, :] = dk_part
         dv[spot, :] = dv_part
 
 
-def own_far_kernel(low, high, q_s, do_s, keys, dq_before, dq_t, dk, dv, k_s, v_s):
-    spread(keys, k_s, v_s)
+def own_far_kernel(low, high, q_s, do_s, k_low, k_high, dq_before, dq_t, dk, dv, k_s, v_s):
+    spread(k_low, k_s, v_s)
+    spread(k_high, k_s, v_s, 4)
     more, parts = tile_step(q_s[...], do_s[...], k_s, v_s, *rows_of([low, high]))
     dq_t[...] = dq_before[...] + more
     for spot, dk_part, dv_part in parts:
@@ -382,19 +410,21 @@
         out[i // 2, :, lanes] = (own[i // 2, :, lanes] + block.astype(F32)).astype(BF16)
 
 
-def unpack_grads_kernel(held, other, dq, dk, dv):
+def unpack_grads_kernel(*refs):
+    kept, given, dq, dk, dv, held, other = refs[0:4], refs[4:8], *refs[8:]
     x, w, c, _ = place()
+    for j in range(4):
+        held[j] = kept[j][:, 0:256]
+        other[j] = given[j][...]
     blocks = []
     for head in range(8):
         xs, cs, ws = head // 4, (head // 2) % 2, head % 2
         j = 2 * (x ^ xs) + (w ^ ws)
-        blocks.append(
-            jnp.where(c == cs, held[j][:, :256].astype(F32), other[j].astype(F32))
-        )
+        blocks.append(jnp.where(c == cs, held[j].astype(F32), other[j].astype(F32)).astype(BF16))
     for k, out in enumerate((dq, dk, dv)):
         out[...] = jnp.concatenate(
             [block[:, HDIM * k : HDIM * (k + 1)] for block in blocks], axis=1
-        ).astype(BF16)
+        )
 
 
 def flipped(array, head_bits, blk_bits):
@@ -425,36 +455,37 @@
         limit=57 * 1024 * 1024,
         scratch=[pltpu.VMEM(queries.shape[1:], BF16)] * 5
         + [pltpu.VMEM(lse.shape[1:], F32), pltpu.VMEM((4, PADDED, 640), BF16)]
-        + [pltpu.SemaphoreType.DMA((6,)), pltpu.SemaphoreType.DMA((4,))],
+        + [pltpu.SemaphoreType.DMA((6,)), pltpu.SemaphoreType.DMA((8,))],
     )
     own = packed[0]
     near = to_chips(packed)
-    other = flipped(jnp.stack([a[:, 256:] for a in [own] + near]), 1, 0)
+    other = [flipped(a[:, 256:], 1, 0) for a in [own] + near]
     low, high = call(
         gather_queries_kernel,
         (shape(PADDED, 640), shape(PADDED, 640)),
-        own, *near, other, lse[0],
+        own, *near, *other, lse[0],
         scratch=[pltpu.VMEM((8, rows), F32)],
     )
     low_far = flipped(low, 0, 4)
     other, low = lax.optimization_barrier((other, low))
-    k_wide = call(gather_keys_kernel, shape(rows, 1280), own, *near, other)
-    k_wide_far = flipped(k_wide, 0, 1)
+    wires_k = call(gather_keys_kernel, (shape(rows, 640),) * 2, own, *near, *other)
+    wires_k_far = [flipped(wire, 0, 1) for wire in wires_k]
 
     grad = shape(padded, HDIM, dtype=F32)
     side = shape(padded, HDIM)
     dq_shape = shape(HDIM, padded, dtype=F32)
     dq_own, dk_own, dv_own, q_s, do_s, k_own, v_own = call(
-        own_own_kernel, (dq_shape, grad, grad, side, side, side, side), low, high, k_wide
+        own_own_kernel, (dq_shape, grad, grad, side, side, side, side), low, high, *wires_k
     )
     high, dq_own = lax.optimization_barrier((high, dq_own))
     high_far = flipped(high, 0, 4)
     dq_own, dk_far, dv_far, k_far, v_far = call(
-        own_far_kernel, (dq_shape, grad, grad, side, side), low, high, q_s, do_s, k_wide_far, dq_own
+        own_far_kernel, (dq_shape, grad, grad, side, side), low, high, q_s, do_s, *wires_k_far, dq_own
     )
     dq_low, dk_far, dv_far, dk_own, dv_own = call(
         low_kernel, (shape(HDIM, half, dtype=F32), grad, grad, grad, grad),
         low_far, k_far, v_far, k_own, v_own, dk_far, dv_far, dk_own, dv_own,
+        flops=1000000000,
         scratch=[pltpu.VMEM((half, HDIM), BF16)] * 2,
     )
     few = shape(half, HDIM)
@@ -472,10 +503,13 @@
     dq_back = flipped(dq_wire, 0, 4)
     own_g = call(own_grads_kernel, shape(4, rows, 512, dtype=F32), dq_own, dk_own, dv_own)
     packed_g = call(pack_grads_kernel, shape(4, rows, 512), own_g, dkv_back, dq_back)
-    held = jnp.stack([packed_g[0]] + to_chips(packed_g))
-    other = flipped(held[:, :, 256:], 1, 0)
+    held = [packed_g[0]] + to_chips(packed_g)
+    other = [flipped(a[:, 256:], 1, 0) for a in held]
     out = shape(rows, queries.shape[2])
-    grads = call(unpack_grads_kernel, (out, out, out), held, other)
+    grads = call(
+        unpack_grads_kernel, (out, out, out), *held, *other,
+        scratch=[pltpu.VMEM((4, rows, 256), BF16)] * 2,
+    )
     return tuple(grad[None] for grad in grads)
 
 

time: 51.9 us -> 51.9 us (level)
  starting transfers between devices: 13.5 us -> 16.2 us
  waiting for transfers between devices: 23.3 us -> 21.1 us
    ppermute x7 -> x8, waiting for transfers between devices: 14.3 us -> 12.5 us  [flipped(): return lax.ppermute(array, 'blk', [(i, i ^ blk_bits) for i in range(blks)])]
    ppermute x4 -> x10, starting transfers between devices: 2.51 us -> 4.05 us  [flipped(): lax.ppermute(array, 'head', [(i, i ^ head_bits) for i in range(heads)])]
    ppermute x4 -> x10, waiting for transfers between devices: 6.68 us -> 5.7 us  [flipped(): lax.ppermute(array, 'head', [(i, i ^ head_bits) for i in range(heads)])]
    ppermute x7 -> x8, starting transfers between devices: 10.9 us -> 11.9 us  [flipped(): return lax.ppermute(array, 'blk', [(i, i ^ blk_bits) for i in range(blks)])]
    another operation x4 -> x0, local copies, waits for them, and re-layouts: 0.92 us -> none  [grid_body(): other = flipped(jnp.stack([a[:, 256:] for a in [own] + near]), 1, 0)]
    slice x2 -> x8, local copies, waits for them, and re-layouts: 0.04 us -> 0.94 us  [the longest x4 0.92 us: grid_body(): other = [flipped(a[:, 256:], 1, 0) for a in [own] + near]]
    ppermute x2, waiting for transfers between devices: 2.34 us -> 2.9 us  [flipped(): lax.ppermute(array, ('head', 'blk'), [(i, i ^ bits) for i in range(heads...]
  transfers between devices with their start and end apart: 13 -> 20, of which waited for: 9 -> 13; matrix products, arithmetic and copies ran while one was open for 2% -> 2% of each run, Pallas kernels for 14% -> 14%
where the time goes in v3:
time: 51.9 us; the launch traced here: 51.7 us
  waiting for transfers between devices  21.1 us (41%)
  starting transfers between devices  16.2 us (31%)
  Pallas kernels  12.5 us (24%)
  local copies, waits for them, and re-layouts  0.97 us (2%)
  between operations  0.84 us (2%)
    pallas_call x11, Pallas kernels, call(): pl.pallas_call(kernel, out_shape=out_shape, in_specs=specs, out_specs=jax...  12.5 us
    ppermute x8, waiting for transfers between devices, flipped(): return lax.ppermute(array, 'blk', [(i, i ^ blk_bits) for i in range(blks)])  12.5 us
    ppermute x8, starting transfers between devices, flipped(): return lax.ppermute(array, 'blk', [(i, i ^ blk_bits) for i in range(blks)])  11.9 us
    ppermute x10, waiting for transfers between devices, flipped(): lax.ppermute(array, 'head', [(i, i ^ head_bits) for i in range(heads)])  5.7 us
    ppermute x10, starting transfers between devices, flipped(): lax.ppermute(array, 'head', [(i, i ^ head_bits) for i in range(heads)])  4.05 us
    ppermute x2, waiting for transfers between devices, flipped(): lax.ppermute(array, ('head', 'blk'), [(i, i ^ bits) for i in range(heads...  2.9 us
  transfers between devices with their start and end apart: 20, of which 13 were waited for; matrix products, arithmetic and copies ran while one was open for 2% of the time, Pallas kernels for 14%

profile of v3, /device:TPU:0, one launch (start us, length us, event | category | flops | bytes accessed | tf_op | source)
XLA Modules:
  0.0 51.7 jit_solution(811691451680002169)
XLA Ops:
  0.6 2.5 %shard_map.85 = (bf16[96,640]{1,0:T(8,128)(2,1)}, bf16[96,640]{1,0:T(8,128)(2,1)}, bf16[96,640]{1,0:T(8,128)(2,1)}, bf16[96,640]{1,0:T(8,128)(2,1)}) custom-call(bf16[88,640]{1,0:T(8,128)(2,1)} %bitcast.19, bf16[88,640]{1,0:T(8,128)(2,1)} %bitcast.20, bf16[88,640]{1,0:T(8,128)(2,1)} %bitcast.21, bf16[88,640]{1,0:T(8,128)(2,1)} %bitcast.22, ...), custom_call_target="tpu_custom_call" | custom-call | tf_op jit(solution)/shard_map/pallas_call | solution.py:116
  3.2 3.1 %collective-permute-start.1 = (bf16[96,640]{1,0:T(8,128)(2,1)}, bf16[96,640]{1,0:T(8,128)(2,1)S(1)}, u32[]{:S(2)}, u32[]{:S(2)}) collective-permute-start(bf16[96,640]{1,0:T(8,128)(2,1)} %get-tuple-element.46), channel_id=1, source_target_pairs={{0,2},{1,3},{2,0},{3,1},{4,6},{5,7},{6,4},{7,5},{8,10},{9,11},{10,... | collective-permute-start | bytes 368648 | tf_op jit(solution)/shard_map/ppermute | solution.py:435
  6.3 1.5 %collective-permute-start.3 = (bf16[96,640]{1,0:T(8,128)(2,1)}, bf16[96,640]{1,0:T(8,128)(2,1)S(1)}, u32[]{:S(2)}, u32[]{:S(2)}) collective-permute-start(bf16[96,640]{1,0:T(8,128)(2,1)} %get-tuple-element.47), channel_id=1, source_target_pairs={{0,16},{8,24},{16,0},{24,8},{1,17},{9,25},{17,1},{25,9},{2,18},{10... | collective-permute-start | bytes 368648 | tf_op jit(solution)/shard_map/ppermute | solution.py:433
  7.7 0.0 collective-permute-start.5
  7.8 0.9 %slice.36 = bf16[96,384]{1,0:T(8,128)(2,1)S(1)} slice(bf16[96,640]{1,0:T(8,128)(2,1)} %get-tuple-element.45.own), slice={[0:96], [256:640]} | slice | bytes 147456 | tf_op jit(solution)/shard_map/slice | solution.py:462
  8.7 1.6 %collective-permute-done.1.near1 = bf16[96,640]{1,0:T(8,128)(2,1)S(1)} collective-permute-done((bf16[96,640]{1,0:T(8,128)(2,1)}, bf16[96,640]{1,0:T(8,128)(2,1)S(1)}, u32[]{:S(2)}, u32[]{:S(2)}) %collective-permute-start.1) | collective-permute-done | bytes 122912 | tf_op jit(solution)/shard_map/ppermute | solution.py:435
  10.3 0.1 collective-permute-start.2
  10.4 3.6 %collective-permute-done.3.near2 = bf16[96,640]{1,0:T(8,128)(2,1)S(1)} collective-permute-done((bf16[96,640]{1,0:T(8,128)(2,1)}, bf16[96,640]{1,0:T(8,128)(2,1)S(1)}, u32[]{:S(2)}, u32[]{:S(2)}) %collective-permute-start.3) | collective-permute-done | bytes 122912 | tf_op jit(solution)/shard_map/ppermute | solution.py:433
  14.0 0.0 copy-start.1
  14.0 0.1 collective-permute-start.4
  14.1 0.0 collective-permute-done.5.near3
  14.1 0.6 %collective-permute-start.6 = (bf16[96,384]{1,0:T(8,128)(2,1)S(1)}, bf16[96,384]{1,0:T(8,128)(2,1)S(1)}, u32[]{:S(2)}, u32[]{:S(2)}) collective-permute-start(bf16[96,384]{1,0:T(8,128)(2,1)S(1)} %slice.50), channel_id=1, source_target_pairs={{0,8},{8,0},{16,24},{24,16},{1,9},{9,1},{17,25},{25,17},{2,10},{10... | collective-permute-start | bytes 221192 | tf_op jit(solution)/shard_map/ppermute | solution.py:433
  14.7 0.0 collective-permute-done.other0
  14.7 0.0 collective-permute-done.2.other1
  14.7 0.7 %collective-permute-done.4.other2 = bf16[96,384]{1,0:T(8,128)(2,1)S(1)} collective-permute-done((bf16[96,384]{1,0:T(8,128)(2,1)S(1)}, bf16[96,384]{1,0:T(8,128)(2,1)S(1)}, u32[]{:S(2)}, u32[]{:S(2)}) %collective-permute-start.4) | collective-permute-done | bytes 73760 | tf_op jit(solution)/shard_map/ppermute | solution.py:433
  15.3 0.2 collective-permute-done.6.other3
  15.6 0.2 shard_map.86
  15.8 2.7 %collective-permute-start.10 = (bf16[96,640]{1,0:T(8,128)(2,1)S(1)}, bf16[96,640]{1,0:T(8,128)(2,1)S(1)}, u32[]{:S(2)}, u32[]{:S(2)}) collective-permute-start(bf16[96,640]{1,0:T(8,128)(2,1)S(1)} %get-tuple-element.50.low), channel_id=1, source_target_pairs={{0,4},{1,5},{2,6},{3,7},{4,0},{5,1},{6,2},{7,3},{8,12},{9,13},{10,... | collective-permute-start | bytes 368648 | tf_op jit(solution)/shard_map/ppermute | solution.py:435
  18.4 0.1 shard_map.87
  18.6 1.6 %collective-permute-start.7 = (bf16[88,640]{1,0:T(8,128)(2,1)S(1)}, bf16[88,640]{1,0:T(8,128)(2,1)S(1)}, u32[]{:S(2)}, u32[]{:S(2)}) collective-permute-start(bf16[88,640]{1,0:T(8,128)(2,1)S(1)} %get-tuple-element.56.k_low), channel_id=1, source_target_pairs={{0,1},{1,0},{2,3},{3,2},{4,5},{5,4},{6,7},{7,6},{8,9},{9,8},{10,11... | collective-permute-start | bytes 337928 | tf_op jit(solution)/shard_map/ppermute | solution.py:435
  20.2 0.5 collective-permute-start.8
  20.7 1.7 %shard_map.88 = (f32[80,768]{1,0:T(8,128)S(1)}, f32[768,80]{1,0:T(8,128)S(1)}, f32[768,80]{1,0:T(8,128)S(1)}, bf16[768,80]{1,0:T(8,128)(2,1)S(1)}, bf16[768,80]{...) custom-call(bf16[96,640]{1,0:T(8,128)(2,1)S(1)} %get-tuple-element.50.low, ...), custom_call_target="tpu_custom_call" | custom-call | tf_op jit(solution)/shard_map/pallas_call | solution.py:116
  22.4 0.4 collective-permute-start.9
  22.8 1.8 %collective-permute-done.7.k_low = bf16[88,640]{1,0:T(8,128)(2,1)S(1)} collective-permute-done((bf16[88,640]{1,0:T(8,128)(2,1)S(1)}, bf16[88,640]{1,0:T(8,128)(2,1)S(1)}, u32[]{:S(2)}, u32[]{:S(2)}) %collective-permute-start.7) | collective-permute-done | bytes 112672 | tf_op jit(solution)/shard_map/ppermute | solution.py:435
  24.6 1.5 %collective-permute-done.8.k_high = bf16[88,640]{1,0:T(8,128)(2,1)S(1)} collective-permute-done((bf16[88,640]{1,0:T(8,128)(2,1)S(1)}, bf16[88,640]{1,0:T(8,128)(2,1)S(1)}, u32[]{:S(2)}, u32[]{:S(2)}) %collective-permute-start.8) | collective-permute-done | bytes 112672 | tf_op jit(solution)/shard_map/ppermute | solution.py:435
  26.1 1.6 %shard_map.89 = (f32[80,768]{1,0:T(8,128)S(1)}, f32[768,80]{1,0:T(8,128)S(1)}, f32[768,80]{1,0:T(8,128)S(1)}, bf16[768,80]{1,0:T(8,128)(2,1)S(1)}, bf16[768,80]{1,0:T(8,128)(2,1)S(1)}) custom-call(bf16[96,640]{1,0:T(8,128)(2,1)S(1)} %get-tuple-element.50.low, bf16[96,640]{1,0:T(8,128)(2,1)S(1)} %get-tuple-element.59.high, ...), custom_call_target="tpu_custom_call" | custom-call | tf_op jit(solution)/shard_map/pallas_call | solution.py:116
  27.8 2.1 %shard_map.90 = (f32[80,384]{1,0:T(8,128)S(1)}, f32[768,80]{1,0:T(8,128)S(1)}, f32[768,80]{1,0:T(8,128)S(1)}, f32[768,80]{1,0:T(8,128)S(1)}, f32[768,80]{1,0:T(8,128)S(1)}) custom-call(bf16[96,640]{1,0:T(8,128)(2,1)S(1)} %collective-permute-done.10.low, bf16[768,80]{1,0:T(8,128)(2,1)S(1)} %get-tuple-element.64.k_far, ...), custom_call_target="tpu_custom_call" | custom-call | flops 1000000000 | tf_op jit(solution)/shard_map/pallas_call | solution.py:116
  29.9 0.8 %collective-permute-done.9.high = bf16[96,640]{1,0:T(8,128)(2,1)S(1)} collective-permute-done((bf16[96,640]{1,0:T(8,128)(2,1)S(1)}, bf16[96,640]{1,0:T(8,128)(2,1)S(1)}, u32[]{:S(2)}, u32[]{:S(2)}) %collective-permute-start.9) | collective-permute-done | bytes 122912 | tf_op jit(solution)/shard_map/ppermute | solution.py:435
  30.7 1.3 %shard_map.91 = (f32[80,384]{1,0:T(8,128)S(1)}, bf16[88,1280]{1,0:T(8,128)(2,1)S(1)}, bf16[384,80]{1,0:T(8,128)(2,1)S(1)}, bf16[384,80]{1,0:T(8,128)(2,1)S(1)}) custom-call(bf16[96,640]{1,0:T(8,128)(2,1)S(1)} %collective-permute-done.9.high, bf16[768,80]{1,0:T(8,128)(2,1)S(1)} %get-tuple-element.64.k_far, bf16[768,80]{1,0:T(8,128)(2,1)S(1)} %get-tuple-element.65.v_far, ...), custom_call_target="tpu_custom_call" | custom-call | tf_op jit(solution)/shard_map/pallas_call | solution.py:116
  32.0 1.6 %collective-permute-start.11 = (bf16[88,1280]{1,0:T(8,128)(2,1)S(1)}, bf16[88,1280]{1,0:T(8,128)(2,1)S(1)}, u32[]{:S(2)}, u32[]{:S(2)}) collective-permute-start(bf16[88,1280]{1,0:T(8,128)(2,1)S(1)} %get-tuple-element.82), channel_id=1, source_target_pairs={{0,1},{1,0},{2,3},{3,2},{4,5},{5,4},{6,7},{7,6},{8,9},{9,8},{10,11... | collective-permute-start | bytes 675848 | tf_op jit(solution)/shard_map/ppermute | solution.py:435
  33.6 1.4 %shard_map.92 = (bf16[88,640]{1,0:T(8,128)(2,1)S(1)}, f32[768,80]{1,0:T(8,128)S(1)}, f32[768,80]{1,0:T(8,128)S(1)}) custom-call(bf16[96,640]{1,0:T(8,128)(2,1)S(1)} %collective-permute-done.9.high, bf16[384,80]{1,0:T(8,128)(2,1)S(1)} %get-tuple-element.74.q_s, bf16[384,80]{1,0:T(8,128)(2,1)S(1)} %get-tuple-element.75.do_s, ...), custom_call_target="tpu_custom_call" | custom-call | tf_op jit(solution)/shard_map/pallas_call | solution.py:116
  35.0 0.1 collective-permute-start.12
  35.1 0.4 shard_map.93.own
  35.5 6.5 %collective-permute-done.12.dq_wire = bf16[88,640]{1,0:T(8,128)(2,1)S(1)} collective-permute-done((bf16[88,640]{1,0:T(8,128)(2,1)S(1)}, bf16[88,640]{1,0:T(8,128)(2,1)S(1)}, u32[]{:S(2)}, u32[]{:S(2)}) %collective-permute-start.12) | collective-permute-done | bytes 112672 | tf_op jit(solution)/shard_map/ppermute | solution.py:435
  42.0 0.2 shard_map.94
  42.3 0.3 collective-permute-start.15
  42.6 1.3 %collective-permute-start.14 = (bf16[88,512]{1,0:T(8,128)(2,1)S(1)}, bf16[88,512]{1,0:T(8,128)(2,1)S(1)}, u32[]{:S(2)}, u32[]{:S(2)}) collective-permute-start(bf16[88,512]{1,0:T(8,128)(2,1)S(1)} %get-tuple-element.88), channel_id=1, source_target_pairs={{0,16},{8,24},{16,0},{24,8},{1,17},{9,25},{17,1},{25,9},{2,18},{10... | collective-permute-start | bytes 270344 | tf_op jit(solution)/shard_map/ppermute | solution.py:433
  43.9 2.0 %collective-permute-start.13 = (bf16[88,512]{1,0:T(8,128)(2,1)S(1)}, bf16[88,512]{1,0:T(8,128)(2,1)S(1)}, u32[]{:S(2)}, u32[]{:S(2)}) collective-permute-start(bf16[88,512]{1,0:T(8,128)(2,1)S(1)} %get-tuple-element.89), channel_id=1, source_target_pairs={{0,2},{1,3},{2,0},{3,1},{4,6},{5,7},{6,4},{7,5},{8,10},{9,11},{10,... | collective-permute-start | bytes 270344 | tf_op jit(solution)/shard_map/ppermute | solution.py:435
  45.9 0.0 collective-permute-start.16
  45.9 2.9 %collective-permute-done.15.refs_3_ = bf16[88,512]{1,0:T(8,128)(2,1)S(1)} collective-permute-done((bf16[88,512]{1,0:T(8,128)(2,1)S(1)}, bf16[88,512]{1,0:T(8,128)(2,1)S(1)}, u32[]{:S(2)}, u32[]{:S(2)}) %collective-permute-start.15) | collective-permute-done | bytes 90144 | tf_op jit(solution)/shard_map/ppermute | solution.py:437
  48.8 0.0 collective-permute-done.14.refs_2_
  48.8 0.5 %collective-permute-start.18 = (bf16[88,256]{1,0:T(8,128)(2,1)S(1)}, bf16[88,256]{1,0:T(8,128)(2,1)S(1)}, u32[]{:S(2)}, u32[]{:S(2)}) collective-permute-start(bf16[88,256]{1,0:T(8,128)(2,1)S(1)} %slice.57), channel_id=1, source_target_pairs={{0,8},{8,0},{16,24},{24,16},{1,9},{9,1},{17,25},{25,17},{2,10},{10... | collective-permute-start | bytes 135176 | tf_op jit(solution)/shard_map/ppermute | solution.py:433
  49.3 0.2 collective-permute-done.13.refs_1_
  49.5 0.0 collective-permute-done.16.refs_4_
  49.5 0.5 collective-permute-done.19.refs_7_
  50.0 0.2 collective-permute-done.18.refs_6_
  50.2 0.5 collective-permute-done.17.refs_5_
  50.7 0.9 %shard_map.95 = (bf16[88,640]{1,0:T(8,128)(2,1)}, bf16[88,640]{1,0:T(8,128)(2,1)}, bf16[88,640]{1,0:T(8,128)(2,1)}) custom-call(bf16[88,512]{1,0:T(8,128)(2,1)S(1)} %get-tuple-element.90.refs_0_, bf16[88,512]{1,0:T(8,128)(2,1)S(1)} %collective-permute-done.13.refs_1_, bf16[88,512]{1,0:T(8,128)(2,1)S(1)} %collective-permute-done.14.refs_2_, ...), custom_call_target="tpu_custom_call" | custom-call | tf_op jit(solution)/shard_map/pallas_call | solution.py:116
  (16 shorter events, 0.1 us)
Async XLA Ops:
  3.2 7.1 %collective-permute-start.1 = (bf16[96,640]{1,0:T(8,128)(2,1)}, bf16[96,640]{1,0:T(8,128)(2,1)S(1)}, u32[]{:S(2)}, u32[]{:S(2)}) collective-permute-start(bf16[96,640]{1,0:T(8,128)(2,1)} %get-tuple-element.46), channel_id=1, source_target_pairs={{0,2},{1,3},{2,0},{3,1},{4,6},{5,7},{6,4},{7,5},{8,10},{9,11},{10,... | collective-permute-start | bytes 368648 | tf_op jit(solution)/shard_map/ppermute | solution.py:435
  6.3 7.7 %collective-permute-start.3 = (bf16[96,640]{1,0:T(8,128)(2,1)}, bf16[96,640]{1,0:T(8,128)(2,1)S(1)}, u32[]{:S(2)}, u32[]{:S(2)}) collective-permute-start(bf16[96,640]{1,0:T(8,128)(2,1)} %get-tuple-element.47), channel_id=1, source_target_pairs={{0,16},{8,24},{16,0},{24,8},{1,17},{9,25},{17,1},{25,9},{2,18},{10... | collective-permute-start | bytes 368648 | tf_op jit(solution)/shard_map/ppermute | solution.py:433
  7.7 6.3 %collective-permute-start.5 = (bf16[96,640]{1,0:T(8,128)(2,1)}, bf16[96,640]{1,0:T(8,128)(2,1)S(1)}, u32[]{:S(2)}, u32[]{:S(2)}) collective-permute-start(bf16[96,640]{1,0:T(8,128)(2,1)} %get-tuple-element.48), channel_id=1, source_target_pairs={{0,18},{1,19},{2,16},{3,17},{4,22},{5,23},{6,20},{7,21},{8,26},{9,... | collective-permute-start | bytes 368648 | tf_op jit(solution)/shard_map/ppermute | solution.py:437
  8.7 6.0 %collective-permute-start = (bf16[96,384]{1,0:T(8,128)(2,1)S(1)}, bf16[96,384]{1,0:T(8,128)(2,1)S(1)}, u32[]{:S(2)}, u32[]{:S(2)}) collective-permute-start(bf16[96,384]{1,0:T(8,128)(2,1)S(1)} %slice.36), channel_id=1, source_target_pairs={{0,8},{8,0},{16,24},{24,16},{1,9},{9,1},{17,25},{25,17},{2,10},{10... | collective-permute-start | bytes 221192 | tf_op jit(solution)/shard_map/ppermute | solution.py:433
  10.3 5.3 %copy-start = (bf16[96,640]{1,0:T(8,128)(2,1)S(1)}, bf16[96,640]{1,0:T(8,128)(2,1)}, u32[]{:S(2)}) copy-start(bf16[96,640]{1,0:T(8,128)(2,1)} %get-tuple-element.45.own) | copy-start | bytes 368644
  10.3 4.3 %collective-permute-start.2 = (bf16[96,384]{1,0:T(8,128)(2,1)S(1)}, bf16[96,384]{1,0:T(8,128)(2,1)S(1)}, u32[]{:S(2)}, u32[]{:S(2)}) collective-permute-start(bf16[96,384]{1,0:T(8,128)(2,1)S(1)} %slice.48), channel_id=1, source_target_pairs={{0,8},{8,0},{16,24},{24,16},{1,9},{9,1},{17,25},{25,17},{2,10},{10... | collective-permute-start | bytes 221192 | tf_op jit(solution)/shard_map/ppermute | solution.py:433
  14.0 1.6 %copy-start.1 = (f32[1,2,352]{2,1,0:T(2,128)S(1)}, f32[1,2,352]{2,1,0:T(2,128)}, u32[]{:S(2)}) copy-start(f32[1,2,352]{2,1,0:T(2,128)} %param.11) | copy-start | bytes 8452
  14.0 1.3 %collective-permute-start.4 = (bf16[96,384]{1,0:T(8,128)(2,1)S(1)}, bf16[96,384]{1,0:T(8,128)(2,1)S(1)}, u32[]{:S(2)}, u32[]{:S(2)}) collective-permute-start(bf16[96,384]{1,0:T(8,128)(2,1)S(1)} %slice.49), channel_id=1, source_target_pairs={{0,8},{8,0},{16,24},{24,16},{1,9},{9,1},{17,25},{25,17},{2,10},{10... | collective-permute-start | bytes 221192 | tf_op jit(solution)/shard_map/ppermute | solution.py:433
  14.1 1.5 %collective-permute-start.6 = (bf16[96,384]{1,0:T(8,128)(2,1)S(1)}, bf16[96,384]{1,0:T(8,128)(2,1)S(1)}, u32[]{:S(2)}, u32[]{:S(2)}) collective-permute-start(bf16[96,384]{1,0:T(8,128)(2,1)S(1)} %slice.50), channel_id=1, source_target_pairs={{0,8},{8,0},{16,24},{24,16},{1,9},{9,1},{17,25},{25,17},{2,10},{10... | collective-permute-start | bytes 221192 | tf_op jit(solution)/shard_map/ppermute | solution.py:433
  15.8 12.0 %collective-permute-start.10 = (bf16[96,640]{1,0:T(8,128)(2,1)S(1)}, bf16[96,640]{1,0:T(8,128)(2,1)S(1)}, u32[]{:S(2)}, u32[]{:S(2)}) collective-permute-start(bf16[96,640]{1,0:T(8,128)(2,1)S(1)} %get-tuple-element.50.low), channel_id=1, source_target_pairs={{0,4},{1,5},{2,6},{3,7},{4,0},{5,1},{6,2},{7,3},{8,12},{9,13},{10,... | collective-permute-start | bytes 368648 | tf_op jit(solution)/shard_map/ppermute | solution.py:435
  18.6 6.0 %collective-permute-start.7 = (bf16[88,640]{1,0:T(8,128)(2,1)S(1)}, bf16[88,640]{1,0:T(8,128)(2,1)S(1)}, u32[]{:S(2)}, u32[]{:S(2)}) collective-permute-start(bf16[88,640]{1,0:T(8,128)(2,1)S(1)} %get-tuple-element.56.k_low), channel_id=1, source_target_pairs={{0,1},{1,0},{2,3},{3,2},{4,5},{5,4},{6,7},{7,6},{8,9},{9,8},{10,11... | collective-permute-start | bytes 337928 | tf_op jit(solution)/shard_map/ppermute | solution.py:435
  20.2 6.0 %collective-permute-start.8 = (bf16[88,640]{1,0:T(8,128)(2,1)S(1)}, bf16[88,640]{1,0:T(8,128)(2,1)S(1)}, u32[]{:S(2)}, u32[]{:S(2)}) collective-permute-start(bf16[88,640]{1,0:T(8,128)(2,1)S(1)} %get-tuple-element.57.k_high), channel_id=1, source_target_pairs={{0,1},{1,0},{2,3},{3,2},{4,5},{5,4},{6,7},{7,6},{8,9},{9,8},{10,11... | collective-permute-start | bytes 337928 | tf_op jit(solution)/shard_map/ppermute | solution.py:435
  22.4 8.3 %collective-permute-start.9 = (bf16[96,640]{1,0:T(8,128)(2,1)S(1)}, bf16[96,640]{1,0:T(8,128)(2,1)S(1)}, u32[]{:S(2)}, u32[]{:S(2)}) collective-permute-start(bf16[96,640]{1,0:T(8,128)(2,1)S(1)} %get-tuple-element.59.high), channel_id=1, source_target_pairs={{0,4},{1,5},{2,6},{3,7},{4,0},{5,1},{6,2},{7,3},{8,12},{9,13},{10,... | collective-permute-start | bytes 368648 | tf_op jit(solution)/shard_map/ppermute | solution.py:435
  32.0 10.0 %collective-permute-start.11 = (bf16[88,1280]{1,0:T(8,128)(2,1)S(1)}, bf16[88,1280]{1,0:T(8,128)(2,1)S(1)}, u32[]{:S(2)}, u32[]{:S(2)}) collective-permute-start(bf16[88,1280]{1,0:T(8,128)(2,1)S(1)} %get-tuple-element.82), channel_id=1, source_target_pairs={{0,1},{1,0},{2,3},{3,2},{4,5},{5,4},{6,7},{7,6},{8,9},{9,8},{10,11... | collective-permute-start | bytes 675848 | tf_op jit(solution)/shard_map/ppermute | solution.py:435
  35.0 7.0 %collective-permute-start.12 = (bf16[88,640]{1,0:T(8,128)(2,1)S(1)}, bf16[88,640]{1,0:T(8,128)(2,1)S(1)}, u32[]{:S(2)}, u32[]{:S(2)}) collective-permute-start(bf16[88,640]{1,0:T(8,128)(2,1)S(1)} %get-tuple-element.83), channel_id=1, source_target_pairs={{0,4},{1,5},{2,6},{3,7},{4,0},{5,1},{6,2},{7,3},{8,12},{9,13},{10,... | collective-permute-start | bytes 337928 | tf_op jit(solution)/shard_map/ppermute | solution.py:435
  42.3 6.5 %collective-permute-start.15 = (bf16[88,512]{1,0:T(8,128)(2,1)S(1)}, bf16[88,512]{1,0:T(8,128)(2,1)S(1)}, u32[]{:S(2)}, u32[]{:S(2)}) collective-permute-start(bf16[88,512]{1,0:T(8,128)(2,1)S(1)} %get-tuple-element.87), channel_id=1, source_target_pairs={{0,18},{1,19},{2,16},{3,17},{4,22},{5,23},{6,20},{7,21},{8,26},{9,... | collective-permute-start | bytes 270344 | tf_op jit(solution)/shard_map/ppermute | solution.py:437
  42.6 6.2 %collective-permute-start.14 = (bf16[88,512]{1,0:T(8,128)(2,1)S(1)}, bf16[88,512]{1,0:T(8,128)(2,1)S(1)}, u32[]{:S(2)}, u32[]{:S(2)}) collective-permute-start(bf16[88,512]{1,0:T(8,128)(2,1)S(1)} %get-tuple-element.88), channel_id=1, source_target_pairs={{0,16},{8,24},{16,0},{24,8},{1,17},{9,25},{17,1},{25,9},{2,18},{10... | collective-permute-start | bytes 270344 | tf_op jit(solution)/shard_map/ppermute | solution.py:433
  43.9 5.6 %collective-permute-start.13 = (bf16[88,512]{1,0:T(8,128)(2,1)S(1)}, bf16[88,512]{1,0:T(8,128)(2,1)S(1)}, u32[]{:S(2)}, u32[]{:S(2)}) collective-permute-start(bf16[88,512]{1,0:T(8,128)(2,1)S(1)} %get-tuple-element.89), channel_id=1, source_target_pairs={{0,2},{1,3},{2,0},{3,1},{4,6},{5,7},{6,4},{7,5},{8,10},{9,11},{10,... | collective-permute-start | bytes 270344 | tf_op jit(solution)/shard_map/ppermute | solution.py:435
  45.9 3.7 %collective-permute-start.16 = (bf16[88,256]{1,0:T(8,128)(2,1)S(1)}, bf16[88,256]{1,0:T(8,128)(2,1)S(1)}, u32[]{:S(2)}, u32[]{:S(2)}) collective-permute-start(bf16[88,256]{1,0:T(8,128)(2,1)S(1)} %slice.55), channel_id=1, source_target_pairs={{0,8},{8,0},{16,24},{24,16},{1,9},{9,1},{17,25},{25,17},{2,10},{10... | collective-permute-start | bytes 135176 | tf_op jit(solution)/shard_map/ppermute | solution.py:433
  48.8 1.2 %collective-permute-start.19 = (bf16[88,256]{1,0:T(8,128)(2,1)S(1)}, bf16[88,256]{1,0:T(8,128)(2,1)S(1)}, u32[]{:S(2)}, u32[]{:S(2)}) collective-permute-start(bf16[88,256]{1,0:T(8,128)(2,1)S(1)} %slice.58), channel_id=1, source_target_pairs={{0,8},{8,0},{16,24},{24,16},{1,9},{9,1},{17,25},{25,17},{2,10},{10... | collective-permute-start | bytes 135176 | tf_op jit(solution)/shard_map/ppermute | solution.py:433
  48.8 1.4 %collective-permute-start.18 = (bf16[88,256]{1,0:T(8,128)(2,1)S(1)}, bf16[88,256]{1,0:T(8,128)(2,1)S(1)}, u32[]{:S(2)}, u32[]{:S(2)}) collective-permute-start(bf16[88,256]{1,0:T(8,128)(2,1)S(1)} %slice.57), channel_id=1, source_target_pairs={{0,8},{8,0},{16,24},{24,16},{1,9},{9,1},{17,25},{25,17},{2,10},{10... | collective-permute-start | bytes 135176 | tf_op jit(solution)/shard_map/ppermute | solution.py:433
  49.5 1.2 %collective-permute-start.17 = (bf16[88,256]{1,0:T(8,128)(2,1)S(1)}, bf16[88,256]{1,0:T(8,128)(2,1)S(1)}, u32[]{:S(2)}, u32[]{:S(2)}) collective-permute-start(bf16[88,256]{1,0:T(8,128)(2,1)S(1)} %slice.56), channel_id=1, source_target_pairs={{0,8},{8,0},{16,24},{24,16},{1,9},{9,1},{17,25},{25,17},{2,10},{10... | collective-permute-start | bytes 135176 | tf_op jit(solution)/shard_map/ppermute | solution.py:433

commit v4 on v3

--- a/solution.py
+++ b/solution.py
@@ -108,7 +108,7 @@
     )
 
 
-def call(kernel, out_shape, *operands, scratch=(), remote=0, flops=0, out_space=pltpu.VMEM, limit=VMEM_LIMIT):
+def call(kernel, out_shape, *operands, scratch=(), remote=0, out_space=pltpu.VMEM, limit=VMEM_LIMIT):
     specs = [
         pl.BlockSpec(memory_space=pltpu.HBM if i < remote else pltpu.VMEM)
         for i in range(len(operands))
@@ -119,7 +119,6 @@
         in_specs=specs,
         out_specs=jax.tree.map(lambda _: pl.BlockSpec(memory_space=out_space), out_shape),
         scratch_shapes=list(scratch),
-        cost_estimate=pl.CostEstimate(flops=flops, bytes_accessed=0, transcendentals=0) if flops else None,
         compiler_params=pltpu.CompilerParams(vmem_limit_bytes=limit),
     )(*operands)
 
@@ -229,16 +228,8 @@
         copy.wait()
 
 
-def parts_of(own, near, other, j, r):
-    if r:
-        return other[j], 320
-    return (own if j == 0 else near[j - 1])[...], 512
-
-
-def gather_queries_kernel(own, near1, near2, near3, other0, other1, other2, other3, lse_in, low, high, lse_s):
-    other = (other0, other1, other2, other3)
-    rows = PADDED - 8
-    near = (near1, near2, near3)
+def gather_kernel(first, block_a, block_b, other_a, other_b, near1, lse_in, queries, keys, lse_s):
+    rows = keys.shape[0]
     _, w, _, h = place()
     lse_own = lse_in[pl.ds(w, 1), :] * LOG2E
     below = near1[rows:PADDED, :].astype(F32)
@@ -247,32 +238,22 @@
     lse_s[...] = jnp.concatenate(
         [lse_own[:, rows * i : rows * (i + 1)] for i in range(4)] + [lse_near], axis=0
     )
-    blocks, spots = [], []
+    q_parts, k_parts, spots = [], [], []
     gap = jnp.zeros((6, PADDED - rows), F32)
-    for j in range(4):
+    for j in (first, first + 1):
         for r in range(2):
-            held, _ = parts_of(own, near, other, j, r)
-            blocks.append(held[0:rows, 0:160])
+            held = ((block_a, block_b), (other_a, other_b))[r][j % 2]
+            deep = (512, 320)[r]
+            q_parts.append(held[0:rows, 0:160])
+            k_parts += [held[0:rows, 160:256], held[0:rows, deep : deep + 64]]
             delta = held[rows:PADDED, 0:128].astype(F32)[0:3, 0:rows]
             lse = lse_s[pl.ds(4 * (j % 2) + (h ^ (2 * (j // 2) + r)), 1), :]
             spots += [jnp.concatenate([delta, pieces_of(lse)], axis=0), gap]
-    for at, wire in ((0, low), (4, high)):
-        wire[0:rows] = jnp.concatenate(blocks[at : at + 4], axis=1)
-        below = jnp.concatenate(spots[2 * at : 2 * at + 8] + [jnp.zeros((6, 256), F32)], axis=1)
-        below = jnp.concatenate([below, jnp.zeros((2, 640), F32)], axis=0)
-        wire[rows:PADDED] = below.astype(BF16)
-
-
-def gather_keys_kernel(own, near1, near2, near3, other0, other1, other2, other3, low, high):
-    other = (other0, other1, other2, other3)
-    rows = low.shape[0]
-    blocks = []
-    for j in range(4):
-        for r in range(2):
-            held, deep = parts_of(own, (near1, near2, near3), other, j, r)
-            blocks += [held[0:rows, 160:256], held[0:rows, deep : deep + 64]]
-    low[...] = jnp.concatenate(blocks[:8], axis=1)
-    high[...] = jnp.concatenate(blocks[8:], axis=1)
+    keys[...] = jnp.concatenate(k_parts, axis=1)
+    queries[0:rows] = jnp.concatenate(q_parts, axis=1)
+    below = jnp.concatenate(spots + [jnp.zeros((6, 256), F32)], axis=1)
+    below = jnp.concatenate([below, jnp.zeros((2, 640), F32)], axis=0)
+    queries[rows:PADDED] = below.astype(BF16)
 
 
 def rows_of(wires):
@@ -460,32 +441,35 @@
     own = packed[0]
     near = to_chips(packed)
     other = [flipped(a[:, 256:], 1, 0) for a in [own] + near]
-    low, high = call(
-        gather_queries_kernel,
-        (shape(PADDED, 640), shape(PADDED, 640)),
-        own, *near, *other, lse[0],
-        scratch=[pltpu.VMEM((8, rows), F32)],
-    )
-    low_far = flipped(low, 0, 4)
-    other, low = lax.optimization_barrier((other, low))
-    wires_k = call(gather_keys_kernel, (shape(rows, 640),) * 2, own, *near, *other)
-    wires_k_far = [flipped(wire, 0, 1) for wire in wires_k]
+    blocks = [own] + near
+
+    def gather(first):
+        return call(
+            functools.partial(gather_kernel, first),
+            (shape(PADDED, 640), shape(rows, 640)),
+            *blocks[first : first + 2], *other[first : first + 2], near[0], lse[0],
+            scratch=[pltpu.VMEM((8, rows), F32)],
+        )
+
+    low, k_low = gather(0)
+    low_far, k_low_far = flipped(low, 0, 4), flipped(k_low, 0, 1)
+    high, k_high = gather(2)
+    k_high, k_low_far = lax.optimization_barrier((k_high, k_low_far))
+    high_far, k_high_far = flipped(high, 0, 4), flipped(k_high, 0, 1)
+    keys_far = [k_low_far, k_high_far]
 
     grad = shape(padded, HDIM, dtype=F32)
     side = shape(padded, HDIM)
     dq_shape = shape(HDIM, padded, dtype=F32)
     dq_own, dk_own, dv_own, q_s, do_s, k_own, v_own = call(
-        own_own_kernel, (dq_shape, grad, grad, side, side, side, side), low, high, *wires_k
-    )
-    high, dq_own = lax.optimization_barrier((high, dq_own))
-    high_far = flipped(high, 0, 4)
+        own_own_kernel, (dq_shape, grad, grad, side, side, side, side), low, high, k_low, k_high
+    )
     dq_own, dk_far, dv_far, k_far, v_far = call(
-        own_far_kernel, (dq_shape, grad, grad, side, side), low, high, q_s, do_s, *wires_k_far, dq_own
+        own_far_kernel, (dq_shape, grad, grad, side, side), low, high, q_s, do_s, *keys_far, dq_own
     )
     dq_low, dk_far, dv_far, dk_own, dv_own = call(
         low_kernel, (shape(HDIM, half, dtype=F32), grad, grad, grad, grad),
         low_far, k_far, v_far, k_own, v_own, dk_far, dv_far, dk_own, dv_own,
-        flops=1000000000,
         scratch=[pltpu.VMEM((half, HDIM), BF16)] * 2,
     )
     few = shape(half, HDIM)

time: 51.9 us -> 50.6 us (0.975)
  waiting for transfers between devices: 21.1 us -> 18.5 us
  starting transfers between devices: 16.2 us -> 17.6 us
    ppermute x10, waiting for transfers between devices: 5.7 us -> 3.05 us  [flipped(): lax.ppermute(array, 'head', [(i, i ^ head_bits) for i in range(heads)])]
    ppermute x8, starting transfers between devices: 11.9 us -> 13.1 us  [flipped(): return lax.ppermute(array, 'blk', [(i, i ^ blk_bits) for i in range(blks)])]
  transfers between devices with their start and end apart: 20 -> 20, of which waited for: 13 -> 11; matrix products, arithmetic and copies ran while one was open for 2% -> 2% of each run, Pallas kernels for 14% -> 15%
where the time goes in v4:
time: 50.6 us; the launch traced here: 50.5 us
  waiting for transfers between devices  18.5 us (37%)
  starting transfers between devices  17.6 us (35%)
  Pallas kernels  12.5 us (25%)
  local copies, waits for them, and re-layouts  1.04 us (2%)
  between operations  0.82 us (2%)
    ppermute x8, starting transfers between devices, flipped(): return lax.ppermute(array, 'blk', [(i, i ^ blk_bits) for i in range(blks)])  13.1 us
    pallas_call x11, Pallas kernels, call(): pl.pallas_call(kernel, out_shape=out_shape, in_specs=specs, out_specs=jax...  12.5 us
    ppermute x8, waiting for transfers between devices, flipped(): return lax.ppermute(array, 'blk', [(i, i ^ blk_bits) for i in range(blks)])  12.5 us
    ppermute x10, starting transfers between devices, flipped(): lax.ppermute(array, 'head', [(i, i ^ head_bits) for i in range(heads)])  4.35 us
    ppermute x10, waiting for transfers between devices, flipped(): lax.ppermute(array, 'head', [(i, i ^ head_bits) for i in range(heads)])  3.05 us
    ppermute x2, waiting for transfers between devices, flipped(): lax.ppermute(array, ('head', 'blk'), [(i, i ^ bits) for i in range(heads...  2.89 us
  transfers between devices with their start and end apart: 20, of which 11 were waited for; matrix products, arithmetic and copies ran while one was open for 2% of the time, Pallas kernels for 15%

profile of v4, /device:TPU:0, one launch (start us, length us, event | category | flops | bytes accessed | tf_op | source)
XLA Modules:
  0.0 50.5 jit_solution(15988108532140594348)
XLA Ops:
  0.6 2.5 %shard_map.85 = (bf16[96,640]{1,0:T(8,128)(2,1)}, bf16[96,640]{1,0:T(8,128)(2,1)}, bf16[96,640]{1,0:T(8,128)(2,1)}, bf16[96,640]{1,0:T(8,128)(2,1)}) custom-call(bf16[88,640]{1,0:T(8,128)(2,1)} %bitcast.20, bf16[88,640]{1,0:T(8,128)(2,1)} %bitcast.21, bf16[88,640]{1,0:T(8,128)(2,1)} %bitcast.22, bf16[88,640]{1,0:T(8,128)(2,1)} %bitcast.23, ...), custom_call_target="tpu_custom_call" | custom-call | tf_op jit(solution)/shard_map/pallas_call | solution.py:116
  3.2 3.1 %collective-permute-start = (bf16[96,640]{1,0:T(8,128)(2,1)}, bf16[96,640]{1,0:T(8,128)(2,1)S(1)}, u32[]{:S(2)}, u32[]{:S(2)}) collective-permute-start(bf16[96,640]{1,0:T(8,128)(2,1)} %get-tuple-element.41), channel_id=1, source_target_pairs={{0,2},{1,3},{2,0},{3,1},{4,6},{5,7},{6,4},{7,5},{8,10},{9,11},{10,... | collective-permute-start | bytes 368648 | tf_op jit(solution)/shard_map/ppermute | solution.py:416
  6.3 1.5 %collective-permute-start.3 = (bf16[96,640]{1,0:T(8,128)(2,1)}, bf16[96,640]{1,0:T(8,128)(2,1)S(1)}, u32[]{:S(2)}, u32[]{:S(2)}) collective-permute-start(bf16[96,640]{1,0:T(8,128)(2,1)} %get-tuple-element.43), channel_id=1, source_target_pairs={{0,16},{8,24},{16,0},{24,8},{1,17},{9,25},{17,1},{25,9},{2,18},{10... | collective-permute-start | bytes 368648 | tf_op jit(solution)/shard_map/ppermute | solution.py:414
  7.7 0.0 collective-permute-start.4
  7.8 1.0 %slice.36 = bf16[96,384]{1,0:T(8,128)(2,1)S(1)} slice(bf16[96,640]{1,0:T(8,128)(2,1)} %get-tuple-element.40.block_a), slice={[0:96], [256:640]} | slice | bytes 147456 | tf_op jit(solution)/shard_map/slice | solution.py:443
  8.8 0.1 collective-permute-start.1
  8.9 1.4 %collective-permute-done.block_b.near1 = bf16[96,640]{1,0:T(8,128)(2,1)S(1)} collective-permute-done((bf16[96,640]{1,0:T(8,128)(2,1)}, bf16[96,640]{1,0:T(8,128)(2,1)S(1)}, u32[]{:S(2)}, u32[]{:S(2)}) %collective-permute-start) | collective-permute-done | bytes 122912 | tf_op jit(solution)/shard_map/ppermute | solution.py:416
  10.3 0.1 collective-permute-start.2
  10.4 0.0 collective-permute-done.1.other_a
  10.4 1.2 %collective-permute-done.2.other_b = bf16[96,384]{1,0:T(8,128)(2,1)S(1)} collective-permute-done((bf16[96,384]{1,0:T(8,128)(2,1)S(1)}, bf16[96,384]{1,0:T(8,128)(2,1)S(1)}, u32[]{:S(2)}, u32[]{:S(2)}) %collective-permute-start.2) | collective-permute-done | bytes 73760 | tf_op jit(solution)/shard_map/ppermute | solution.py:414
  11.7 0.2 shard_map.86
  11.8 1.6 %collective-permute-start.7 = (bf16[88,640]{1,0:T(8,128)(2,1)S(1)}, bf16[88,640]{1,0:T(8,128)(2,1)S(1)}, u32[]{:S(2)}, u32[]{:S(2)}) collective-permute-start(bf16[88,640]{1,0:T(8,128)(2,1)S(1)} %get-tuple-element.46.k_low), channel_id=1, source_target_pairs={{0,1},{1,0},{2,3},{3,2},{4,5},{5,4},{6,7},{7,6},{8,9},{9,8},{10,11... | collective-permute-start | bytes 337928 | tf_op jit(solution)/shard_map/ppermute | solution.py:416
  13.4 0.6 %collective-permute-done.3.block_a = bf16[96,640]{1,0:T(8,128)(2,1)S(1)} collective-permute-done((bf16[96,640]{1,0:T(8,128)(2,1)}, bf16[96,640]{1,0:T(8,128)(2,1)S(1)}, u32[]{:S(2)}, u32[]{:S(2)}) %collective-permute-start.3) | collective-permute-done | bytes 122912 | tf_op jit(solution)/shard_map/ppermute | solution.py:414
  14.0 0.1 collective-permute-start.5
  14.1 0.0 collective-permute-done.4.block_b
  14.1 0.6 %collective-permute-start.6 = (bf16[96,384]{1,0:T(8,128)(2,1)S(1)}, bf16[96,384]{1,0:T(8,128)(2,1)S(1)}, u32[]{:S(2)}, u32[]{:S(2)}) collective-permute-start(bf16[96,384]{1,0:T(8,128)(2,1)S(1)} %slice.50), channel_id=1, source_target_pairs={{0,8},{8,0},{16,24},{24,16},{1,9},{9,1},{17,25},{25,17},{2,10},{10... | collective-permute-start | bytes 221192 | tf_op jit(solution)/shard_map/ppermute | solution.py:414
  14.7 2.6 %collective-permute-start.10 = (bf16[96,640]{1,0:T(8,128)(2,1)S(1)}, bf16[96,640]{1,0:T(8,128)(2,1)S(1)}, u32[]{:S(2)}, u32[]{:S(2)}) collective-permute-start(bf16[96,640]{1,0:T(8,128)(2,1)S(1)} %get-tuple-element.42.low), channel_id=1, source_target_pairs={{0,4},{1,5},{2,6},{3,7},{4,0},{5,1},{6,2},{7,3},{8,12},{9,13},{10,... | collective-permute-start | bytes 368648 | tf_op jit(solution)/shard_map/ppermute | solution.py:416
  17.2 0.0 collective-permute-done.5.other_a
  17.2 0.0 collective-permute-done.6.other_b
  17.2 0.2 shard_map.87
  17.4 1.0 %collective-permute-start.9 = (bf16[96,640]{1,0:T(8,128)(2,1)S(1)}, bf16[96,640]{1,0:T(8,128)(2,1)S(1)}, u32[]{:S(2)}, u32[]{:S(2)}) collective-permute-start(bf16[96,640]{1,0:T(8,128)(2,1)S(1)} %get-tuple-element.45.high), channel_id=1, source_target_pairs={{0,4},{1,5},{2,6},{3,7},{4,0},{5,1},{6,2},{7,3},{8,12},{9,13},{10,... | collective-permute-start | bytes 368648 | tf_op jit(solution)/shard_map/ppermute | solution.py:416
  18.4 0.0 collective-permute-done.7.k_low
  18.4 1.5 %collective-permute-start.8 = (bf16[88,640]{1,0:T(8,128)(2,1)S(1)}, bf16[88,640]{1,0:T(8,128)(2,1)S(1)}, u32[]{:S(2)}, u32[]{:S(2)}) collective-permute-start(bf16[88,640]{1,0:T(8,128)(2,1)S(1)} %get-tuple-element.48.k_high), channel_id=1, source_target_pairs={{0,1},{1,0},{2,3},{3,2},{4,5},{5,4},{6,7},{7,6},{8,9},{9,8},{10,11... | collective-permute-start | bytes 337928 | tf_op jit(solution)/shard_map/ppermute | solution.py:416
  19.9 1.7 %shard_map.88 = (f32[80,768]{1,0:T(8,128)S(1)}, f32[768,80]{1,0:T(8,128)S(1)}, f32[768,80]{1,0:T(8,128)S(1)}, bf16[768,80]{1,0:T(8,128)(2,1)S(1)}, bf16[768,80]{...) custom-call(bf16[96,640]{1,0:T(8,128)(2,1)S(1)} %get-tuple-element.42.low, ...), custom_call_target="tpu_custom_call" | custom-call | tf_op jit(solution)/shard_map/pallas_call | solution.py:116
  21.6 1.9 %collective-permute-done.8.k_high = bf16[88,640]{1,0:T(8,128)(2,1)S(1)} collective-permute-done((bf16[88,640]{1,0:T(8,128)(2,1)S(1)}, bf16[88,640]{1,0:T(8,128)(2,1)S(1)}, u32[]{:S(2)}, u32[]{:S(2)}) %collective-permute-start.8) | collective-permute-done | bytes 112672 | tf_op jit(solution)/shard_map/ppermute | solution.py:416
  23.5 1.6 %shard_map.89 = (f32[80,768]{1,0:T(8,128)S(1)}, f32[768,80]{1,0:T(8,128)S(1)}, f32[768,80]{1,0:T(8,128)S(1)}, bf16[768,80]{1,0:T(8,128)(2,1)S(1)}, bf16[768,80]{1,0:T(8,128)(2,1)S(1)}) custom-call(bf16[96,640]{1,0:T(8,128)(2,1)S(1)} %get-tuple-element.42.low, bf16[96,640]{1,0:T(8,128)(2,1)S(1)} %get-tuple-element.45.high, ...), custom_call_target="tpu_custom_call" | custom-call | tf_op jit(solution)/shard_map/pallas_call | solution.py:116
  25.1 1.9 %collective-permute-done.10.low = bf16[96,640]{1,0:T(8,128)(2,1)S(1)} collective-permute-done((bf16[96,640]{1,0:T(8,128)(2,1)S(1)}, bf16[96,640]{1,0:T(8,128)(2,1)S(1)}, u32[]{:S(2)}, u32[]{:S(2)}) %collective-permute-start.10) | collective-permute-done | bytes 122912 | tf_op jit(solution)/shard_map/ppermute | solution.py:416
  27.0 2.1 %shard_map.90 = (f32[80,384]{1,0:T(8,128)S(1)}, f32[768,80]{1,0:T(8,128)S(1)}, f32[768,80]{1,0:T(8,128)S(1)}, f32[768,80]{1,0:T(8,128)S(1)}, f32[768,80]{1,0:T(8,128)S(1)}) custom-call(bf16[96,640]{1,0:T(8,128)(2,1)S(1)} %collective-permute-done.10.low, bf16[768,80]{1,0:T(8,128)(2,1)S(1)} %get-tuple-element.54.k_far, ...), custom_call_target="tpu_custom_call" | custom-call | tf_op jit(solution)/shard_map/pallas_call | solution.py:116
  29.1 1.3 %shard_map.91 = (f32[80,384]{1,0:T(8,128)S(1)}, bf16[88,1280]{1,0:T(8,128)(2,1)S(1)}, bf16[384,80]{1,0:T(8,128)(2,1)S(1)}, bf16[384,80]{1,0:T(8,128)(2,1)S(1)}) custom-call(bf16[96,640]{1,0:T(8,128)(2,1)S(1)} %collective-permute-done.9.high, bf16[768,80]{1,0:T(8,128)(2,1)S(1)} %get-tuple-element.54.k_far, bf16[768,80]{1,0:T(8,128)(2,1)S(1)} %get-tuple-element.55.v_far, ...), custom_call_target="tpu_custom_call" | custom-call | tf_op jit(solution)/shard_map/pallas_call | solution.py:116
  30.5 1.2 %collective-permute-start.11 = (bf16[88,1280]{1,0:T(8,128)(2,1)S(1)}, bf16[88,1280]{1,0:T(8,128)(2,1)S(1)}, u32[]{:S(2)}, u32[]{:S(2)}) collective-permute-start(bf16[88,1280]{1,0:T(8,128)(2,1)S(1)} %get-tuple-element.72), channel_id=1, source_target_pairs={{0,1},{1,0},{2,3},{3,2},{4,5},{5,4},{6,7},{7,6},{8,9},{9,8},{10,11... | collective-permute-start | bytes 675848 | tf_op jit(solution)/shard_map/ppermute | solution.py:416
  31.7 1.4 %shard_map.92 = (bf16[88,640]{1,0:T(8,128)(2,1)S(1)}, f32[768,80]{1,0:T(8,128)S(1)}, f32[768,80]{1,0:T(8,128)S(1)}) custom-call(bf16[96,640]{1,0:T(8,128)(2,1)S(1)} %collective-permute-done.9.high, bf16[384,80]{1,0:T(8,128)(2,1)S(1)} %get-tuple-element.64.q_s, bf16[384,80]{1,0:T(8,128)(2,1)S(1)} %get-tuple-element.65.do_s, ...), custom_call_target="tpu_custom_call" | custom-call | tf_op jit(solution)/shard_map/pallas_call | solution.py:116
  33.0 0.2 collective-permute-start.12
  33.3 0.4 shard_map.93.own
  33.7 7.1 %collective-permute-done.12.dq_wire = bf16[88,640]{1,0:T(8,128)(2,1)S(1)} collective-permute-done((bf16[88,640]{1,0:T(8,128)(2,1)S(1)}, bf16[88,640]{1,0:T(8,128)(2,1)S(1)}, u32[]{:S(2)}, u32[]{:S(2)}) %collective-permute-start.12) | collective-permute-done | bytes 112672 | tf_op jit(solution)/shard_map/ppermute | solution.py:416
  40.8 0.2 shard_map.94
  41.1 0.1 collective-permute-start.15
  41.2 1.5 %collective-permute-start.14 = (bf16[88,512]{1,0:T(8,128)(2,1)S(1)}, bf16[88,512]{1,0:T(8,128)(2,1)S(1)}, u32[]{:S(2)}, u32[]{:S(2)}) collective-permute-start(bf16[88,512]{1,0:T(8,128)(2,1)S(1)} %get-tuple-element.78), channel_id=1, source_target_pairs={{0,16},{8,24},{16,0},{24,8},{1,17},{9,25},{17,1},{25,9},{2,18},{10... | collective-permute-start | bytes 270344 | tf_op jit(solution)/shard_map/ppermute | solution.py:414
  42.7 1.9 %collective-permute-start.13 = (bf16[88,512]{1,0:T(8,128)(2,1)S(1)}, bf16[88,512]{1,0:T(8,128)(2,1)S(1)}, u32[]{:S(2)}, u32[]{:S(2)}) collective-permute-start(bf16[88,512]{1,0:T(8,128)(2,1)S(1)} %get-tuple-element.79), channel_id=1, source_target_pairs={{0,2},{1,3},{2,0},{3,1},{4,6},{5,7},{6,4},{7,5},{8,10},{9,11},{10,... | collective-permute-start | bytes 270344 | tf_op jit(solution)/shard_map/ppermute | solution.py:416
  44.6 0.0 collective-permute-start.16
  44.6 2.9 %collective-permute-done.15.refs_3_ = bf16[88,512]{1,0:T(8,128)(2,1)S(1)} collective-permute-done((bf16[88,512]{1,0:T(8,128)(2,1)S(1)}, bf16[88,512]{1,0:T(8,128)(2,1)S(1)}, u32[]{:S(2)}, u32[]{:S(2)}) %collective-permute-start.15) | collective-permute-done | bytes 90144 | tf_op jit(solution)/shard_map/ppermute | solution.py:418
  47.5 0.0 collective-permute-start.19
  47.6 0.5 %collective-permute-start.18 = (bf16[88,256]{1,0:T(8,128)(2,1)S(1)}, bf16[88,256]{1,0:T(8,128)(2,1)S(1)}, u32[]{:S(2)}, u32[]{:S(2)}) collective-permute-start(bf16[88,256]{1,0:T(8,128)(2,1)S(1)} %slice.57), channel_id=1, source_target_pairs={{0,8},{8,0},{16,24},{24,16},{1,9},{9,1},{17,25},{25,17},{2,10},{10... | collective-permute-start | bytes 135176 | tf_op jit(solution)/shard_map/ppermute | solution.py:414
  48.1 0.2 collective-permute-done.13.refs_1_
  48.3 0.0 collective-permute-done.16.refs_4_
  48.3 0.5 collective-permute-done.19.refs_7_
  48.8 0.2 collective-permute-done.18.refs_6_
  49.0 0.5 %collective-permute-done.17.refs_5_ = bf16[88,256]{1,0:T(8,128)(2,1)S(1)} collective-permute-done((bf16[88,256]{1,0:T(8,128)(2,1)S(1)}, bf16[88,256]{1,0:T(8,128)(2,1)S(1)}, u32[]{:S(2)}, u32[]{:S(2)}) %collective-permute-start.17) | collective-permute-done | bytes 45088 | tf_op jit(solution)/shard_map/ppermute | solution.py:414
  49.5 0.9 %shard_map.95 = (bf16[88,640]{1,0:T(8,128)(2,1)}, bf16[88,640]{1,0:T(8,128)(2,1)}, bf16[88,640]{1,0:T(8,128)(2,1)}) custom-call(bf16[88,512]{1,0:T(8,128)(2,1)S(1)} %get-tuple-element.80.refs_0_, bf16[88,512]{1,0:T(8,128)(2,1)S(1)} %collective-permute-done.13.refs_1_, bf16[88,512]{1,0:T(8,128)(2,1)S(1)} %collective-permute-done.14.refs_2_, ...), custom_call_target="tpu_custom_call" | custom-call | tf_op jit(solution)/shard_map/pallas_call | solution.py:116
  (16 shorter events, 0.1 us)
Async XLA Ops:
  3.2 7.1 %collective-permute-start = (bf16[96,640]{1,0:T(8,128)(2,1)}, bf16[96,640]{1,0:T(8,128)(2,1)S(1)}, u32[]{:S(2)}, u32[]{:S(2)}) collective-permute-start(bf16[96,640]{1,0:T(8,128)(2,1)} %get-tuple-element.41), channel_id=1, source_target_pairs={{0,2},{1,3},{2,0},{3,1},{4,6},{5,7},{6,4},{7,5},{8,10},{9,11},{10,... | collective-permute-start | bytes 368648 | tf_op jit(solution)/shard_map/ppermute | solution.py:416
  6.3 7.7 %collective-permute-start.3 = (bf16[96,640]{1,0:T(8,128)(2,1)}, bf16[96,640]{1,0:T(8,128)(2,1)S(1)}, u32[]{:S(2)}, u32[]{:S(2)}) collective-permute-start(bf16[96,640]{1,0:T(8,128)(2,1)} %get-tuple-element.43), channel_id=1, source_target_pairs={{0,16},{8,24},{16,0},{24,8},{1,17},{9,25},{17,1},{25,9},{2,18},{10... | collective-permute-start | bytes 368648 | tf_op jit(solution)/shard_map/ppermute | solution.py:414
  7.7 6.3 %collective-permute-start.4 = (bf16[96,640]{1,0:T(8,128)(2,1)}, bf16[96,640]{1,0:T(8,128)(2,1)S(1)}, u32[]{:S(2)}, u32[]{:S(2)}) collective-permute-start(bf16[96,640]{1,0:T(8,128)(2,1)} %get-tuple-element.44), channel_id=1, source_target_pairs={{0,18},{1,19},{2,16},{3,17},{4,22},{5,23},{6,20},{7,21},{8,26},{9,... | collective-permute-start | bytes 368648 | tf_op jit(solution)/shard_map/ppermute | solution.py:418
  7.8 3.8 %copy-start = (bf16[96,640]{1,0:T(8,128)(2,1)S(1)}, bf16[96,640]{1,0:T(8,128)(2,1)}, u32[]{:S(2)}) copy-start(bf16[96,640]{1,0:T(8,128)(2,1)} %get-tuple-element.40.block_a) | copy-start | bytes 368644
  8.8 2.9 %copy-start.1 = (f32[1,2,352]{2,1,0:T(2,128)S(1)}, f32[1,2,352]{2,1,0:T(2,128)}, u32[]{:S(2)}) copy-start(f32[1,2,352]{2,1,0:T(2,128)} %param.11) | copy-start | bytes 8452
  8.8 1.6 %collective-permute-start.1 = (bf16[96,384]{1,0:T(8,128)(2,1)S(1)}, bf16[96,384]{1,0:T(8,128)(2,1)S(1)}, u32[]{:S(2)}, u32[]{:S(2)}) collective-permute-start(bf16[96,384]{1,0:T(8,128)(2,1)S(1)} %slice.36), channel_id=1, source_target_pairs={{0,8},{8,0},{16,24},{24,16},{1,9},{9,1},{17,25},{25,17},{2,10},{10... | collective-permute-start | bytes 221192 | tf_op jit(solution)/shard_map/ppermute | solution.py:414
  10.3 1.3 %collective-permute-start.2 = (bf16[96,384]{1,0:T(8,128)(2,1)S(1)}, bf16[96,384]{1,0:T(8,128)(2,1)S(1)}, u32[]{:S(2)}, u32[]{:S(2)}) collective-permute-start(bf16[96,384]{1,0:T(8,128)(2,1)S(1)} %slice.48), channel_id=1, source_target_pairs={{0,8},{8,0},{16,24},{24,16},{1,9},{9,1},{17,25},{25,17},{2,10},{10... | collective-permute-start | bytes 221192 | tf_op jit(solution)/shard_map/ppermute | solution.py:414
  11.8 6.6 %collective-permute-start.7 = (bf16[88,640]{1,0:T(8,128)(2,1)S(1)}, bf16[88,640]{1,0:T(8,128)(2,1)S(1)}, u32[]{:S(2)}, u32[]{:S(2)}) collective-permute-start(bf16[88,640]{1,0:T(8,128)(2,1)S(1)} %get-tuple-element.46.k_low), channel_id=1, source_target_pairs={{0,1},{1,0},{2,3},{3,2},{4,5},{5,4},{6,7},{7,6},{8,9},{9,8},{10,11... | collective-permute-start | bytes 337928 | tf_op jit(solution)/shard_map/ppermute | solution.py:416
  14.0 3.2 %collective-permute-start.5 = (bf16[96,384]{1,0:T(8,128)(2,1)S(1)}, bf16[96,384]{1,0:T(8,128)(2,1)S(1)}, u32[]{:S(2)}, u32[]{:S(2)}) collective-permute-start(bf16[96,384]{1,0:T(8,128)(2,1)S(1)} %slice.49), channel_id=1, source_target_pairs={{0,8},{8,0},{16,24},{24,16},{1,9},{9,1},{17,25},{25,17},{2,10},{10... | collective-permute-start | bytes 221192 | tf_op jit(solution)/shard_map/ppermute | solution.py:414
  14.1 3.1 %collective-permute-start.6 = (bf16[96,384]{1,0:T(8,128)(2,1)S(1)}, bf16[96,384]{1,0:T(8,128)(2,1)S(1)}, u32[]{:S(2)}, u32[]{:S(2)}) collective-permute-start(bf16[96,384]{1,0:T(8,128)(2,1)S(1)} %slice.50), channel_id=1, source_target_pairs={{0,8},{8,0},{16,24},{24,16},{1,9},{9,1},{17,25},{25,17},{2,10},{10... | collective-permute-start | bytes 221192 | tf_op jit(solution)/shard_map/ppermute | solution.py:414
  14.7 12.3 %collective-permute-start.10 = (bf16[96,640]{1,0:T(8,128)(2,1)S(1)}, bf16[96,640]{1,0:T(8,128)(2,1)S(1)}, u32[]{:S(2)}, u32[]{:S(2)}) collective-permute-start(bf16[96,640]{1,0:T(8,128)(2,1)S(1)} %get-tuple-element.42.low), channel_id=1, source_target_pairs={{0,4},{1,5},{2,6},{3,7},{4,0},{5,1},{6,2},{7,3},{8,12},{9,13},{10,... | collective-permute-start | bytes 368648 | tf_op jit(solution)/shard_map/ppermute | solution.py:416
  17.4 11.7 %collective-permute-start.9 = (bf16[96,640]{1,0:T(8,128)(2,1)S(1)}, bf16[96,640]{1,0:T(8,128)(2,1)S(1)}, u32[]{:S(2)}, u32[]{:S(2)}) collective-permute-start(bf16[96,640]{1,0:T(8,128)(2,1)S(1)} %get-tuple-element.45.high), channel_id=1, source_target_pairs={{0,4},{1,5},{2,6},{3,7},{4,0},{5,1},{6,2},{7,3},{8,12},{9,13},{10,... | collective-permute-start | bytes 368648 | tf_op jit(solution)/shard_map/ppermute | solution.py:416
  18.4 5.1 %collective-permute-start.8 = (bf16[88,640]{1,0:T(8,128)(2,1)S(1)}, bf16[88,640]{1,0:T(8,128)(2,1)S(1)}, u32[]{:S(2)}, u32[]{:S(2)}) collective-permute-start(bf16[88,640]{1,0:T(8,128)(2,1)S(1)} %get-tuple-element.48.k_high), channel_id=1, source_target_pairs={{0,1},{1,0},{2,3},{3,2},{4,5},{5,4},{6,7},{7,6},{8,9},{9,8},{10,11... | collective-permute-start | bytes 337928 | tf_op jit(solution)/shard_map/ppermute | solution.py:416
  30.5 10.3 %collective-permute-start.11 = (bf16[88,1280]{1,0:T(8,128)(2,1)S(1)}, bf16[88,1280]{1,0:T(8,128)(2,1)S(1)}, u32[]{:S(2)}, u32[]{:S(2)}) collective-permute-start(bf16[88,1280]{1,0:T(8,128)(2,1)S(1)} %get-tuple-element.72), channel_id=1, source_target_pairs={{0,1},{1,0},{2,3},{3,2},{4,5},{5,4},{6,7},{7,6},{8,9},{9,8},{10,11... | collective-permute-start | bytes 675848 | tf_op jit(solution)/shard_map/ppermute | solution.py:416
  33.0 7.8 %collective-permute-start.12 = (bf16[88,640]{1,0:T(8,128)(2,1)S(1)}, bf16[88,640]{1,0:T(8,128)(2,1)S(1)}, u32[]{:S(2)}, u32[]{:S(2)}) collective-permute-start(bf16[88,640]{1,0:T(8,128)(2,1)S(1)} %get-tuple-element.73), channel_id=1, source_target_pairs={{0,4},{1,5},{2,6},{3,7},{4,0},{5,1},{6,2},{7,3},{8,12},{9,13},{10,... | collective-permute-start | bytes 337928 | tf_op jit(solution)/shard_map/ppermute | solution.py:416
  41.1 6.5 %collective-permute-start.15 = (bf16[88,512]{1,0:T(8,128)(2,1)S(1)}, bf16[88,512]{1,0:T(8,128)(2,1)S(1)}, u32[]{:S(2)}, u32[]{:S(2)}) collective-permute-start(bf16[88,512]{1,0:T(8,128)(2,1)S(1)} %get-tuple-element.77), channel_id=1, source_target_pairs={{0,18},{1,19},{2,16},{3,17},{4,22},{5,23},{6,20},{7,21},{8,26},{9,... | collective-permute-start | bytes 270344 | tf_op jit(solution)/shard_map/ppermute | solution.py:418
  41.2 6.4 %collective-permute-start.14 = (bf16[88,512]{1,0:T(8,128)(2,1)S(1)}, bf16[88,512]{1,0:T(8,128)(2,1)S(1)}, u32[]{:S(2)}, u32[]{:S(2)}) collective-permute-start(bf16[88,512]{1,0:T(8,128)(2,1)S(1)} %get-tuple-element.78), channel_id=1, source_target_pairs={{0,16},{8,24},{16,0},{24,8},{1,17},{9,25},{17,1},{25,9},{2,18},{10... | collective-permute-start | bytes 270344 | tf_op jit(solution)/shard_map/ppermute | solution.py:414
  42.7 5.6 %collective-permute-start.13 = (bf16[88,512]{1,0:T(8,128)(2,1)S(1)}, bf16[88,512]{1,0:T(8,128)(2,1)S(1)}, u32[]{:S(2)}, u32[]{:S(2)}) collective-permute-start(bf16[88,512]{1,0:T(8,128)(2,1)S(1)} %get-tuple-element.79), channel_id=1, source_target_pairs={{0,2},{1,3},{2,0},{3,1},{4,6},{5,7},{6,4},{7,5},{8,10},{9,11},{10,... | collective-permute-start | bytes 270344 | tf_op jit(solution)/shard_map/ppermute | solution.py:416
  44.6 3.7 %collective-permute-start.16 = (bf16[88,256]{1,0:T(8,128)(2,1)S(1)}, bf16[88,256]{1,0:T(8,128)(2,1)S(1)}, u32[]{:S(2)}, u32[]{:S(2)}) collective-permute-start(bf16[88,256]{1,0:T(8,128)(2,1)S(1)} %slice.55), channel_id=1, source_target_pairs={{0,8},{8,0},{16,24},{24,16},{1,9},{9,1},{17,25},{25,17},{2,10},{10... | collective-permute-start | bytes 135176 | tf_op jit(solution)/shard_map/ppermute | solution.py:414
  47.5 1.2 %collective-permute-start.19 = (bf16[88,256]{1,0:T(8,128)(2,1)S(1)}, bf16[88,256]{1,0:T(8,128)(2,1)S(1)}, u32[]{:S(2)}, u32[]{:S(2)}) collective-permute-start(bf16[88,256]{1,0:T(8,128)(2,1)S(1)} %slice.58), channel_id=1, source_target_pairs={{0,8},{8,0},{16,24},{24,16},{1,9},{9,1},{17,25},{25,17},{2,10},{10... | collective-permute-start | bytes 135176 | tf_op jit(solution)/shard_map/ppermute | solution.py:414
  47.6 1.4 %collective-permute-start.18 = (bf16[88,256]{1,0:T(8,128)(2,1)S(1)}, bf16[88,256]{1,0:T(8,128)(2,1)S(1)}, u32[]{:S(2)}, u32[]{:S(2)}) collective-permute-start(bf16[88,256]{1,0:T(8,128)(2,1)S(1)} %slice.57), channel_id=1, source_target_pairs={{0,8},{8,0},{16,24},{24,16},{1,9},{9,1},{17,25},{25,17},{2,10},{10... | collective-permute-start | bytes 135176 | tf_op jit(solution)/shard_map/ppermute | solution.py:414
  48.3 1.2 %collective-permute-start.17 = (bf16[88,256]{1,0:T(8,128)(2,1)S(1)}, bf16[88,256]{1,0:T(8,128)(2,1)S(1)}, u32[]{:S(2)}, u32[]{:S(2)}) collective-permute-start(bf16[88,256]{1,0:T(8,128)(2,1)S(1)} %slice.56), channel_id=1, source_target_pairs={{0,8},{8,0},{16,24},{24,16},{1,9},{9,1},{17,25},{25,17},{2,10},{10... | collective-permute-start | bytes 135176 | tf_op jit(solution)/shard_map/ppermute | solution.py:414

commit v5 on v4

--- a/solution.py
+++ b/solution.py
@@ -12,6 +12,8 @@
 SCALING = HDIM ** (-0.5)
 LOG2E = math.log2(math.e)
 PADDED = 96
+LOW = 3
+LOW_KEYS = 3
 VMEM_LIMIT = 24 * 1024 * 1024
 F32 = jnp.float32
 BF16 = jnp.bfloat16
@@ -228,38 +230,50 @@
         copy.wait()
 
 
-def gather_kernel(first, block_a, block_b, other_a, other_b, near1, lse_in, queries, keys, lse_s):
-    rows = keys.shape[0]
+def gather_queries_kernel(spots, *refs):
+    *parts, near1, lse_in, wire, lse_s = refs
+    rows = PADDED - 8
     _, w, _, h = place()
-    lse_own = lse_in[pl.ds(w, 1), :] * LOG2E
+    own = lse_in[pl.ds(w, 1), :] * LOG2E
     below = near1[rows:PADDED, :].astype(F32)
-    lse_near = below[0:4, 128 : 128 + rows] + below[4:8, 128 : 128 + rows]
-    lse_near = lse_near + below[0:4, 384 : 384 + rows]
+    near = below[0:4, 128 : 128 + rows] + below[4:8, 128 : 128 + rows]
+    near = near + below[0:4, 384 : 384 + rows]
     lse_s[...] = jnp.concatenate(
-        [lse_own[:, rows * i : rows * (i + 1)] for i in range(4)] + [lse_near], axis=0
-    )
-    q_parts, k_parts, spots = [], [], []
+        [own[:, rows * i : rows * (i + 1)] for i in range(4)] + [near], axis=0
+    )
+    lower = []
     gap = jnp.zeros((6, PADDED - rows), F32)
-    for j in (first, first + 1):
-        for r in range(2):
-            held = ((block_a, block_b), (other_a, other_b))[r][j % 2]
-            deep = (512, 320)[r]
-            q_parts.append(held[0:rows, 0:160])
-            k_parts += [held[0:rows, 160:256], held[0:rows, deep : deep + 64]]
-            delta = held[rows:PADDED, 0:128].astype(F32)[0:3, 0:rows]
-            lse = lse_s[pl.ds(4 * (j % 2) + (h ^ (2 * (j // 2) + r)), 1), :]
-            spots += [jnp.concatenate([delta, pieces_of(lse)], axis=0), gap]
-    keys[...] = jnp.concatenate(k_parts, axis=1)
-    queries[0:rows] = jnp.concatenate(q_parts, axis=1)
-    below = jnp.concatenate(spots + [jnp.zeros((6, 256), F32)], axis=1)
-    below = jnp.concatenate([below, jnp.zeros((2, 640), F32)], axis=0)
-    queries[rows:PADDED] = below.astype(BF16)
+    for (j, r), ref in zip(spots, parts):
+        delta = ref[rows:PADDED, 0:128].astype(F32)[0:3, 0:rows]
+        lse = lse_s[pl.ds(4 * (j % 2) + (h ^ (2 * (j // 2) + r)), 1), :]
+        lower += [jnp.concatenate([delta, pieces_of(lse)], axis=0), gap]
+    wire[0:rows] = jnp.concatenate([ref[0:rows, 0:160] for ref in parts], axis=1)
+    width = wire.shape[1] - len(parts) * PADDED
+    lower = jnp.concatenate(lower + [jnp.zeros((6, width), F32)], axis=1)
+    lower = jnp.concatenate([lower, jnp.zeros((2, wire.shape[1]), F32)], axis=0)
+    wire[rows:PADDED] = lower.astype(BF16)
+
+
+def gather_keys_kernel(spots, *refs):
+    *parts, keys = refs
+    rows = PADDED - 8
+    pieces = []
+    for (_, r), ref in zip(spots, parts):
+        deep = 320 if r else 512
+        pieces += [ref[0:rows, 160:256], ref[0:rows, deep : deep + 64]]
+    keys[0:rows] = jnp.concatenate(pieces, axis=1)
+    if keys.shape[0] > rows:
+        keys[rows:PADDED] = jnp.zeros((PADDED - rows, keys.shape[1]), BF16)
 
 
 def rows_of(wires):
     rows = PADDED - 8
     below = jnp.concatenate(
-        [wire[rows:PADDED, 0 : 4 * PADDED].astype(F32) for wire in wires], axis=1
+        [
+            wire[rows:PADDED, 0 : wire.shape[1] // (2 * HDIM) * PADDED].astype(F32)
+            for wire in wires
+        ],
+        axis=1,
     )
     return below[3:4] + below[4:5] + below[5:6], below[0:1] + below[1:2] + below[2:3]
 
@@ -304,18 +318,18 @@
 
 def own_own_kernel(low, high, k_low, k_high, dq_t, dk, dv, q_s, do_s, k_s, v_s):
     spread(low, q_s, do_s)
-    spread(high, q_s, do_s, 4)
+    spread(high, q_s, do_s, LOW)
     spread(k_low, k_s, v_s)
-    spread(k_high, k_s, v_s, 4)
+    spread(k_high, k_s, v_s, LOW_KEYS)
     dq_t[...], parts = tile_step(q_s[...], do_s[...], k_s, v_s, *rows_of([low, high]))
     for spot, dk_part, dv_part in parts:
         dk[spot, :] = dk_part
         dv[spot, :] = dv_part
 
 
-def own_far_kernel(low, high, q_s, do_s, k_low, k_high, dq_before, dq_t, dk, dv, k_s, v_s):
+def own_far_kernel(after, low, high, q_s, do_s, k_low, k_high, dq_before, dq_t, dk, dv, k_s, v_s):
     spread(k_low, k_s, v_s)
-    spread(k_high, k_s, v_s, 4)
+    spread(k_high, k_s, v_s, LOW_KEYS)
     more, parts = tile_step(q_s[...], do_s[...], k_s, v_s, *rows_of([low, high]))
     dq_t[...] = dq_before[...] + more
     for spot, dk_part, dv_part in parts:
@@ -323,24 +337,20 @@
         dv[spot, :] = dv_part
 
 
-def low_kernel(
-    low, k_far, v_far, k_own, v_own, dk_far_in, dv_far_in, dk_own_in, dv_own_in,
-    dq_t, dk_far, dv_far, dk_own, dv_own, q_s, do_s,
-):
-    spread(low, q_s, do_s)
-    q, do = q_s[...], do_s[...]
-    lse, delta = rows_of([low])
-    total = None
-    for k_s, v_s, dk_in, dv_in, dk, dv in (
-        (k_far, v_far, dk_far_in, dv_far_in, dk_far, dv_far),
-        (k_own, v_own, dk_own_in, dv_own_in, dk_own, dv_own),
-    ):
-        more, parts = tile_step(q, do, k_s, v_s, lse, delta)
-        total = more if total is None else total + more
-        for spot, dk_part, dv_part in parts:
-            dk[spot, :] = dk_in[spot, :] + dk_part
-            dv[spot, :] = dv_in[spot, :] + dv_part
-    dq_t[...] = total
+def low_own_kernel(wire, k_own, v_own, dk_in, dv_in, dq_t, dk, dv, q_s, do_s):
+    spread(wire, q_s, do_s)
+    dq_t[...], parts = tile_step(q_s[...], do_s[...], k_own, v_own, *rows_of([wire]))
+    for spot, dk_part, dv_part in parts:
+        dk[spot, :] = dk_in[spot, :] + dk_part
+        dv[spot, :] = dv_in[spot, :] + dv_part
+
+
+def low_far_kernel(wire, q_s, do_s, k_far, v_far, dq_before, dk_in, dv_in, dq_t, dk, dv):
+    more, parts = tile_step(q_s[...], do_s[...], k_far, v_far, *rows_of([wire]))
+    dq_t[...] = dq_before[...] + more
+    for spot, dk_part, dv_part in parts:
+        dk[spot, :] = dk_in[spot, :] + dk_part
+        dv[spot, :] = dv_in[spot, :] + dv_part
 
 
 def high_far_kernel(high, k_far, v_far, dk_in, dv_in, dq_t, wire, q_s, do_s, dk, dv):
@@ -425,7 +435,7 @@
 def grid_body(queries, keys, values, outputs, grad_out, lse):
     rows = queries.shape[1]
     padded = 8 * PADDED
-    half = padded // 2
+    few = LOW * PADDED
 
     packed = call(
         pack_inputs_kernel,
@@ -441,21 +451,30 @@
     own = packed[0]
     near = to_chips(packed)
     other = [flipped(a[:, 256:], 1, 0) for a in [own] + near]
-    blocks = [own] + near
-
-    def gather(first):
+    blocks = [ref for pair in zip([own] + near, other) for ref in pair]
+    spots = [(j, r) for j in range(4) for r in range(2)]
+
+    def gather_queries(first, last):
         return call(
-            functools.partial(gather_kernel, first),
-            (shape(PADDED, 640), shape(rows, 640)),
-            *blocks[first : first + 2], *other[first : first + 2], near[0], lse[0],
+            functools.partial(gather_queries_kernel, spots[first:last]),
+            shape(PADDED, 160 * (last - first)),
+            *blocks[first:last], near[0], lse[0],
             scratch=[pltpu.VMEM((8, rows), F32)],
         )
 
-    low, k_low = gather(0)
+    def gather_keys(first, last, tall):
+        return call(
+            functools.partial(gather_keys_kernel, spots[first:last]),
+            shape(tall, 160 * (last - first)),
+            *blocks[first:last],
+        )
+
+    low, k_low = gather_queries(0, LOW), gather_keys(0, LOW_KEYS, PADDED)
     low_far, k_low_far = flipped(low, 0, 4), flipped(k_low, 0, 1)
-    high, k_high = gather(2)
-    k_high, k_low_far = lax.optimization_barrier((k_high, k_low_far))
-    high_far, k_high_far = flipped(high, 0, 4), flipped(k_high, 0, 1)
+    high, k_high = gather_queries(LOW, 8), gather_keys(LOW_KEYS, 8, rows)
+    high_far = flipped(high, 0, 4)
+    k_high, k_low_far, low_far = lax.optimization_barrier((k_high, k_low_far, low_far))
+    k_high_far = flipped(k_high, 0, 1)
     keys_far = [k_low_far, k_high_far]
 
     grad = shape(padded, HDIM, dtype=F32)
@@ -464,18 +483,23 @@
     dq_own, dk_own, dv_own, q_s, do_s, k_own, v_own = call(
         own_own_kernel, (dq_shape, grad, grad, side, side, side, side), low, high, k_low, k_high
     )
+    some = shape(few, HDIM)
+    dq_low, dk_own, dv_own, q_low_s, do_low_s = call(
+        low_own_kernel, (shape(HDIM, few, dtype=F32), grad, grad, some, some),
+        low_far, k_own, v_own, dk_own, dv_own,
+    )
     dq_own, dk_far, dv_far, k_far, v_far = call(
-        own_far_kernel, (dq_shape, grad, grad, side, side), low, high, q_s, do_s, *keys_far, dq_own
-    )
-    dq_low, dk_far, dv_far, dk_own, dv_own = call(
-        low_kernel, (shape(HDIM, half, dtype=F32), grad, grad, grad, grad),
-        low_far, k_far, v_far, k_own, v_own, dk_far, dv_far, dk_own, dv_own,
-        scratch=[pltpu.VMEM((half, HDIM), BF16)] * 2,
-    )
-    few = shape(half, HDIM)
+        own_far_kernel, (dq_shape, grad, grad, side, side),
+        dq_low, low, high, q_s, do_s, *keys_far, dq_own,
+    )
+    dq_low, dk_far, dv_far = call(
+        low_far_kernel, (shape(HDIM, few, dtype=F32), grad, grad),
+        low_far, q_low_s, do_low_s, k_far, v_far, dq_low, dk_far, dv_far,
+    )
+    most = shape(padded - few, HDIM)
     dq_high, dkv_wire, q_s, do_s = call(
         high_far_kernel,
-        (shape(HDIM, half, dtype=F32), shape(rows, 1280), few, few),
+        (shape(HDIM, padded - few, dtype=F32), shape(rows, 1280), most, most),
         high_far, k_far, v_far, dk_far, dv_far,
         scratch=[pltpu.VMEM((padded, HDIM), F32)] * 2,
     )

time: 50.6 us -> 48.9 us (0.966)
  waiting for transfers between devices: 18.5 us -> 16.2 us
  Pallas kernels: 12.5 us -> 13.2 us
    ppermute x2, starting transfers between devices: 0.12 us -> 2.05 us  [flipped(): lax.ppermute(array, ('head', 'blk'), [(i, i ^ bits) for i in range(heads...]
    ppermute x8, waiting for transfers between devices: 12.5 us -> 10.6 us  [flipped(): return lax.ppermute(array, 'blk', [(i, i ^ blk_bits) for i in range(blks)])]
    ppermute x2, waiting for transfers between devices: 2.89 us -> 1.31 us  [flipped(): lax.ppermute(array, ('head', 'blk'), [(i, i ^ bits) for i in range(heads...]
    ppermute x8, starting transfers between devices: 13.1 us -> 11.7 us  [flipped(): return lax.ppermute(array, 'blk', [(i, i ^ blk_bits) for i in range(blks)])]
    ppermute x10, waiting for transfers between devices: 3.05 us -> 4.23 us  [flipped(): lax.ppermute(array, 'head', [(i, i ^ head_bits) for i in range(heads)])]
    pallas_call x11 -> x14, Pallas kernels: 12.5 us -> 13.2 us  [call(): pl.pallas_call(kernel, out_shape=out_shape, in_specs=specs, out_specs=jax...]
    ppermute x10, starting transfers between devices: 4.35 us -> 3.72 us  [flipped(): lax.ppermute(array, 'head', [(i, i ^ head_bits) for i in range(heads)])]
  transfers between devices with their start and end apart: 20 -> 20, of which waited for: 11 -> 12; matrix products, arithmetic and copies ran while one was open for 2% -> 2% of each run, Pallas kernels for 15% -> 17%
where the time goes in v5:
time: 48.9 us; the launch traced here: 48.7 us
  starting transfers between devices  17.5 us (36%)
  waiting for transfers between devices  16.2 us (33%)
  Pallas kernels  13.2 us (27%)
  local copies, waits for them, and re-layouts  0.98 us (2%)
  between operations  0.84 us (2%)
    pallas_call x14, Pallas kernels, call(): pl.pallas_call(kernel, out_shape=out_shape, in_specs=specs, out_specs=jax...  13.2 us
    ppermute x8, starting transfers between devices, flipped(): return lax.ppermute(array, 'blk', [(i, i ^ blk_bits) for i in range(blks)])  11.7 us
    ppermute x8, waiting for transfers between devices, flipped(): return lax.ppermute(array, 'blk', [(i, i ^ blk_bits) for i in range(blks)])  10.6 us
    ppermute x10, waiting for transfers between devices, flipped(): lax.ppermute(array, 'head', [(i, i ^ head_bits) for i in range(heads)])  4.23 us
    ppermute x10, starting transfers between devices, flipped(): lax.ppermute(array, 'head', [(i, i ^ head_bits) for i in range(heads)])  3.72 us
    ppermute x2, starting transfers between devices, flipped(): lax.ppermute(array, ('head', 'blk'), [(i, i ^ bits) for i in range(heads...  2.05 us
    ppermute x2, waiting for transfers between devices, flipped(): lax.ppermute(array, ('head', 'blk'), [(i, i ^ bits) for i in range(heads...  1.31 us
  transfers between devices with their start and end apart: 20, of which 12 were waited for; matrix products, arithmetic and copies ran while one was open for 2% of the time, Pallas kernels for 17%

profile of v5, /device:TPU:0, one launch (start us, length us, event | category | flops | bytes accessed | tf_op | source)
XLA Modules:
  0.0 48.7 jit_solution(14022618329330850744)
XLA Ops:
  0.6 2.5 %shard_map.85 = (bf16[96,640]{1,0:T(8,128)(2,1)}, bf16[96,640]{1,0:T(8,128)(2,1)}, bf16[96,640]{1,0:T(8,128)(2,1)}, bf16[96,640]{1,0:T(8,128)(2,1)}) custom-call(bf16[88,640]{1,0:T(8,128)(2,1)} %bitcast.20, bf16[88,640]{1,0:T(8,128)(2,1)} %bitcast.21, bf16[88,640]{1,0:T(8,128)(2,1)} %bitcast.22, bf16[88,640]{1,0:T(8,128)(2,1)} %bitcast.23, ...), custom_call_target="tpu_custom_call" | custom-call | tf_op jit(solution)/shard_map/pallas_call | solution.py:118
  3.2 3.1 %collective-permute-start = (bf16[96,640]{1,0:T(8,128)(2,1)}, bf16[96,640]{1,0:T(8,128)(2,1)S(1)}, u32[]{:S(2)}, u32[]{:S(2)}) collective-permute-start(bf16[96,640]{1,0:T(8,128)(2,1)} %get-tuple-element.40), channel_id=1, source_target_pairs={{0,2},{1,3},{2,0},{3,1},{4,6},{5,7},{6,4},{7,5},{8,10},{9,11},{10,... | collective-permute-start | bytes 368648 | tf_op jit(solution)/shard_map/ppermute | solution.py:426
  6.3 1.5 %collective-permute-start.2 = (bf16[96,640]{1,0:T(8,128)(2,1)}, bf16[96,640]{1,0:T(8,128)(2,1)S(1)}, u32[]{:S(2)}, u32[]{:S(2)}) collective-permute-start(bf16[96,640]{1,0:T(8,128)(2,1)} %get-tuple-element.41), channel_id=1, source_target_pairs={{0,16},{8,24},{16,0},{24,8},{1,17},{9,25},{17,1},{25,9},{2,18},{10... | collective-permute-start | bytes 368648 | tf_op jit(solution)/shard_map/ppermute | solution.py:424
  7.8 0.0 collective-permute-start.4
  7.8 0.9 %slice.39 = bf16[96,384]{1,0:T(8,128)(2,1)S(1)} slice(bf16[96,640]{1,0:T(8,128)(2,1)} %get-tuple-element.43.refs_0_), slice={[0:96], [256:640]} | slice | bytes 147456 | tf_op jit(solution)/shard_map/slice | solution.py:453
  8.7 1.3 %collective-permute-done.6.refs_1_ = bf16[96,384]{1,0:T(8,128)(2,1)S(1)} collective-permute-done((bf16[96,384]{1,0:T(8,128)(2,1)S(1)}, bf16[96,384]{1,0:T(8,128)(2,1)S(1)}, u32[]{:S(2)}, u32[]{:S(2)}) %collective-permute-start.6) | collective-permute-done | bytes 73760 | tf_op jit(solution)/shard_map/ppermute | solution.py:424
  10.0 0.3 collective-permute-done.refs_2_.refs_3_.refs_5_
  10.3 0.2 shard_map.88.low
  10.5 2.7 %collective-permute-start.8 = (bf16[96,480]{1,0:T(8,128)(2,1)S(1)}, bf16[96,480]{1,0:T(8,128)(2,1)S(1)}, u32[]{:S(2)}, u32[]{:S(2)}) collective-permute-start(bf16[96,480]{1,0:T(8,128)(2,1)S(1)} %shard_map.88.low), channel_id=1, source_target_pairs={{0,4},{1,5},{2,6},{3,7},{4,0},{5,1},{6,2},{7,3},{8,12},{9,13},{10,... | collective-permute-start | bytes 276488 | tf_op jit(solution)/shard_map/ppermute | solution.py:426
  13.2 0.1 shard_map.87.k_low
  13.3 1.6 %collective-permute-start.7 = (bf16[96,480]{1,0:T(8,128)(2,1)S(1)}, bf16[96,480]{1,0:T(8,128)(2,1)S(1)}, u32[]{:S(2)}, u32[]{:S(2)}) collective-permute-start(bf16[96,480]{1,0:T(8,128)(2,1)S(1)} %shard_map.87.k_low), channel_id=1, source_target_pairs={{0,1},{1,0},{2,3},{3,2},{4,5},{5,4},{6,7},{7,6},{8,9},{9,8},{10,11... | collective-permute-start | bytes 276488 | tf_op jit(solution)/shard_map/ppermute | solution.py:426
  14.9 0.1 collective-permute-start.1
  14.9 0.0 collective-permute-done.2.refs_1_
  15.0 0.6 %collective-permute-start.3 = (bf16[96,384]{1,0:T(8,128)(2,1)S(1)}, bf16[96,384]{1,0:T(8,128)(2,1)S(1)}, u32[]{:S(2)}, u32[]{:S(2)}) collective-permute-start(bf16[96,384]{1,0:T(8,128)(2,1)S(1)} %slice.49), channel_id=1, source_target_pairs={{0,8},{8,0},{16,24},{24,16},{1,9},{9,1},{17,25},{25,17},{2,10},{10... | collective-permute-start | bytes 221192 | tf_op jit(solution)/shard_map/ppermute | solution.py:424
  15.5 0.0 collective-permute-done.4.refs_3_
  15.5 0.1 collective-permute-start.5
  15.6 0.6 %collective-permute-done.1.refs_0_ = bf16[96,384]{1,0:T(8,128)(2,1)S(1)} collective-permute-done((bf16[96,384]{1,0:T(8,128)(2,1)S(1)}, bf16[96,384]{1,0:T(8,128)(2,1)S(1)}, u32[]{:S(2)}, u32[]{:S(2)}) %collective-permute-start.1) | collective-permute-done | bytes 73760 | tf_op jit(solution)/shard_map/ppermute | solution.py:424
  16.2 0.2 collective-permute-done.3.refs_2_
  16.4 0.4 collective-permute-done.5.refs_4_
  16.9 0.2 shard_map.89.high
  17.0 1.3 %collective-permute-start.10 = (bf16[96,800]{1,0:T(8,128)(2,1)S(1)}, bf16[96,800]{1,0:T(8,128)(2,1)S(1)}, u32[]{:S(2)}, u32[]{:S(2)}) collective-permute-start(bf16[96,800]{1,0:T(8,128)(2,1)S(1)} %shard_map.89.high), channel_id=1, source_target_pairs={{0,4},{1,5},{2,6},{3,7},{4,0},{5,1},{6,2},{7,3},{8,12},{9,13},{10,... | collective-permute-start | bytes 460808 | tf_op jit(solution)/shard_map/ppermute | solution.py:426
  18.4 0.1 shard_map.86.k_high
  18.5 0.0 collective-permute-done.8.wire
  18.5 1.6 %collective-permute-start.9 = (bf16[88,800]{1,0:T(8,128)(2,1)S(1)}, bf16[88,800]{1,0:T(8,128)(2,1)S(1)}, u32[]{:S(2)}, u32[]{:S(2)}) collective-permute-start(bf16[88,800]{1,0:T(8,128)(2,1)S(1)} %shard_map.86.k_high), channel_id=1, source_target_pairs={{0,1},{1,0},{2,3},{3,2},{4,5},{5,4},{6,7},{7,6},{8,9},{9,8},{10,11... | collective-permute-start | bytes 422408 | tf_op jit(solution)/shard_map/ppermute | solution.py:426
  20.1 1.7 %shard_map.90 = (f32[80,768]{1,0:T(8,128)S(1)}, f32[768,80]{1,0:T(8,128)S(1)}, f32[768,80]{1,0:T(8,128)S(1)}, bf16[768,80]{1,0:T(8,128)(2,1)S(1)}, bf16[768,80]{...) custom-call(bf16[96,480]{1,0:T(8,128)(2,1)S(1)} %shard_map.88.low, ...), custom_call_target="tpu_custom_call" | custom-call | tf_op jit(solution)/shard_map/pallas_call | solution.py:118
  21.8 1.2 %shard_map.91 = (f32[80,288]{1,0:T(8,128)S(1)}, f32[768,80]{1,0:T(8,128)S(1)}, f32[768,80]{1,0:T(8,128)S(1)}, bf16[288,80]{1,0:T(8,128)(2,1)S(1)}, bf16[288,80]{1,0:T(8,128)(2,1)S(1)}) custom-call(bf16[96,480]{1,0:T(8,128)(2,1)S(1)} %collective-permute-done.8.wire, bf16[768,80]{1,0:T(8,128)(2,1)S(1)} %get-tuple-element.46.k_own, ...), custom_call_target="tpu_custom_call" | custom-call | tf_op jit(solution)/shard_map/pallas_call | solution.py:118
  23.1 1.6 %collective-permute-done.9.k_high = bf16[88,800]{1,0:T(8,128)(2,1)S(1)} collective-permute-done((bf16[88,800]{1,0:T(8,128)(2,1)S(1)}, bf16[88,800]{1,0:T(8,128)(2,1)S(1)}, u32[]{:S(2)}, u32[]{:S(2)}) %collective-permute-start.9) | collective-permute-done | bytes 140832 | tf_op jit(solution)/shard_map/ppermute | solution.py:426
  24.6 1.6 %shard_map.92 = (f32[80,768]{1,0:T(8,128)S(1)}, f32[768,80]{1,0:T(8,128)S(1)}, f32[768,80]{1,0:T(8,128)S(1)}, bf16[768,80]{1,0:T(8,128)(2,1)S(1)}, bf16[768,80]{1,0:T(8,128)(2,1)S(1)}) custom-call(f32[80,288]{1,0:T(8,128)S(1)} %get-tuple-element.50.after.dq_before, bf16[96,480]{1,0:T(8,128)(2,1)S(1)} %shard_map.88.low, bf16[96,800]{1,0:T(8,128)(2,1)S(1)} %shard_map.89.high, ...), custom_call_target="tpu_custom_call" | custom-call | tf_op jit(solution)/shard_map/pallas_call | solution.py:118
  26.2 1.2 %shard_map.93 = (f32[80,288]{1,0:T(8,128)S(1)}, f32[768,80]{1,0:T(8,128)S(1)}, f32[768,80]{1,0:T(8,128)S(1)}) custom-call(bf16[96,480]{1,0:T(8,128)(2,1)S(1)} %collective-permute-done.8.wire, bf16[288,80]{1,0:T(8,128)(2,1)S(1)} %get-tuple-element.58.q_s, bf16[288,80]{1,0:T(8,128)(2,1)S(1)} %get-tuple-element.59.do_s, ...), custom_call_target="tpu_custom_call" | custom-call | tf_op jit(solution)/shard_map/pallas_call | solution.py:118
  27.4 0.7 %collective-permute-done.10.high = bf16[96,800]{1,0:T(8,128)(2,1)S(1)} collective-permute-done((bf16[96,800]{1,0:T(8,128)(2,1)S(1)}, bf16[96,800]{1,0:T(8,128)(2,1)S(1)}, u32[]{:S(2)}, u32[]{:S(2)}) %collective-permute-start.10) | collective-permute-done | bytes 153632 | tf_op jit(solution)/shard_map/ppermute | solution.py:426
  28.1 1.4 %shard_map.94 = (f32[80,480]{1,0:T(8,128)S(1)}, bf16[88,1280]{1,0:T(8,128)(2,1)S(1)}, bf16[480,80]{1,0:T(8,128)(2,1)S(1)}, bf16[480,80]{1,0:T(8,128)(2,1)S(1)}) custom-call(bf16[96,800]{1,0:T(8,128)(2,1)S(1)} %collective-permute-done.10.high, bf16[768,80]{1,0:T(8,128)(2,1)S(1)} %get-tuple-element.56.k_far, bf16[768,80]{1,0:T(8,128)(2,1)S(1)} %get-tuple-element.57.v_far, ...), custom_call_target="tpu_custom_call" | custom-call | tf_op jit(solution)/shard_map/pallas_call | solution.py:118
  29.5 0.9 %collective-permute-start.11 = (bf16[88,1280]{1,0:T(8,128)(2,1)S(1)}, bf16[88,1280]{1,0:T(8,128)(2,1)S(1)}, u32[]{:S(2)}, u32[]{:S(2)}) collective-permute-start(bf16[88,1280]{1,0:T(8,128)(2,1)S(1)} %get-tuple-element.72), channel_id=1, source_target_pairs={{0,1},{1,0},{2,3},{3,2},{4,5},{5,4},{6,7},{7,6},{8,9},{9,8},{10,11... | collective-permute-start | bytes 675848 | tf_op jit(solution)/shard_map/ppermute | solution.py:426
  30.5 1.4 %shard_map.95 = (bf16[88,640]{1,0:T(8,128)(2,1)S(1)}, f32[768,80]{1,0:T(8,128)S(1)}, f32[768,80]{1,0:T(8,128)S(1)}) custom-call(bf16[96,800]{1,0:T(8,128)(2,1)S(1)} %collective-permute-done.10.high, bf16[480,80]{1,0:T(8,128)(2,1)S(1)} %get-tuple-element.64.q_s, bf16[480,80]{1,0:T(8,128)(2,1)S(1)} %get-tuple-element.65.do_s, ...), custom_call_target="tpu_custom_call" | custom-call | tf_op jit(solution)/shard_map/pallas_call | solution.py:118
  31.9 0.5 collective-permute-start.12
  32.4 0.4 shard_map.96.own
  32.8 6.5 %collective-permute-done.12.dq_wire = bf16[88,640]{1,0:T(8,128)(2,1)S(1)} collective-permute-done((bf16[88,640]{1,0:T(8,128)(2,1)S(1)}, bf16[88,640]{1,0:T(8,128)(2,1)S(1)}, u32[]{:S(2)}, u32[]{:S(2)}) %collective-permute-start.12) | collective-permute-done | bytes 112672 | tf_op jit(solution)/shard_map/ppermute | solution.py:426
  39.3 0.0 collective-permute-done.11.dkv_wire
  39.3 0.2 shard_map.97
  39.5 0.1 collective-permute-start.13
  39.6 1.5 %collective-permute-start.14 = (bf16[88,512]{1,0:T(8,128)(2,1)S(1)}, bf16[88,512]{1,0:T(8,128)(2,1)S(1)}, u32[]{:S(2)}, u32[]{:S(2)}) collective-permute-start(bf16[88,512]{1,0:T(8,128)(2,1)S(1)} %get-tuple-element.78), channel_id=1, source_target_pairs={{0,16},{8,24},{16,0},{24,8},{1,17},{9,25},{17,1},{25,9},{2,18},{10... | collective-permute-start | bytes 270344 | tf_op jit(solution)/shard_map/ppermute | solution.py:424
  41.1 2.0 %collective-permute-start.15 = (bf16[88,512]{1,0:T(8,128)(2,1)S(1)}, bf16[88,512]{1,0:T(8,128)(2,1)S(1)}, u32[]{:S(2)}, u32[]{:S(2)}) collective-permute-start(bf16[88,512]{1,0:T(8,128)(2,1)S(1)} %get-tuple-element.77), channel_id=1, source_target_pairs={{0,18},{1,19},{2,16},{3,17},{4,22},{5,23},{6,20},{7,21},{8,26},{9,... | collective-permute-start | bytes 270344 | tf_op jit(solution)/shard_map/ppermute | solution.py:428
  43.1 1.5 %collective-permute-done.13.refs_1_ = bf16[88,512]{1,0:T(8,128)(2,1)S(1)} collective-permute-done((bf16[88,512]{1,0:T(8,128)(2,1)S(1)}, bf16[88,512]{1,0:T(8,128)(2,1)S(1)}, u32[]{:S(2)}, u32[]{:S(2)}) %collective-permute-start.13) | collective-permute-done | bytes 90144 | tf_op jit(solution)/shard_map/ppermute | solution.py:426
  44.6 0.5 %collective-permute-done.14.refs_2_ = bf16[88,512]{1,0:T(8,128)(2,1)S(1)} collective-permute-done((bf16[88,512]{1,0:T(8,128)(2,1)S(1)}, bf16[88,512]{1,0:T(8,128)(2,1)S(1)}, u32[]{:S(2)}, u32[]{:S(2)}) %collective-permute-start.14) | collective-permute-done | bytes 90144 | tf_op jit(solution)/shard_map/ppermute | solution.py:424
  45.2 0.0 collective-permute-start.18
  45.2 1.3 %collective-permute-done.15.refs_3_ = bf16[88,512]{1,0:T(8,128)(2,1)S(1)} collective-permute-done((bf16[88,512]{1,0:T(8,128)(2,1)S(1)}, bf16[88,512]{1,0:T(8,128)(2,1)S(1)}, u32[]{:S(2)}, u32[]{:S(2)}) %collective-permute-start.15) | collective-permute-done | bytes 90144 | tf_op jit(solution)/shard_map/ppermute | solution.py:428
  46.5 0.0 collective-permute-done.16.refs_4_
  46.6 1.2 %collective-permute-done.19.refs_7_ = bf16[88,256]{1,0:T(8,128)(2,1)S(1)} collective-permute-done((bf16[88,256]{1,0:T(8,128)(2,1)S(1)}, bf16[88,256]{1,0:T(8,128)(2,1)S(1)}, u32[]{:S(2)}, u32[]{:S(2)}) %collective-permute-start.19) | collective-permute-done | bytes 45088 | tf_op jit(solution)/shard_map/ppermute | solution.py:424
  47.8 0.9 %shard_map.98 = (bf16[88,640]{1,0:T(8,128)(2,1)}, bf16[88,640]{1,0:T(8,128)(2,1)}, bf16[88,640]{1,0:T(8,128)(2,1)}) custom-call(bf16[88,512]{1,0:T(8,128)(2,1)S(1)} %get-tuple-element.80.refs_0_, bf16[88,512]{1,0:T(8,128)(2,1)S(1)} %collective-permute-done.13.refs_1_, bf16[88,512]{1,0:T(8,128)(2,1)S(1)} %collective-permute-done.14.refs_2_, ...), custom_call_target="tpu_custom_call" | custom-call | tf_op jit(solution)/shard_map/pallas_call | solution.py:118
  (19 shorter events, 0.1 us)
Async XLA Ops:
  3.2 7.1 %copy-start = (bf16[96,640]{1,0:T(8,128)(2,1)S(1)}, bf16[96,640]{1,0:T(8,128)(2,1)}, u32[]{:S(2)}) copy-start(bf16[96,640]{1,0:T(8,128)(2,1)} %get-tuple-element.43.refs_0_) | copy-start | bytes 368644
  3.2 7.1 %collective-permute-start = (bf16[96,640]{1,0:T(8,128)(2,1)}, bf16[96,640]{1,0:T(8,128)(2,1)S(1)}, u32[]{:S(2)}, u32[]{:S(2)}) collective-permute-start(bf16[96,640]{1,0:T(8,128)(2,1)} %get-tuple-element.40), channel_id=1, source_target_pairs={{0,2},{1,3},{2,0},{3,1},{4,6},{5,7},{6,4},{7,5},{8,10},{9,11},{10,... | collective-permute-start | bytes 368648 | tf_op jit(solution)/shard_map/ppermute | solution.py:426
  6.3 8.7 %collective-permute-start.2 = (bf16[96,640]{1,0:T(8,128)(2,1)}, bf16[96,640]{1,0:T(8,128)(2,1)S(1)}, u32[]{:S(2)}, u32[]{:S(2)}) collective-permute-start(bf16[96,640]{1,0:T(8,128)(2,1)} %get-tuple-element.41), channel_id=1, source_target_pairs={{0,16},{8,24},{16,0},{24,8},{1,17},{9,25},{17,1},{25,9},{2,18},{10... | collective-permute-start | bytes 368648 | tf_op jit(solution)/shard_map/ppermute | solution.py:424
  7.8 7.7 %collective-permute-start.4 = (bf16[96,640]{1,0:T(8,128)(2,1)}, bf16[96,640]{1,0:T(8,128)(2,1)S(1)}, u32[]{:S(2)}, u32[]{:S(2)}) collective-permute-start(bf16[96,640]{1,0:T(8,128)(2,1)} %get-tuple-element.42), channel_id=1, source_target_pairs={{0,18},{1,19},{2,16},{3,17},{4,22},{5,23},{6,20},{7,21},{8,26},{9,... | collective-permute-start | bytes 368648 | tf_op jit(solution)/shard_map/ppermute | solution.py:428
  7.8 2.5 %copy-start.1 = (f32[1,2,352]{2,1,0:T(2,128)S(1)}, f32[1,2,352]{2,1,0:T(2,128)}, u32[]{:S(2)}) copy-start(f32[1,2,352]{2,1,0:T(2,128)} %param.11) | copy-start | bytes 8452
  8.7 1.3 %collective-permute-start.6 = (bf16[96,384]{1,0:T(8,128)(2,1)S(1)}, bf16[96,384]{1,0:T(8,128)(2,1)S(1)}, u32[]{:S(2)}, u32[]{:S(2)}) collective-permute-start(bf16[96,384]{1,0:T(8,128)(2,1)S(1)} %slice.39), channel_id=1, source_target_pairs={{0,8},{8,0},{16,24},{24,16},{1,9},{9,1},{17,25},{25,17},{2,10},{10... | collective-permute-start | bytes 221192 | tf_op jit(solution)/shard_map/ppermute | solution.py:424
  10.5 8.0 %collective-permute-start.8 = (bf16[96,480]{1,0:T(8,128)(2,1)S(1)}, bf16[96,480]{1,0:T(8,128)(2,1)S(1)}, u32[]{:S(2)}, u32[]{:S(2)}) collective-permute-start(bf16[96,480]{1,0:T(8,128)(2,1)S(1)} %shard_map.88.low), channel_id=1, source_target_pairs={{0,4},{1,5},{2,6},{3,7},{4,0},{5,1},{6,2},{7,3},{8,12},{9,13},{10,... | collective-permute-start | bytes 276488 | tf_op jit(solution)/shard_map/ppermute | solution.py:426
  13.3 5.3 %collective-permute-start.7 = (bf16[96,480]{1,0:T(8,128)(2,1)S(1)}, bf16[96,480]{1,0:T(8,128)(2,1)S(1)}, u32[]{:S(2)}, u32[]{:S(2)}) collective-permute-start(bf16[96,480]{1,0:T(8,128)(2,1)S(1)} %shard_map.87.k_low), channel_id=1, source_target_pairs={{0,1},{1,0},{2,3},{3,2},{4,5},{5,4},{6,7},{7,6},{8,9},{9,8},{10,11... | collective-permute-start | bytes 276488 | tf_op jit(solution)/shard_map/ppermute | solution.py:426
  14.9 1.3 %collective-permute-start.1 = (bf16[96,384]{1,0:T(8,128)(2,1)S(1)}, bf16[96,384]{1,0:T(8,128)(2,1)S(1)}, u32[]{:S(2)}, u32[]{:S(2)}) collective-permute-start(bf16[96,384]{1,0:T(8,128)(2,1)S(1)} %slice.48), channel_id=1, source_target_pairs={{0,8},{8,0},{16,24},{24,16},{1,9},{9,1},{17,25},{25,17},{2,10},{10... | collective-permute-start | bytes 221192 | tf_op jit(solution)/shard_map/ppermute | solution.py:424
  15.0 1.5 %collective-permute-start.3 = (bf16[96,384]{1,0:T(8,128)(2,1)S(1)}, bf16[96,384]{1,0:T(8,128)(2,1)S(1)}, u32[]{:S(2)}, u32[]{:S(2)}) collective-permute-start(bf16[96,384]{1,0:T(8,128)(2,1)S(1)} %slice.49), channel_id=1, source_target_pairs={{0,8},{8,0},{16,24},{24,16},{1,9},{9,1},{17,25},{25,17},{2,10},{10... | collective-permute-start | bytes 221192 | tf_op jit(solution)/shard_map/ppermute | solution.py:424
  15.5 1.3 %collective-permute-start.5 = (bf16[96,384]{1,0:T(8,128)(2,1)S(1)}, bf16[96,384]{1,0:T(8,128)(2,1)S(1)}, u32[]{:S(2)}, u32[]{:S(2)}) collective-permute-start(bf16[96,384]{1,0:T(8,128)(2,1)S(1)} %slice.50), channel_id=1, source_target_pairs={{0,8},{8,0},{16,24},{24,16},{1,9},{9,1},{17,25},{25,17},{2,10},{10... | collective-permute-start | bytes 221192 | tf_op jit(solution)/shard_map/ppermute | solution.py:424
  17.0 11.0 %collective-permute-start.10 = (bf16[96,800]{1,0:T(8,128)(2,1)S(1)}, bf16[96,800]{1,0:T(8,128)(2,1)S(1)}, u32[]{:S(2)}, u32[]{:S(2)}) collective-permute-start(bf16[96,800]{1,0:T(8,128)(2,1)S(1)} %shard_map.89.high), channel_id=1, source_target_pairs={{0,4},{1,5},{2,6},{3,7},{4,0},{5,1},{6,2},{7,3},{8,12},{9,13},{10,... | collective-permute-start | bytes 460808 | tf_op jit(solution)/shard_map/ppermute | solution.py:426
  18.5 6.1 %collective-permute-start.9 = (bf16[88,800]{1,0:T(8,128)(2,1)S(1)}, bf16[88,800]{1,0:T(8,128)(2,1)S(1)}, u32[]{:S(2)}, u32[]{:S(2)}) collective-permute-start(bf16[88,800]{1,0:T(8,128)(2,1)S(1)} %shard_map.86.k_high), channel_id=1, source_target_pairs={{0,1},{1,0},{2,3},{3,2},{4,5},{5,4},{6,7},{7,6},{8,9},{9,8},{10,11... | collective-permute-start | bytes 422408 | tf_op jit(solution)/shard_map/ppermute | solution.py:426
  29.5 9.7 %collective-permute-start.11 = (bf16[88,1280]{1,0:T(8,128)(2,1)S(1)}, bf16[88,1280]{1,0:T(8,128)(2,1)S(1)}, u32[]{:S(2)}, u32[]{:S(2)}) collective-permute-start(bf16[88,1280]{1,0:T(8,128)(2,1)S(1)} %get-tuple-element.72), channel_id=1, source_target_pairs={{0,1},{1,0},{2,3},{3,2},{4,5},{5,4},{6,7},{7,6},{8,9},{9,8},{10,11... | collective-permute-start | bytes 675848 | tf_op jit(solution)/shard_map/ppermute | solution.py:426
  31.9 7.3 %collective-permute-start.12 = (bf16[88,640]{1,0:T(8,128)(2,1)S(1)}, bf16[88,640]{1,0:T(8,128)(2,1)S(1)}, u32[]{:S(2)}, u32[]{:S(2)}) collective-permute-start(bf16[88,640]{1,0:T(8,128)(2,1)S(1)} %get-tuple-element.73), channel_id=1, source_target_pairs={{0,4},{1,5},{2,6},{3,7},{4,0},{5,1},{6,2},{7,3},{8,12},{9,13},{10,... | collective-permute-start | bytes 337928 | tf_op jit(solution)/shard_map/ppermute | solution.py:426
  39.5 5.1 %collective-permute-start.13 = (bf16[88,512]{1,0:T(8,128)(2,1)S(1)}, bf16[88,512]{1,0:T(8,128)(2,1)S(1)}, u32[]{:S(2)}, u32[]{:S(2)}) collective-permute-start(bf16[88,512]{1,0:T(8,128)(2,1)S(1)} %get-tuple-element.79), channel_id=1, source_target_pairs={{0,2},{1,3},{2,0},{3,1},{4,6},{5,7},{6,4},{7,5},{8,10},{9,11},{10,... | collective-permute-start | bytes 270344 | tf_op jit(solution)/shard_map/ppermute | solution.py:426
  39.6 5.6 %collective-permute-start.14 = (bf16[88,512]{1,0:T(8,128)(2,1)S(1)}, bf16[88,512]{1,0:T(8,128)(2,1)S(1)}, u32[]{:S(2)}, u32[]{:S(2)}) collective-permute-start(bf16[88,512]{1,0:T(8,128)(2,1)S(1)} %get-tuple-element.78), channel_id=1, source_target_pairs={{0,16},{8,24},{16,0},{24,8},{1,17},{9,25},{17,1},{25,9},{2,18},{10... | collective-permute-start | bytes 270344 | tf_op jit(solution)/shard_map/ppermute | solution.py:424
  41.1 5.4 %collective-permute-start.15 = (bf16[88,512]{1,0:T(8,128)(2,1)S(1)}, bf16[88,512]{1,0:T(8,128)(2,1)S(1)}, u32[]{:S(2)}, u32[]{:S(2)}) collective-permute-start(bf16[88,512]{1,0:T(8,128)(2,1)S(1)} %get-tuple-element.77), channel_id=1, source_target_pairs={{0,18},{1,19},{2,16},{3,17},{4,22},{5,23},{6,20},{7,21},{8,26},{9,... | collective-permute-start | bytes 270344 | tf_op jit(solution)/shard_map/ppermute | solution.py:428
  43.1 3.4 %collective-permute-start.16 = (bf16[88,256]{1,0:T(8,128)(2,1)S(1)}, bf16[88,256]{1,0:T(8,128)(2,1)S(1)}, u32[]{:S(2)}, u32[]{:S(2)}) collective-permute-start(bf16[88,256]{1,0:T(8,128)(2,1)S(1)} %slice.55), channel_id=1, source_target_pairs={{0,8},{8,0},{16,24},{24,16},{1,9},{9,1},{17,25},{25,17},{2,10},{10... | collective-permute-start | bytes 135176 | tf_op jit(solution)/shard_map/ppermute | solution.py:424
  44.6 1.9 %collective-permute-start.17 = (bf16[88,256]{1,0:T(8,128)(2,1)S(1)}, bf16[88,256]{1,0:T(8,128)(2,1)S(1)}, u32[]{:S(2)}, u32[]{:S(2)}) collective-permute-start(bf16[88,256]{1,0:T(8,128)(2,1)S(1)} %slice.56), channel_id=1, source_target_pairs={{0,8},{8,0},{16,24},{24,16},{1,9},{9,1},{17,25},{25,17},{2,10},{10... | collective-permute-start | bytes 135176 | tf_op jit(solution)/shard_map/ppermute | solution.py:424
  45.2 1.4 %collective-permute-start.18 = (bf16[88,256]{1,0:T(8,128)(2,1)S(1)}, bf16[88,256]{1,0:T(8,128)(2,1)S(1)}, u32[]{:S(2)}, u32[]{:S(2)}) collective-permute-start(bf16[88,256]{1,0:T(8,128)(2,1)S(1)} %slice.57), channel_id=1, source_target_pairs={{0,8},{8,0},{16,24},{24,16},{1,9},{9,1},{17,25},{25,17},{2,10},{10... | collective-permute-start | bytes 135176 | tf_op jit(solution)/shard_map/ppermute | solution.py:424
  46.5 1.2 %collective-permute-start.19 = (bf16[88,256]{1,0:T(8,128)(2,1)S(1)}, bf16[88,256]{1,0:T(8,128)(2,1)S(1)}, u32[]{:S(2)}, u32[]{:S(2)}) collective-permute-start(bf16[88,256]{1,0:T(8,128)(2,1)S(1)} %slice.58), channel_id=1, source_target_pairs={{0,8},{8,0},{16,24},{24,16},{1,9},{9,1},{17,25},{25,17},{2,10},{10... | collective-permute-start | bytes 135176 | tf_op jit(solution)/shard_map/ppermute | solution.py:424

commit v6 on v5

--- a/solution.py
+++ b/solution.py
@@ -154,12 +154,14 @@
     copies = [
         pltpu.make_async_copy(source, target, done.at[i])
         for i, (source, target) in enumerate(
-            ((q_in, q_s), (k_in, k_s), (v_in, v_s), (do_in, do_s), (o_in, o_s), (lse_in, lse_s))
-        )
-    ]
+            (source.at[spot], target.at[spot])
+            for source, target in ((q_in, q_s), (do_in, do_s), (k_in, k_s), (v_in, v_s), (o_in, o_s))
+            for spot in (pl.ds(0, 48), pl.ds(48, 40))
+        )
+    ] + [pltpu.make_async_copy(lse_in, lse_s, done.at[10])]
     for copy in copies:
         copy.start()
-    for copy in copies:
+    for copy in copies[:8]:
         copy.wait()
     rows = q_s.shape[0]
     q, k, v, do = q_s[...], k_s[...], v_s[...], do_s[...]
@@ -189,6 +191,8 @@
     most = leave(0, pl.ds(0, PADDED - 16))
     for copy in most:
         copy.start()
+    for copy in copies[8:]:
+        copy.wait()
     products = do.astype(F32) * o_s[...].astype(F32)
     high = products.astype(BF16)
     rest = products - high.astype(F32)
@@ -288,7 +292,7 @@
             target[pl.ds(at, rows), :] = wide[0:rows, start : start + HDIM]
 
 
-def tile_step(q, do, k_s, v_s, lse, delta, chunk=384):
+def tile_step(q, do, k_s, v_s, lse, delta, chunk=768):
     q_t, do_t = q.T, do.T
     k_t = k_s[...].T
     dq_t = None
@@ -353,24 +357,24 @@
         dv[spot, :] = dv_in[spot, :] + dv_part
 
 
-def high_far_kernel(high, k_far, v_far, dk_in, dv_in, dq_t, wire, q_s, do_s, dk, dv):
-    spread(high, q_s, do_s)
-    dq_t[...], parts = tile_step(q_s[...], do_s[...], k_far, v_far, *rows_of([high]))
+def high_kernel(
+    wire, k_far, v_far, k_own, v_own, dk_far, dv_far, dq_low, dk_in, dv_in,
+    dkv_wire, dq_wire, dk_own, dv_own, q_s, do_s, dk, dv,
+):
+    spread(wire, q_s, do_s)
+    q, do = q_s[...], do_s[...]
+    rows = rows_of([wire])
+    first, parts = tile_step(q, do, k_far, v_far, *rows)
     for spot, dk_part, dv_part in parts:
-        dk[spot, :] = (dk_in[spot, :] + dk_part) * SCALING
-        dv[spot, :] = dv_in[spot, :] + dv_part
-    wire[...] = to_wire([dk[...], dv[...]], wire.shape[0])
-
-
-def high_own_kernel(
-    high, q_s, do_s, k_own, v_own, dq_low, dq_high, dk_in, dv_in, wire, dk, dv
-):
-    more, parts = tile_step(q_s[...], do_s[...], k_own, v_own, *rows_of([high]))
-    dq = jnp.concatenate([dq_low[...], dq_high[...] + more], axis=1) * SCALING
-    wire[...] = to_wire([dq.T], wire.shape[0])
+        dk[spot, :] = (dk_far[spot, :] + dk_part) * SCALING
+        dv[spot, :] = dv_far[spot, :] + dv_part
+    dkv_wire[...] = to_wire([dk[...], dv[...]], dkv_wire.shape[0])
+    more, parts = tile_step(q, do, k_own, v_own, *rows)
+    dq = jnp.concatenate([dq_low[...], first + more], axis=1) * SCALING
+    dq_wire[...] = to_wire([dq.T], dq_wire.shape[0])
     for spot, dk_part, dv_part in parts:
-        dk[spot, :] = dk_in[spot, :] + dk_part
-        dv[spot, :] = dv_in[spot, :] + dv_part
+        dk_own[spot, :] = dk_in[spot, :] + dk_part
+        dv_own[spot, :] = dv_in[spot, :] + dv_part
 
 
 def own_grads_kernel(dq_t, dk, dv, out):
@@ -446,7 +450,7 @@
         limit=57 * 1024 * 1024,
         scratch=[pltpu.VMEM(queries.shape[1:], BF16)] * 5
         + [pltpu.VMEM(lse.shape[1:], F32), pltpu.VMEM((4, PADDED, 640), BF16)]
-        + [pltpu.SemaphoreType.DMA((6,)), pltpu.SemaphoreType.DMA((8,))],
+        + [pltpu.SemaphoreType.DMA((11,)), pltpu.SemaphoreType.DMA((8,))],
     )
     own = packed[0]
     near = to_chips(packed)
@@ -496,18 +500,12 @@
         low_far_kernel, (shape(HDIM, few, dtype=F32), grad, grad),
         low_far, q_low_s, do_low_s, k_far, v_far, dq_low, dk_far, dv_far,
     )
-    most = shape(padded - few, HDIM)
-    dq_high, dkv_wire, q_s, do_s = call(
-        high_far_kernel,
-        (shape(HDIM, padded - few, dtype=F32), shape(rows, 1280), most, most),
-        high_far, k_far, v_far, dk_far, dv_far,
-        scratch=[pltpu.VMEM((padded, HDIM), F32)] * 2,
+    dkv_wire, dq_wire, dk_own, dv_own = call(
+        high_kernel, (shape(rows, 1280), shape(rows, 640), grad, grad),
+        high_far, k_far, v_far, k_own, v_own, dk_far, dv_far, dq_low, dk_own, dv_own,
+        scratch=[pltpu.VMEM((padded - few, HDIM), BF16)] * 2 + [pltpu.VMEM((padded, HDIM), F32)] * 2,
     )
     dkv_back = flipped(dkv_wire, 0, 1)
-    dq_wire, dk_own, dv_own = call(
-        high_own_kernel, (shape(rows, 640), grad, grad),
-        high_far, q_s, do_s, k_own, v_own, dq_low, dq_high, dk_own, dv_own,
-    )
     dq_back = flipped(dq_wire, 0, 4)
     own_g = call(own_grads_kernel, shape(4, rows, 512, dtype=F32), dq_own, dk_own, dv_own)
     packed_g = call(pack_grads_kernel, shape(4, rows, 512), own_g, dkv_back, dq_back)

time: 48.9 us -> 48.2 us (0.986)
  Pallas kernels: 13.2 us -> 12.3 us
    pallas_call x14 -> x13, Pallas kernels: 13.2 us -> 12.3 us  [call(): pl.pallas_call(kernel, out_shape=out_shape, in_specs=specs, out_specs=jax...]
  transfers between devices with their start and end apart: 20 -> 20, of which waited for: 12 -> 12; matrix products, arithmetic and copies ran while one was open for 2% -> 2% of each run, Pallas kernels for 17% -> 13%
where the time goes in v6:
time: 48.2 us; the launch traced here: 48 us
  starting transfers between devices  17.3 us (36%)
  waiting for transfers between devices  16.6 us (34%)
  Pallas kernels  12.3 us (26%)
  local copies, waits for them, and re-layouts  0.98 us (2%)
  between operations  0.83 us (2%)
    pallas_call x13, Pallas kernels, call(): pl.pallas_call(kernel, out_shape=out_shape, in_specs=specs, out_specs=jax...  12.3 us
    ppermute x8, starting transfers between devices, flipped(): return lax.ppermute(array, 'blk', [(i, i ^ blk_bits) for i in range(blks)])  11.4 us
    ppermute x8, waiting for transfers between devices, flipped(): return lax.ppermute(array, 'blk', [(i, i ^ blk_bits) for i in range(blks)])  11.1 us
    ppermute x10, waiting for transfers between devices, flipped(): lax.ppermute(array, 'head', [(i, i ^ head_bits) for i in range(heads)])  4.16 us
    ppermute x10, starting transfers between devices, flipped(): lax.ppermute(array, 'head', [(i, i ^ head_bits) for i in range(heads)])  3.84 us
    ppermute x2, starting transfers between devices, flipped(): lax.ppermute(array, ('head', 'blk'), [(i, i ^ bits) for i in range(heads...  2 us
    ppermute x2, waiting for transfers between devices, flipped(): lax.ppermute(array, ('head', 'blk'), [(i, i ^ bits) for i in range(heads...  1.37 us
  transfers between devices with their start and end apart: 20, of which 12 were waited for; matrix products, arithmetic and copies ran while one was open for 2% of the time, Pallas kernels for 13%

profile of v6, /device:TPU:0, one launch (start us, length us, event | category | flops | bytes accessed | tf_op | source)
XLA Modules:
  0.0 48.0 jit_solution(9341345223153696760)
XLA Ops:
  0.6 2.5 %shard_map.85 = (bf16[96,640]{1,0:T(8,128)(2,1)}, bf16[96,640]{1,0:T(8,128)(2,1)}, bf16[96,640]{1,0:T(8,128)(2,1)}, bf16[96,640]{1,0:T(8,128)(2,1)}) custom-call(bf16[88,640]{1,0:T(8,128)(2,1)} %bitcast.20, bf16[88,640]{1,0:T(8,128)(2,1)} %bitcast.21, bf16[88,640]{1,0:T(8,128)(2,1)} %bitcast.22, bf16[88,640]{1,0:T(8,128)(2,1)} %bitcast.23, ...), custom_call_target="tpu_custom_call" | custom-call | tf_op jit(solution)/shard_map/pallas_call | solution.py:118
  3.1 3.1 %collective-permute-start = (bf16[96,640]{1,0:T(8,128)(2,1)}, bf16[96,640]{1,0:T(8,128)(2,1)S(1)}, u32[]{:S(2)}, u32[]{:S(2)}) collective-permute-start(bf16[96,640]{1,0:T(8,128)(2,1)} %get-tuple-element.37), channel_id=1, source_target_pairs={{0,2},{1,3},{2,0},{3,1},{4,6},{5,7},{6,4},{7,5},{8,10},{9,11},{10,... | collective-permute-start | bytes 368648 | tf_op jit(solution)/shard_map/ppermute | solution.py:430
  6.2 1.5 %collective-permute-start.2 = (bf16[96,640]{1,0:T(8,128)(2,1)}, bf16[96,640]{1,0:T(8,128)(2,1)S(1)}, u32[]{:S(2)}, u32[]{:S(2)}) collective-permute-start(bf16[96,640]{1,0:T(8,128)(2,1)} %get-tuple-element.38), channel_id=1, source_target_pairs={{0,16},{8,24},{16,0},{24,8},{1,17},{9,25},{17,1},{25,9},{2,18},{10... | collective-permute-start | bytes 368648 | tf_op jit(solution)/shard_map/ppermute | solution.py:428
  7.7 0.0 collective-permute-start.4
  7.7 0.9 %slice.39 = bf16[96,384]{1,0:T(8,128)(2,1)S(1)} slice(bf16[96,640]{1,0:T(8,128)(2,1)} %get-tuple-element.40.refs_0_), slice={[0:96], [256:640]} | slice | bytes 147456 | tf_op jit(solution)/shard_map/slice | solution.py:457
  8.6 0.0 collective-permute-start.6
  8.7 1.3 %collective-permute-done.6.refs_1_ = bf16[96,384]{1,0:T(8,128)(2,1)S(1)} collective-permute-done((bf16[96,384]{1,0:T(8,128)(2,1)S(1)}, bf16[96,384]{1,0:T(8,128)(2,1)S(1)}, u32[]{:S(2)}, u32[]{:S(2)}) %collective-permute-start.6) | collective-permute-done | bytes 73760 | tf_op jit(solution)/shard_map/ppermute | solution.py:428
  9.9 0.3 collective-permute-done.refs_2_.refs_3_.refs_5_
  10.2 0.2 shard_map.88.low
  10.4 2.7 %collective-permute-start.8 = (bf16[96,480]{1,0:T(8,128)(2,1)S(1)}, bf16[96,480]{1,0:T(8,128)(2,1)S(1)}, u32[]{:S(2)}, u32[]{:S(2)}) collective-permute-start(bf16[96,480]{1,0:T(8,128)(2,1)S(1)} %shard_map.88.low), channel_id=1, source_target_pairs={{0,4},{1,5},{2,6},{3,7},{4,0},{5,1},{6,2},{7,3},{8,12},{9,13},{10,... | collective-permute-start | bytes 276488 | tf_op jit(solution)/shard_map/ppermute | solution.py:430
  13.1 0.1 shard_map.87.k_low
  13.2 1.6 %collective-permute-start.7 = (bf16[96,480]{1,0:T(8,128)(2,1)S(1)}, bf16[96,480]{1,0:T(8,128)(2,1)S(1)}, u32[]{:S(2)}, u32[]{:S(2)}) collective-permute-start(bf16[96,480]{1,0:T(8,128)(2,1)S(1)} %shard_map.87.k_low), channel_id=1, source_target_pairs={{0,1},{1,0},{2,3},{3,2},{4,5},{5,4},{6,7},{7,6},{8,9},{9,8},{10,11... | collective-permute-start | bytes 276488 | tf_op jit(solution)/shard_map/ppermute | solution.py:430
  14.8 0.1 collective-permute-start.1
  14.8 0.0 collective-permute-done.2.refs_1_
  14.9 0.6 %collective-permute-start.3 = (bf16[96,384]{1,0:T(8,128)(2,1)S(1)}, bf16[96,384]{1,0:T(8,128)(2,1)S(1)}, u32[]{:S(2)}, u32[]{:S(2)}) collective-permute-start(bf16[96,384]{1,0:T(8,128)(2,1)S(1)} %slice.49), channel_id=1, source_target_pairs={{0,8},{8,0},{16,24},{24,16},{1,9},{9,1},{17,25},{25,17},{2,10},{10... | collective-permute-start | bytes 221192 | tf_op jit(solution)/shard_map/ppermute | solution.py:428
  15.4 0.0 collective-permute-done.4.refs_3_
  15.4 0.1 collective-permute-start.5
  15.5 0.6 %collective-permute-done.1.refs_0_ = bf16[96,384]{1,0:T(8,128)(2,1)S(1)} collective-permute-done((bf16[96,384]{1,0:T(8,128)(2,1)S(1)}, bf16[96,384]{1,0:T(8,128)(2,1)S(1)}, u32[]{:S(2)}, u32[]{:S(2)}) %collective-permute-start.1) | collective-permute-done | bytes 73760 | tf_op jit(solution)/shard_map/ppermute | solution.py:428
  16.1 0.2 collective-permute-done.3.refs_2_
  16.3 0.4 collective-permute-done.5.refs_4_
  16.8 0.2 shard_map.89.high
  17.0 1.3 %collective-permute-start.10 = (bf16[96,800]{1,0:T(8,128)(2,1)S(1)}, bf16[96,800]{1,0:T(8,128)(2,1)S(1)}, u32[]{:S(2)}, u32[]{:S(2)}) collective-permute-start(bf16[96,800]{1,0:T(8,128)(2,1)S(1)} %shard_map.89.high), channel_id=1, source_target_pairs={{0,4},{1,5},{2,6},{3,7},{4,0},{5,1},{6,2},{7,3},{8,12},{9,13},{10,... | collective-permute-start | bytes 460808 | tf_op jit(solution)/shard_map/ppermute | solution.py:430
  18.3 0.1 shard_map.86.k_high
  18.4 1.6 %collective-permute-start.9 = (bf16[88,800]{1,0:T(8,128)(2,1)S(1)}, bf16[88,800]{1,0:T(8,128)(2,1)S(1)}, u32[]{:S(2)}, u32[]{:S(2)}) collective-permute-start(bf16[88,800]{1,0:T(8,128)(2,1)S(1)} %shard_map.86.k_high), channel_id=1, source_target_pairs={{0,1},{1,0},{2,3},{3,2},{4,5},{5,4},{6,7},{7,6},{8,9},{9,8},{10,11... | collective-permute-start | bytes 422408 | tf_op jit(solution)/shard_map/ppermute | solution.py:430
  20.0 1.7 %shard_map.90 = (f32[80,768]{1,0:T(8,128)S(1)}, f32[768,80]{1,0:T(8,128)S(1)}, f32[768,80]{1,0:T(8,128)S(1)}, bf16[768,80]{1,0:T(8,128)(2,1)S(1)}, bf16[768,80]{...) custom-call(bf16[96,480]{1,0:T(8,128)(2,1)S(1)} %shard_map.88.low, ...), custom_call_target="tpu_custom_call" | custom-call | tf_op jit(solution)/shard_map/pallas_call | solution.py:118
  21.7 1.0 %shard_map.91 = (f32[80,288]{1,0:T(8,128)S(1)}, f32[768,80]{1,0:T(8,128)S(1)}, f32[768,80]{1,0:T(8,128)S(1)}, bf16[288,80]{1,0:T(8,128)(2,1)S(1)}, bf16[288,80]{1,0:T(8,128)(2,1)S(1)}) custom-call(bf16[96,480]{1,0:T(8,128)(2,1)S(1)} %collective-permute-done.8.wire, bf16[768,80]{1,0:T(8,128)(2,1)S(1)} %get-tuple-element.43.k_own, ...), custom_call_target="tpu_custom_call" | custom-call | tf_op jit(solution)/shard_map/pallas_call | solution.py:118
  22.7 1.8 %collective-permute-done.9.k_high = bf16[88,800]{1,0:T(8,128)(2,1)S(1)} collective-permute-done((bf16[88,800]{1,0:T(8,128)(2,1)S(1)}, bf16[88,800]{1,0:T(8,128)(2,1)S(1)}, u32[]{:S(2)}, u32[]{:S(2)}) %collective-permute-start.9) | collective-permute-done | bytes 140832 | tf_op jit(solution)/shard_map/ppermute | solution.py:430
  24.5 1.6 %shard_map.92 = (f32[80,768]{1,0:T(8,128)S(1)}, f32[768,80]{1,0:T(8,128)S(1)}, f32[768,80]{1,0:T(8,128)S(1)}, bf16[768,80]{1,0:T(8,128)(2,1)S(1)}, bf16[768,80]{1,0:T(8,128)(2,1)S(1)}) custom-call(f32[80,288]{1,0:T(8,128)S(1)} %get-tuple-element.47.after.dq_before, bf16[96,480]{1,0:T(8,128)(2,1)S(1)} %shard_map.88.low, bf16[96,800]{1,0:T(8,128)(2,1)S(1)} %shard_map.89.high, ...), custom_call_target="tpu_custom_call" | custom-call | tf_op jit(solution)/shard_map/pallas_call | solution.py:118
  26.2 0.9 %shard_map.93 = (f32[80,288]{1,0:T(8,128)S(1)}, f32[768,80]{1,0:T(8,128)S(1)}, f32[768,80]{1,0:T(8,128)S(1)}) custom-call(bf16[96,480]{1,0:T(8,128)(2,1)S(1)} %collective-permute-done.8.wire, bf16[288,80]{1,0:T(8,128)(2,1)S(1)} %get-tuple-element.55.q_s, bf16[288,80]{1,0:T(8,128)(2,1)S(1)} %get-tuple-element.56.do_s, ...), custom_call_target="tpu_custom_call" | custom-call | tf_op jit(solution)/shard_map/pallas_call | solution.py:118
  27.1 0.9 %collective-permute-done.10.wire = bf16[96,800]{1,0:T(8,128)(2,1)S(1)} collective-permute-done((bf16[96,800]{1,0:T(8,128)(2,1)S(1)}, bf16[96,800]{1,0:T(8,128)(2,1)S(1)}, u32[]{:S(2)}, u32[]{:S(2)}) %collective-permute-start.10) | collective-permute-done | bytes 153632 | tf_op jit(solution)/shard_map/ppermute | solution.py:430
  28.0 2.6 %shard_map.94 = (bf16[88,1280]{1,0:T(8,128)(2,1)S(1)}, bf16[88,640]{1,0:T(8,128)(2,1)S(1)}, f32[768,80]{1,0:T(8,128)S(1)}, f32[768,80]{1,0:T(8,128)S(1)}) custom-call(bf16[96,800]{1,0:T(8,128)(2,1)S(1)} %collective-permute-done.10.wire, bf16[768,80]{1,0:T(8,128)(2,1)S(1)} %get-tuple-element.53.k_far, bf16[768,80]{1,0:T(8,128)(2,1)S(1)} %get-tuple-element.54.v_far, ...), custom_call_target="tpu_custom_call" | custom-call | tf_op jit(solution)/shard_map/pallas_call | solution.py:118
  30.6 0.7 %collective-permute-start.11 = (bf16[88,1280]{1,0:T(8,128)(2,1)S(1)}, bf16[88,1280]{1,0:T(8,128)(2,1)S(1)}, u32[]{:S(2)}, u32[]{:S(2)}) collective-permute-start(bf16[88,1280]{1,0:T(8,128)(2,1)S(1)} %get-tuple-element.66), channel_id=1, source_target_pairs={{0,1},{1,0},{2,3},{3,2},{4,5},{5,4},{6,7},{7,6},{8,9},{9,8},{10,11... | collective-permute-start | bytes 675848 | tf_op jit(solution)/shard_map/ppermute | solution.py:430
  31.3 0.4 collective-permute-start.12
  31.7 0.4 shard_map.95.own
  32.0 6.5 %collective-permute-done.12.dq_wire = bf16[88,640]{1,0:T(8,128)(2,1)S(1)} collective-permute-done((bf16[88,640]{1,0:T(8,128)(2,1)S(1)}, bf16[88,640]{1,0:T(8,128)(2,1)S(1)}, u32[]{:S(2)}, u32[]{:S(2)}) %collective-permute-start.12) | collective-permute-done | bytes 112672 | tf_op jit(solution)/shard_map/ppermute | solution.py:430
  38.5 0.2 shard_map.96
  38.8 0.1 collective-permute-start.13
  38.9 1.5 %collective-permute-start.14 = (bf16[88,512]{1,0:T(8,128)(2,1)S(1)}, bf16[88,512]{1,0:T(8,128)(2,1)S(1)}, u32[]{:S(2)}, u32[]{:S(2)}) collective-permute-start(bf16[88,512]{1,0:T(8,128)(2,1)S(1)} %get-tuple-element.72), channel_id=1, source_target_pairs={{0,16},{8,24},{16,0},{24,8},{1,17},{9,25},{17,1},{25,9},{2,18},{10... | collective-permute-start | bytes 270344 | tf_op jit(solution)/shard_map/ppermute | solution.py:428
  40.4 1.9 %collective-permute-start.15 = (bf16[88,512]{1,0:T(8,128)(2,1)S(1)}, bf16[88,512]{1,0:T(8,128)(2,1)S(1)}, u32[]{:S(2)}, u32[]{:S(2)}) collective-permute-start(bf16[88,512]{1,0:T(8,128)(2,1)S(1)} %get-tuple-element.71), channel_id=1, source_target_pairs={{0,18},{1,19},{2,16},{3,17},{4,22},{5,23},{6,20},{7,21},{8,26},{9,... | collective-permute-start | bytes 270344 | tf_op jit(solution)/shard_map/ppermute | solution.py:432
  42.4 1.5 %collective-permute-done.13.refs_1_ = bf16[88,512]{1,0:T(8,128)(2,1)S(1)} collective-permute-done((bf16[88,512]{1,0:T(8,128)(2,1)S(1)}, bf16[88,512]{1,0:T(8,128)(2,1)S(1)}, u32[]{:S(2)}, u32[]{:S(2)}) %collective-permute-start.13) | collective-permute-done | bytes 90144 | tf_op jit(solution)/shard_map/ppermute | solution.py:430
  43.9 0.0 collective-permute-start.17
  43.9 0.5 collective-permute-done.14.refs_2_
  44.4 0.1 collective-permute-start.18
  44.5 1.4 %collective-permute-done.15.refs_3_ = bf16[88,512]{1,0:T(8,128)(2,1)S(1)} collective-permute-done((bf16[88,512]{1,0:T(8,128)(2,1)S(1)}, bf16[88,512]{1,0:T(8,128)(2,1)S(1)}, u32[]{:S(2)}, u32[]{:S(2)}) %collective-permute-start.15) | collective-permute-done | bytes 90144 | tf_op jit(solution)/shard_map/ppermute | solution.py:432
  45.9 0.0 collective-permute-start.19
  45.9 0.0 collective-permute-done.18.refs_6_
  45.9 1.2 %collective-permute-done.19.refs_7_ = bf16[88,256]{1,0:T(8,128)(2,1)S(1)} collective-permute-done((bf16[88,256]{1,0:T(8,128)(2,1)S(1)}, bf16[88,256]{1,0:T(8,128)(2,1)S(1)}, u32[]{:S(2)}, u32[]{:S(2)}) %collective-permute-start.19) | collective-permute-done | bytes 45088 | tf_op jit(solution)/shard_map/ppermute | solution.py:428
  47.1 0.9 %shard_map.97 = (bf16[88,640]{1,0:T(8,128)(2,1)}, bf16[88,640]{1,0:T(8,128)(2,1)}, bf16[88,640]{1,0:T(8,128)(2,1)}) custom-call(bf16[88,512]{1,0:T(8,128)(2,1)S(1)} %get-tuple-element.74.refs_0_, bf16[88,512]{1,0:T(8,128)(2,1)S(1)} %collective-permute-done.13.refs_1_, bf16[88,512]{1,0:T(8,128)(2,1)S(1)} %collective-permute-done.14.refs_2_, ...), custom_call_target="tpu_custom_call" | custom-call | tf_op jit(solution)/shard_map/pallas_call | solution.py:118
  (18 shorter events, 0.1 us)
Async XLA Ops:
  3.1 7.1 %copy-start = (bf16[96,640]{1,0:T(8,128)(2,1)S(1)}, bf16[96,640]{1,0:T(8,128)(2,1)}, u32[]{:S(2)}) copy-start(bf16[96,640]{1,0:T(8,128)(2,1)} %get-tuple-element.40.refs_0_) | copy-start | bytes 368644
  3.1 7.1 %collective-permute-start = (bf16[96,640]{1,0:T(8,128)(2,1)}, bf16[96,640]{1,0:T(8,128)(2,1)S(1)}, u32[]{:S(2)}, u32[]{:S(2)}) collective-permute-start(bf16[96,640]{1,0:T(8,128)(2,1)} %get-tuple-element.37), channel_id=1, source_target_pairs={{0,2},{1,3},{2,0},{3,1},{4,6},{5,7},{6,4},{7,5},{8,10},{9,11},{10,... | collective-permute-start | bytes 368648 | tf_op jit(solution)/shard_map/ppermute | solution.py:430
  6.2 8.7 %collective-permute-start.2 = (bf16[96,640]{1,0:T(8,128)(2,1)}, bf16[96,640]{1,0:T(8,128)(2,1)S(1)}, u32[]{:S(2)}, u32[]{:S(2)}) collective-permute-start(bf16[96,640]{1,0:T(8,128)(2,1)} %get-tuple-element.38), channel_id=1, source_target_pairs={{0,16},{8,24},{16,0},{24,8},{1,17},{9,25},{17,1},{25,9},{2,18},{10... | collective-permute-start | bytes 368648 | tf_op jit(solution)/shard_map/ppermute | solution.py:428
  7.7 7.7 %collective-permute-start.4 = (bf16[96,640]{1,0:T(8,128)(2,1)}, bf16[96,640]{1,0:T(8,128)(2,1)S(1)}, u32[]{:S(2)}, u32[]{:S(2)}) collective-permute-start(bf16[96,640]{1,0:T(8,128)(2,1)} %get-tuple-element.39), channel_id=1, source_target_pairs={{0,18},{1,19},{2,16},{3,17},{4,22},{5,23},{6,20},{7,21},{8,26},{9,... | collective-permute-start | bytes 368648 | tf_op jit(solution)/shard_map/ppermute | solution.py:432
  7.7 2.5 %copy-start.1 = (f32[1,2,352]{2,1,0:T(2,128)S(1)}, f32[1,2,352]{2,1,0:T(2,128)}, u32[]{:S(2)}) copy-start(f32[1,2,352]{2,1,0:T(2,128)} %param.11) | copy-start | bytes 8452
  8.6 1.3 %collective-permute-start.6 = (bf16[96,384]{1,0:T(8,128)(2,1)S(1)}, bf16[96,384]{1,0:T(8,128)(2,1)S(1)}, u32[]{:S(2)}, u32[]{:S(2)}) collective-permute-start(bf16[96,384]{1,0:T(8,128)(2,1)S(1)} %slice.39), channel_id=1, source_target_pairs={{0,8},{8,0},{16,24},{24,16},{1,9},{9,1},{17,25},{25,17},{2,10},{10... | collective-permute-start | bytes 221192 | tf_op jit(solution)/shard_map/ppermute | solution.py:428
  10.4 8.0 %collective-permute-start.8 = (bf16[96,480]{1,0:T(8,128)(2,1)S(1)}, bf16[96,480]{1,0:T(8,128)(2,1)S(1)}, u32[]{:S(2)}, u32[]{:S(2)}) collective-permute-start(bf16[96,480]{1,0:T(8,128)(2,1)S(1)} %shard_map.88.low), channel_id=1, source_target_pairs={{0,4},{1,5},{2,6},{3,7},{4,0},{5,1},{6,2},{7,3},{8,12},{9,13},{10,... | collective-permute-start | bytes 276488 | tf_op jit(solution)/shard_map/ppermute | solution.py:430
  13.2 5.3 %collective-permute-start.7 = (bf16[96,480]{1,0:T(8,128)(2,1)S(1)}, bf16[96,480]{1,0:T(8,128)(2,1)S(1)}, u32[]{:S(2)}, u32[]{:S(2)}) collective-permute-start(bf16[96,480]{1,0:T(8,128)(2,1)S(1)} %shard_map.87.k_low), channel_id=1, source_target_pairs={{0,1},{1,0},{2,3},{3,2},{4,5},{5,4},{6,7},{7,6},{8,9},{9,8},{10,11... | collective-permute-start | bytes 276488 | tf_op jit(solution)/shard_map/ppermute | solution.py:430
  14.8 1.3 %collective-permute-start.1 = (bf16[96,384]{1,0:T(8,128)(2,1)S(1)}, bf16[96,384]{1,0:T(8,128)(2,1)S(1)}, u32[]{:S(2)}, u32[]{:S(2)}) collective-permute-start(bf16[96,384]{1,0:T(8,128)(2,1)S(1)} %slice.48), channel_id=1, source_target_pairs={{0,8},{8,0},{16,24},{24,16},{1,9},{9,1},{17,25},{25,17},{2,10},{10... | collective-permute-start | bytes 221192 | tf_op jit(solution)/shard_map/ppermute | solution.py:428
  14.9 1.5 %collective-permute-start.3 = (bf16[96,384]{1,0:T(8,128)(2,1)S(1)}, bf16[96,384]{1,0:T(8,128)(2,1)S(1)}, u32[]{:S(2)}, u32[]{:S(2)}) collective-permute-start(bf16[96,384]{1,0:T(8,128)(2,1)S(1)} %slice.49), channel_id=1, source_target_pairs={{0,8},{8,0},{16,24},{24,16},{1,9},{9,1},{17,25},{25,17},{2,10},{10... | collective-permute-start | bytes 221192 | tf_op jit(solution)/shard_map/ppermute | solution.py:428
  15.4 1.3 %collective-permute-start.5 = (bf16[96,384]{1,0:T(8,128)(2,1)S(1)}, bf16[96,384]{1,0:T(8,128)(2,1)S(1)}, u32[]{:S(2)}, u32[]{:S(2)}) collective-permute-start(bf16[96,384]{1,0:T(8,128)(2,1)S(1)} %slice.50), channel_id=1, source_target_pairs={{0,8},{8,0},{16,24},{24,16},{1,9},{9,1},{17,25},{25,17},{2,10},{10... | collective-permute-start | bytes 221192 | tf_op jit(solution)/shard_map/ppermute | solution.py:428
  17.0 11.0 %collective-permute-start.10 = (bf16[96,800]{1,0:T(8,128)(2,1)S(1)}, bf16[96,800]{1,0:T(8,128)(2,1)S(1)}, u32[]{:S(2)}, u32[]{:S(2)}) collective-permute-start(bf16[96,800]{1,0:T(8,128)(2,1)S(1)} %shard_map.89.high), channel_id=1, source_target_pairs={{0,4},{1,5},{2,6},{3,7},{4,0},{5,1},{6,2},{7,3},{8,12},{9,13},{10,... | collective-permute-start | bytes 460808 | tf_op jit(solution)/shard_map/ppermute | solution.py:430
  18.4 6.1 %collective-permute-start.9 = (bf16[88,800]{1,0:T(8,128)(2,1)S(1)}, bf16[88,800]{1,0:T(8,128)(2,1)S(1)}, u32[]{:S(2)}, u32[]{:S(2)}) collective-permute-start(bf16[88,800]{1,0:T(8,128)(2,1)S(1)} %shard_map.86.k_high), channel_id=1, source_target_pairs={{0,1},{1,0},{2,3},{3,2},{4,5},{5,4},{6,7},{7,6},{8,9},{9,8},{10,11... | collective-permute-start | bytes 422408 | tf_op jit(solution)/shard_map/ppermute | solution.py:430
  30.6 8.0 %collective-permute-start.11 = (bf16[88,1280]{1,0:T(8,128)(2,1)S(1)}, bf16[88,1280]{1,0:T(8,128)(2,1)S(1)}, u32[]{:S(2)}, u32[]{:S(2)}) collective-permute-start(bf16[88,1280]{1,0:T(8,128)(2,1)S(1)} %get-tuple-element.66), channel_id=1, source_target_pairs={{0,1},{1,0},{2,3},{3,2},{4,5},{5,4},{6,7},{7,6},{8,9},{9,8},{10,11... | collective-permute-start | bytes 675848 | tf_op jit(solution)/shard_map/ppermute | solution.py:430
  31.3 7.3 %collective-permute-start.12 = (bf16[88,640]{1,0:T(8,128)(2,1)S(1)}, bf16[88,640]{1,0:T(8,128)(2,1)S(1)}, u32[]{:S(2)}, u32[]{:S(2)}) collective-permute-start(bf16[88,640]{1,0:T(8,128)(2,1)S(1)} %get-tuple-element.67), channel_id=1, source_target_pairs={{0,4},{1,5},{2,6},{3,7},{4,0},{5,1},{6,2},{7,3},{8,12},{9,13},{10,... | collective-permute-start | bytes 337928 | tf_op jit(solution)/shard_map/ppermute | solution.py:430
  38.8 5.1 %collective-permute-start.13 = (bf16[88,512]{1,0:T(8,128)(2,1)S(1)}, bf16[88,512]{1,0:T(8,128)(2,1)S(1)}, u32[]{:S(2)}, u32[]{:S(2)}) collective-permute-start(bf16[88,512]{1,0:T(8,128)(2,1)S(1)} %get-tuple-element.73), channel_id=1, source_target_pairs={{0,2},{1,3},{2,0},{3,1},{4,6},{5,7},{6,4},{7,5},{8,10},{9,11},{10,... | collective-permute-start | bytes 270344 | tf_op jit(solution)/shard_map/ppermute | solution.py:430
  38.9 5.5 %collective-permute-start.14 = (bf16[88,512]{1,0:T(8,128)(2,1)S(1)}, bf16[88,512]{1,0:T(8,128)(2,1)S(1)}, u32[]{:S(2)}, u32[]{:S(2)}) collective-permute-start(bf16[88,512]{1,0:T(8,128)(2,1)S(1)} %get-tuple-element.72), channel_id=1, source_target_pairs={{0,16},{8,24},{16,0},{24,8},{1,17},{9,25},{17,1},{25,9},{2,18},{10... | collective-permute-start | bytes 270344 | tf_op jit(solution)/shard_map/ppermute | solution.py:428
  40.4 5.4 %collective-permute-start.15 = (bf16[88,512]{1,0:T(8,128)(2,1)S(1)}, bf16[88,512]{1,0:T(8,128)(2,1)S(1)}, u32[]{:S(2)}, u32[]{:S(2)}) collective-permute-start(bf16[88,512]{1,0:T(8,128)(2,1)S(1)} %get-tuple-element.71), channel_id=1, source_target_pairs={{0,18},{1,19},{2,16},{3,17},{4,22},{5,23},{6,20},{7,21},{8,26},{9,... | collective-permute-start | bytes 270344 | tf_op jit(solution)/shard_map/ppermute | solution.py:432
  42.4 3.5 %collective-permute-start.16 = (bf16[88,256]{1,0:T(8,128)(2,1)S(1)}, bf16[88,256]{1,0:T(8,128)(2,1)S(1)}, u32[]{:S(2)}, u32[]{:S(2)}) collective-permute-start(bf16[88,256]{1,0:T(8,128)(2,1)S(1)} %slice.55), channel_id=1, source_target_pairs={{0,8},{8,0},{16,24},{24,16},{1,9},{9,1},{17,25},{25,17},{2,10},{10... | collective-permute-start | bytes 135176 | tf_op jit(solution)/shard_map/ppermute | solution.py:428
  43.9 2.0 %collective-permute-start.17 = (bf16[88,256]{1,0:T(8,128)(2,1)S(1)}, bf16[88,256]{1,0:T(8,128)(2,1)S(1)}, u32[]{:S(2)}, u32[]{:S(2)}) collective-permute-start(bf16[88,256]{1,0:T(8,128)(2,1)S(1)} %slice.56), channel_id=1, source_target_pairs={{0,8},{8,0},{16,24},{24,16},{1,9},{9,1},{17,25},{25,17},{2,10},{10... | collective-permute-start | bytes 135176 | tf_op jit(solution)/shard_map/ppermute | solution.py:428
  44.4 1.5 %collective-permute-start.18 = (bf16[88,256]{1,0:T(8,128)(2,1)S(1)}, bf16[88,256]{1,0:T(8,128)(2,1)S(1)}, u32[]{:S(2)}, u32[]{:S(2)}) collective-permute-start(bf16[88,256]{1,0:T(8,128)(2,1)S(1)} %slice.57), channel_id=1, source_target_pairs={{0,8},{8,0},{16,24},{24,16},{1,9},{9,1},{17,25},{25,17},{2,10},{10... | collective-permute-start | bytes 135176 | tf_op jit(solution)/shard_map/ppermute | solution.py:428
  45.9 1.2 %collective-permute-start.19 = (bf16[88,256]{1,0:T(8,128)(2,1)S(1)}, bf16[88,256]{1,0:T(8,128)(2,1)S(1)}, u32[]{:S(2)}, u32[]{:S(2)}) collective-permute-start(bf16[88,256]{1,0:T(8,128)(2,1)S(1)} %slice.58), channel_id=1, source_target_pairs={{0,8},{8,0},{16,24},{24,16},{1,9},{9,1},{17,25},{25,17},{2,10},{10... | collective-permute-start | bytes 135176 | tf_op jit(solution)/shard_map/ppermute | solution.py:428

commit v7 on v6

--- a/solution.py
+++ b/solution.py
@@ -147,28 +147,29 @@
 
 
 def pack_inputs_kernel(
-    q_in, k_in, v_in, o_in, do_in, lse_in, out0, out1, out2, out3,
+    q_in, k_in, v_in, o_in, do_in, lse_in, out0, out1, out2, out3, give,
     q_s, k_s, v_s, o_s, do_s, lse_s, out_ref, done, sent,
 ):
     x, w, c, _ = place()
     copies = [
         pltpu.make_async_copy(source, target, done.at[i])
         for i, (source, target) in enumerate(
-            (source.at[spot], target.at[spot])
-            for source, target in ((q_in, q_s), (do_in, do_s), (k_in, k_s), (v_in, v_s), (o_in, o_s))
-            for spot in (pl.ds(0, 48), pl.ds(48, 40))
-        )
-    ] + [pltpu.make_async_copy(lse_in, lse_s, done.at[10])]
+            ((q_in, q_s), (do_in, do_s), (k_in, k_s), (v_in, v_s), (o_in, o_s), (lse_in, lse_s))
+        )
+    ]
     for copy in copies:
         copy.start()
-    for copy in copies[:8]:
+    for copy in copies[:4]:
         copy.wait()
     rows = q_s.shape[0]
     q, k, v, do = q_s[...], k_s[...], v_s[...], do_s[...]
     outs = (out0, out1, out2, out3)
 
     def leave(part, spot):
-        return [
+        mine = pltpu.make_async_copy(
+            out_ref.at[0, spot, pl.ds(256, 384)], give.at[spot], sent.at[8 + part]
+        )
+        return [mine] + [
             pltpu.make_async_copy(out_ref.at[j, spot], out.at[spot], sent.at[4 * part + j])
             for j, out in enumerate(outs)
         ]
@@ -191,7 +192,7 @@
     most = leave(0, pl.ds(0, PADDED - 16))
     for copy in most:
         copy.start()
-    for copy in copies[8:]:
+    for copy in copies[4:]:
         copy.wait()
     products = do.astype(F32) * o_s[...].astype(F32)
     high = products.astype(BF16)
@@ -234,6 +235,10 @@
         copy.wait()
 
 
+def hold_kernel(block, held):
+    held[...] = block[...]
+
+
 def gather_queries_kernel(spots, *refs):
     *parts, near1, lse_in, wire, lse_s = refs
     rows = PADDED - 8
@@ -331,16 +336,6 @@
         dv[spot, :] = dv_part
 
 
-def own_far_kernel(after, low, high, q_s, do_s, k_low, k_high, dq_before, dq_t, dk, dv, k_s, v_s):
-    spread(k_low, k_s, v_s)
-    spread(k_high, k_s, v_s, LOW_KEYS)
-    more, parts = tile_step(q_s[...], do_s[...], k_s, v_s, *rows_of([low, high]))
-    dq_t[...] = dq_before[...] + more
-    for spot, dk_part, dv_part in parts:
-        dk[spot, :] = dk_part
-        dv[spot, :] = dv_part
-
-
 def low_own_kernel(wire, k_own, v_own, dk_in, dv_in, dq_t, dk, dv, q_s, do_s):
     spread(wire, q_s, do_s)
     dq_t[...], parts = tile_step(q_s[...], do_s[...], k_own, v_own, *rows_of([wire]))
@@ -349,12 +344,23 @@
         dv[spot, :] = dv_in[spot, :] + dv_part
 
 
-def low_far_kernel(wire, q_s, do_s, k_far, v_far, dq_before, dk_in, dv_in, dq_t, dk, dv):
-    more, parts = tile_step(q_s[...], do_s[...], k_far, v_far, *rows_of([wire]))
-    dq_t[...] = dq_before[...] + more
+def far_keys_kernel(
+    low, high, low_far, q_s, do_s, q_low_s, do_low_s, k_low, k_high, dq_before, dq_low_before,
+    dq_t, dq_low, dk, dv, k_s, v_s, all_q, all_do,
+):
+    spread(k_low, k_s, v_s)
+    spread(k_high, k_s, v_s, LOW_KEYS)
+    own = q_s.shape[0]
+    all_q[0:own], all_q[own:] = q_s[...], q_low_s[...]
+    all_do[0:own], all_do[own:] = do_s[...], do_low_s[...]
+    more, parts = tile_step(
+        all_q[...], all_do[...], k_s, v_s, *rows_of([low, high, low_far])
+    )
+    dq_t[...] = dq_before[...] + more[:, 0:own]
+    dq_low[...] = dq_low_before[...] + more[:, own:]
     for spot, dk_part, dv_part in parts:
-        dk[spot, :] = dk_in[spot, :] + dk_part
-        dv[spot, :] = dv_in[spot, :] + dv_part
+        dk[spot, :] = dk_part
+        dv[spot, :] = dv_part
 
 
 def high_kernel(
@@ -406,11 +412,11 @@
 
 
 def unpack_grads_kernel(*refs):
-    kept, given, dq, dk, dv, held, other = refs[0:4], refs[4:8], *refs[8:]
+    kept, given, dq, dk, dv, held, other = refs[0:4], refs[4], *refs[5:]
     x, w, c, _ = place()
     for j in range(4):
         held[j] = kept[j][:, 0:256]
-        other[j] = given[j][...]
+        other[j] = given[j]
     blocks = []
     for head in range(8):
         xs, cs, ws = head // 4, (head // 2) % 2, head % 2
@@ -443,18 +449,18 @@
 
     packed = call(
         pack_inputs_kernel,
-        (shape(PADDED, 640),) * 4,
+        (shape(PADDED, 640),) * 4 + (shape(PADDED, 384),),
         queries[0], keys[0], values[0], outputs[0], grad_out[0], lse[0],
         remote=6,
         out_space=pltpu.HBM,
         limit=57 * 1024 * 1024,
         scratch=[pltpu.VMEM(queries.shape[1:], BF16)] * 5
         + [pltpu.VMEM(lse.shape[1:], F32), pltpu.VMEM((4, PADDED, 640), BF16)]
-        + [pltpu.SemaphoreType.DMA((11,)), pltpu.SemaphoreType.DMA((8,))],
-    )
-    own = packed[0]
+        + [pltpu.SemaphoreType.DMA((6,)), pltpu.SemaphoreType.DMA((10,))],
+    )
+    own = call(hold_kernel, shape(PADDED, 640), packed[0])
     near = to_chips(packed)
-    other = [flipped(a[:, 256:], 1, 0) for a in [own] + near]
+    other = [flipped(a, 1, 0) for a in [packed[4]] + [b[:, 256:] for b in near]]
     blocks = [ref for pair in zip([own] + near, other) for ref in pair]
     spots = [(j, r) for j in range(4) for r in range(2)]
 
@@ -492,13 +498,10 @@
         low_own_kernel, (shape(HDIM, few, dtype=F32), grad, grad, some, some),
         low_far, k_own, v_own, dk_own, dv_own,
     )
-    dq_own, dk_far, dv_far, k_far, v_far = call(
-        own_far_kernel, (dq_shape, grad, grad, side, side),
-        dq_low, low, high, q_s, do_s, *keys_far, dq_own,
-    )
-    dq_low, dk_far, dv_far = call(
-        low_far_kernel, (shape(HDIM, few, dtype=F32), grad, grad),
-        low_far, q_low_s, do_low_s, k_far, v_far, dq_low, dk_far, dv_far,
+    dq_own, dq_low, dk_far, dv_far, k_far, v_far = call(
+        far_keys_kernel, (dq_shape, shape(HDIM, few, dtype=F32), grad, grad, side, side),
+        low, high, low_far, q_s, do_s, q_low_s, do_low_s, *keys_far, dq_own, dq_low,
+        scratch=[pltpu.VMEM((padded + few, HDIM), BF16)] * 2,
     )
     dkv_wire, dq_wire, dk_own, dv_own = call(
         high_kernel, (shape(rows, 1280), shape(rows, 640), grad, grad),
@@ -510,10 +513,10 @@
     own_g = call(own_grads_kernel, shape(4, rows, 512, dtype=F32), dq_own, dk_own, dv_own)
     packed_g = call(pack_grads_kernel, shape(4, rows, 512), own_g, dkv_back, dq_back)
     held = [packed_g[0]] + to_chips(packed_g)
-    other = [flipped(a[:, 256:], 1, 0) for a in held]
+    other = flipped(jnp.stack([a[:, 256:] for a in held]), 1, 0)
     out = shape(rows, queries.shape[2])
     grads = call(
-        unpack_grads_kernel, (out, out, out), *held, *other,
+        unpack_grads_kernel, (out, out, out), *held, other,
         scratch=[pltpu.VMEM((4, rows, 256), BF16)] * 2,
     )
     return tuple(grad[None] for grad in grads)

time: 48.2 us -> 48.1 us (level)
    ppermute x8, starting transfers between devices: 11.4 us -> 13.2 us  [flipped(): return lax.ppermute(array, 'blk', [(i, i ^ blk_bits) for i in range(blks)])]
    ppermute x2, starting transfers between devices: 2 us -> 0.4 us  [flipped(): lax.ppermute(array, ('head', 'blk'), [(i, i ^ bits) for i in range(heads...]
    ppermute x2, waiting for transfers between devices: 1.37 us -> 2.48 us  [flipped(): lax.ppermute(array, ('head', 'blk'), [(i, i ^ bits) for i in range(heads...]
    ppermute x10 -> x7, waiting for transfers between devices: 4.16 us -> 3.2 us  [flipped(): lax.ppermute(array, 'head', [(i, i ^ head_bits) for i in range(heads)])]
    slice x8 -> x3, local copies, waits for them, and re-layouts: 0.95 us -> 0.03 us  [grid_body(): other = [flipped(a, 1, 0) for a in [packed[4]] + [b[:, 256:] for b in near]]]
    unnamed x4, local copies, waits for them, and re-layouts: 0.01 us -> 0.91 us
    ppermute x10 -> x7, starting transfers between devices: 3.84 us -> 3.56 us  [flipped(): lax.ppermute(array, 'head', [(i, i ^ head_bits) for i in range(heads)])]
  transfers between devices with their start and end apart: 20 -> 17, of which waited for: 12 -> 11; matrix products, arithmetic and copies ran while one was open for 2% -> 0% of each run, Pallas kernels for 13% -> 13%
where the time goes in v7:
time: 48.1 us; the launch traced here: 48 us
  starting transfers between devices  17.1 us (36%)
  waiting for transfers between devices  16.8 us (35%)
  Pallas kernels  12.3 us (26%)
  local copies, waits for them, and re-layouts  0.98 us (2%)
  between operations  0.79 us (2%)
    ppermute x8, starting transfers between devices, flipped(): return lax.ppermute(array, 'blk', [(i, i ^ blk_bits) for i in range(blks)])  13.2 us
    pallas_call x13, Pallas kernels, call(): pl.pallas_call(kernel, out_shape=out_shape, in_specs=specs, out_specs=jax...  12.3 us
    ppermute x8, waiting for transfers between devices, flipped(): return lax.ppermute(array, 'blk', [(i, i ^ blk_bits) for i in range(blks)])  11.1 us
    ppermute x7, starting transfers between devices, flipped(): lax.ppermute(array, 'head', [(i, i ^ head_bits) for i in range(heads)])  3.56 us
    ppermute x7, waiting for transfers between devices, flipped(): lax.ppermute(array, 'head', [(i, i ^ head_bits) for i in range(heads)])  3.2 us
    ppermute x2, waiting for transfers between devices, flipped(): lax.ppermute(array, ('head', 'blk'), [(i, i ^ bits) for i in range(heads...  2.48 us
  transfers between devices with their start and end apart: 17, of which 11 were waited for; matrix products, arithmetic and copies ran while one was open for 0% of the time, Pallas kernels for 13%

profile of v7, /device:TPU:0, one launch (start us, length us, event | category | flops | bytes accessed | tf_op | source)
XLA Modules:
  0.0 48.0 jit_solution(6570602842923728035)
XLA Ops:
  0.6 2.5 %shard_map.85 = (bf16[96,640]{1,0:T(8,128)(2,1)}, bf16[96,640]{1,0:T(8,128)(2,1)}, bf16[96,640]{1,0:T(8,128)(2,1)}, bf16[96,640]{1,0:T(8,128)(2,1)}, bf16[96,384]{1,0:T(8,128)(2,1)}) custom-call(bf16[88,640]{1,0:T(8,128)(2,1)} %bitcast.28, bf16[88,640]{1,0:T(8,128)(2,1)} %bitcast.29, bf16[88,640]{1,0:T(8,128)(2,1)} %bitcast.30, bf16[88,640]{1,0:T(8,128)(2,1)} %bitcast.31, ...), custom_call_target="tpu_custom_call" | custom-call | tf_op jit(solution)/shard_map/pallas_call | solution.py:118
  3.1 3.1 %collective-permute-start.1 = (bf16[96,640]{1,0:T(8,128)(2,1)}, bf16[96,640]{1,0:T(8,128)(2,1)S(1)}, u32[]{:S(2)}, u32[]{:S(2)}) collective-permute-start(bf16[96,640]{1,0:T(8,128)(2,1)} %get-tuple-element.38), channel_id=1, source_target_pairs={{0,2},{1,3},{2,0},{3,1},{4,6},{5,7},{6,4},{7,5},{8,10},{9,11},{10,... | collective-permute-start | bytes 368648 | tf_op jit(solution)/shard_map/ppermute | solution.py:436
  6.2 1.5 %collective-permute-start.3 = (bf16[96,640]{1,0:T(8,128)(2,1)}, bf16[96,640]{1,0:T(8,128)(2,1)S(1)}, u32[]{:S(2)}, u32[]{:S(2)}) collective-permute-start(bf16[96,640]{1,0:T(8,128)(2,1)} %get-tuple-element.39), channel_id=1, source_target_pairs={{0,16},{8,24},{16,0},{24,8},{1,17},{9,25},{17,1},{25,9},{2,18},{10... | collective-permute-start | bytes 368648 | tf_op jit(solution)/shard_map/ppermute | solution.py:434
  7.7 0.0 collective-permute-start.5
  7.8 0.0 collective-permute-start
  7.8 0.9 %copy-done = bf16[96,640]{1,0:T(8,128)(2,1)S(1)} copy-done((bf16[96,640]{1,0:T(8,128)(2,1)S(1)}, bf16[96,640]{1,0:T(8,128)(2,1)}, u32[]{:S(2)}) %copy-start) | copy-done | bytes 122904
  8.7 0.6 %collective-permute-done.refs_1_ = bf16[96,384]{1,0:T(8,128)(2,1)S(1)} collective-permute-done((bf16[96,384]{1,0:T(8,128)(2,1)}, bf16[96,384]{1,0:T(8,128)(2,1)S(1)}, u32[]{:S(2)}, u32[]{:S(2)}) %collective-permute-start) | collective-permute-done | bytes 73760 | tf_op jit(solution)/shard_map/ppermute | solution.py:434
  9.2 1.0 %collective-permute-done.1.refs_2_.refs_3_.refs_5_ = bf16[96,640]{1,0:T(8,128)(2,1)S(1)} collective-permute-done((bf16[96,640]{1,0:T(8,128)(2,1)}, bf16[96,640]{1,0:T(8,128)(2,1)S(1)}, u32[]{:S(2)}, u32[]{:S(2)}) %collective-permute-start.1) | collective-permute-done | bytes 122912 | tf_op jit(solution)/shard_map/ppermute | solution.py:436
  10.3 0.0 copy-done.1
  10.3 0.2 shard_map.87.low
  10.4 2.6 %collective-permute-start.8 = (bf16[96,480]{1,0:T(8,128)(2,1)S(1)}, bf16[96,480]{1,0:T(8,128)(2,1)S(1)}, u32[]{:S(2)}, u32[]{:S(2)}) collective-permute-start(bf16[96,480]{1,0:T(8,128)(2,1)S(1)} %shard_map.87.low), channel_id=1, source_target_pairs={{0,4},{1,5},{2,6},{3,7},{4,0},{5,1},{6,2},{7,3},{8,12},{9,13},{10,... | collective-permute-start | bytes 276488 | tf_op jit(solution)/shard_map/ppermute | solution.py:436
  13.0 0.1 shard_map.90.k_low
  13.1 1.6 %collective-permute-start.7 = (bf16[96,480]{1,0:T(8,128)(2,1)S(1)}, bf16[96,480]{1,0:T(8,128)(2,1)S(1)}, u32[]{:S(2)}, u32[]{:S(2)}) collective-permute-start(bf16[96,480]{1,0:T(8,128)(2,1)S(1)} %shard_map.90.k_low), channel_id=1, source_target_pairs={{0,1},{1,0},{2,3},{3,2},{4,5},{5,4},{6,7},{7,6},{8,9},{9,8},{10,11... | collective-permute-start | bytes 276488 | tf_op jit(solution)/shard_map/ppermute | solution.py:436
  14.7 0.1 collective-permute-start.2
  14.8 0.0 collective-permute-done.3.refs_1_
  14.8 0.6 %collective-permute-start.4 = (bf16[96,384]{1,0:T(8,128)(2,1)S(1)}, bf16[96,384]{1,0:T(8,128)(2,1)S(1)}, u32[]{:S(2)}, u32[]{:S(2)}) collective-permute-start(bf16[96,384]{1,0:T(8,128)(2,1)S(1)} %slice.45), channel_id=1, source_target_pairs={{0,8},{8,0},{16,24},{24,16},{1,9},{9,1},{17,25},{25,17},{2,10},{10... | collective-permute-start | bytes 221192 | tf_op jit(solution)/shard_map/ppermute | solution.py:434
  15.4 0.0 collective-permute-done.5.refs_3_
  15.4 0.1 collective-permute-start.6
  15.5 0.6 %collective-permute-done.2.refs_0_ = bf16[96,384]{1,0:T(8,128)(2,1)S(1)} collective-permute-done((bf16[96,384]{1,0:T(8,128)(2,1)S(1)}, bf16[96,384]{1,0:T(8,128)(2,1)S(1)}, u32[]{:S(2)}, u32[]{:S(2)}) %collective-permute-start.2) | collective-permute-done | bytes 73760 | tf_op jit(solution)/shard_map/ppermute | solution.py:434
  16.1 0.2 collective-permute-done.4.refs_2_
  16.3 0.4 collective-permute-done.6.refs_4_
  16.7 0.2 shard_map.88.high
  16.9 1.4 %collective-permute-start.10 = (bf16[96,800]{1,0:T(8,128)(2,1)S(1)}, bf16[96,800]{1,0:T(8,128)(2,1)S(1)}, u32[]{:S(2)}, u32[]{:S(2)}) collective-permute-start(bf16[96,800]{1,0:T(8,128)(2,1)S(1)} %shard_map.88.high), channel_id=1, source_target_pairs={{0,4},{1,5},{2,6},{3,7},{4,0},{5,1},{6,2},{7,3},{8,12},{9,13},{10,... | collective-permute-start | bytes 460808 | tf_op jit(solution)/shard_map/ppermute | solution.py:436
  18.3 0.1 shard_map.89.k_high
  18.4 0.0 collective-permute-done.8.wire.low_far
  18.4 0.0 collective-permute-done.7.k_low
  18.5 1.6 %collective-permute-start.9 = (bf16[88,800]{1,0:T(8,128)(2,1)S(1)}, bf16[88,800]{1,0:T(8,128)(2,1)S(1)}, u32[]{:S(2)}, u32[]{:S(2)}) collective-permute-start(bf16[88,800]{1,0:T(8,128)(2,1)S(1)} %shard_map.89.k_high), channel_id=1, source_target_pairs={{0,1},{1,0},{2,3},{3,2},{4,5},{5,4},{6,7},{7,6},{8,9},{9,8},{10,11... | collective-permute-start | bytes 422408 | tf_op jit(solution)/shard_map/ppermute | solution.py:436
  20.0 1.7 %shard_map.91 = (f32[80,768]{1,0:T(8,128)S(1)}, f32[768,80]{1,0:T(8,128)S(1)}, f32[768,80]{1,0:T(8,128)S(1)}, bf16[768,80]{1,0:T(8,128)(2,1)S(1)}, bf16[768,80]{...) custom-call(bf16[96,480]{1,0:T(8,128)(2,1)S(1)} %shard_map.87.low, ...), custom_call_target="tpu_custom_call" | custom-call | tf_op jit(solution)/shard_map/pallas_call | solution.py:118
  21.7 1.0 %shard_map.92 = (f32[80,288]{1,0:T(8,128)S(1)}, f32[768,80]{1,0:T(8,128)S(1)}, f32[768,80]{1,0:T(8,128)S(1)}, bf16[288,80]{1,0:T(8,128)(2,1)S(1)}, bf16[288,80]{1,0:T(8,128)(2,1)S(1)}) custom-call(bf16[96,480]{1,0:T(8,128)(2,1)S(1)} %collective-permute-done.8.wire.low_far, bf16[768,80]{1,0:T(8,128)(2,1)S(1)} %get-tuple-element.45.k_own, ...), custom_call_target="tpu_custom_call" | custom-call | tf_op jit(solution)/shard_map/pallas_call | solution.py:118
  22.7 1.8 %collective-permute-done.9.k_high = bf16[88,800]{1,0:T(8,128)(2,1)S(1)} collective-permute-done((bf16[88,800]{1,0:T(8,128)(2,1)S(1)}, bf16[88,800]{1,0:T(8,128)(2,1)S(1)}, u32[]{:S(2)}, u32[]{:S(2)}) %collective-permute-start.9) | collective-permute-done | bytes 140832 | tf_op jit(solution)/shard_map/ppermute | solution.py:436
  24.6 2.4 %shard_map.93 = (f32[80,768]{1,0:T(8,128)S(1)}, f32[80,288]{1,0:T(8,128)S(1)}, f32[768,80]{1,0:T(8,128)S(1)}, f32[768,80]{1,0:T(8,128)S(1)}, bf16[768,80]{1,0:T(8,128)(2,1)S(1)}, /*index=5*/bf16[768,80]{1,0:T(8,128)(2,1)S(1)}) custom-call(bf16[96,480]{1,0:T(8,128)(2,1)S(1)} %shard_map.87.low, bf16[96,800]{1,0:T(8,128)(2,1)S(1)} %shard_map.88.high, ...), custom_call_target="tpu_custom_call" | custom-call | tf_op jit(solution)/shard_map/pallas_call | solution.py:118
  27.0 1.0 %collective-permute-done.10.wire = bf16[96,800]{1,0:T(8,128)(2,1)S(1)} collective-permute-done((bf16[96,800]{1,0:T(8,128)(2,1)S(1)}, bf16[96,800]{1,0:T(8,128)(2,1)S(1)}, u32[]{:S(2)}, u32[]{:S(2)}) %collective-permute-start.10) | collective-permute-done | bytes 153632 | tf_op jit(solution)/shard_map/ppermute | solution.py:436
  28.0 2.6 %shard_map.94 = (bf16[88,1280]{1,0:T(8,128)(2,1)S(1)}, bf16[88,640]{1,0:T(8,128)(2,1)S(1)}, f32[768,80]{1,0:T(8,128)S(1)}, f32[768,80]{1,0:T(8,128)S(1)}) custom-call(bf16[96,800]{1,0:T(8,128)(2,1)S(1)} %collective-permute-done.10.wire, bf16[768,80]{1,0:T(8,128)(2,1)S(1)} %get-tuple-element.55.k_far, bf16[768,80]{1,0:T(8,128)(2,1)S(1)} %get-tuple-element.56.v_far, ...), custom_call_target="tpu_custom_call" | custom-call | tf_op jit(solution)/shard_map/pallas_call | solution.py:118
  30.5 0.7 %collective-permute-start.11 = (bf16[88,1280]{1,0:T(8,128)(2,1)S(1)}, bf16[88,1280]{1,0:T(8,128)(2,1)S(1)}, u32[]{:S(2)}, u32[]{:S(2)}) collective-permute-start(bf16[88,1280]{1,0:T(8,128)(2,1)S(1)} %get-tuple-element.64), channel_id=1, source_target_pairs={{0,1},{1,0},{2,3},{3,2},{4,5},{5,4},{6,7},{7,6},{8,9},{9,8},{10,11... | collective-permute-start | bytes 675848 | tf_op jit(solution)/shard_map/ppermute | solution.py:436
  31.2 0.3 collective-permute-start.12
  31.5 0.4 shard_map.95.own
  31.9 6.6 %collective-permute-done.12.dq_wire = bf16[88,640]{1,0:T(8,128)(2,1)S(1)} collective-permute-done((bf16[88,640]{1,0:T(8,128)(2,1)S(1)}, bf16[88,640]{1,0:T(8,128)(2,1)S(1)}, u32[]{:S(2)}, u32[]{:S(2)}) %collective-permute-start.12) | collective-permute-done | bytes 112672 | tf_op jit(solution)/shard_map/ppermute | solution.py:436
  38.5 0.0 collective-permute-done.11.dkv_wire
  38.5 0.2 shard_map.96
  38.8 0.3 collective-permute-start.15
  39.1 1.3 %collective-permute-start.14 = (bf16[88,512]{1,0:T(8,128)(2,1)S(1)}, bf16[88,512]{1,0:T(8,128)(2,1)S(1)}, u32[]{:S(2)}, u32[]{:S(2)}) collective-permute-start(bf16[88,512]{1,0:T(8,128)(2,1)S(1)} %get-tuple-element.70), channel_id=1, source_target_pairs={{0,16},{8,24},{16,0},{24,8},{1,17},{9,25},{17,1},{25,9},{2,18},{10... | collective-permute-start | bytes 270344 | tf_op jit(solution)/shard_map/ppermute | solution.py:434
  40.4 1.9 %collective-permute-start.13 = (bf16[88,512]{1,0:T(8,128)(2,1)S(1)}, bf16[88,512]{1,0:T(8,128)(2,1)S(1)}, u32[]{:S(2)}, u32[]{:S(2)}) collective-permute-start(bf16[88,512]{1,0:T(8,128)(2,1)S(1)} %get-tuple-element.71), channel_id=1, source_target_pairs={{0,2},{1,3},{2,0},{3,1},{4,6},{5,7},{6,4},{7,5},{8,10},{9,11},{10,... | collective-permute-start | bytes 270344 | tf_op jit(solution)/shard_map/ppermute | solution.py:436
  42.3 2.5 %collective-permute-done.15.refs_3_ = bf16[88,512]{1,0:T(8,128)(2,1)S(1)} collective-permute-done((bf16[88,512]{1,0:T(8,128)(2,1)S(1)}, bf16[88,512]{1,0:T(8,128)(2,1)S(1)}, u32[]{:S(2)}, u32[]{:S(2)}) %collective-permute-start.15) | collective-permute-done | bytes 90144 | tf_op jit(solution)/shard_map/ppermute | solution.py:438
  44.8 0.0 collective-permute-done.14.refs_2_
  44.8 0.7 %collective-permute-done.13.refs_1_ = bf16[88,512]{1,0:T(8,128)(2,1)S(1)} collective-permute-done((bf16[88,512]{1,0:T(8,128)(2,1)S(1)}, bf16[88,512]{1,0:T(8,128)(2,1)S(1)}, u32[]{:S(2)}, u32[]{:S(2)}) %collective-permute-start.13) | collective-permute-done | bytes 90144 | tf_op jit(solution)/shard_map/ppermute | solution.py:436
  45.6 0.1 collective-permute-start.16
  45.6 1.4 %collective-permute-done.16.refs_4_ = bf16[4,88,256]{2,1,0:T(8,128)(2,1)S(1)} collective-permute-done((bf16[4,88,256]{2,1,0:T(8,128)(2,1)S(1)}, bf16[4,88,256]{2,1,0:T(8,128)(2,1)S(1)}, u32[]{:S(2)}, u32[]{:S(2)}) %collective-permute-start.16) | collective-permute-done | bytes 180256 | tf_op jit(solution)/shard_map/ppermute | solution.py:434
  47.1 0.9 %shard_map.97 = (bf16[88,640]{1,0:T(8,128)(2,1)}, bf16[88,640]{1,0:T(8,128)(2,1)}, bf16[88,640]{1,0:T(8,128)(2,1)}) custom-call(bf16[88,512]{1,0:T(8,128)(2,1)S(1)} %get-tuple-element.72.refs_0_, bf16[88,512]{1,0:T(8,128)(2,1)S(1)} %collective-permute-done.13.refs_1_, bf16[88,512]{1,0:T(8,128)(2,1)S(1)} %collective-permute-done.14.refs_2_, ...), custom_call_target="tpu_custom_call" | custom-call | tf_op jit(solution)/shard_map/pallas_call | solution.py:118
  (12 shorter events, 0.1 us)
Async XLA Ops:
  3.1 7.1 %collective-permute-start.1 = (bf16[96,640]{1,0:T(8,128)(2,1)}, bf16[96,640]{1,0:T(8,128)(2,1)S(1)}, u32[]{:S(2)}, u32[]{:S(2)}) collective-permute-start(bf16[96,640]{1,0:T(8,128)(2,1)} %get-tuple-element.38), channel_id=1, source_target_pairs={{0,2},{1,3},{2,0},{3,1},{4,6},{5,7},{6,4},{7,5},{8,10},{9,11},{10,... | collective-permute-start | bytes 368648 | tf_op jit(solution)/shard_map/ppermute | solution.py:436
  6.2 8.6 %collective-permute-start.3 = (bf16[96,640]{1,0:T(8,128)(2,1)}, bf16[96,640]{1,0:T(8,128)(2,1)S(1)}, u32[]{:S(2)}, u32[]{:S(2)}) collective-permute-start(bf16[96,640]{1,0:T(8,128)(2,1)} %get-tuple-element.39), channel_id=1, source_target_pairs={{0,16},{8,24},{16,0},{24,8},{1,17},{9,25},{17,1},{25,9},{2,18},{10... | collective-permute-start | bytes 368648 | tf_op jit(solution)/shard_map/ppermute | solution.py:434
  7.7 7.7 %collective-permute-start.5 = (bf16[96,640]{1,0:T(8,128)(2,1)}, bf16[96,640]{1,0:T(8,128)(2,1)S(1)}, u32[]{:S(2)}, u32[]{:S(2)}) collective-permute-start(bf16[96,640]{1,0:T(8,128)(2,1)} %get-tuple-element.40), channel_id=1, source_target_pairs={{0,18},{1,19},{2,16},{3,17},{4,22},{5,23},{6,20},{7,21},{8,26},{9,... | collective-permute-start | bytes 368648 | tf_op jit(solution)/shard_map/ppermute | solution.py:438
  7.8 1.5 %collective-permute-start = (bf16[96,384]{1,0:T(8,128)(2,1)}, bf16[96,384]{1,0:T(8,128)(2,1)S(1)}, u32[]{:S(2)}, u32[]{:S(2)}) collective-permute-start(bf16[96,384]{1,0:T(8,128)(2,1)} %get-tuple-element.37), channel_id=1, source_target_pairs={{0,8},{8,0},{16,24},{24,16},{1,9},{9,1},{17,25},{25,17},{2,10},{10... | collective-permute-start | bytes 221192 | tf_op jit(solution)/shard_map/ppermute | solution.py:434
  7.8 0.9 %copy-start = (bf16[96,640]{1,0:T(8,128)(2,1)S(1)}, bf16[96,640]{1,0:T(8,128)(2,1)}, u32[]{:S(2)}) copy-start(bf16[96,640]{1,0:T(8,128)(2,1)} %get-tuple-element.36.block) | copy-start | bytes 368644
  8.7 1.6 %copy-start.1 = (f32[1,2,352]{2,1,0:T(2,128)S(1)}, f32[1,2,352]{2,1,0:T(2,128)}, u32[]{:S(2)}) copy-start(f32[1,2,352]{2,1,0:T(2,128)} %param.11) | copy-start | bytes 8452
  10.4 8.0 %collective-permute-start.8 = (bf16[96,480]{1,0:T(8,128)(2,1)S(1)}, bf16[96,480]{1,0:T(8,128)(2,1)S(1)}, u32[]{:S(2)}, u32[]{:S(2)}) collective-permute-start(bf16[96,480]{1,0:T(8,128)(2,1)S(1)} %shard_map.87.low), channel_id=1, source_target_pairs={{0,4},{1,5},{2,6},{3,7},{4,0},{5,1},{6,2},{7,3},{8,12},{9,13},{10,... | collective-permute-start | bytes 276488 | tf_op jit(solution)/shard_map/ppermute | solution.py:436
  13.1 5.3 %collective-permute-start.7 = (bf16[96,480]{1,0:T(8,128)(2,1)S(1)}, bf16[96,480]{1,0:T(8,128)(2,1)S(1)}, u32[]{:S(2)}, u32[]{:S(2)}) collective-permute-start(bf16[96,480]{1,0:T(8,128)(2,1)S(1)} %shard_map.90.k_low), channel_id=1, source_target_pairs={{0,1},{1,0},{2,3},{3,2},{4,5},{5,4},{6,7},{7,6},{8,9},{9,8},{10,11... | collective-permute-start | bytes 276488 | tf_op jit(solution)/shard_map/ppermute | solution.py:436
  14.7 1.3 %collective-permute-start.2 = (bf16[96,384]{1,0:T(8,128)(2,1)S(1)}, bf16[96,384]{1,0:T(8,128)(2,1)S(1)}, u32[]{:S(2)}, u32[]{:S(2)}) collective-permute-start(bf16[96,384]{1,0:T(8,128)(2,1)S(1)} %slice.44), channel_id=1, source_target_pairs={{0,8},{8,0},{16,24},{24,16},{1,9},{9,1},{17,25},{25,17},{2,10},{10... | collective-permute-start | bytes 221192 | tf_op jit(solution)/shard_map/ppermute | solution.py:434
  14.8 1.5 %collective-permute-start.4 = (bf16[96,384]{1,0:T(8,128)(2,1)S(1)}, bf16[96,384]{1,0:T(8,128)(2,1)S(1)}, u32[]{:S(2)}, u32[]{:S(2)}) collective-permute-start(bf16[96,384]{1,0:T(8,128)(2,1)S(1)} %slice.45), channel_id=1, source_target_pairs={{0,8},{8,0},{16,24},{24,16},{1,9},{9,1},{17,25},{25,17},{2,10},{10... | collective-permute-start | bytes 221192 | tf_op jit(solution)/shard_map/ppermute | solution.py:434
  15.4 1.3 %collective-permute-start.6 = (bf16[96,384]{1,0:T(8,128)(2,1)S(1)}, bf16[96,384]{1,0:T(8,128)(2,1)S(1)}, u32[]{:S(2)}, u32[]{:S(2)}) collective-permute-start(bf16[96,384]{1,0:T(8,128)(2,1)S(1)} %slice.46), channel_id=1, source_target_pairs={{0,8},{8,0},{16,24},{24,16},{1,9},{9,1},{17,25},{25,17},{2,10},{10... | collective-permute-start | bytes 221192 | tf_op jit(solution)/shard_map/ppermute | solution.py:434
  16.9 11.0 %collective-permute-start.10 = (bf16[96,800]{1,0:T(8,128)(2,1)S(1)}, bf16[96,800]{1,0:T(8,128)(2,1)S(1)}, u32[]{:S(2)}, u32[]{:S(2)}) collective-permute-start(bf16[96,800]{1,0:T(8,128)(2,1)S(1)} %shard_map.88.high), channel_id=1, source_target_pairs={{0,4},{1,5},{2,6},{3,7},{4,0},{5,1},{6,2},{7,3},{8,12},{9,13},{10,... | collective-permute-start | bytes 460808 | tf_op jit(solution)/shard_map/ppermute | solution.py:436
  18.5 6.1 %collective-permute-start.9 = (bf16[88,800]{1,0:T(8,128)(2,1)S(1)}, bf16[88,800]{1,0:T(8,128)(2,1)S(1)}, u32[]{:S(2)}, u32[]{:S(2)}) collective-permute-start(bf16[88,800]{1,0:T(8,128)(2,1)S(1)} %shard_map.89.k_high), channel_id=1, source_target_pairs={{0,1},{1,0},{2,3},{3,2},{4,5},{5,4},{6,7},{7,6},{8,9},{9,8},{10,11... | collective-permute-start | bytes 422408 | tf_op jit(solution)/shard_map/ppermute | solution.py:436
  30.5 7.9 %collective-permute-start.11 = (bf16[88,1280]{1,0:T(8,128)(2,1)S(1)}, bf16[88,1280]{1,0:T(8,128)(2,1)S(1)}, u32[]{:S(2)}, u32[]{:S(2)}) collective-permute-start(bf16[88,1280]{1,0:T(8,128)(2,1)S(1)} %get-tuple-element.64), channel_id=1, source_target_pairs={{0,1},{1,0},{2,3},{3,2},{4,5},{5,4},{6,7},{7,6},{8,9},{9,8},{10,11... | collective-permute-start | bytes 675848 | tf_op jit(solution)/shard_map/ppermute | solution.py:436
  31.2 7.3 %collective-permute-start.12 = (bf16[88,640]{1,0:T(8,128)(2,1)S(1)}, bf16[88,640]{1,0:T(8,128)(2,1)S(1)}, u32[]{:S(2)}, u32[]{:S(2)}) collective-permute-start(bf16[88,640]{1,0:T(8,128)(2,1)S(1)} %get-tuple-element.65), channel_id=1, source_target_pairs={{0,4},{1,5},{2,6},{3,7},{4,0},{5,1},{6,2},{7,3},{8,12},{9,13},{10,... | collective-permute-start | bytes 337928 | tf_op jit(solution)/shard_map/ppermute | solution.py:436
  38.8 6.0 %collective-permute-start.15 = (bf16[88,512]{1,0:T(8,128)(2,1)S(1)}, bf16[88,512]{1,0:T(8,128)(2,1)S(1)}, u32[]{:S(2)}, u32[]{:S(2)}) collective-permute-start(bf16[88,512]{1,0:T(8,128)(2,1)S(1)} %get-tuple-element.69), channel_id=1, source_target_pairs={{0,18},{1,19},{2,16},{3,17},{4,22},{5,23},{6,20},{7,21},{8,26},{9,... | collective-permute-start | bytes 270344 | tf_op jit(solution)/shard_map/ppermute | solution.py:438
  39.1 5.7 %collective-permute-start.14 = (bf16[88,512]{1,0:T(8,128)(2,1)S(1)}, bf16[88,512]{1,0:T(8,128)(2,1)S(1)}, u32[]{:S(2)}, u32[]{:S(2)}) collective-permute-start(bf16[88,512]{1,0:T(8,128)(2,1)S(1)} %get-tuple-element.70), channel_id=1, source_target_pairs={{0,16},{8,24},{16,0},{24,8},{1,17},{9,25},{17,1},{25,9},{2,18},{10... | collective-permute-start | bytes 270344 | tf_op jit(solution)/shard_map/ppermute | solution.py:434
  40.4 5.1 %collective-permute-start.13 = (bf16[88,512]{1,0:T(8,128)(2,1)S(1)}, bf16[88,512]{1,0:T(8,128)(2,1)S(1)}, u32[]{:S(2)}, u32[]{:S(2)}) collective-permute-start(bf16[88,512]{1,0:T(8,128)(2,1)S(1)} %get-tuple-element.71), channel_id=1, source_target_pairs={{0,2},{1,3},{2,0},{3,1},{4,6},{5,7},{6,4},{7,5},{8,10},{9,11},{10,... | collective-permute-start | bytes 270344 | tf_op jit(solution)/shard_map/ppermute | solution.py:436
  45.6 1.5 %collective-permute-start.16 = (bf16[4,88,256]{2,1,0:T(8,128)(2,1)S(1)}, bf16[4,88,256]{2,1,0:T(8,128)(2,1)S(1)}, u32[]{:S(2)}, u32[]{:S(2)}) collective-permute-start(bf16[4,88,256]{2,1,0:T(8,128)(2,1)S(1)} %pad_maximum_fusion), channel_id=1, source_target_pairs={{0,8},{8,0},{16,24},{24,16},{1,9},{9,1},{17,25},{25,17},{2,10},{10... | collective-permute-start | bytes 540680 | tf_op jit(solution)/shard_map/ppermute | solution.py:434

commit v8 on v7

--- a/solution.py
+++ b/solution.py
@@ -251,16 +251,14 @@
         [own[:, rows * i : rows * (i + 1)] for i in range(4)] + [near], axis=0
     )
     lower = []
-    gap = jnp.zeros((6, PADDED - rows), F32)
     for (j, r), ref in zip(spots, parts):
         delta = ref[rows:PADDED, 0:128].astype(F32)[0:3, 0:rows]
         lse = lse_s[pl.ds(4 * (j % 2) + (h ^ (2 * (j // 2) + r)), 1), :]
-        lower += [jnp.concatenate([delta, pieces_of(lse)], axis=0), gap]
-    wire[0:rows] = jnp.concatenate([ref[0:rows, 0:160] for ref in parts], axis=1)
-    width = wire.shape[1] - len(parts) * PADDED
-    lower = jnp.concatenate(lower + [jnp.zeros((6, width), F32)], axis=1)
-    lower = jnp.concatenate([lower, jnp.zeros((2, wire.shape[1]), F32)], axis=0)
-    wire[rows:PADDED] = lower.astype(BF16)
+        lower += [delta, pieces_of(lse)]
+    lower = jnp.concatenate(lower + [jnp.zeros((32 - 6 * len(parts), rows), F32)], axis=0)
+    wire[...] = jnp.concatenate(
+        [ref[0:rows, 0:160] for ref in parts] + [lower.T.astype(BF16)], axis=1
+    )
 
 
 def gather_keys_kernel(spots, *refs):
@@ -276,15 +274,16 @@
 
 
 def rows_of(wires):
-    rows = PADDED - 8
-    below = jnp.concatenate(
-        [
-            wire[rows:PADDED, 0 : wire.shape[1] // (2 * HDIM) * PADDED].astype(F32)
-            for wire in wires
-        ],
-        axis=1,
-    )
-    return below[3:4] + below[4:5] + below[5:6], below[0:1] + below[1:2] + below[2:3]
+    lse, delta = [], []
+    for wire in wires:
+        rows = wire.shape[0]
+        count = wire.shape[1] // (2 * HDIM)
+        gap = jnp.zeros((1, PADDED - rows), F32)
+        pieces = wire[:, 2 * HDIM * count : 2 * HDIM * count + 32].astype(F32).T
+        for i in range(0, 6 * count, 6):
+            delta += [pieces[i : i + 1] + pieces[i + 1 : i + 2] + pieces[i + 2 : i + 3], gap]
+            lse += [pieces[i + 3 : i + 4] + pieces[i + 4 : i + 5] + pieces[i + 5 : i + 6], gap]
+    return jnp.concatenate(lse, axis=1), jnp.concatenate(delta, axis=1)
 
 
 def spread(wide, left, right, first=0):
@@ -467,7 +466,7 @@
     def gather_queries(first, last):
         return call(
             functools.partial(gather_queries_kernel, spots[first:last]),
-            shape(PADDED, 160 * (last - first)),
+            shape(rows, 160 * (last - first) + 32),
             *blocks[first:last], near[0], lse[0],
             scratch=[pltpu.VMEM((8, rows), F32)],
         )

time: 48.1 us -> 48 us (level)
  waiting for transfers between devices: 16.8 us -> 15.4 us
  starting transfers between devices: 17.1 us -> 17.8 us
  Pallas kernels: 12.3 us -> 12.8 us
    ppermute x8, waiting for transfers between devices: 11.1 us -> 10 us  [flipped(): return lax.ppermute(array, 'blk', [(i, i ^ blk_bits) for i in range(blks)])]
    ppermute x8, starting transfers between devices: 13.2 us -> 14 us  [flipped(): return lax.ppermute(array, 'blk', [(i, i ^ blk_bits) for i in range(blks)])]
    pallas_call x13, Pallas kernels: 12.3 us -> 12.8 us  [call(): pl.pallas_call(kernel, out_shape=out_shape, in_specs=specs, out_specs=jax...]
  transfers between devices with their start and end apart: 17 -> 17, of which waited for: 11 -> 11; matrix products, arithmetic and copies ran while one was open for 0% -> 0% of each run, Pallas kernels for 13% -> 14%
where the time goes in v8:
time: 48 us; the launch traced here: 47.8 us
  starting transfers between devices  17.8 us (37%)
  waiting for transfers between devices  15.4 us (32%)
  Pallas kernels  12.8 us (27%)
  local copies, waits for them, and re-layouts  0.98 us (2%)
  between operations  0.8 us (2%)
    ppermute x8, starting transfers between devices, flipped(): return lax.ppermute(array, 'blk', [(i, i ^ blk_bits) for i in range(blks)])  14 us
    pallas_call x13, Pallas kernels, call(): pl.pallas_call(kernel, out_shape=out_shape, in_specs=specs, out_specs=jax...  12.8 us
    ppermute x8, waiting for transfers between devices, flipped(): return lax.ppermute(array, 'blk', [(i, i ^ blk_bits) for i in range(blks)])  10 us
    ppermute x7, starting transfers between devices, flipped(): lax.ppermute(array, 'head', [(i, i ^ head_bits) for i in range(heads)])  3.68 us
    ppermute x7, waiting for transfers between devices, flipped(): lax.ppermute(array, 'head', [(i, i ^ head_bits) for i in range(heads)])  3.24 us
    ppermute x2, waiting for transfers between devices, flipped(): lax.ppermute(array, ('head', 'blk'), [(i, i ^ bits) for i in range(heads...  2.13 us
  transfers between devices with their start and end apart: 17, of which 11 were waited for; matrix products, arithmetic and copies ran while one was open for 0% of the time, Pallas kernels for 14%

profile of v8, /device:TPU:0, one launch (start us, length us, event | category | flops | bytes accessed | tf_op | source)
XLA Modules:
  0.0 47.8 jit_solution(2818164542187913601)
XLA Ops:
  0.6 2.5 %shard_map.85 = (bf16[96,640]{1,0:T(8,128)(2,1)}, bf16[96,640]{1,0:T(8,128)(2,1)}, bf16[96,640]{1,0:T(8,128)(2,1)}, bf16[96,640]{1,0:T(8,128)(2,1)}, bf16[96,384]{1,0:T(8,128)(2,1)}) custom-call(bf16[88,640]{1,0:T(8,128)(2,1)} %bitcast.28, bf16[88,640]{1,0:T(8,128)(2,1)} %bitcast.29, bf16[88,640]{1,0:T(8,128)(2,1)} %bitcast.30, bf16[88,640]{1,0:T(8,128)(2,1)} %bitcast.31, ...), custom_call_target="tpu_custom_call" | custom-call | tf_op jit(solution)/shard_map/pallas_call | solution.py:118
  3.1 3.1 %collective-permute-start.1 = (bf16[96,640]{1,0:T(8,128)(2,1)}, bf16[96,640]{1,0:T(8,128)(2,1)S(1)}, u32[]{:S(2)}, u32[]{:S(2)}) collective-permute-start(bf16[96,640]{1,0:T(8,128)(2,1)} %get-tuple-element.38), channel_id=1, source_target_pairs={{0,2},{1,3},{2,0},{3,1},{4,6},{5,7},{6,4},{7,5},{8,10},{9,11},{10,... | collective-permute-start | bytes 368648 | tf_op jit(solution)/shard_map/ppermute | solution.py:435
  6.2 1.5 %collective-permute-start.3 = (bf16[96,640]{1,0:T(8,128)(2,1)}, bf16[96,640]{1,0:T(8,128)(2,1)S(1)}, u32[]{:S(2)}, u32[]{:S(2)}) collective-permute-start(bf16[96,640]{1,0:T(8,128)(2,1)} %get-tuple-element.39), channel_id=1, source_target_pairs={{0,16},{8,24},{16,0},{24,8},{1,17},{9,25},{17,1},{25,9},{2,18},{10... | collective-permute-start | bytes 368648 | tf_op jit(solution)/shard_map/ppermute | solution.py:433
  7.7 0.0 collective-permute-start.5
  7.8 0.0 collective-permute-start
  7.8 0.9 %copy-done = bf16[96,640]{1,0:T(8,128)(2,1)S(1)} copy-done((bf16[96,640]{1,0:T(8,128)(2,1)S(1)}, bf16[96,640]{1,0:T(8,128)(2,1)}, u32[]{:S(2)}) %copy-start) | copy-done | bytes 122904
  8.7 0.0 copy-start.1
  8.7 0.5 %collective-permute-done.refs_1_ = bf16[96,384]{1,0:T(8,128)(2,1)S(1)} collective-permute-done((bf16[96,384]{1,0:T(8,128)(2,1)}, bf16[96,384]{1,0:T(8,128)(2,1)S(1)}, u32[]{:S(2)}, u32[]{:S(2)}) %collective-permute-start) | collective-permute-done | bytes 73760 | tf_op jit(solution)/shard_map/ppermute | solution.py:433
  9.2 1.0 %collective-permute-done.1.refs_2_.refs_3_.refs_5_ = bf16[96,640]{1,0:T(8,128)(2,1)S(1)} collective-permute-done((bf16[96,640]{1,0:T(8,128)(2,1)}, bf16[96,640]{1,0:T(8,128)(2,1)S(1)}, u32[]{:S(2)}, u32[]{:S(2)}) %collective-permute-start.1) | collective-permute-done | bytes 122912 | tf_op jit(solution)/shard_map/ppermute | solution.py:435
  10.3 0.1 shard_map.90.k_low
  10.4 1.6 %collective-permute-start.7 = (bf16[96,480]{1,0:T(8,128)(2,1)S(1)}, bf16[96,480]{1,0:T(8,128)(2,1)S(1)}, u32[]{:S(2)}, u32[]{:S(2)}) collective-permute-start(bf16[96,480]{1,0:T(8,128)(2,1)S(1)} %shard_map.90.k_low), channel_id=1, source_target_pairs={{0,1},{1,0},{2,3},{3,2},{4,5},{5,4},{6,7},{7,6},{8,9},{9,8},{10,11... | collective-permute-start | bytes 276488 | tf_op jit(solution)/shard_map/ppermute | solution.py:435
  11.9 0.3 shard_map.87.low
  12.2 2.7 %collective-permute-start.8 = (bf16[88,512]{1,0:T(8,128)(2,1)S(1)}, bf16[88,512]{1,0:T(8,128)(2,1)S(1)}, u32[]{:S(2)}, u32[]{:S(2)}) collective-permute-start(bf16[88,512]{1,0:T(8,128)(2,1)S(1)} %shard_map.87.low), channel_id=1, source_target_pairs={{0,4},{1,5},{2,6},{3,7},{4,0},{5,1},{6,2},{7,3},{8,12},{9,13},{10,... | collective-permute-start | bytes 270344 | tf_op jit(solution)/shard_map/ppermute | solution.py:435
  14.9 0.1 collective-permute-start.2
  14.9 0.0 collective-permute-done.3.refs_1_
  15.0 0.6 %collective-permute-start.4 = (bf16[96,384]{1,0:T(8,128)(2,1)S(1)}, bf16[96,384]{1,0:T(8,128)(2,1)S(1)}, u32[]{:S(2)}, u32[]{:S(2)}) collective-permute-start(bf16[96,384]{1,0:T(8,128)(2,1)S(1)} %slice.45), channel_id=1, source_target_pairs={{0,8},{8,0},{16,24},{24,16},{1,9},{9,1},{17,25},{25,17},{2,10},{10... | collective-permute-start | bytes 221192 | tf_op jit(solution)/shard_map/ppermute | solution.py:433
  15.5 0.0 collective-permute-done.5.refs_3_
  15.5 0.1 collective-permute-start.6
  15.6 0.6 %collective-permute-done.2.refs_0_ = bf16[96,384]{1,0:T(8,128)(2,1)S(1)} collective-permute-done((bf16[96,384]{1,0:T(8,128)(2,1)S(1)}, bf16[96,384]{1,0:T(8,128)(2,1)S(1)}, u32[]{:S(2)}, u32[]{:S(2)}) %collective-permute-start.2) | collective-permute-done | bytes 73760 | tf_op jit(solution)/shard_map/ppermute | solution.py:433
  16.2 0.2 collective-permute-done.4.refs_2_
  16.4 0.4 collective-permute-done.6.refs_4_
  16.9 0.3 shard_map.88.high
  17.1 1.3 %collective-permute-start.10 = (bf16[88,832]{1,0:T(8,128)(2,1)S(1)}, bf16[88,832]{1,0:T(8,128)(2,1)S(1)}, u32[]{:S(2)}, u32[]{:S(2)}) collective-permute-start(bf16[88,832]{1,0:T(8,128)(2,1)S(1)} %shard_map.88.high), channel_id=1, source_target_pairs={{0,4},{1,5},{2,6},{3,7},{4,0},{5,1},{6,2},{7,3},{8,12},{9,13},{10,... | collective-permute-start | bytes 439304 | tf_op jit(solution)/shard_map/ppermute | solution.py:435
  18.4 0.1 shard_map.89.k_high
  18.6 0.0 collective-permute-done.8.wire.low_far
  18.6 0.0 collective-permute-done.7.k_low
  18.6 1.6 %collective-permute-start.9 = (bf16[88,800]{1,0:T(8,128)(2,1)S(1)}, bf16[88,800]{1,0:T(8,128)(2,1)S(1)}, u32[]{:S(2)}, u32[]{:S(2)}) collective-permute-start(bf16[88,800]{1,0:T(8,128)(2,1)S(1)} %shard_map.89.k_high), channel_id=1, source_target_pairs={{0,1},{1,0},{2,3},{3,2},{4,5},{5,4},{6,7},{7,6},{8,9},{9,8},{10,11... | collective-permute-start | bytes 422408 | tf_op jit(solution)/shard_map/ppermute | solution.py:435
  20.2 1.8 %shard_map.91 = (f32[80,768]{1,0:T(8,128)S(1)}, f32[768,80]{1,0:T(8,128)S(1)}, f32[768,80]{1,0:T(8,128)S(1)}, bf16[768,80]{1,0:T(8,128)(2,1)S(1)}, bf16[768,80]{...) custom-call(bf16[88,512]{1,0:T(8,128)(2,1)S(1)} %shard_map.87.low, ...), custom_call_target="tpu_custom_call" | custom-call | tf_op jit(solution)/shard_map/pallas_call | solution.py:118
  21.9 1.0 %shard_map.92 = (f32[80,288]{1,0:T(8,128)S(1)}, f32[768,80]{1,0:T(8,128)S(1)}, f32[768,80]{1,0:T(8,128)S(1)}, bf16[288,80]{1,0:T(8,128)(2,1)S(1)}, bf16[288,80]{1,0:T(8,128)(2,1)S(1)}) custom-call(bf16[88,512]{1,0:T(8,128)(2,1)S(1)} %collective-permute-done.8.wire.low_far, bf16[768,80]{1,0:T(8,128)(2,1)S(1)} %get-tuple-element.45.k_own, ...), custom_call_target="tpu_custom_call" | custom-call | tf_op jit(solution)/shard_map/pallas_call | solution.py:118
  23.0 1.7 %collective-permute-done.9.k_high = bf16[88,800]{1,0:T(8,128)(2,1)S(1)} collective-permute-done((bf16[88,800]{1,0:T(8,128)(2,1)S(1)}, bf16[88,800]{1,0:T(8,128)(2,1)S(1)}, u32[]{:S(2)}, u32[]{:S(2)}) %collective-permute-start.9) | collective-permute-done | bytes 140832 | tf_op jit(solution)/shard_map/ppermute | solution.py:435
  24.7 2.6 %shard_map.93 = (f32[80,768]{1,0:T(8,128)S(1)}, f32[80,288]{1,0:T(8,128)S(1)}, f32[768,80]{1,0:T(8,128)S(1)}, f32[768,80]{1,0:T(8,128)S(1)}, bf16[768,80]{1,0:T(8,128)(2,1)S(1)}, /*index=5*/bf16[768,80]{1,0:T(8,128)(2,1)S(1)}) custom-call(bf16[88,512]{1,0:T(8,128)(2,1)S(1)} %shard_map.87.low, bf16[88,832]{1,0:T(8,128)(2,1)S(1)} %shard_map.88.high, ...), custom_call_target="tpu_custom_call" | custom-call | tf_op jit(solution)/shard_map/pallas_call | solution.py:118
  27.3 0.3 collective-permute-done.10.wire
  27.6 2.7 %shard_map.94 = (bf16[88,1280]{1,0:T(8,128)(2,1)S(1)}, bf16[88,640]{1,0:T(8,128)(2,1)S(1)}, f32[768,80]{1,0:T(8,128)S(1)}, f32[768,80]{1,0:T(8,128)S(1)}) custom-call(bf16[88,832]{1,0:T(8,128)(2,1)S(1)} %collective-permute-done.10.wire, bf16[768,80]{1,0:T(8,128)(2,1)S(1)} %get-tuple-element.55.k_far, bf16[768,80]{1,0:T(8,128)(2,1)S(1)} %get-tuple-element.56.v_far, ...), custom_call_target="tpu_custom_call" | custom-call | tf_op jit(solution)/shard_map/pallas_call | solution.py:118
  30.3 1.3 %collective-permute-start.11 = (bf16[88,1280]{1,0:T(8,128)(2,1)S(1)}, bf16[88,1280]{1,0:T(8,128)(2,1)S(1)}, u32[]{:S(2)}, u32[]{:S(2)}) collective-permute-start(bf16[88,1280]{1,0:T(8,128)(2,1)S(1)} %get-tuple-element.64), channel_id=1, source_target_pairs={{0,1},{1,0},{2,3},{3,2},{4,5},{5,4},{6,7},{7,6},{8,9},{9,8},{10,11... | collective-permute-start | bytes 675848 | tf_op jit(solution)/shard_map/ppermute | solution.py:435
  31.5 0.5 %collective-permute-start.12 = (bf16[88,640]{1,0:T(8,128)(2,1)S(1)}, bf16[88,640]{1,0:T(8,128)(2,1)S(1)}, u32[]{:S(2)}, u32[]{:S(2)}) collective-permute-start(bf16[88,640]{1,0:T(8,128)(2,1)S(1)} %get-tuple-element.65), channel_id=1, source_target_pairs={{0,4},{1,5},{2,6},{3,7},{4,0},{5,1},{6,2},{7,3},{8,12},{9,13},{10,... | collective-permute-start | bytes 337928 | tf_op jit(solution)/shard_map/ppermute | solution.py:435
  32.0 0.4 shard_map.95.own
  32.4 6.3 %collective-permute-done.12.dq_wire = bf16[88,640]{1,0:T(8,128)(2,1)S(1)} collective-permute-done((bf16[88,640]{1,0:T(8,128)(2,1)S(1)}, bf16[88,640]{1,0:T(8,128)(2,1)S(1)}, u32[]{:S(2)}, u32[]{:S(2)}) %collective-permute-start.12) | collective-permute-done | bytes 112672 | tf_op jit(solution)/shard_map/ppermute | solution.py:435
  38.7 0.0 collective-permute-done.11.dkv_wire
  38.7 0.2 shard_map.96
  39.0 0.1 collective-permute-start.15
  39.1 1.4 %collective-permute-start.14 = (bf16[88,512]{1,0:T(8,128)(2,1)S(1)}, bf16[88,512]{1,0:T(8,128)(2,1)S(1)}, u32[]{:S(2)}, u32[]{:S(2)}) collective-permute-start(bf16[88,512]{1,0:T(8,128)(2,1)S(1)} %get-tuple-element.70), channel_id=1, source_target_pairs={{0,16},{8,24},{16,0},{24,8},{1,17},{9,25},{17,1},{25,9},{2,18},{10... | collective-permute-start | bytes 270344 | tf_op jit(solution)/shard_map/ppermute | solution.py:433
  40.5 2.1 %collective-permute-start.13 = (bf16[88,512]{1,0:T(8,128)(2,1)S(1)}, bf16[88,512]{1,0:T(8,128)(2,1)S(1)}, u32[]{:S(2)}, u32[]{:S(2)}) collective-permute-start(bf16[88,512]{1,0:T(8,128)(2,1)S(1)} %get-tuple-element.71), channel_id=1, source_target_pairs={{0,2},{1,3},{2,0},{3,1},{4,6},{5,7},{6,4},{7,5},{8,10},{9,11},{10,... | collective-permute-start | bytes 270344 | tf_op jit(solution)/shard_map/ppermute | solution.py:435
  42.6 2.1 %collective-permute-done.15.refs_3_ = bf16[88,512]{1,0:T(8,128)(2,1)S(1)} collective-permute-done((bf16[88,512]{1,0:T(8,128)(2,1)S(1)}, bf16[88,512]{1,0:T(8,128)(2,1)S(1)}, u32[]{:S(2)}, u32[]{:S(2)}) %collective-permute-start.15) | collective-permute-done | bytes 90144 | tf_op jit(solution)/shard_map/ppermute | solution.py:437
  44.7 0.0 collective-permute-done.14.refs_2_
  44.7 0.6 %collective-permute-done.13.refs_1_ = bf16[88,512]{1,0:T(8,128)(2,1)S(1)} collective-permute-done((bf16[88,512]{1,0:T(8,128)(2,1)S(1)}, bf16[88,512]{1,0:T(8,128)(2,1)S(1)}, u32[]{:S(2)}, u32[]{:S(2)}) %collective-permute-start.13) | collective-permute-done | bytes 90144 | tf_op jit(solution)/shard_map/ppermute | solution.py:435
  45.4 0.1 collective-permute-start.16
  45.5 1.4 %collective-permute-done.16.refs_4_ = bf16[4,88,256]{2,1,0:T(8,128)(2,1)S(1)} collective-permute-done((bf16[4,88,256]{2,1,0:T(8,128)(2,1)S(1)}, bf16[4,88,256]{2,1,0:T(8,128)(2,1)S(1)}, u32[]{:S(2)}, u32[]{:S(2)}) %collective-permute-start.16) | collective-permute-done | bytes 180256 | tf_op jit(solution)/shard_map/ppermute | solution.py:433
  46.9 0.9 %shard_map.97 = (bf16[88,640]{1,0:T(8,128)(2,1)}, bf16[88,640]{1,0:T(8,128)(2,1)}, bf16[88,640]{1,0:T(8,128)(2,1)}) custom-call(bf16[88,512]{1,0:T(8,128)(2,1)S(1)} %get-tuple-element.72.refs_0_, bf16[88,512]{1,0:T(8,128)(2,1)S(1)} %collective-permute-done.13.refs_1_, bf16[88,512]{1,0:T(8,128)(2,1)S(1)} %collective-permute-done.14.refs_2_, ...), custom_call_target="tpu_custom_call" | custom-call | tf_op jit(solution)/shard_map/pallas_call | solution.py:118
  (12 shorter events, 0.1 us)
Async XLA Ops:
  3.1 7.1 %collective-permute-start.1 = (bf16[96,640]{1,0:T(8,128)(2,1)}, bf16[96,640]{1,0:T(8,128)(2,1)S(1)}, u32[]{:S(2)}, u32[]{:S(2)}) collective-permute-start(bf16[96,640]{1,0:T(8,128)(2,1)} %get-tuple-element.38), channel_id=1, source_target_pairs={{0,2},{1,3},{2,0},{3,1},{4,6},{5,7},{6,4},{7,5},{8,10},{9,11},{10,... | collective-permute-start | bytes 368648 | tf_op jit(solution)/shard_map/ppermute | solution.py:435
  6.2 8.7 %collective-permute-start.3 = (bf16[96,640]{1,0:T(8,128)(2,1)}, bf16[96,640]{1,0:T(8,128)(2,1)S(1)}, u32[]{:S(2)}, u32[]{:S(2)}) collective-permute-start(bf16[96,640]{1,0:T(8,128)(2,1)} %get-tuple-element.39), channel_id=1, source_target_pairs={{0,16},{8,24},{16,0},{24,8},{1,17},{9,25},{17,1},{25,9},{2,18},{10... | collective-permute-start | bytes 368648 | tf_op jit(solution)/shard_map/ppermute | solution.py:433
  7.7 7.8 %collective-permute-start.5 = (bf16[96,640]{1,0:T(8,128)(2,1)}, bf16[96,640]{1,0:T(8,128)(2,1)S(1)}, u32[]{:S(2)}, u32[]{:S(2)}) collective-permute-start(bf16[96,640]{1,0:T(8,128)(2,1)} %get-tuple-element.40), channel_id=1, source_target_pairs={{0,18},{1,19},{2,16},{3,17},{4,22},{5,23},{6,20},{7,21},{8,26},{9,... | collective-permute-start | bytes 368648 | tf_op jit(solution)/shard_map/ppermute | solution.py:437
  7.8 1.5 %collective-permute-start = (bf16[96,384]{1,0:T(8,128)(2,1)}, bf16[96,384]{1,0:T(8,128)(2,1)S(1)}, u32[]{:S(2)}, u32[]{:S(2)}) collective-permute-start(bf16[96,384]{1,0:T(8,128)(2,1)} %get-tuple-element.37), channel_id=1, source_target_pairs={{0,8},{8,0},{16,24},{24,16},{1,9},{9,1},{17,25},{25,17},{2,10},{10... | collective-permute-start | bytes 221192 | tf_op jit(solution)/shard_map/ppermute | solution.py:433
  7.8 0.9 %copy-start = (bf16[96,640]{1,0:T(8,128)(2,1)S(1)}, bf16[96,640]{1,0:T(8,128)(2,1)}, u32[]{:S(2)}) copy-start(bf16[96,640]{1,0:T(8,128)(2,1)} %get-tuple-element.36.block) | copy-start | bytes 368644
  8.7 3.3 %copy-start.1 = (f32[1,2,352]{2,1,0:T(2,128)S(1)}, f32[1,2,352]{2,1,0:T(2,128)}, u32[]{:S(2)}) copy-start(f32[1,2,352]{2,1,0:T(2,128)} %param.11) | copy-start | bytes 8452
  10.4 8.2 %collective-permute-start.7 = (bf16[96,480]{1,0:T(8,128)(2,1)S(1)}, bf16[96,480]{1,0:T(8,128)(2,1)S(1)}, u32[]{:S(2)}, u32[]{:S(2)}) collective-permute-start(bf16[96,480]{1,0:T(8,128)(2,1)S(1)} %shard_map.90.k_low), channel_id=1, source_target_pairs={{0,1},{1,0},{2,3},{3,2},{4,5},{5,4},{6,7},{7,6},{8,9},{9,8},{10,11... | collective-permute-start | bytes 276488 | tf_op jit(solution)/shard_map/ppermute | solution.py:435
  12.2 6.4 %collective-permute-start.8 = (bf16[88,512]{1,0:T(8,128)(2,1)S(1)}, bf16[88,512]{1,0:T(8,128)(2,1)S(1)}, u32[]{:S(2)}, u32[]{:S(2)}) collective-permute-start(bf16[88,512]{1,0:T(8,128)(2,1)S(1)} %shard_map.87.low), channel_id=1, source_target_pairs={{0,4},{1,5},{2,6},{3,7},{4,0},{5,1},{6,2},{7,3},{8,12},{9,13},{10,... | collective-permute-start | bytes 270344 | tf_op jit(solution)/shard_map/ppermute | solution.py:435
  14.9 1.3 %collective-permute-start.2 = (bf16[96,384]{1,0:T(8,128)(2,1)S(1)}, bf16[96,384]{1,0:T(8,128)(2,1)S(1)}, u32[]{:S(2)}, u32[]{:S(2)}) collective-permute-start(bf16[96,384]{1,0:T(8,128)(2,1)S(1)} %slice.44), channel_id=1, source_target_pairs={{0,8},{8,0},{16,24},{24,16},{1,9},{9,1},{17,25},{25,17},{2,10},{10... | collective-permute-start | bytes 221192 | tf_op jit(solution)/shard_map/ppermute | solution.py:433
  15.0 1.5 %collective-permute-start.4 = (bf16[96,384]{1,0:T(8,128)(2,1)S(1)}, bf16[96,384]{1,0:T(8,128)(2,1)S(1)}, u32[]{:S(2)}, u32[]{:S(2)}) collective-permute-start(bf16[96,384]{1,0:T(8,128)(2,1)S(1)} %slice.45), channel_id=1, source_target_pairs={{0,8},{8,0},{16,24},{24,16},{1,9},{9,1},{17,25},{25,17},{2,10},{10... | collective-permute-start | bytes 221192 | tf_op jit(solution)/shard_map/ppermute | solution.py:433
  15.5 1.3 %collective-permute-start.6 = (bf16[96,384]{1,0:T(8,128)(2,1)S(1)}, bf16[96,384]{1,0:T(8,128)(2,1)S(1)}, u32[]{:S(2)}, u32[]{:S(2)}) collective-permute-start(bf16[96,384]{1,0:T(8,128)(2,1)S(1)} %slice.46), channel_id=1, source_target_pairs={{0,8},{8,0},{16,24},{24,16},{1,9},{9,1},{17,25},{25,17},{2,10},{10... | collective-permute-start | bytes 221192 | tf_op jit(solution)/shard_map/ppermute | solution.py:433
  17.1 10.5 %collective-permute-start.10 = (bf16[88,832]{1,0:T(8,128)(2,1)S(1)}, bf16[88,832]{1,0:T(8,128)(2,1)S(1)}, u32[]{:S(2)}, u32[]{:S(2)}) collective-permute-start(bf16[88,832]{1,0:T(8,128)(2,1)S(1)} %shard_map.88.high), channel_id=1, source_target_pairs={{0,4},{1,5},{2,6},{3,7},{4,0},{5,1},{6,2},{7,3},{8,12},{9,13},{10,... | collective-permute-start | bytes 439304 | tf_op jit(solution)/shard_map/ppermute | solution.py:435
  18.6 6.1 %collective-permute-start.9 = (bf16[88,800]{1,0:T(8,128)(2,1)S(1)}, bf16[88,800]{1,0:T(8,128)(2,1)S(1)}, u32[]{:S(2)}, u32[]{:S(2)}) collective-permute-start(bf16[88,800]{1,0:T(8,128)(2,1)S(1)} %shard_map.89.k_high), channel_id=1, source_target_pairs={{0,1},{1,0},{2,3},{3,2},{4,5},{5,4},{6,7},{7,6},{8,9},{9,8},{10,11... | collective-permute-start | bytes 422408 | tf_op jit(solution)/shard_map/ppermute | solution.py:435
  30.3 8.4 %collective-permute-start.11 = (bf16[88,1280]{1,0:T(8,128)(2,1)S(1)}, bf16[88,1280]{1,0:T(8,128)(2,1)S(1)}, u32[]{:S(2)}, u32[]{:S(2)}) collective-permute-start(bf16[88,1280]{1,0:T(8,128)(2,1)S(1)} %get-tuple-element.64), channel_id=1, source_target_pairs={{0,1},{1,0},{2,3},{3,2},{4,5},{5,4},{6,7},{7,6},{8,9},{9,8},{10,11... | collective-permute-start | bytes 675848 | tf_op jit(solution)/shard_map/ppermute | solution.py:435
  31.5 7.2 %collective-permute-start.12 = (bf16[88,640]{1,0:T(8,128)(2,1)S(1)}, bf16[88,640]{1,0:T(8,128)(2,1)S(1)}, u32[]{:S(2)}, u32[]{:S(2)}) collective-permute-start(bf16[88,640]{1,0:T(8,128)(2,1)S(1)} %get-tuple-element.65), channel_id=1, source_target_pairs={{0,4},{1,5},{2,6},{3,7},{4,0},{5,1},{6,2},{7,3},{8,12},{9,13},{10,... | collective-permute-start | bytes 337928 | tf_op jit(solution)/shard_map/ppermute | solution.py:435
  39.0 5.7 %collective-permute-start.15 = (bf16[88,512]{1,0:T(8,128)(2,1)S(1)}, bf16[88,512]{1,0:T(8,128)(2,1)S(1)}, u32[]{:S(2)}, u32[]{:S(2)}) collective-permute-start(bf16[88,512]{1,0:T(8,128)(2,1)S(1)} %get-tuple-element.69), channel_id=1, source_target_pairs={{0,18},{1,19},{2,16},{3,17},{4,22},{5,23},{6,20},{7,21},{8,26},{9,... | collective-permute-start | bytes 270344 | tf_op jit(solution)/shard_map/ppermute | solution.py:437
  39.1 5.7 %collective-permute-start.14 = (bf16[88,512]{1,0:T(8,128)(2,1)S(1)}, bf16[88,512]{1,0:T(8,128)(2,1)S(1)}, u32[]{:S(2)}, u32[]{:S(2)}) collective-permute-start(bf16[88,512]{1,0:T(8,128)(2,1)S(1)} %get-tuple-element.70), channel_id=1, source_target_pairs={{0,16},{8,24},{16,0},{24,8},{1,17},{9,25},{17,1},{25,9},{2,18},{10... | collective-permute-start | bytes 270344 | tf_op jit(solution)/shard_map/ppermute | solution.py:433
  40.5 4.9 %collective-permute-start.13 = (bf16[88,512]{1,0:T(8,128)(2,1)S(1)}, bf16[88,512]{1,0:T(8,128)(2,1)S(1)}, u32[]{:S(2)}, u32[]{:S(2)}) collective-permute-start(bf16[88,512]{1,0:T(8,128)(2,1)S(1)} %get-tuple-element.71), channel_id=1, source_target_pairs={{0,2},{1,3},{2,0},{3,1},{4,6},{5,7},{6,4},{7,5},{8,10},{9,11},{10,... | collective-permute-start | bytes 270344 | tf_op jit(solution)/shard_map/ppermute | solution.py:435
  45.4 1.5 %collective-permute-start.16 = (bf16[4,88,256]{2,1,0:T(8,128)(2,1)S(1)}, bf16[4,88,256]{2,1,0:T(8,128)(2,1)S(1)}, u32[]{:S(2)}, u32[]{:S(2)}) collective-permute-start(bf16[4,88,256]{2,1,0:T(8,128)(2,1)S(1)} %pad_maximum_fusion), channel_id=1, source_target_pairs={{0,8},{8,0},{16,24},{24,16},{1,9},{9,1},{17,25},{25,17},{2,10},{10... | collective-permute-start | bytes 540680 | tf_op jit(solution)/shard_map/ppermute | solution.py:433
